TPU v7x, 512 devices: a whole 4x4x16 slice. The times are simulated.
512 devices in a mesh: row: 8 (over x, y_lo), col: 16 (over z), rep: 4 (over y_hi, core).
Axes of the slice: x: 4, y: 4 (y_hi: 2, y_lo: 2; y = y_hi * 2 + y_lo), z: 16, core: 2. Of those that a mesh axis runs over, the one named last changes fastest.
Arguments:
- layer_input: bfloat16 [2048, 12288], P('col', ('row', 'rep')), may hold values from -0.75 to 0.75
- weight: bfloat16 [12288, 24576], P(('row', 'rep'), 'col'), may hold values from -0.0546875 to 0.0546875
- gelu_input: bfloat16 [2048, 24576], P(('row', 'rep'), 'col'), may hold values from -8 to 8
- upstream: bfloat16 [2048, 24576], P(('row', 'rep'), 'col'), may hold values from -6 to 6
Outputs:
- grad_input: bfloat16 [2048, 12288], P('col', ('row', 'rep'))
- grad_weight: float32 [12288, 24576], P(('row', 'rep'), 'col')
All inputs are finite; a program needn't handle non-finite values.
Results may differ from a plain program's by a relative error of at most 0.024.
Values may be sent and summed in bfloat16 or wider, within the bound.
No kernel may reach another device: no remote copies, remote signals or barrier semaphores. Data moves between devices by JAX's collectives and lax.ppermute only.
A program may use at most 64 MiB of HBM per device.

v0:
```python
import math

import jax
import jax.numpy as jnp
from jax import lax
from jax.sharding import PartitionSpec as P

cubic_term = 0.044715


def gelu_slope(values):
    scale = math.sqrt(2.0 / math.pi)
    inner = scale * (values + cubic_term * values * values * values)
    tangent = jnp.tanh(inner)
    return 0.5 * (1.0 + tangent) + 0.5 * values * (1.0 - tangent * tangent) * scale * (
        1.0 + 3.0 * cubic_term * values * values
    )


def local(layer_input, weight, gelu_input, upstream):
    gelu_grad = (upstream.astype(jnp.float32) * gelu_slope(gelu_input.astype(jnp.float32))).astype(
        jnp.bfloat16
    )
    input_whole = lax.all_gather(layer_input, "col", axis=0, tiled=True)
    grad_whole = lax.all_gather(gelu_grad, ("row", "rep"), axis=0, tiled=True)
    summed = lax.psum_scatter(
        lax.dot_general(
            grad_whole, weight, (((1,), (1,)), ((), ())), preferred_element_type=jnp.float32
        ).astype(jnp.bfloat16),
        "col",
        scatter_dimension=0,
        tiled=True,
    )
    grad_weight = lax.dot_general(
        input_whole, grad_whole, (((0,), (0,)), ((), ())), preferred_element_type=jnp.float32
    )
    return (summed, grad_weight)


def solution(mesh):
    in_specs = (
        P("col", ("row", "rep")),
        P(("row", "rep"), "col"),
        P(("row", "rep"), "col"),
        P(("row", "rep"), "col"),
    )
    out_specs = (P("col", ("row", "rep")), P(("row", "rep"), "col"))
    return jax.shard_map(local, mesh=mesh, in_specs=in_specs, out_specs=out_specs, check_vma=False)
```

profile of v0, /device:TPU:6, one launch (start us, length us, event | category | flops | bytes accessed | tf_op | source)
XLA Modules:
  0.0 239.0 jit_solution(18092450138063354621)
XLA Ops:
  7.2 0.0 copy-start
  7.2 0.0 all-gather.3.cloned.1.call-start
  7.2 2.1 fusion.7
  9.3 0.0 all-gather.3.cloned.1.call-update
  9.3 0.0 all-gather.5.cloned.1.call-start
  9.4 0.7 all-gather.5.cloned.1.call-update
  10.1 0.0 reduce-scatter.2.cloned.1.call-start
  10.1 75.5 %all-gather.3.cloned.1.call-done = bf16[2048,1536]{1,0:T(8,128)(2,1)} async-done(((bf16[64,1536]{1,0:T(8,128)(2,1)}), bf16[2048,1536]{1,0:T(8,128)(2,1)}) %all-gather.3.cloned.1.call-update) | async-done | bytes 6291472 | tf_op jit(solution)/shard_map/all_gather | solution.py:25
  85.6 0.0 copy-done
  85.6 7.5 %convolution_convert_fusion = bf16[2048,384]{1,0:T(8,128)(2,1)} fusion(bf16[2048,1536]{1,0:T(8,128)(2,1)} %all-gather.3.cloned.1.call-done, bf16[384,1536]{1,0:T(8,128)(2,1)S(1)} %copy-done), kind=kOutput, calls=%fused_computation.1 | convolution fusion | flops 2416705536 | bytes 9043968 | tf_op jit(solution)/shard_map/dot_general | solution.py:27
  93.1 0.0 reduce-scatter.2.cloned.1.call-update
  93.1 67.1 %all-gather.5.cloned.1.call-done = bf16[2048,384]{1,0:T(8,128)(2,1)} async-done(((bf16[128,384]{1,0:T(8,128)(2,1)}), bf16[2048,384]{1,0:T(8,128)(2,1)}) %all-gather.5.cloned.1.call-update) | async-done | bytes 1572880 | tf_op jit(solution)/shard_map/all_gather | solution.py:24
  160.2 6.0 %convolution_bitcast_fusion = f32[384,1536]{0,1:T(8,128)S(1)} fusion(bf16[2048,1536]{1,0:T(8,128)(2,1)} %all-gather.3.cloned.1.call-done, bf16[2048,384]{1,0:T(8,128)(2,1)} %all-gather.5.cloned.1.call-done), kind=kOutput, calls=%fused_computation | convolution fusion | flops 2415919104 | bytes 10223616 | tf_op jit(solution)/shard_map/dot_general | solution.py:34
  166.2 2.0 copy.6
  168.2 64.3 %reduce-scatter.2.cloned.1.call-done = bf16[128,384]{1,0:T(8,128)(2,1)} async-done(((bf16[2048,384]{1,0:T(8,128)(2,1)}), bf16[128,384]{1,0:T(8,128)(2,1)}) %reduce-scatter.2.cloned.1.call-update) | async-done | bytes 98320 | tf_op jit(solution)/shard_map/reduce_scatter | solution.py:26
Async XLA Ops:
  7.2 78.5 %copy-start = (bf16[384,1536]{1,0:T(8,128)(2,1)S(1)}, bf16[384,1536]{1,0:T(8,128)(2,1)}, u32[]{:S(2)}) copy-start(bf16[384,1536]{1,0:T(8,128)(2,1)} %param.5) | copy-start | bytes 3538948
  7.2 78.5 %all-gather.3.cloned.1.call-start = ((), (), s32[]{:S(2)}) async-start(), calls=%async_computation.1 | async-start | bytes 6488064 | tf_op jit(solution)/shard_map/all_gather | solution.py:25
  9.3 150.9 %all-gather.5.cloned.1.call-start = ((), (), s32[]{:S(2)}) async-start(), calls=%async_computation.3 | async-start | bytes 1671168 | tf_op jit(solution)/shard_map/all_gather | solution.py:24
  10.1 222.4 %reduce-scatter.2.cloned.1.call-start = ((), (), s32[]{:S(2)}) async-start(), calls=%async_computation.2 | async-start | bytes 1671168 | tf_op jit(solution)/shard_map/reduce_scatter | solution.py:26
Sparse Core Ops, SparseCore 0:
  10.7 74.8 all-gather.2
  87.7 72.4 all-gather.4
  163.6 68.8 reduce-scatter.1
where the time goes:
time: 239 us
  waiting for transfers between devices  208 us (87%)
  between operations  13.8 us (6%)
  matrix products  13.5 us (6%)
    all_gather x1, waiting for transfers between devices, local(): grad_whole = lax.all_gather(gelu_grad, ('row', 'rep'), axis=0, tiled=True)  75.5 us
    all_gather x1, waiting for transfers between devices, local(): input_whole = lax.all_gather(layer_input, 'col', axis=0, tiled=True)  67.1 us
    reduce_scatter x1, waiting for transfers between devices, local(): lax.psum_scatter(lax.dot_general(grad_whole, weight, (((1,), (1,)), ((),...  64.3 us
    dot_general x1, matrix products, local(): lax.dot_general(grad_whole, weight, (((1,), (1,)), ((), ())), preferred_e...  7.47 us
    dot_general x1, matrix products, local(): lax.dot_general(input_whole, grad_whole, (((0,), (0,)), ((), ())), prefer...  6 us
  transfers between devices with their start and end apart: 3, of which 3 were waited for; matrix products, arithmetic and copies ran while one was open for 6% of the time, Pallas kernels for 0%

commit v1 on v0

v1 whole, which is shorter than its diff:
```python
import functools
import math

import jax
import jax.numpy as jnp
import numpy as np
from jax import lax
from jax.experimental import pallas as pl
from jax.experimental.pallas import tpu as pltpu
from jax.sharding import PartitionSpec as P

cubic_term = 0.044715
plane = ("row", "rep")
ring = ("col", "rep")


def gelu_slope(values):
    scale = math.sqrt(2.0 / math.pi)
    inner = scale * (values + cubic_term * values * values * values)
    tangent = jnp.tanh(inner)
    return 0.5 * (1.0 + tangent) + 0.5 * values * (1.0 - tangent * tangent) * scale * (
        1.0 + 3.0 * cubic_term * values * values
    )


def index(x, y, core):
    return ((x * 2 + y % 2) * 2 + y // 2) * 2 + core


y_order = (0, 2, 1, 3)
along_x = [[[index(x, y, core) for x in range(4)] for y in y_order] for core in range(2)]
along_y = [[[index(x, y, core) for y in y_order] for x in range(4)] for core in range(2)]


early_steps = (7, 5, 3, 1, 8, -7, -5, -3, -1)
late_steps = (6, 4, 2, 0, -6, -4, -2)


def order_of(steps):
    table = np.zeros((32, len(steps)), np.int32)
    for z in range(16):
        for i, step in enumerate(steps):
            up, down = (z + step) % 16, (z - step) % 16
            table[z * 2, i] = (up % 4) * 4 + up // 4
            table[z * 2 + 1, i] = down
    return table


def gather(values, groups):
    copies = jnp.broadcast_to(values[None], (4,) + values.shape)
    parts = lax.all_to_all(copies, plane, 0, 0, axis_index_groups=groups)
    return parts.reshape((4 * values.shape[0],) + values.shape[1:])


def swap_cores(values):
    return lax.ppermute(values, "rep", [(0, 1), (1, 0), (2, 3), (3, 2)])


def send(values, distance):
    pairs = []
    for z in range(16):
        for rep in range(4):
            target = (z + (-distance if rep % 2 else distance)) % 16
            pairs.append((z * 4 + rep, target * 4 + rep))
    return lax.ppermute(values, ring, pairs)


def matmul_nt(a, b):
    return lax.dot_general(a, b, (((1,), (1,)), ((), ())), preferred_element_type=jnp.float32)


def matmul_tn(a, b):
    return lax.dot_general(a, b, (((0,), (0,)), ((), ())), preferred_element_type=jnp.float32)


def partial_kernel(groups, order_ref, grad_ref, own_ref, other_ref, out_ref):
    width = own_ref.shape[0]
    for start, count, flipped in groups:
        rows = jnp.concatenate([grad_ref[order_ref[start + i]] for i in range(count)], axis=0)
        for side, ref in enumerate((other_ref, own_ref) if flipped else (own_ref, other_ref)):
            part = matmul_nt(rows, ref[...]).astype(out_ref.dtype)
            out_ref[start : start + count, :, side * width : (side + 1) * width] = part.reshape(
                count, -1, width
            )


def partials(order, grad_blocks, weight_own, weight_other, groups):
    count = sum(g[1] for g in groups)
    rows, depth = grad_blocks.shape[1:]
    width = weight_own.shape[0]
    vmem = pl.BlockSpec(memory_space=pltpu.VMEM)
    return pl.pallas_call(
        functools.partial(partial_kernel, groups),
        out_shape=jax.ShapeDtypeStruct((count, rows, 2 * width), jnp.bfloat16),
        in_specs=[pl.BlockSpec(memory_space=pltpu.SMEM), vmem, vmem, vmem],
        out_specs=vmem,
        compiler_params=pltpu.CompilerParams(vmem_limit_bytes=32 * 1024 * 1024),
        cost_estimate=pl.CostEstimate(
            flops=4 * count * rows * depth * width,
            bytes_accessed=2 * (grad_blocks.size + 2 * width * depth + 2 * count * rows * width),
            transcendentals=0,
        ),
    )(order, grad_blocks, weight_own, weight_other)


def local(layer_input, weight, gelu_input, upstream):
    core = lax.axis_index("rep") % 2
    z = lax.axis_index("col")
    first = core == 0
    tokens, width = layer_input.shape
    half = tokens // 2
    f32, bf16 = jnp.float32, jnp.bfloat16

    input_whole = lax.all_gather(layer_input, "col", axis=0, tiled=True)
    weight_other = swap_cores(weight)
    gelu_grad = (upstream.astype(f32) * gelu_slope(gelu_input.astype(f32))).astype(bf16)

    line = gather(gelu_grad, along_x[0] + along_y[1])
    grad_tokens = gather(line, along_y[0] + along_x[1])
    grad_blocks = grad_tokens.reshape((16, half) + grad_tokens.shape[1:])

    early = lax.dynamic_index_in_dim(jnp.asarray(order_of(early_steps)), z * 2 + core, 0, False)
    late = lax.dynamic_index_in_dim(jnp.asarray(order_of(late_steps)), z * 2 + core, 0, False)
    ahead = partials(
        early, grad_blocks, weight, weight_other, ((0, 4, False), (4, 1, False), (5, 4, True))
    )
    from_sibling = swap_cores(ahead[5:])
    rest = partials(late, grad_blocks, weight, weight_other, ((0, 4, False), (4, 3, True)))
    rest_sibling = swap_cores(rest[4:])

    moved = send(jnp.concatenate([ahead[:4], from_sibling]), 1).reshape(2, 4, half, 2 * width)
    moved_far = send(ahead[4], 2)
    sums = [
        moved[:, i].astype(f32) + jnp.stack([rest[i], rest_sibling[i]]).astype(f32)
        for i in range(3)
    ]
    sums[0] = sums[0].at[0].add(moved_far.astype(f32))
    here = moved[:, 3].astype(f32).at[0].add(rest[3].astype(f32))
    moved = send(jnp.stack([sums[0], sums[2]]).astype(bf16), 2)
    moved, input_whole = lax.optimization_barrier((moved, input_whole))
    here = here + moved[1].astype(f32)
    moved = send((sums[1] + moved[0].astype(f32)).astype(bf16), 4)
    here = here + moved.astype(f32)

    from_other = swap_cores(here[:, :, width:].astype(bf16)).astype(f32)
    own = here[0, :, :width] + from_other[1]
    other = here[1, :, :width] + from_other[0]
    grad_input = jnp.where(
        first, jnp.concatenate([own, other]), jnp.concatenate([other, own])
    ).astype(bf16)

    blocks = input_whole.reshape(16, 2, half, width)
    mine = lax.dynamic_index_in_dim(blocks, core, 1, keepdims=False)
    other = swap_cores(lax.dynamic_index_in_dim(blocks, 1 - core, 1, keepdims=False))

    def ordered(values):
        chips = values.reshape(4, 4, half, width)
        return jnp.where(first, jnp.swapaxes(chips, 0, 1), chips).reshape(16 * half, width)

    sibling = swap_cores(matmul_tn(ordered(other), grad_tokens))
    grad_weight = matmul_tn(ordered(mine), grad_tokens) + sibling
    return (grad_input, grad_weight)


def solution(mesh):
    in_specs = (
        P("col", ("row", "rep")),
        P(("row", "rep"), "col"),
        P(("row", "rep"), "col"),
        P(("row", "rep"), "col"),
    )
    out_specs = (P("col", ("row", "rep")), P(("row", "rep"), "col"))
    return jax.shard_map(local, mesh=mesh, in_specs=in_specs, out_specs=out_specs, check_vma=False)
```

time: 239 us -> 157 us (0.66)
  the two profiles are of different devices: /device:TPU:6 before, /device:TPU:1 now
where the time goes in v1:
time: 157 us; the launch traced here: 156 us
  starting transfers between devices  58.8 us (37%)
  waiting for transfers between devices  40.8 us (26%)
  between operations  14.3 us (9%)
  blocking collectives  12.9 us (8%)
  other arithmetic  10.3 us (7%)
  local copies, waits for them, and re-layouts  8.74 us (6%)
  Pallas kernels  6.8 us (4%)
  matrix products  2.85 us (2%)
    ppermute x6, starting transfers between devices, swap_cores(): return lax.ppermute(values, 'rep', [(0, 1), (1, 0), (2, 3), (3, 2)])  32.8 us
    ppermute x4, starting transfers between devices, send(): return lax.ppermute(values, ring, pairs)  21.9 us
    ppermute x4, waiting for transfers between devices, send(): return lax.ppermute(values, ring, pairs)  19 us
    all_to_all x1, blocking collectives, gather(): parts = lax.all_to_all(copies, plane, 0, 0, axis_index_groups=groups)  12.9 us
    all_to_all x1, waiting for transfers between devices, gather(): parts = lax.all_to_all(copies, plane, 0, 0, axis_index_groups=groups)  10.7 us
    pallas_call x2, Pallas kernels, partials(): pl.pallas_call(functools.partial(partial_kernel, groups), out_shape=jax.S...  6.8 us
    all_gather x1, waiting for transfers between devices, local(): input_whole = lax.all_gather(layer_input, 'col', axis=0, tiled=True)  6.12 us
    ppermute x6, waiting for transfers between devices, swap_cores(): return lax.ppermute(values, 'rep', [(0, 1), (1, 0), (2, 3), (3, 2)])  4.91 us
  transfers between devices with their start and end apart: 12, of which 9 were waited for; matrix products, arithmetic and copies ran while one was open for 6% of the time, Pallas kernels for 4%

profile of v1, /device:TPU:1, one launch (start us, length us, event | category | flops | bytes accessed | tf_op | source)
XLA Modules:
  0.0 155.5 jit_solution(14216508203009199453)
XLA Ops:
  8.5 12.9 %all_to_all.10 = bf16[4,64,1536]{2,1,0:T(8,128)(2,1)S(1)} all-to-all(bf16[4,64,1536]{2,1,0:T(8,128)(2,1)S(1)} %broadcast_in_dim.6), channel_id=1, replica_groups={{0,128,256,384},{2,130,258,386},{64,192,320,448},{66,194,322,450},{1,3,..., dimensions={0} | all-to-all | bytes 1572864 | tf_op jit(solution)/shard_map/all_to_all | solution.py:51
  21.4 1.9 %broadcast_in_dim.15 = bf16[4,256,1536]{2,1,0:T(8,128)(2,1)} broadcast(bf16[256,1536]{1,0:T(8,128)(2,1)S(1)} %bitcast.97), dimensions={1,2} | broadcast | bytes 3932160 | tf_op jit(solution)/shard_map/broadcast_in_dim | solution.py:50
  23.3 4.2 %all-to-all-start.1 = ((bf16[4,256,1536]{2,1,0:T(8,128)(2,1)}), bf16[4,256,1536]{2,1,0:T(8,128)(2,1)S(1)}, u32[]{:S(2)}, u32[]{:S(2)}) async-start(bf16[4,256,1536]{2,1,0:T(8,128)(2,1)} %broadcast_in_dim.15), calls=%async_computation.1 | async-start | bytes 6291456 | tf_op jit(solution)/shard_map/all_to_all | solution.py:51
  27.4 7.4 %collective-permute-start = (bf16[384,1536]{1,0:T(8,128)(2,1)}, bf16[384,1536]{1,0:T(8,128)(2,1)}, u32[]{:S(2)}, u32[]{:S(2)}) collective-permute-start(bf16[384,1536]{1,0:T(8,128)(2,1)} %own_ref.3), channel_id=1, source_target_pairs={{0,1},{1,0},{2,3},{3,2},{4,5},{5,4},{6,7},{7,6},{8,9},{9,8},{10,11... | collective-permute-start | bytes 3538952 | tf_op jit(solution)/shard_map/ppermute | solution.py:56
  35.6 2.1 %collective-permute-done.other_ref = bf16[384,1536]{1,0:T(8,128)(2,1)} collective-permute-done((bf16[384,1536]{1,0:T(8,128)(2,1)}, bf16[384,1536]{1,0:T(8,128)(2,1)}, u32[]{:S(2)}, u32[]{:S(2)}) %collective-permute-start) | collective-permute-done | bytes 1179680 | tf_op jit(solution)/shard_map/ppermute | solution.py:56
  37.6 10.7 %all-to-all-done.1 = bf16[4,256,1536]{2,1,0:T(8,128)(2,1)S(1)} async-done(((bf16[4,256,1536]{2,1,0:T(8,128)(2,1)}), bf16[4,256,1536]{2,1,0:T(8,128)(2,1)S(1)}, u32[]{:S(2)}, u32[]{:S(2)}) %all-to-all-start.1) | async-done | bytes 3145760 | tf_op jit(solution)/shard_map/all_to_all | solution.py:51
  49.7 3.8 %shard_map.77 = bf16[9,64,768]{2,1,0:T(8,128)(2,1)S(1)} custom-call(s32[9]{0:T(128)S(1)} %fusion.22.order_ref, bf16[16,64,1536]{2,1,0:T(8,128)(2,1)S(1)} %bitcast.91, bf16[384,1536]{1,0:T(8,128)(2,1)S(1)} %copy-done, bf16[384,1536]{1,0:T(8,128)(2,1)} %collective-permute-done.other_ref), custom_call_target="tpu_custom_call" | custom-call | flops 1358954496 | bytes 6389760 | tf_op jit(solution)/shard_map/pallas_call | solution.py:92
  53.5 8.2 %collective-permute-start.1 = (bf16[4,64,768]{2,1,0:T(8,128)(2,1)S(1)}, bf16[4,64,768]{2,1,0:T(8,128)(2,1)S(1)}, u32[]{:S(2)}, u32[]{:S(2)}) collective-permute-start(bf16[4,64,768]{2,1,0:T(8,128)(2,1)S(1)} %get-tuple-element.33), channel_id=1, source_target_pairs={{0,1},{1,0},{2,3},{3,2},{4,5},{5,4},{6,7},{7,6},{8,9},{9,8},{10,11... | collective-permute-start | bytes 1179656 | tf_op jit(solution)/shard_map/ppermute | solution.py:56
  63.1 8.2 %collective-permute-start.2 = (bf16[8,64,768]{2,1,0:T(8,128)(2,1)S(1)}, bf16[8,64,768]{2,1,0:T(8,128)(2,1)S(1)}, u32[]{:S(2)}, u32[]{:S(2)}) collective-permute-start(bf16[8,64,768]{2,1,0:T(8,128)(2,1)S(1)} %pad_maximum_fusion), channel_id=1, source_target_pairs={{0,4},{1,61},{2,6},{3,63},{4,8},{5,1},{6,10},{7,3},{8,12},{9,5},{1... | collective-permute-start | bytes 2359304 | tf_op jit(solution)/shard_map/ppermute | solution.py:65
  71.4 3.0 %shard_map.78 = bf16[7,64,768]{2,1,0:T(8,128)(2,1)S(1)} custom-call(s32[7]{0:T(128)S(1)} %fusion.23.order_ref, bf16[16,64,1536]{2,1,0:T(8,128)(2,1)S(1)} %bitcast.92, bf16[384,1536]{1,0:T(8,128)(2,1)S(1)} %copy-done, bf16[384,1536]{1,0:T(8,128)(2,1)} %collective-permute-done.other_ref), custom_call_target="tpu_custom_call" | custom-call | flops 1056964608 | bytes 6193152 | tf_op jit(solution)/shard_map/pallas_call | solution.py:92
  74.4 1.9 %collective-permute-start.3 = (bf16[3,64,768]{2,1,0:T(8,128)(2,1)S(1)}, bf16[3,64,768]{2,1,0:T(8,128)(2,1)S(1)}, u32[]{:S(2)}, u32[]{:S(2)}) collective-permute-start(bf16[3,64,768]{2,1,0:T(8,128)(2,1)S(1)} %slice.143), channel_id=1, source_target_pairs={{0,1},{1,0},{2,3},{3,2},{4,5},{5,4},{6,7},{7,6},{8,9},{9,8},{10,11... | collective-permute-start | bytes 884744 | tf_op jit(solution)/shard_map/ppermute | solution.py:56
  76.4 3.7 %collective-permute-start.4 = (bf16[64,768]{1,0:T(8,128)(2,1)S(1)}, bf16[64,768]{1,0:T(8,128)(2,1)S(1)}, u32[]{:S(2)}, u32[]{:S(2)}) collective-permute-start(bf16[64,768]{1,0:T(8,128)(2,1)S(1)} %slice_bitcast_fusion.6), channel_id=1, source_target_pairs={{0,8},{1,57},{2,10},{3,59},{4,12},{5,61},{6,14},{7,63},{8,16},{9,1... | collective-permute-start | bytes 294920 | tf_op jit(solution)/shard_map/ppermute | solution.py:65
  81.4 4.3 %collective-permute-done.2 = bf16[8,64,768]{2,1,0:T(8,128)(2,1)S(1)} collective-permute-done((bf16[8,64,768]{2,1,0:T(8,128)(2,1)S(1)}, bf16[8,64,768]{2,1,0:T(8,128)(2,1)S(1)}, u32[]{:S(2)}, u32[]{:S(2)}) %collective-permute-start.2) | collective-permute-done | bytes 786464 | tf_op jit(solution)/shard_map/ppermute | solution.py:65
  88.2 5.9 %collective-permute-start.5 = (bf16[2,2,64,768]{3,2,1,0:T(8,128)(2,1)}, bf16[2,2,64,768]{3,2,1,0:T(8,128)(2,1)}, u32[]{:S(2)}, u32[]{:S(2)}) collective-permute-start(bf16[2,2,64,768]{3,2,1,0:T(8,128)(2,1)} %pad_maximum_fusion.1), channel_id=1, source_target_pairs={{0,8},{1,57},{2,10},{3,59},{4,12},{5,61},{6,14},{7,63},{8,16},{9,1... | collective-permute-start | bytes 1179656 | tf_op jit(solution)/shard_map/ppermute | solution.py:65
  94.2 6.1 %all-gather.2.cloned.1.call-done = bf16[2048,384]{1,0:T(8,128)(2,1)} async-done(((bf16[128,384]{1,0:T(8,128)(2,1)}), bf16[2048,384]{1,0:T(8,128)(2,1)}) %all-gather.2.cloned.1.call-update) | async-done | bytes 1572880 | tf_op jit(solution)/shard_map/all_gather | solution.py:114
  100.3 2.8 %collective-permute-done.5 = bf16[2,2,64,768]{3,2,1,0:T(8,128)(2,1)} collective-permute-done((bf16[2,2,64,768]{3,2,1,0:T(8,128)(2,1)}, bf16[2,2,64,768]{3,2,1,0:T(8,128)(2,1)}, u32[]{:S(2)}, u32[]{:S(2)}) %collective-permute-start.5) | collective-permute-done | bytes 393248 | tf_op jit(solution)/shard_map/ppermute | solution.py:65
  103.1 2.7 %dynamic-slice_bitcast_fusion = (bf16[16,64,384]{2,1,0:T(8,128)(2,1)}, bf16[16,1,64,384]{3,2,1,0:T(8,128)(2,1)}) fusion(bf16[16,2,64,384]{3,2,1,0:T(8,128)(2,1)} %bitcast.98, s32[]{:T(128)S(6)} %select_n.47, s32[]{:T(128)S(6)} %select_n.45), kind=kLoop, calls=%fused_computation.10 | loop fusion | bytes 3145736 | tf_op jit(solution)/shard_map/jit(dynamic_index_in_dim)/squeeze | solution.py:154
  105.8 11.0 %collective-permute-start.8 = (bf16[16,64,384]{2,1,0:T(8,128)(2,1)}, bf16[16,64,384]{2,1,0:T(8,128)(2,1)}, u32[]{:S(2)}, u32[]{:S(2)}) collective-permute-start(bf16[16,64,384]{2,1,0:T(8,128)(2,1)} %get-tuple-element.30), channel_id=1, source_target_pairs={{0,1},{1,0},{2,3},{3,2},{4,5},{5,4},{6,7},{7,6},{8,9},{9,8},{10,11... | collective-permute-start | bytes 2359304 | tf_op jit(solution)/shard_map/ppermute | solution.py:56
  116.8 2.2 %collective-permute-done.8 = bf16[16,64,384]{2,1,0:T(8,128)(2,1)} collective-permute-done((bf16[16,64,384]{2,1,0:T(8,128)(2,1)}, bf16[16,64,384]{2,1,0:T(8,128)(2,1)}, u32[]{:S(2)}, u32[]{:S(2)}) %collective-permute-start.8) | collective-permute-done | bytes 786464 | tf_op jit(solution)/shard_map/ppermute | solution.py:56
  121.9 2.3 %collective-permute-start.9 = (f32[384,1536]{1,0:T(8,128)S(1)}, f32[384,1536]{1,0:T(8,128)S(1)}, u32[]{:S(2)}, u32[]{:S(2)}) collective-permute-start(f32[384,1536]{1,0:T(8,128)S(1)} %fusion.28), channel_id=1, source_target_pairs={{0,1},{1,0},{2,3},{3,2},{4,5},{5,4},{6,7},{7,6},{8,9},{9,8},{10,11... | collective-permute-start | bytes 7077896 | tf_op jit(solution)/shard_map/ppermute | solution.py:56
  126.3 4.0 %collective-permute-start.6 = (bf16[2,64,768]{2,1,0:T(8,128)(2,1)S(1)}, bf16[2,64,768]{2,1,0:T(8,128)(2,1)S(1)}, u32[]{:S(2)}, u32[]{:S(2)}) collective-permute-start(bf16[2,64,768]{2,1,0:T(8,128)(2,1)S(1)} %fusion.10), channel_id=1, source_target_pairs={{0,16},{1,49},{2,18},{3,51},{4,20},{5,53},{6,22},{7,55},{8,24},{9,... | collective-permute-start | bytes 589832 | tf_op jit(solution)/shard_map/ppermute | solution.py:65
  130.4 11.4 %collective-permute-done.6 = bf16[2,64,768]{2,1,0:T(8,128)(2,1)S(1)} collective-permute-done((bf16[2,64,768]{2,1,0:T(8,128)(2,1)S(1)}, bf16[2,64,768]{2,1,0:T(8,128)(2,1)S(1)}, u32[]{:S(2)}, u32[]{:S(2)}) %collective-permute-start.6) | collective-permute-done | bytes 196640 | tf_op jit(solution)/shard_map/ppermute | solution.py:65
  142.8 1.9 %collective-permute-start.7 = (bf16[2,64,384]{2,1,0:T(8,128)(2,1)S(1)}, bf16[2,64,384]{2,1,0:T(8,128)(2,1)S(1)}, u32[]{:S(2)}, u32[]{:S(2)}) collective-permute-start(bf16[2,64,384]{2,1,0:T(8,128)(2,1)S(1)} %slice.201), channel_id=1, source_target_pairs={{0,1},{1,0},{2,3},{3,2},{4,5},{5,4},{6,7},{7,6},{8,9},{9,8},{10,11... | collective-permute-start | bytes 294920 | tf_op jit(solution)/shard_map/ppermute | solution.py:56
  146.9 1.8 %add.119 = f32[384,1536]{1,0:T(8,128)} add(f32[384,1536]{1,0:T(8,128)S(1)} %fusion.27, f32[384,1536]{1,0:T(8,128)S(1)} %collective-permute-done.9) | non-fusion elementwise | flops 589824 | bytes 7077888 | tf_op jit(solution)/shard_map/add | solution.py:161
  (47 shorter events, 16.8 us)
Async XLA Ops:
  23.3 25.1 %all-to-all-start.1 = ((bf16[4,256,1536]{2,1,0:T(8,128)(2,1)}), bf16[4,256,1536]{2,1,0:T(8,128)(2,1)S(1)}, u32[]{:S(2)}, u32[]{:S(2)}) async-start(bf16[4,256,1536]{2,1,0:T(8,128)(2,1)} %broadcast_in_dim.15), calls=%async_computation.1 | async-start | bytes 6291456 | tf_op jit(solution)/shard_map/all_to_all | solution.py:51
  27.4 72.9 %all-gather.2.cloned.1.call-start = ((), (), s32[]{:S(2)}) async-start(), calls=%async_computation.2 | async-start | bytes 1671168 | tf_op jit(solution)/shard_map/all_gather | solution.py:114
  27.4 10.2 %collective-permute-start = (bf16[384,1536]{1,0:T(8,128)(2,1)}, bf16[384,1536]{1,0:T(8,128)(2,1)}, u32[]{:S(2)}, u32[]{:S(2)}) collective-permute-start(bf16[384,1536]{1,0:T(8,128)(2,1)} %own_ref.3), channel_id=1, source_target_pairs={{0,1},{1,0},{2,3},{3,2},{4,5},{5,4},{6,7},{7,6},{8,9},{9,8},{10,11... | collective-permute-start | bytes 3538952 | tf_op jit(solution)/shard_map/ppermute | solution.py:56
  48.4 1.3 copy-start
  53.5 9.5 %collective-permute-start.1 = (bf16[4,64,768]{2,1,0:T(8,128)(2,1)S(1)}, bf16[4,64,768]{2,1,0:T(8,128)(2,1)S(1)}, u32[]{:S(2)}, u32[]{:S(2)}) collective-permute-start(bf16[4,64,768]{2,1,0:T(8,128)(2,1)S(1)} %get-tuple-element.33), channel_id=1, source_target_pairs={{0,1},{1,0},{2,3},{3,2},{4,5},{5,4},{6,7},{7,6},{8,9},{9,8},{10,11... | collective-permute-start | bytes 1179656 | tf_op jit(solution)/shard_map/ppermute | solution.py:56
  63.1 22.6 %collective-permute-start.2 = (bf16[8,64,768]{2,1,0:T(8,128)(2,1)S(1)}, bf16[8,64,768]{2,1,0:T(8,128)(2,1)S(1)}, u32[]{:S(2)}, u32[]{:S(2)}) collective-permute-start(bf16[8,64,768]{2,1,0:T(8,128)(2,1)S(1)} %pad_maximum_fusion), channel_id=1, source_target_pairs={{0,4},{1,61},{2,6},{3,63},{4,8},{5,1},{6,10},{7,3},{8,12},{9,5},{1... | collective-permute-start | bytes 2359304 | tf_op jit(solution)/shard_map/ppermute | solution.py:65
  74.4 12.4 %copy-start.1 = (bf16[7,64,768]{2,1,0:T(8,128)(2,1)}, bf16[7,64,768]{2,1,0:T(8,128)(2,1)S(1)}, u32[]{:S(2)}) copy-start(bf16[7,64,768]{2,1,0:T(8,128)(2,1)S(1)} %shard_map.78) | copy-start | bytes 2064388
  74.4 6.4 %collective-permute-start.3 = (bf16[3,64,768]{2,1,0:T(8,128)(2,1)S(1)}, bf16[3,64,768]{2,1,0:T(8,128)(2,1)S(1)}, u32[]{:S(2)}, u32[]{:S(2)}) collective-permute-start(bf16[3,64,768]{2,1,0:T(8,128)(2,1)S(1)} %slice.143), channel_id=1, source_target_pairs={{0,1},{1,0},{2,3},{3,2},{4,5},{5,4},{6,7},{7,6},{8,9},{9,8},{10,11... | collective-permute-start | bytes 884744 | tf_op jit(solution)/shard_map/ppermute | solution.py:56
  76.4 11.0 %collective-permute-start.4 = (bf16[64,768]{1,0:T(8,128)(2,1)S(1)}, bf16[64,768]{1,0:T(8,128)(2,1)S(1)}, u32[]{:S(2)}, u32[]{:S(2)}) collective-permute-start(bf16[64,768]{1,0:T(8,128)(2,1)S(1)} %slice_bitcast_fusion.6), channel_id=1, source_target_pairs={{0,8},{1,57},{2,10},{3,59},{4,12},{5,61},{6,14},{7,63},{8,16},{9,1... | collective-permute-start | bytes 294920 | tf_op jit(solution)/shard_map/ppermute | solution.py:65
  85.7 1.7 %copy-start.3 = (bf16[8,64,768]{2,1,0:T(8,128)(2,1)}, bf16[8,64,768]{2,1,0:T(8,128)(2,1)S(1)}, u32[]{:S(2)}) copy-start(bf16[8,64,768]{2,1,0:T(8,128)(2,1)S(1)} %collective-permute-done.2) | copy-start | bytes 2359300
  88.2 14.8 %collective-permute-start.5 = (bf16[2,2,64,768]{3,2,1,0:T(8,128)(2,1)}, bf16[2,2,64,768]{3,2,1,0:T(8,128)(2,1)}, u32[]{:S(2)}, u32[]{:S(2)}) collective-permute-start(bf16[2,2,64,768]{3,2,1,0:T(8,128)(2,1)} %pad_maximum_fusion.1), channel_id=1, source_target_pairs={{0,8},{1,57},{2,10},{3,59},{4,12},{5,61},{6,14},{7,63},{8,16},{9,1... | collective-permute-start | bytes 1179656 | tf_op jit(solution)/shard_map/ppermute | solution.py:65
  105.8 13.2 %collective-permute-start.8 = (bf16[16,64,384]{2,1,0:T(8,128)(2,1)}, bf16[16,64,384]{2,1,0:T(8,128)(2,1)}, u32[]{:S(2)}, u32[]{:S(2)}) collective-permute-start(bf16[16,64,384]{2,1,0:T(8,128)(2,1)} %get-tuple-element.30), channel_id=1, source_target_pairs={{0,1},{1,0},{2,3},{3,2},{4,5},{5,4},{6,7},{7,6},{8,9},{9,8},{10,11... | collective-permute-start | bytes 2359304 | tf_op jit(solution)/shard_map/ppermute | solution.py:56
  120.5 3.8 %copy-start.4 = (f32[2,1,64,768]{3,2,1,0:T(8,128)S(1)}, f32[2,1,64,768]{3,2,1,0:T(8,128)}, u32[]{:S(2)}) copy-start(f32[2,1,64,768]{3,2,1,0:T(8,128)} %get-tuple-element.36) | copy-start | bytes 1179652
  120.5 4.7 %copy-start.5 = (bf16[1,64,768]{2,1,0:T(8,128)(2,1)S(1)}, bf16[1,64,768]{2,1,0:T(8,128)(2,1)}, u32[]{:S(2)}) copy-start(bf16[1,64,768]{2,1,0:T(8,128)(2,1)} %get-tuple-element.39) | copy-start | bytes 294916
  120.5 4.7 %copy-start.6 = (bf16[1,64,768]{2,1,0:T(8,128)(2,1)S(1)}, bf16[1,64,768]{2,1,0:T(8,128)(2,1)}, u32[]{:S(2)}) copy-start(bf16[1,64,768]{2,1,0:T(8,128)(2,1)} %get-tuple-element.45) | copy-start | bytes 294916
  120.5 9.8 %copy-start.2 = (bf16[16,1,64,384]{3,2,1,0:T(8,128)(2,1)S(1)}, bf16[16,1,64,384]{3,2,1,0:T(8,128)(2,1)}, u32[]{:S(2)}) copy-start(bf16[16,1,64,384]{3,2,1,0:T(8,128)(2,1)} %get-tuple-element.31) | copy-start | bytes 2359300
  121.9 25.0 %collective-permute-start.9 = (f32[384,1536]{1,0:T(8,128)S(1)}, f32[384,1536]{1,0:T(8,128)S(1)}, u32[]{:S(2)}, u32[]{:S(2)}) collective-permute-start(f32[384,1536]{1,0:T(8,128)S(1)} %fusion.28), channel_id=1, source_target_pairs={{0,1},{1,0},{2,3},{3,2},{4,5},{5,4},{6,7},{7,6},{8,9},{9,8},{10,11... | collective-permute-start | bytes 7077896 | tf_op jit(solution)/shard_map/ppermute | solution.py:56
  126.3 15.5 %collective-permute-start.6 = (bf16[2,64,768]{2,1,0:T(8,128)(2,1)S(1)}, bf16[2,64,768]{2,1,0:T(8,128)(2,1)S(1)}, u32[]{:S(2)}, u32[]{:S(2)}) collective-permute-start(bf16[2,64,768]{2,1,0:T(8,128)(2,1)S(1)} %fusion.10), channel_id=1, source_target_pairs={{0,16},{1,49},{2,18},{3,51},{4,20},{5,53},{6,22},{7,55},{8,24},{9,... | collective-permute-start | bytes 589832 | tf_op jit(solution)/shard_map/ppermute | solution.py:65
  142.8 3.4 %collective-permute-start.7 = (bf16[2,64,384]{2,1,0:T(8,128)(2,1)S(1)}, bf16[2,64,384]{2,1,0:T(8,128)(2,1)S(1)}, u32[]{:S(2)}, u32[]{:S(2)}) collective-permute-start(bf16[2,64,384]{2,1,0:T(8,128)(2,1)S(1)} %slice.201), channel_id=1, source_target_pairs={{0,1},{1,0},{2,3},{3,2},{4,5},{5,4},{6,7},{7,6},{8,9},{9,8},{10,11... | collective-permute-start | bytes 294920 | tf_op jit(solution)/shard_map/ppermute | solution.py:56
Sparse Core Ops, SparseCore 0:
  35.0 65.2 all-gather.1

commit v2 on v1

--- a/solution.py
+++ b/solution.py
@@ -34,6 +34,7 @@
 
 early_steps = (7, 5, 3, 1, 8, -7, -5, -3, -1)
 late_steps = (6, 4, 2, 0, -6, -4, -2)
+input_steps = (0, 2, 4, 6, 1, 3, 5, 7, 8, -2, -4, -6, -1, -3, -5, -7)
 
 
 def order_of(steps):
@@ -44,6 +45,10 @@
             table[z * 2, i] = (up % 4) * 4 + up // 4
             table[z * 2 + 1, i] = down
     return table
+
+
+def input_order():
+    return np.argsort(order_of(input_steps), axis=1).astype(np.int32)
 
 
 def gather(values, groups):
@@ -103,6 +108,42 @@
     )(order, grad_blocks, weight_own, weight_other)
 
 
+def weight_kernel(side, add, order_ref, input_ref, grad_ref, *rest):
+    sibling_ref = rest[0] if add else None
+    out_ref, rows_ref = rest[-2:]
+    width, half = out_ref.shape[0], input_ref.shape[1]
+    for i in range(16):
+        block = input_ref[order_ref[i]]
+        rows_ref[i * half : (i + 1) * half, :] = block[:, side * width : (side + 1) * width]
+    tile = 256
+    for start in range(0, out_ref.shape[1], tile):
+        grad = grad_ref[:, :, start : start + tile].reshape(16 * half, tile)
+        part = matmul_tn(rows_ref[...], grad)
+        if add:
+            part = part + sibling_ref[:, start : start + tile]
+        out_ref[:, start : start + tile] = part
+
+
+def weight_part(order, input_blocks, grad_blocks, side, sibling=None):
+    rows, both = input_blocks.shape[1:]
+    width, depth = both // 2, grad_blocks.shape[2]
+    vmem = pl.BlockSpec(memory_space=pltpu.VMEM)
+    more = () if sibling is None else (sibling,)
+    return pl.pallas_call(
+        functools.partial(weight_kernel, side, sibling is not None),
+        out_shape=jax.ShapeDtypeStruct((width, depth), jnp.float32),
+        in_specs=[pl.BlockSpec(memory_space=pltpu.SMEM)] + [vmem] * (2 + len(more)),
+        out_specs=vmem,
+        scratch_shapes=[pltpu.VMEM((16 * rows, width), jnp.bfloat16)],
+        compiler_params=pltpu.CompilerParams(vmem_limit_bytes=32 * 1024 * 1024),
+        cost_estimate=pl.CostEstimate(
+            flops=2 * 16 * rows * width * depth,
+            bytes_accessed=2 * (grad_blocks.size + 16 * rows * width) + 4 * width * depth,
+            transcendentals=0,
+        ),
+    )(order, input_blocks, grad_blocks, *more)
+
+
 def local(layer_input, weight, gelu_input, upstream):
     core = lax.axis_index("rep") % 2
     z = lax.axis_index("col")
@@ -111,13 +152,24 @@
     half = tokens // 2
     f32, bf16 = jnp.float32, jnp.bfloat16
 
-    input_whole = lax.all_gather(layer_input, "col", axis=0, tiled=True)
+    gelu_grad = (upstream.astype(f32) * gelu_slope(gelu_input.astype(f32))).astype(bf16)
     weight_other = swap_cores(weight)
-    gelu_grad = (upstream.astype(f32) * gelu_slope(gelu_input.astype(f32))).astype(bf16)
+
+    block = jnp.concatenate(
+        [v.reshape(2, half, width) for v in (layer_input, swap_cores(layer_input))], axis=2
+    )
+    block = jnp.where(first, block, block[::-1])
 
     line = gather(gelu_grad, along_x[0] + along_y[1])
+    input_4 = send(block, -4)
+    line, input_4 = lax.optimization_barrier((line, input_4))
     grad_tokens = gather(line, along_y[0] + along_x[1])
+    input_2_6 = send(jnp.stack([block, input_4]), -2)
+    input_8 = send(input_4[0], -4)
+    grad_tokens, input_2_6, input_8 = lax.optimization_barrier((grad_tokens, input_2_6, input_8))
     grad_blocks = grad_tokens.reshape((16, half) + grad_tokens.shape[1:])
+    evens = jnp.stack([block, input_2_6[0], input_4, input_2_6[1]])
+    odds = send(evens, -1)
 
     early = lax.dynamic_index_in_dim(jnp.asarray(order_of(early_steps)), z * 2 + core, 0, False)
     late = lax.dynamic_index_in_dim(jnp.asarray(order_of(late_steps)), z * 2 + core, 0, False)
@@ -126,6 +178,7 @@
     )
     from_sibling = swap_cores(ahead[5:])
     rest = partials(late, grad_blocks, weight, weight_other, ((0, 4, False), (4, 3, True)))
+    rest, odds = lax.optimization_barrier((rest, odds))
     rest_sibling = swap_cores(rest[4:])
 
     moved = send(jnp.concatenate([ahead[:4], from_sibling]), 1).reshape(2, 4, half, 2 * width)
@@ -137,28 +190,24 @@
     sums[0] = sums[0].at[0].add(moved_far.astype(f32))
     here = moved[:, 3].astype(f32).at[0].add(rest[3].astype(f32))
     moved = send(jnp.stack([sums[0], sums[2]]).astype(bf16), 2)
-    moved, input_whole = lax.optimization_barrier((moved, input_whole))
     here = here + moved[1].astype(f32)
     moved = send((sums[1] + moved[0].astype(f32)).astype(bf16), 4)
+
+    others = jnp.concatenate([evens[1:, 1], odds[:, 1]])
+    others = jnp.concatenate([others[:, :, width:], others[:, :, :width]], axis=2)
+    input_blocks = jnp.concatenate([evens[:, 0], odds[:, 0], input_8[None], swap_cores(others)])
+    order = lax.dynamic_index_in_dim(jnp.asarray(input_order()), z * 2 + core, 0, False)
+    sibling = swap_cores(weight_part(order, input_blocks, grad_blocks, 1))
+    grad_weight = weight_part(order, input_blocks, grad_blocks, 0, sibling)
+
+    moved, grad_weight = lax.optimization_barrier((moved, grad_weight))
     here = here + moved.astype(f32)
-
     from_other = swap_cores(here[:, :, width:].astype(bf16)).astype(f32)
     own = here[0, :, :width] + from_other[1]
     other = here[1, :, :width] + from_other[0]
     grad_input = jnp.where(
         first, jnp.concatenate([own, other]), jnp.concatenate([other, own])
     ).astype(bf16)
-
-    blocks = input_whole.reshape(16, 2, half, width)
-    mine = lax.dynamic_index_in_dim(blocks, core, 1, keepdims=False)
-    other = swap_cores(lax.dynamic_index_in_dim(blocks, 1 - core, 1, keepdims=False))
-
-    def ordered(values):
-        chips = values.reshape(4, 4, half, width)
-        return jnp.where(first, jnp.swapaxes(chips, 0, 1), chips).reshape(16 * half, width)
-
-    sibling = swap_cores(matmul_tn(ordered(other), grad_tokens))
-    grad_weight = matmul_tn(ordered(mine), grad_tokens) + sibling
     return (grad_input, grad_weight)
 
 

time: 157 us -> 138 us (0.88)
  starting transfers between devices: 58.8 us -> 79.1 us
  between operations: 14.3 us -> 1.06 us
  blocking collectives: 12.9 us -> 0 us
  waiting for transfers between devices: 40.8 us -> 31.1 us
  Pallas kernels: 6.8 us -> 12.2 us
  other arithmetic: 10.3 us -> 5.74 us
  matrix products: 2.85 us -> 0 us
  local copies, waits for them, and re-layouts: 8.74 us -> 6.95 us
    all_to_all x1 -> x0, blocking collectives: 12.9 us -> none  [gather(): parts = lax.all_to_all(copies, plane, 0, 0, axis_index_groups=groups)]
    ppermute x4 -> x8, starting transfers between devices: 21.9 us -> 33.8 us  [send(): return lax.ppermute(values, ring, pairs)]
    ppermute x4 -> x8, waiting for transfers between devices: 19 us -> 30.2 us  [send(): return lax.ppermute(values, ring, pairs)]
    all_to_all x1 -> x2, waiting for transfers between devices: 10.7 us -> 0.01 us  [gather(): parts = lax.all_to_all(copies, plane, 0, 0, axis_index_groups=groups)]
    all_gather x1 -> x0, waiting for transfers between devices: 6.12 us -> none  [local(): input_whole = lax.all_gather(layer_input, 'col', axis=0, tiled=True)]
    pallas_call x0 -> x2, Pallas kernels: none -> 5.43 us  [weight_part(): pl.pallas_call(functools.partial(weight_kernel, side, sibling is not None...]
    ppermute x6 -> x7, starting transfers between devices: 32.8 us -> 37.8 us  [swap_cores(): return lax.ppermute(values, 'rep', [(0, 1), (1, 0), (2, 3), (3, 2)])]
    ppermute x6 -> x7, waiting for transfers between devices: 4.91 us -> 0.94 us  [swap_cores(): return lax.ppermute(values, 'rep', [(0, 1), (1, 0), (2, 3), (3, 2)])]
  transfers between devices with their start and end apart: 12 -> 17, of which waited for: 9 -> 7; matrix products, arithmetic and copies ran while one was open for 6% -> 7% of each run, Pallas kernels for 4% -> 9%
where the time goes in v2:
time: 138 us; the launch traced here: 136 us
  starting transfers between devices  79.1 us (57%)
  waiting for transfers between devices  31.1 us (23%)
  Pallas kernels  12.2 us (9%)
  local copies, waits for them, and re-layouts  6.95 us (5%)
  other arithmetic  5.74 us (4%)
    ppermute x7, starting transfers between devices, swap_cores(): return lax.ppermute(values, 'rep', [(0, 1), (1, 0), (2, 3), (3, 2)])  37.8 us
    ppermute x8, starting transfers between devices, send(): return lax.ppermute(values, ring, pairs)  33.8 us
    ppermute x8, waiting for transfers between devices, send(): return lax.ppermute(values, ring, pairs)  30.2 us
    all_to_all x2, starting transfers between devices, gather(): parts = lax.all_to_all(copies, plane, 0, 0, axis_index_groups=groups)  7.51 us
    pallas_call x2, Pallas kernels, partials(): pl.pallas_call(functools.partial(partial_kernel, groups), out_shape=jax.S...  6.81 us
    pallas_call x2, Pallas kernels, weight_part(): pl.pallas_call(functools.partial(weight_kernel, side, sibling is not None...  5.43 us
    broadcast_in_dim x2, local copies, waits for them, and re-layouts, gather(): copies = jnp.broadcast_to(values[None], (4,) + values.shape)  2.82 us
  transfers between devices with their start and end apart: 17, of which 7 were waited for; matrix products, arithmetic and copies ran while one was open for 7% of the time, Pallas kernels for 9%

profile of v2, /device:TPU:1, one launch (start us, length us, event | category | flops | bytes accessed | tf_op | source)
XLA Modules:
  0.0 136.2 jit_solution(10931620298478146367)
XLA Ops:
  0.6 8.9 %collective-permute-start = (bf16[128,384]{1,0:T(8,128)(2,1)}, bf16[128,384]{1,0:T(8,128)(2,1)S(1)}, u32[]{:S(2)}, u32[]{:S(2)}) collective-permute-start(bf16[128,384]{1,0:T(8,128)(2,1)} %param.11), channel_id=1, source_target_pairs={{0,1},{1,0},{2,3},{3,2},{4,5},{5,4},{6,7},{7,6},{8,9},{9,8},{10,11... | collective-permute-start | bytes 294920 | tf_op jit(solution)/shard_map/ppermute | solution.py:61
  11.8 3.5 %all-to-all-start = ((bf16[4,64,1536]{2,1,0:T(8,128)(2,1)}), bf16[4,64,1536]{2,1,0:T(8,128)(2,1)S(1)}, u32[]{:S(2)}, u32[]{:S(2)}) async-start(bf16[4,64,1536]{2,1,0:T(8,128)(2,1)} %broadcast_in_dim.6), calls=%async_computation | async-start | bytes 1572864 | tf_op jit(solution)/shard_map/all_to_all | solution.py:56
  15.4 4.1 %collective-permute-start.1 = (bf16[2,64,768]{2,1,0:T(8,128)(2,1)S(1)}, bf16[2,64,768]{2,1,0:T(8,128)(2,1)S(1)}, u32[]{:S(2)}, u32[]{:S(2)}) collective-permute-start(bf16[2,64,768]{2,1,0:T(8,128)(2,1)S(1)} %reverse_select_fusion), channel_id=1, source_target_pairs={{0,48},{1,17},{2,50},{3,19},{4,52},{5,21},{6,54},{7,23},{8,56},{9,... | collective-permute-start | bytes 589832 | tf_op jit(solution)/shard_map/ppermute | solution.py:70
  19.5 7.1 %collective-permute-done.1 = bf16[2,64,768]{2,1,0:T(8,128)(2,1)S(1)} collective-permute-done((bf16[2,64,768]{2,1,0:T(8,128)(2,1)S(1)}, bf16[2,64,768]{2,1,0:T(8,128)(2,1)S(1)}, u32[]{:S(2)}, u32[]{:S(2)}) %collective-permute-start.1) | collective-permute-done | bytes 196640 | tf_op jit(solution)/shard_map/ppermute | solution.py:70
  28.5 4.0 %all-to-all-start.1 = ((bf16[4,256,1536]{2,1,0:T(8,128)(2,1)}), bf16[4,256,1536]{2,1,0:T(8,128)(2,1)S(1)}, u32[]{:S(2)}, u32[]{:S(2)}) async-start(bf16[4,256,1536]{2,1,0:T(8,128)(2,1)} %broadcast_in_dim.7), calls=%async_computation.1 | async-start | bytes 6291456 | tf_op jit(solution)/shard_map/all_to_all | solution.py:56
  32.5 8.8 %collective-permute-start.4 = (bf16[384,1536]{1,0:T(8,128)(2,1)}, bf16[384,1536]{1,0:T(8,128)(2,1)}, u32[]{:S(2)}, u32[]{:S(2)}) collective-permute-start(bf16[384,1536]{1,0:T(8,128)(2,1)} %own_ref.3), channel_id=1, source_target_pairs={{0,1},{1,0},{2,3},{3,2},{4,5},{5,4},{6,7},{7,6},{8,9},{9,8},{10,11... | collective-permute-start | bytes 3538952 | tf_op jit(solution)/shard_map/ppermute | solution.py:61
  45.8 5.6 %collective-permute-start.3 = (bf16[64,768]{1,0:T(8,128)(2,1)}, bf16[64,768]{1,0:T(8,128)(2,1)}, u32[]{:S(2)}, u32[]{:S(2)}) collective-permute-start(bf16[64,768]{1,0:T(8,128)(2,1)} %slice_bitcast_fusion.12), channel_id=1, source_target_pairs={{0,48},{1,17},{2,50},{3,19},{4,52},{5,21},{6,54},{7,23},{8,56},{9,... | collective-permute-start | bytes 294920 | tf_op jit(solution)/shard_map/ppermute | solution.py:70
  51.4 9.7 %collective-permute-done.3 = bf16[64,768]{1,0:T(8,128)(2,1)} collective-permute-done((bf16[64,768]{1,0:T(8,128)(2,1)}, bf16[64,768]{1,0:T(8,128)(2,1)}, u32[]{:S(2)}, u32[]{:S(2)}) %collective-permute-start.3) | collective-permute-done | bytes 98336 | tf_op jit(solution)/shard_map/ppermute | solution.py:70
  62.3 4.1 %collective-permute-start.7 = (bf16[4,2,64,768]{3,2,0,1:T(8,128)(2,1)S(1)}, bf16[4,2,64,768]{3,2,0,1:T(8,128)(2,1)S(1)}, u32[]{:S(2)}, u32[]{:S(2)}) collective-permute-start(bf16[4,2,64,768]{3,2,0,1:T(8,128)(2,1)S(1)} %pad_maximum_fusion.2), channel_id=1, source_target_pairs={{0,60},{1,5},{2,62},{3,7},{4,0},{5,9},{6,2},{7,11},{8,4},{9,13},{1... | collective-permute-start | bytes 2359304 | tf_op jit(solution)/shard_map/ppermute | solution.py:70
  67.8 3.8 %shard_map.86 = bf16[9,64,768]{2,1,0:T(8,128)(2,1)S(1)} custom-call(s32[9]{0:T(128)S(1)} %fusion.25.order_ref, bf16[16,64,1536]{2,1,0:T(8,128)(2,1)S(1)} %bitcast.91, bf16[384,1536]{1,0:T(8,128)(2,1)S(1)} %copy-done, bf16[384,1536]{1,0:T(8,128)(2,1)} %collective-permute-done.4.other_ref), custom_call_target="tpu_custom_call" | custom-call | flops 1358954496 | bytes 6389760 | tf_op jit(solution)/shard_map/pallas_call | solution.py:97
  71.7 5.9 %collective-permute-start.5 = (bf16[4,64,768]{2,1,0:T(8,128)(2,1)S(1)}, bf16[4,64,768]{2,1,0:T(8,128)(2,1)S(1)}, u32[]{:S(2)}, u32[]{:S(2)}) collective-permute-start(bf16[4,64,768]{2,1,0:T(8,128)(2,1)S(1)} %get-tuple-element.45), channel_id=1, source_target_pairs={{0,1},{1,0},{2,3},{3,2},{4,5},{5,4},{6,7},{7,6},{8,9},{9,8},{10,11... | collective-permute-start | bytes 1179656 | tf_op jit(solution)/shard_map/ppermute | solution.py:61
  77.6 3.0 %shard_map.87 = bf16[7,64,768]{2,1,0:T(8,128)(2,1)S(1)} custom-call(s32[7]{0:T(128)S(1)} %fusion.26.order_ref, bf16[16,64,1536]{2,1,0:T(8,128)(2,1)S(1)} %bitcast.92, bf16[384,1536]{1,0:T(8,128)(2,1)S(1)} %copy-done, bf16[384,1536]{1,0:T(8,128)(2,1)} %collective-permute-done.4.other_ref), custom_call_target="tpu_custom_call" | custom-call | flops 1056964608 | bytes 6193152 | tf_op jit(solution)/shard_map/pallas_call | solution.py:97
  80.8 1.9 %collective-permute-start.12 = (bf16[7,64,768]{2,1,0:T(8,128)(2,1)S(1)}, bf16[7,64,768]{2,1,0:T(8,128)(2,1)S(1)}, u32[]{:S(2)}, u32[]{:S(2)}) collective-permute-start(bf16[7,64,768]{2,1,0:T(8,128)(2,1)S(1)} %fusion), channel_id=1, source_target_pairs={{0,1},{1,0},{2,3},{3,2},{4,5},{5,4},{6,7},{7,6},{8,9},{9,8},{10,11... | collective-permute-start | bytes 2064392 | tf_op jit(solution)/shard_map/ppermute | solution.py:61
  83.6 4.5 %collective-permute-start.6 = (bf16[8,64,768]{2,1,0:T(8,128)(2,1)S(1)}, bf16[8,64,768]{2,1,0:T(8,128)(2,1)S(1)}, u32[]{:S(2)}, u32[]{:S(2)}) collective-permute-start(bf16[8,64,768]{2,1,0:T(8,128)(2,1)S(1)} %pad_maximum_fusion.1), channel_id=1, source_target_pairs={{0,4},{1,61},{2,6},{3,63},{4,8},{5,1},{6,10},{7,3},{8,12},{9,5},{1... | collective-permute-start | bytes 2359304 | tf_op jit(solution)/shard_map/ppermute | solution.py:70
  88.1 1.9 %collective-permute-start.9 = (bf16[64,768]{1,0:T(8,128)(2,1)S(1)}, bf16[64,768]{1,0:T(8,128)(2,1)S(1)}, u32[]{:S(2)}, u32[]{:S(2)}) collective-permute-start(bf16[64,768]{1,0:T(8,128)(2,1)S(1)} %slice_bitcast_fusion.10), channel_id=1, source_target_pairs={{0,8},{1,57},{2,10},{3,59},{4,12},{5,61},{6,14},{7,63},{8,16},{9,1... | collective-permute-start | bytes 294920 | tf_op jit(solution)/shard_map/ppermute | solution.py:70
  90.1 1.9 %collective-permute-start.8 = (bf16[3,64,768]{2,1,0:T(8,128)(2,1)S(1)}, bf16[3,64,768]{2,1,0:T(8,128)(2,1)S(1)}, u32[]{:S(2)}, u32[]{:S(2)}) collective-permute-start(bf16[3,64,768]{2,1,0:T(8,128)(2,1)S(1)} %slice.150), channel_id=1, source_target_pairs={{0,1},{1,0},{2,3},{3,2},{4,5},{5,4},{6,7},{7,6},{8,9},{9,8},{10,11... | collective-permute-start | bytes 884744 | tf_op jit(solution)/shard_map/ppermute | solution.py:61
  93.1 2.0 %shard_map.88 = f32[384,1536]{1,0:T(8,128)S(1)} custom-call(s32[16]{0:T(128)S(1)} %fusion.27.order_ref, bf16[16,64,768]{2,1,0:T(8,128)(2,1)S(1)} %pad_maximum_fusion.input_ref, bf16[16,64,1536]{2,1,0:T(8,128)(2,1)S(1)} %bitcast.93), custom_call_target="tpu_custom_call" | custom-call | flops 1207959552 | bytes 6291456 | tf_op jit(solution)/shard_map/pallas_call | solution.py:132
  95.1 2.4 %collective-permute-start.13 = (f32[384,1536]{1,0:T(8,128)S(1)}, f32[384,1536]{1,0:T(8,128)S(1)}, u32[]{:S(2)}, u32[]{:S(2)}) collective-permute-start(f32[384,1536]{1,0:T(8,128)S(1)} %shard_map.88), channel_id=1, source_target_pairs={{0,1},{1,0},{2,3},{3,2},{4,5},{5,4},{6,7},{7,6},{8,9},{9,8},{10,11... | collective-permute-start | bytes 7077896 | tf_op jit(solution)/shard_map/ppermute | solution.py:61
  99.2 5.9 %collective-permute-start.10 = (bf16[2,2,64,768]{3,2,1,0:T(8,128)(2,1)S(1)}, bf16[2,2,64,768]{3,2,1,0:T(8,128)(2,1)S(1)}, u32[]{:S(2)}, u32[]{:S(2)}) collective-permute-start(bf16[2,2,64,768]{3,2,1,0:T(8,128)(2,1)S(1)} %pad_maximum_fusion.5), channel_id=1, source_target_pairs={{0,8},{1,57},{2,10},{3,59},{4,12},{5,61},{6,14},{7,63},{8,16},{9,1... | collective-permute-start | bytes 1179656 | tf_op jit(solution)/shard_map/ppermute | solution.py:70
  105.1 7.7 %collective-permute-done.10 = bf16[2,2,64,768]{3,2,1,0:T(8,128)(2,1)S(1)} collective-permute-done((bf16[2,2,64,768]{3,2,1,0:T(8,128)(2,1)S(1)}, bf16[2,2,64,768]{3,2,1,0:T(8,128)(2,1)S(1)}, u32[]{:S(2)}, u32[]{:S(2)}) %collective-permute-start.10) | collective-permute-done | bytes 393248 | tf_op jit(solution)/shard_map/ppermute | solution.py:70
  112.9 5.7 %collective-permute-start.11 = (bf16[2,64,768]{2,1,0:T(8,128)(2,1)S(1)}, bf16[2,64,768]{2,1,0:T(8,128)(2,1)S(1)}, u32[]{:S(2)}, u32[]{:S(2)}) collective-permute-start(bf16[2,64,768]{2,1,0:T(8,128)(2,1)S(1)} %fusion.11), channel_id=1, source_target_pairs={{0,16},{1,49},{2,18},{3,51},{4,20},{5,53},{6,22},{7,55},{8,24},{9,... | collective-permute-start | bytes 589832 | tf_op jit(solution)/shard_map/ppermute | solution.py:70
  118.6 3.4 %shard_map.89 = f32[384,1536]{1,0:T(8,128)} custom-call(s32[16]{0:T(128)S(1)} %fusion.27.order_ref, bf16[16,64,768]{2,1,0:T(8,128)(2,1)S(1)} %pad_maximum_fusion.input_ref, bf16[16,64,1536]{2,1,0:T(8,128)(2,1)S(1)} %bitcast.94, f32[384,1536]{1,0:T(8,128)S(1)} %collective-permute-done.13.rest_0_), custom_call_target="tpu_custom_call" | custom-call | flops 1207959552 | bytes 6291456 | tf_op jit(solution)/shard_map/pallas_call | solution.py:132
  122.0 4.4 %collective-permute-done.11 = bf16[2,64,768]{2,1,0:T(8,128)(2,1)S(1)} collective-permute-done((bf16[2,64,768]{2,1,0:T(8,128)(2,1)S(1)}, bf16[2,64,768]{2,1,0:T(8,128)(2,1)S(1)}, u32[]{:S(2)}, u32[]{:S(2)}) %collective-permute-start.11) | collective-permute-done | bytes 196640 | tf_op jit(solution)/shard_map/ppermute | solution.py:70
  126.6 8.0 %collective-permute-start.14 = (bf16[2,64,384]{2,1,0:T(8,128)(2,1)S(1)}, bf16[2,64,384]{2,1,0:T(8,128)(2,1)S(1)}, u32[]{:S(2)}, u32[]{:S(2)}) collective-permute-start(bf16[2,64,384]{2,1,0:T(8,128)(2,1)S(1)} %slice.252), channel_id=1, source_target_pairs={{0,1},{1,0},{2,3},{3,2},{4,5},{5,4},{6,7},{7,6},{8,9},{9,8},{10,11... | collective-permute-start | bytes 294920 | tf_op jit(solution)/shard_map/ppermute | solution.py:61
  (57 shorter events, 16.9 us)
Async XLA Ops:
  0.6 14.7 %copy-start.2 = (bf16[128,384]{1,0:T(8,128)(2,1)S(1)}, bf16[128,384]{1,0:T(8,128)(2,1)}, u32[]{:S(2)}) copy-start(bf16[128,384]{1,0:T(8,128)(2,1)} %param.11) | copy-start | bytes 294916
  0.6 14.7 %collective-permute-start = (bf16[128,384]{1,0:T(8,128)(2,1)}, bf16[128,384]{1,0:T(8,128)(2,1)S(1)}, u32[]{:S(2)}, u32[]{:S(2)}) collective-permute-start(bf16[128,384]{1,0:T(8,128)(2,1)} %param.11), channel_id=1, source_target_pairs={{0,1},{1,0},{2,3},{3,2},{4,5},{5,4},{6,7},{7,6},{8,9},{9,8},{10,11... | collective-permute-start | bytes 294920 | tf_op jit(solution)/shard_map/ppermute | solution.py:61
  11.8 14.8 %all-to-all-start = ((bf16[4,64,1536]{2,1,0:T(8,128)(2,1)}), bf16[4,64,1536]{2,1,0:T(8,128)(2,1)S(1)}, u32[]{:S(2)}, u32[]{:S(2)}) async-start(bf16[4,64,1536]{2,1,0:T(8,128)(2,1)} %broadcast_in_dim.6), calls=%async_computation | async-start | bytes 1572864 | tf_op jit(solution)/shard_map/all_to_all | solution.py:56
  15.4 13.2 %copy-start.1 = (bf16[2,64,768]{2,1,0:T(8,128)(2,1)}, bf16[2,64,768]{2,1,0:T(8,128)(2,1)S(1)}, u32[]{:S(2)}) copy-start(bf16[2,64,768]{2,1,0:T(8,128)(2,1)S(1)} %pad_maximum_fusion.8) | copy-start | bytes 589828
  15.4 11.2 %collective-permute-start.1 = (bf16[2,64,768]{2,1,0:T(8,128)(2,1)S(1)}, bf16[2,64,768]{2,1,0:T(8,128)(2,1)S(1)}, u32[]{:S(2)}, u32[]{:S(2)}) collective-permute-start(bf16[2,64,768]{2,1,0:T(8,128)(2,1)S(1)} %reverse_select_fusion), channel_id=1, source_target_pairs={{0,48},{1,17},{2,50},{3,19},{4,52},{5,21},{6,54},{7,23},{8,56},{9,... | collective-permute-start | bytes 589832 | tf_op jit(solution)/shard_map/ppermute | solution.py:70
  28.5 32.5 %all-to-all-start.1 = ((bf16[4,256,1536]{2,1,0:T(8,128)(2,1)}), bf16[4,256,1536]{2,1,0:T(8,128)(2,1)S(1)}, u32[]{:S(2)}, u32[]{:S(2)}) async-start(bf16[4,256,1536]{2,1,0:T(8,128)(2,1)} %broadcast_in_dim.7), calls=%async_computation.1 | async-start | bytes 6291456 | tf_op jit(solution)/shard_map/all_to_all | solution.py:56
  32.5 35.3 %collective-permute-start.4 = (bf16[384,1536]{1,0:T(8,128)(2,1)}, bf16[384,1536]{1,0:T(8,128)(2,1)}, u32[]{:S(2)}, u32[]{:S(2)}) collective-permute-start(bf16[384,1536]{1,0:T(8,128)(2,1)} %own_ref.3), channel_id=1, source_target_pairs={{0,1},{1,0},{2,3},{3,2},{4,5},{5,4},{6,7},{7,6},{8,9},{9,8},{10,11... | collective-permute-start | bytes 3538952 | tf_op jit(solution)/shard_map/ppermute | solution.py:61
  43.2 17.8 %collective-permute-start.2 = (bf16[2,2,64,768]{3,2,0,1:T(8,128)(2,1)}, bf16[2,2,64,768]{3,2,0,1:T(8,128)(2,1)}, u32[]{:S(2)}, u32[]{:S(2)}) collective-permute-start(bf16[2,2,64,768]{3,2,0,1:T(8,128)(2,1)} %pad_maximum_fusion.4), channel_id=1, source_target_pairs={{0,56},{1,9},{2,58},{3,11},{4,60},{5,13},{6,62},{7,15},{8,0},{9,17... | collective-permute-start | bytes 1179656 | tf_op jit(solution)/shard_map/ppermute | solution.py:70
  45.8 15.3 %collective-permute-start.3 = (bf16[64,768]{1,0:T(8,128)(2,1)}, bf16[64,768]{1,0:T(8,128)(2,1)}, u32[]{:S(2)}, u32[]{:S(2)}) collective-permute-start(bf16[64,768]{1,0:T(8,128)(2,1)} %slice_bitcast_fusion.12), channel_id=1, source_target_pairs={{0,48},{1,17},{2,50},{3,19},{4,52},{5,21},{6,54},{7,23},{8,56},{9,... | collective-permute-start | bytes 294920 | tf_op jit(solution)/shard_map/ppermute | solution.py:70
  61.1 6.8 %copy-start = (bf16[384,1536]{1,0:T(8,128)(2,1)S(1)}, bf16[384,1536]{1,0:T(8,128)(2,1)}, u32[]{:S(2)}) copy-start(bf16[384,1536]{1,0:T(8,128)(2,1)} %own_ref.3) | copy-start | bytes 3538948
  62.3 18.3 %collective-permute-start.7 = (bf16[4,2,64,768]{3,2,0,1:T(8,128)(2,1)S(1)}, bf16[4,2,64,768]{3,2,0,1:T(8,128)(2,1)S(1)}, u32[]{:S(2)}, u32[]{:S(2)}) collective-permute-start(bf16[4,2,64,768]{3,2,0,1:T(8,128)(2,1)S(1)} %pad_maximum_fusion.2), channel_id=1, source_target_pairs={{0,60},{1,5},{2,62},{3,7},{4,0},{5,9},{6,2},{7,11},{8,4},{9,13},{1... | collective-permute-start | bytes 2359304 | tf_op jit(solution)/shard_map/ppermute | solution.py:70
  71.7 11.8 %collective-permute-start.5 = (bf16[4,64,768]{2,1,0:T(8,128)(2,1)S(1)}, bf16[4,64,768]{2,1,0:T(8,128)(2,1)S(1)}, u32[]{:S(2)}, u32[]{:S(2)}) collective-permute-start(bf16[4,64,768]{2,1,0:T(8,128)(2,1)S(1)} %get-tuple-element.45), channel_id=1, source_target_pairs={{0,1},{1,0},{2,3},{3,2},{4,5},{5,4},{6,7},{7,6},{8,9},{9,8},{10,11... | collective-permute-start | bytes 1179656 | tf_op jit(solution)/shard_map/ppermute | solution.py:61
  80.8 11.2 %collective-permute-start.12 = (bf16[7,64,768]{2,1,0:T(8,128)(2,1)S(1)}, bf16[7,64,768]{2,1,0:T(8,128)(2,1)S(1)}, u32[]{:S(2)}, u32[]{:S(2)}) collective-permute-start(bf16[7,64,768]{2,1,0:T(8,128)(2,1)S(1)} %fusion), channel_id=1, source_target_pairs={{0,1},{1,0},{2,3},{3,2},{4,5},{5,4},{6,7},{7,6},{8,9},{9,8},{10,11... | collective-permute-start | bytes 2064392 | tf_op jit(solution)/shard_map/ppermute | solution.py:61
  83.6 14.5 %collective-permute-start.6 = (bf16[8,64,768]{2,1,0:T(8,128)(2,1)S(1)}, bf16[8,64,768]{2,1,0:T(8,128)(2,1)S(1)}, u32[]{:S(2)}, u32[]{:S(2)}) collective-permute-start(bf16[8,64,768]{2,1,0:T(8,128)(2,1)S(1)} %pad_maximum_fusion.1), channel_id=1, source_target_pairs={{0,4},{1,61},{2,6},{3,63},{4,8},{5,1},{6,10},{7,3},{8,12},{9,5},{1... | collective-permute-start | bytes 2359304 | tf_op jit(solution)/shard_map/ppermute | solution.py:70
  88.1 11.0 %collective-permute-start.9 = (bf16[64,768]{1,0:T(8,128)(2,1)S(1)}, bf16[64,768]{1,0:T(8,128)(2,1)S(1)}, u32[]{:S(2)}, u32[]{:S(2)}) collective-permute-start(bf16[64,768]{1,0:T(8,128)(2,1)S(1)} %slice_bitcast_fusion.10), channel_id=1, source_target_pairs={{0,8},{1,57},{2,10},{3,59},{4,12},{5,61},{6,14},{7,63},{8,16},{9,1... | collective-permute-start | bytes 294920 | tf_op jit(solution)/shard_map/ppermute | solution.py:70
  90.1 7.5 %collective-permute-start.8 = (bf16[3,64,768]{2,1,0:T(8,128)(2,1)S(1)}, bf16[3,64,768]{2,1,0:T(8,128)(2,1)S(1)}, u32[]{:S(2)}, u32[]{:S(2)}) collective-permute-start(bf16[3,64,768]{2,1,0:T(8,128)(2,1)S(1)} %slice.150), channel_id=1, source_target_pairs={{0,1},{1,0},{2,3},{3,2},{4,5},{5,4},{6,7},{7,6},{8,9},{9,8},{10,11... | collective-permute-start | bytes 884744 | tf_op jit(solution)/shard_map/ppermute | solution.py:61
  95.1 23.5 %collective-permute-start.13 = (f32[384,1536]{1,0:T(8,128)S(1)}, f32[384,1536]{1,0:T(8,128)S(1)}, u32[]{:S(2)}, u32[]{:S(2)}) collective-permute-start(f32[384,1536]{1,0:T(8,128)S(1)} %shard_map.88), channel_id=1, source_target_pairs={{0,1},{1,0},{2,3},{3,2},{4,5},{5,4},{6,7},{7,6},{8,9},{9,8},{10,11... | collective-permute-start | bytes 7077896 | tf_op jit(solution)/shard_map/ppermute | solution.py:61
  99.2 13.6 %collective-permute-start.10 = (bf16[2,2,64,768]{3,2,1,0:T(8,128)(2,1)S(1)}, bf16[2,2,64,768]{3,2,1,0:T(8,128)(2,1)S(1)}, u32[]{:S(2)}, u32[]{:S(2)}) collective-permute-start(bf16[2,2,64,768]{3,2,1,0:T(8,128)(2,1)S(1)} %pad_maximum_fusion.5), channel_id=1, source_target_pairs={{0,8},{1,57},{2,10},{3,59},{4,12},{5,61},{6,14},{7,63},{8,16},{9,1... | collective-permute-start | bytes 1179656 | tf_op jit(solution)/shard_map/ppermute | solution.py:70
  112.9 13.6 %collective-permute-start.11 = (bf16[2,64,768]{2,1,0:T(8,128)(2,1)S(1)}, bf16[2,64,768]{2,1,0:T(8,128)(2,1)S(1)}, u32[]{:S(2)}, u32[]{:S(2)}) collective-permute-start(bf16[2,64,768]{2,1,0:T(8,128)(2,1)S(1)} %fusion.11), channel_id=1, source_target_pairs={{0,16},{1,49},{2,18},{3,51},{4,20},{5,53},{6,22},{7,55},{8,24},{9,... | collective-permute-start | bytes 589832 | tf_op jit(solution)/shard_map/ppermute | solution.py:70
  126.6 8.9 %collective-permute-start.14 = (bf16[2,64,384]{2,1,0:T(8,128)(2,1)S(1)}, bf16[2,64,384]{2,1,0:T(8,128)(2,1)S(1)}, u32[]{:S(2)}, u32[]{:S(2)}) collective-permute-start(bf16[2,64,384]{2,1,0:T(8,128)(2,1)S(1)} %slice.252), channel_id=1, source_target_pairs={{0,1},{1,0},{2,3},{3,2},{4,5},{5,4},{6,7},{7,6},{8,9},{9,8},{10,11... | collective-permute-start | bytes 294920 | tf_op jit(solution)/shard_map/ppermute | solution.py:61

commit v3 on v2

v3 whole, which is shorter than its diff:
```python
import functools
import math

import jax
import jax.numpy as jnp
from jax import lax
from jax.experimental import pallas as pl
from jax.experimental.pallas import tpu as pltpu
from jax.sharding import PartitionSpec as P

cubic_term = 0.044715
plane = ("row", "rep")
ring = ("col", "rep")


def gelu_slope(values):
    scale = math.sqrt(2.0 / math.pi)
    inner = scale * (values + cubic_term * values * values * values)
    tangent = jnp.tanh(inner)
    return 0.5 * (1.0 + tangent) + 0.5 * values * (1.0 - tangent * tangent) * scale * (
        1.0 + 3.0 * cubic_term * values * values
    )


def index(x, y, core):
    return ((x * 2 + y % 2) * 2 + y // 2) * 2 + core


y_order = (0, 2, 1, 3)
along_x = [[[index(x, y, core) for x in range(4)] for y in y_order] for core in range(2)]
along_y = [[[index(x, y, core) for y in y_order] for x in range(4)] for core in range(2)]


early_steps = (7, 5, 3, 1, -7, -5, -3, -1, 8)
late_steps = (6, 4, 2, 0, -6, -4, -2)
input_steps = (0, 2, 4, 6, 1, 3, 5, 7, 8, -2, -4, -6, -1, -3, -5, -7)


def place(step):
    core = lax.rem(lax.axis_index("rep"), 2)
    chip = lax.rem(lax.axis_index("col") + (1 - 2 * core) * step + 16, 16)
    return jnp.where(core == 0, lax.rem(chip, 4) * 4 + lax.div(chip, 4), chip)


def gather(values, groups):
    copies = jnp.broadcast_to(values[None], (4,) + values.shape)
    parts = lax.all_to_all(copies, plane, 0, 0, axis_index_groups=groups)
    return parts.reshape((4 * values.shape[0],) + values.shape[1:])


def swap_cores(values):
    return lax.ppermute(values, "rep", [(0, 1), (1, 0), (2, 3), (3, 2)])


def send(values, distance, cross=False):
    pairs = []
    for z in range(16):
        for rep in range(4):
            target = (z + (-distance if rep % 2 else distance)) % 16
            pairs.append((z * 4 + rep, target * 4 + (rep ^ 1 if cross else rep)))
    return lax.ppermute(values, ring, pairs)


def matmul_nt(a, b):
    return lax.dot_general(a, b, (((1,), (1,)), ((), ())), preferred_element_type=jnp.float32)


def matmul_tn(a, b):
    return lax.dot_general(a, b, (((0,), (0,)), ((), ())), preferred_element_type=jnp.float32)


def partial_kernel(steps, groups, grad_ref, own_ref, other_ref, out_ref):
    width = own_ref.shape[0]
    for start, count, flipped in groups:
        rows = jnp.concatenate([grad_ref[place(steps[start + i])] for i in range(count)], axis=0)
        for side, ref in enumerate((other_ref, own_ref) if flipped else (own_ref, other_ref)):
            part = matmul_nt(rows, ref[...]).astype(out_ref.dtype)
            out_ref[start : start + count, :, side * width : (side + 1) * width] = part.reshape(
                count, -1, width
            )


def partials(steps, grad_blocks, weight_own, weight_other, groups):
    count = len(steps)
    rows, depth = grad_blocks.shape[1:]
    width = weight_own.shape[0]
    vmem = pl.BlockSpec(memory_space=pltpu.VMEM)
    return pl.pallas_call(
        functools.partial(partial_kernel, steps, groups),
        out_shape=jax.ShapeDtypeStruct((count, rows, 2 * width), jnp.bfloat16),
        in_specs=[vmem] * 3,
        out_specs=vmem,
        compiler_params=pltpu.CompilerParams(vmem_limit_bytes=32 * 1024 * 1024),
        cost_estimate=pl.CostEstimate(
            flops=4 * count * rows * depth * width,
            bytes_accessed=2 * (grad_blocks.size + 2 * width * depth + 2 * count * rows * width),
            transcendentals=0,
        ),
    )(grad_blocks, weight_own, weight_other)


def weight_kernel(side, add, evens_ref, odds_ref, far_ref, evens_other_ref, odds_other_ref,
                  grad_ref, *rest):
    sibling_ref = rest[0] if add else None
    out_ref, rows_ref = rest[-2:]
    width, half = out_ref.shape[0], far_ref.shape[0]
    sources = (
        [(evens_ref, (i, 0)) for i in range(4)]
        + [(odds_ref, (i,)) for i in range(4)]
        + [(far_ref, ())]
        + [(evens_other_ref, (i,)) for i in range(3)]
        + [(odds_other_ref, (i,)) for i in range(4)]
    )
    for (ref, at), step in zip(sources, input_steps):
        rows = pl.ds(pl.multiple_of(place(step) * half, half), half)
        rows_ref[rows, :] = ref[at + (slice(None), slice(side * width, (side + 1) * width))]
    tile = 256
    for start in range(0, out_ref.shape[1], tile):
        grad = grad_ref[:, :, start : start + tile].reshape(16 * half, tile)
        part = matmul_tn(rows_ref[...], grad)
        if add:
            part = part + sibling_ref[:, start : start + tile].astype(jnp.float32)
        out_ref[:, start : start + tile] = part.astype(out_ref.dtype)


def weight_part(input_blocks, grad_blocks, side, dtype, sibling=None):
    rows, both = input_blocks[2].shape
    width, depth = both // 2, grad_blocks.shape[2]
    vmem = pl.BlockSpec(memory_space=pltpu.VMEM)
    more = () if sibling is None else (sibling,)
    return pl.pallas_call(
        functools.partial(weight_kernel, side, sibling is not None),
        out_shape=jax.ShapeDtypeStruct((width, depth), dtype),
        in_specs=[vmem] * (6 + len(more)),
        out_specs=vmem,
        scratch_shapes=[pltpu.VMEM((16 * rows, width), jnp.bfloat16)],
        compiler_params=pltpu.CompilerParams(vmem_limit_bytes=32 * 1024 * 1024),
        cost_estimate=pl.CostEstimate(
            flops=2 * 16 * rows * width * depth,
            bytes_accessed=2 * (grad_blocks.size + 16 * rows * width) + 4 * width * depth,
            transcendentals=0,
        ),
    )(*input_blocks, grad_blocks, *more)


def local(layer_input, weight, gelu_input, upstream):
    core = lax.axis_index("rep") % 2
    first = core == 0
    tokens, width = layer_input.shape
    half = tokens // 2
    f32, bf16 = jnp.float32, jnp.bfloat16

    gelu_grad = (upstream.astype(f32) * gelu_slope(gelu_input.astype(f32))).astype(bf16)
    weight_other = swap_cores(weight)

    block = jnp.concatenate(
        [v.reshape(2, half, width) for v in (layer_input, swap_cores(layer_input))], axis=2
    )
    block = jnp.where(first, block, block[::-1])

    gelu_grad, block = lax.optimization_barrier((gelu_grad, block))
    line = gather(gelu_grad, along_x[0] + along_y[1])
    input_4 = send(block, -4)
    line, input_4 = lax.optimization_barrier((line, input_4))
    grad_tokens = gather(line, along_y[0] + along_x[1])
    input_2_6 = send(jnp.stack([block, input_4]), -2)
    input_8 = send(input_4[0], -4)
    grad_tokens, input_2_6 = lax.optimization_barrier((grad_tokens, input_2_6))
    evens = jnp.stack([block, input_2_6[0], input_4, input_2_6[1]])
    flipped = jnp.concatenate([evens[:, 1, :, width:], evens[:, 1, :, :width]], axis=2)
    odds = send(evens[:, 0], -1)
    odds_other = send(flipped, -1, cross=True)
    evens_other = swap_cores(flipped[1:])
    grad_blocks = grad_tokens.reshape((16, half) + grad_tokens.shape[1:])

    ahead = partials(
        early_steps, grad_blocks, weight, weight_other, ((0, 4, False), (4, 4, True), (8, 1, False))
    )
    ahead, later_blocks = lax.optimization_barrier((ahead, grad_blocks))
    moved = (send(ahead[:4], 1), send(ahead[4:8], -1, cross=True))
    moved_far = send(ahead[8], 4)
    rest = partials(late_steps, later_blocks, weight, weight_other, ((0, 4, False), (4, 3, True)))
    rest_sibling = swap_cores(rest[4:])
    input_blocks = (evens, odds, input_8, evens_other, odds_other)
    moved, rest, rest_sibling, input_blocks = lax.optimization_barrier(
        (moved, rest, rest_sibling, input_blocks)
    )

    sums = [
        jnp.stack([m[i].astype(f32) + r[i].astype(f32) for m, r in zip(moved, (rest, rest_sibling))])
        for i in range(3)
    ]
    here = jnp.stack([moved[0][3].astype(f32) + rest[3].astype(f32), moved[1][3].astype(f32)])
    moved = send(jnp.stack([sums[0], sums[2]]).astype(bf16), 2)
    for_sibling = weight_part(input_blocks, grad_blocks, 1, bf16)
    moved, moved_far, for_sibling = lax.optimization_barrier((moved, moved_far, for_sibling))
    here = here + moved[1].astype(f32)
    last = (sums[1] + moved[0].astype(f32)).at[0].add(moved_far.astype(f32)).astype(bf16)
    moved = send(last[:, :, :width], 4)
    moved_cross = send(last[:, :, width:], 4, cross=True)
    here_cross = swap_cores(here[:, :, width:].astype(bf16))

    sibling = swap_cores(for_sibling)
    grad_weight = weight_part(input_blocks, grad_blocks, 0, f32, sibling)

    moved, grad_weight = lax.optimization_barrier((moved, grad_weight))
    cross = moved_cross.astype(f32) + here_cross.astype(f32)
    summed = here[:, :, :width] + moved.astype(f32) + cross[::-1]
    own, other = summed[0], summed[1]
    grad_input = jnp.where(
        first, jnp.concatenate([own, other]), jnp.concatenate([other, own])
    ).astype(bf16)
    return (grad_input, grad_weight)


def solution(mesh):
    in_specs = (
        P("col", ("row", "rep")),
        P(("row", "rep"), "col"),
        P(("row", "rep"), "col"),
        P(("row", "rep"), "col"),
    )
    out_specs = (P("col", ("row", "rep")), P(("row", "rep"), "col"))
    return jax.shard_map(local, mesh=mesh, in_specs=in_specs, out_specs=out_specs, check_vma=False)
```

time: 138 us -> 136 us (0.986)
  the two profiles are of different devices: /device:TPU:1 before, /device:TPU:34 now
where the time goes in v3:
time: 136 us; the launch traced here: 135 us
  starting transfers between devices  83.9 us (62%)
  waiting for transfers between devices  28.1 us (21%)
  Pallas kernels  11.2 us (8%)
  other arithmetic  5.4 us (4%)
  local copies, waits for them, and re-layouts  5.03 us (4%)
    ppermute x11, starting transfers between devices, send(): return lax.ppermute(values, ring, pairs)  62 us
    ppermute x11, waiting for transfers between devices, send(): return lax.ppermute(values, ring, pairs)  20.1 us
    ppermute x6, starting transfers between devices, swap_cores(): return lax.ppermute(values, 'rep', [(0, 1), (1, 0), (2, 3), (3, 2)])  13.3 us
    all_to_all x2, starting transfers between devices, gather(): parts = lax.all_to_all(copies, plane, 0, 0, axis_index_groups=groups)  8.52 us
    pallas_call x2, Pallas kernels, partials(): pl.pallas_call(functools.partial(partial_kernel, steps, groups), out_shap...  6.71 us
    all_to_all x2, waiting for transfers between devices, gather(): parts = lax.all_to_all(copies, plane, 0, 0, axis_index_groups=groups)  6.66 us
    pallas_call x2, Pallas kernels, weight_part(): pl.pallas_call(functools.partial(weight_kernel, side, sibling is not None...  4.53 us
    broadcast_in_dim x2, local copies, waits for them, and re-layouts, gather(): copies = jnp.broadcast_to(values[None], (4,) + values.shape)  2.81 us
  transfers between devices with their start and end apart: 19, of which 8 were waited for; matrix products, arithmetic and copies ran while one was open for 4% of the time, Pallas kernels for 8%

profile of v3, /device:TPU:34, one launch (start us, length us, event | category | flops | bytes accessed | tf_op | source)
XLA Modules:
  0.0 134.7 jit_solution(396031035743825221)
XLA Ops:
  5.9 4.8 %all-to-all-start = ((bf16[4,64,1536]{2,1,0:T(8,128)(2,1)}), bf16[4,64,1536]{2,1,0:T(8,128)(2,1)S(1)}, u32[]{:S(2)}, u32[]{:S(2)}) async-start(bf16[4,64,1536]{2,1,0:T(8,128)(2,1)} %broadcast_in_dim.4), calls=%async_computation | async-start | bytes 1572864 | tf_op jit(solution)/shard_map/all_to_all | solution.py:47
  10.8 11.8 %collective-permute-start.1 = (bf16[2,64,768]{2,1,0:T(8,128)(2,1)S(1)}, bf16[2,64,768]{2,1,0:T(8,128)(2,1)S(1)}, u32[]{:S(2)}, u32[]{:S(2)}) collective-permute-start(bf16[2,64,768]{2,1,0:T(8,128)(2,1)S(1)} %reverse_select_fusion), channel_id=1, source_target_pairs={{0,48},{1,17},{2,50},{3,19},{4,52},{5,21},{6,54},{7,23},{8,56},{9,... | collective-permute-start | bytes 589832 | tf_op jit(solution)/shard_map/ppermute | solution.py:61
  22.6 9.4 %collective-permute-done.1 = bf16[2,64,768]{2,1,0:T(8,128)(2,1)S(1)} collective-permute-done((bf16[2,64,768]{2,1,0:T(8,128)(2,1)S(1)}, bf16[2,64,768]{2,1,0:T(8,128)(2,1)S(1)}, u32[]{:S(2)}, u32[]{:S(2)}) %collective-permute-start.1) | collective-permute-done | bytes 196640 | tf_op jit(solution)/shard_map/ppermute | solution.py:61
  33.9 3.7 %all-to-all-start.1 = ((bf16[4,256,1536]{2,1,0:T(8,128)(2,1)}), bf16[4,256,1536]{2,1,0:T(8,128)(2,1)S(1)}, u32[]{:S(2)}, u32[]{:S(2)}) async-start(bf16[4,256,1536]{2,1,0:T(8,128)(2,1)} %broadcast_in_dim.5), calls=%async_computation.1 | async-start | bytes 6291456 | tf_op jit(solution)/shard_map/all_to_all | solution.py:47
  38.6 4.6 %collective-permute-start.2 = (bf16[2,2,64,768]{3,2,0,1:T(8,128)(2,1)S(1)}, bf16[2,2,64,768]{3,2,0,1:T(8,128)(2,1)}, u32[]{:S(2)}, u32[]{:S(2)}) collective-permute-start(bf16[2,2,64,768]{3,2,0,1:T(8,128)(2,1)S(1)} %pad_maximum_fusion.2), channel_id=1, source_target_pairs={{0,56},{1,9},{2,58},{3,11},{4,60},{5,13},{6,62},{7,15},{8,0},{9,17... | collective-permute-start | bytes 1179656 | tf_op jit(solution)/shard_map/ppermute | solution.py:61
  43.2 1.9 %collective-permute-start.3 = (bf16[384,1536]{1,0:T(8,128)(2,1)}, bf16[384,1536]{1,0:T(8,128)(2,1)}, u32[]{:S(2)}, u32[]{:S(2)}) collective-permute-start(bf16[384,1536]{1,0:T(8,128)(2,1)} %own_ref.3), channel_id=1, source_target_pairs={{0,1},{1,0},{2,3},{3,2},{4,5},{5,4},{6,7},{7,6},{8,9},{9,8},{10,11... | collective-permute-start | bytes 3538952 | tf_op jit(solution)/shard_map/ppermute | solution.py:52
  46.0 6.5 %collective-permute-start.8 = (bf16[64,768]{1,0:T(8,128)(2,1)S(1)}, bf16[64,768]{1,0:T(8,128)(2,1)S(1)}, u32[]{:S(2)}, u32[]{:S(2)}) collective-permute-start(bf16[64,768]{1,0:T(8,128)(2,1)S(1)} %slice_bitcast_fusion.6), channel_id=1, source_target_pairs={{0,48},{1,17},{2,50},{3,19},{4,52},{5,21},{6,54},{7,23},{8,56},{9,... | collective-permute-start | bytes 294920 | tf_op jit(solution)/shard_map/ppermute | solution.py:61
  52.8 6.7 %all-to-all-done.1 = bf16[4,256,1536]{2,1,0:T(8,128)(2,1)S(1)} async-done(((bf16[4,256,1536]{2,1,0:T(8,128)(2,1)}), bf16[4,256,1536]{2,1,0:T(8,128)(2,1)S(1)}, u32[]{:S(2)}, u32[]{:S(2)}) %all-to-all-start.1) | async-done | bytes 3145760 | tf_op jit(solution)/shard_map/all_to_all | solution.py:47
  61.6 2.1 %collective-permute-start.9 = (bf16[3,64,768]{2,1,0:T(8,128)(2,1)S(1)}, bf16[3,64,768]{2,1,0:T(8,128)(2,1)S(1)}, u32[]{:S(2)}, u32[]{:S(2)}) collective-permute-start(bf16[3,64,768]{2,1,0:T(8,128)(2,1)S(1)} %fusion.9), channel_id=1, source_target_pairs={{0,1},{1,0},{2,3},{3,2},{4,5},{5,4},{6,7},{7,6},{8,9},{9,8},{10,11... | collective-permute-start | bytes 884744 | tf_op jit(solution)/shard_map/ppermute | solution.py:52
  63.7 3.9 %collective-permute-start.10 = (bf16[4,64,768]{2,1,0:T(8,128)(2,1)S(1)}, bf16[4,64,768]{2,1,0:T(8,128)(2,1)S(1)}, u32[]{:S(2)}, u32[]{:S(2)}) collective-permute-start(bf16[4,64,768]{2,1,0:T(8,128)(2,1)S(1)} %pad_maximum_fusion.1), channel_id=1, source_target_pairs={{0,61},{1,4},{2,63},{3,6},{4,1},{5,8},{6,3},{7,10},{8,5},{9,12},{1... | collective-permute-start | bytes 1179656 | tf_op jit(solution)/shard_map/ppermute | solution.py:61
  67.6 3.3 %collective-permute-start.7 = (bf16[4,64,768]{2,1,0:T(8,128)(2,1)S(1)}, bf16[4,64,768]{2,1,0:T(8,128)(2,1)S(1)}, u32[]{:S(2)}, u32[]{:S(2)}) collective-permute-start(bf16[4,64,768]{2,1,0:T(8,128)(2,1)S(1)} %slice_bitcast_fusion), channel_id=1, source_target_pairs={{0,60},{1,5},{2,62},{3,7},{4,0},{5,9},{6,2},{7,11},{8,4},{9,13},{1... | collective-permute-start | bytes 1179656 | tf_op jit(solution)/shard_map/ppermute | solution.py:61
  70.9 3.7 %shard_map.59 = bf16[9,64,768]{2,1,0:T(8,128)(2,1)S(1)} custom-call(bf16[16,64,1536]{2,1,0:T(8,128)(2,1)S(1)} %bitcast.36, bf16[384,1536]{1,0:T(8,128)(2,1)S(1)} %copy-done, bf16[384,1536]{1,0:T(8,128)(2,1)} %collective-permute-done.3.other_ref), custom_call_target="tpu_custom_call" | custom-call | flops 1358954496 | bytes 6389760 | tf_op jit(solution)/shard_map/pallas_call | solution.py:88
  76.7 2.6 %collective-permute-start.4 = (bf16[4,64,768]{2,1,0:T(8,128)(2,1)S(1)}, bf16[4,64,768]{2,1,0:T(8,128)(2,1)S(1)}, u32[]{:S(2)}, u32[]{:S(2)}) collective-permute-start(bf16[4,64,768]{2,1,0:T(8,128)(2,1)S(1)} %get-tuple-element.63), channel_id=1, source_target_pairs={{0,4},{1,61},{2,6},{3,63},{4,8},{5,1},{6,10},{7,3},{8,12},{9,5},{1... | collective-permute-start | bytes 1179656 | tf_op jit(solution)/shard_map/ppermute | solution.py:61
  79.2 3.0 %shard_map.60 = bf16[7,64,768]{2,1,0:T(8,128)(2,1)S(1)} custom-call(bf16[16,64,1536]{2,1,0:T(8,128)(2,1)S(1)} %bitcast.37, bf16[384,1536]{1,0:T(8,128)(2,1)S(1)} %copy-done, bf16[384,1536]{1,0:T(8,128)(2,1)} %collective-permute-done.3.other_ref), custom_call_target="tpu_custom_call" | custom-call | flops 1056964608 | bytes 6193152 | tf_op jit(solution)/shard_map/pallas_call | solution.py:88
  82.3 3.1 %collective-permute-start.6 = (bf16[3,64,768]{2,1,0:T(8,128)(2,1)S(1)}, bf16[3,64,768]{2,1,0:T(8,128)(2,1)S(1)}, u32[]{:S(2)}, u32[]{:S(2)}) collective-permute-start(bf16[3,64,768]{2,1,0:T(8,128)(2,1)S(1)} %slice.160), channel_id=1, source_target_pairs={{0,1},{1,0},{2,3},{3,2},{4,5},{5,4},{6,7},{7,6},{8,9},{9,8},{10,11... | collective-permute-start | bytes 884744 | tf_op jit(solution)/shard_map/ppermute | solution.py:52
  88.3 3.7 %collective-permute-start.11 = (bf16[2,2,64,768]{3,2,1,0:T(8,128)(2,1)S(1)}, bf16[2,2,64,768]{3,2,1,0:T(8,128)(2,1)S(1)}, u32[]{:S(2)}, u32[]{:S(2)}) collective-permute-start(bf16[2,2,64,768]{3,2,1,0:T(8,128)(2,1)S(1)} %pad_maximum_fusion.3), channel_id=1, source_target_pairs={{0,8},{1,57},{2,10},{3,59},{4,12},{5,61},{6,14},{7,63},{8,16},{9,1... | collective-permute-start | bytes 1179656 | tf_op jit(solution)/shard_map/ppermute | solution.py:61
  92.0 7.8 %collective-permute-start.12 = (bf16[64,768]{1,0:T(8,128)(2,1)S(1)}, bf16[64,768]{1,0:T(8,128)(2,1)S(1)}, u32[]{:S(2)}, u32[]{:S(2)}) collective-permute-start(bf16[64,768]{1,0:T(8,128)(2,1)S(1)} %slice_bitcast_fusion.5), channel_id=1, source_target_pairs={{0,16},{1,49},{2,18},{3,51},{4,20},{5,53},{6,22},{7,55},{8,24},{9,... | collective-permute-start | bytes 294920 | tf_op jit(solution)/shard_map/ppermute | solution.py:61
  101.5 4.0 %collective-permute-done.12 = bf16[64,768]{1,0:T(8,128)(2,1)S(1)} collective-permute-done((bf16[64,768]{1,0:T(8,128)(2,1)S(1)}, bf16[64,768]{1,0:T(8,128)(2,1)S(1)}, u32[]{:S(2)}, u32[]{:S(2)}) %collective-permute-start.12) | collective-permute-done | bytes 98336 | tf_op jit(solution)/shard_map/ppermute | solution.py:61
  105.5 2.2 %collective-permute-start.14 = (bf16[384,1536]{1,0:T(8,128)(2,1)S(1)}, bf16[384,1536]{1,0:T(8,128)(2,1)S(1)}, u32[]{:S(2)}, u32[]{:S(2)}) collective-permute-start(bf16[384,1536]{1,0:T(8,128)(2,1)S(1)} %shard_map.61), channel_id=1, source_target_pairs={{0,1},{1,0},{2,3},{3,2},{4,5},{5,4},{6,7},{7,6},{8,9},{9,8},{10,11... | collective-permute-start | bytes 3538952 | tf_op jit(solution)/shard_map/ppermute | solution.py:52
  107.9 2.2 %collective-permute-start.16 = (bf16[2,64,384]{2,1,0:T(8,128)(2,1)S(1)}, bf16[2,64,384]{2,1,0:T(8,128)(2,1)S(1)}, u32[]{:S(2)}, u32[]{:S(2)}) collective-permute-start(bf16[2,64,384]{2,1,0:T(8,128)(2,1)S(1)} %slice.210), channel_id=1, source_target_pairs={{0,1},{1,0},{2,3},{3,2},{4,5},{5,4},{6,7},{7,6},{8,9},{9,8},{10,11... | collective-permute-start | bytes 294920 | tf_op jit(solution)/shard_map/ppermute | solution.py:52
  110.1 11.1 %collective-permute-start.15 = (bf16[2,64,384]{2,1,0:T(8,128)(2,1)S(1)}, bf16[2,64,384]{2,1,0:T(8,128)(2,1)S(1)}, u32[]{:S(2)}, u32[]{:S(2)}) collective-permute-start(bf16[2,64,384]{2,1,0:T(8,128)(2,1)S(1)} %get-tuple-element.74), channel_id=1, source_target_pairs={{0,17},{1,48},{2,19},{3,50},{4,21},{5,52},{6,23},{7,54},{8,25},{9,... | collective-permute-start | bytes 294920 | tf_op jit(solution)/shard_map/ppermute | solution.py:61
  121.2 4.9 %collective-permute-start.13 = (bf16[2,64,384]{2,1,0:T(8,128)(2,1)S(1)}, bf16[2,64,384]{2,1,0:T(8,128)(2,1)S(1)}, u32[]{:S(2)}, u32[]{:S(2)}) collective-permute-start(bf16[2,64,384]{2,1,0:T(8,128)(2,1)S(1)} %get-tuple-element.73), channel_id=1, source_target_pairs={{0,16},{1,49},{2,18},{3,51},{4,20},{5,53},{6,22},{7,55},{8,24},{9,... | collective-permute-start | bytes 294920 | tf_op jit(solution)/shard_map/ppermute | solution.py:61
  126.1 3.0 %shard_map.62 = f32[384,1536]{1,0:T(8,128)} custom-call(bf16[4,2,64,768]{3,2,1,0:T(8,128)(2,1)S(1)} %copy.8.evens_ref, bf16[4,64,768]{2,1,0:T(8,128)(2,1)S(1)} %collective-permute-done.7.odds_ref, bf16[64,768]{1,0:T(8,128)(2,1)S(1)} %collective-permute-done.8.far_ref, bf16[3,64,768]{2,1,0:T(8,128)(2,1)S(1)} %collective-permute-done.9.evens_other_ref, ...), custom_call_target="tpu_custom_call" | custom-call | flops 1207959552 | bytes 6291456 | tf_op jit(solution)/shard_map/pallas_call | solution.py:131
  129.1 4.9 %collective-permute-done.13 = bf16[2,64,384]{2,1,0:T(8,128)(2,1)S(1)} collective-permute-done((bf16[2,64,384]{2,1,0:T(8,128)(2,1)S(1)}, bf16[2,64,384]{2,1,0:T(8,128)(2,1)S(1)}, u32[]{:S(2)}, u32[]{:S(2)}) %collective-permute-start.13) | collective-permute-done | bytes 98336 | tf_op jit(solution)/shard_map/ppermute | solution.py:61
  (53 shorter events, 18.9 us)
Async XLA Ops:
  0.6 3.4 %collective-permute-start = (bf16[128,384]{1,0:T(8,128)(2,1)}, bf16[128,384]{1,0:T(8,128)(2,1)S(1)}, u32[]{:S(2)}, u32[]{:S(2)}) collective-permute-start(bf16[128,384]{1,0:T(8,128)(2,1)} %param.6), channel_id=1, source_target_pairs={{0,1},{1,0},{2,3},{3,2},{4,5},{5,4},{6,7},{7,6},{8,9},{9,8},{10,11... | collective-permute-start | bytes 294920 | tf_op jit(solution)/shard_map/ppermute | solution.py:52
  5.9 26.1 %all-to-all-start = ((bf16[4,64,1536]{2,1,0:T(8,128)(2,1)}), bf16[4,64,1536]{2,1,0:T(8,128)(2,1)S(1)}, u32[]{:S(2)}, u32[]{:S(2)}) async-start(bf16[4,64,1536]{2,1,0:T(8,128)(2,1)} %broadcast_in_dim.4), calls=%async_computation | async-start | bytes 1572864 | tf_op jit(solution)/shard_map/all_to_all | solution.py:47
  10.8 21.3 %collective-permute-start.1 = (bf16[2,64,768]{2,1,0:T(8,128)(2,1)S(1)}, bf16[2,64,768]{2,1,0:T(8,128)(2,1)S(1)}, u32[]{:S(2)}, u32[]{:S(2)}) collective-permute-start(bf16[2,64,768]{2,1,0:T(8,128)(2,1)S(1)} %reverse_select_fusion), channel_id=1, source_target_pairs={{0,48},{1,17},{2,50},{3,19},{4,52},{5,21},{6,54},{7,23},{8,56},{9,... | collective-permute-start | bytes 589832 | tf_op jit(solution)/shard_map/ppermute | solution.py:61
  32.0 1.9 %copy-start.1 = (bf16[2,64,768]{2,1,0:T(8,128)(2,1)}, bf16[2,64,768]{2,1,0:T(8,128)(2,1)S(1)}, u32[]{:S(2)}) copy-start(bf16[2,64,768]{2,1,0:T(8,128)(2,1)S(1)} %collective-permute-done.1) | copy-start | bytes 589828
  33.9 25.5 %all-to-all-start.1 = ((bf16[4,256,1536]{2,1,0:T(8,128)(2,1)}), bf16[4,256,1536]{2,1,0:T(8,128)(2,1)S(1)}, u32[]{:S(2)}, u32[]{:S(2)}) async-start(bf16[4,256,1536]{2,1,0:T(8,128)(2,1)} %broadcast_in_dim.5), calls=%async_computation.1 | async-start | bytes 6291456 | tf_op jit(solution)/shard_map/all_to_all | solution.py:47
  38.6 14.2 %collective-permute-start.2 = (bf16[2,2,64,768]{3,2,0,1:T(8,128)(2,1)S(1)}, bf16[2,2,64,768]{3,2,0,1:T(8,128)(2,1)}, u32[]{:S(2)}, u32[]{:S(2)}) collective-permute-start(bf16[2,2,64,768]{3,2,0,1:T(8,128)(2,1)S(1)} %pad_maximum_fusion.2), channel_id=1, source_target_pairs={{0,56},{1,9},{2,58},{3,11},{4,60},{5,13},{6,62},{7,15},{8,0},{9,17... | collective-permute-start | bytes 1179656 | tf_op jit(solution)/shard_map/ppermute | solution.py:61
  43.2 27.7 %collective-permute-start.3 = (bf16[384,1536]{1,0:T(8,128)(2,1)}, bf16[384,1536]{1,0:T(8,128)(2,1)}, u32[]{:S(2)}, u32[]{:S(2)}) collective-permute-start(bf16[384,1536]{1,0:T(8,128)(2,1)} %own_ref.3), channel_id=1, source_target_pairs={{0,1},{1,0},{2,3},{3,2},{4,5},{5,4},{6,7},{7,6},{8,9},{9,8},{10,11... | collective-permute-start | bytes 3538952 | tf_op jit(solution)/shard_map/ppermute | solution.py:52
  46.0 30.6 %collective-permute-start.8 = (bf16[64,768]{1,0:T(8,128)(2,1)S(1)}, bf16[64,768]{1,0:T(8,128)(2,1)S(1)}, u32[]{:S(2)}, u32[]{:S(2)}) collective-permute-start(bf16[64,768]{1,0:T(8,128)(2,1)S(1)} %slice_bitcast_fusion.6), channel_id=1, source_target_pairs={{0,48},{1,17},{2,50},{3,19},{4,52},{5,21},{6,54},{7,23},{8,56},{9,... | collective-permute-start | bytes 294920 | tf_op jit(solution)/shard_map/ppermute | solution.py:61
  61.6 9.4 %copy-start = (bf16[384,1536]{1,0:T(8,128)(2,1)S(1)}, bf16[384,1536]{1,0:T(8,128)(2,1)}, u32[]{:S(2)}) copy-start(bf16[384,1536]{1,0:T(8,128)(2,1)} %own_ref.3) | copy-start | bytes 3538948
  61.6 20.7 %collective-permute-start.9 = (bf16[3,64,768]{2,1,0:T(8,128)(2,1)S(1)}, bf16[3,64,768]{2,1,0:T(8,128)(2,1)S(1)}, u32[]{:S(2)}, u32[]{:S(2)}) collective-permute-start(bf16[3,64,768]{2,1,0:T(8,128)(2,1)S(1)} %fusion.9), channel_id=1, source_target_pairs={{0,1},{1,0},{2,3},{3,2},{4,5},{5,4},{6,7},{7,6},{8,9},{9,8},{10,11... | collective-permute-start | bytes 884744 | tf_op jit(solution)/shard_map/ppermute | solution.py:52
  63.7 22.9 %collective-permute-start.10 = (bf16[4,64,768]{2,1,0:T(8,128)(2,1)S(1)}, bf16[4,64,768]{2,1,0:T(8,128)(2,1)S(1)}, u32[]{:S(2)}, u32[]{:S(2)}) collective-permute-start(bf16[4,64,768]{2,1,0:T(8,128)(2,1)S(1)} %pad_maximum_fusion.1), channel_id=1, source_target_pairs={{0,61},{1,4},{2,63},{3,6},{4,1},{5,8},{6,3},{7,10},{8,5},{9,12},{1... | collective-permute-start | bytes 1179656 | tf_op jit(solution)/shard_map/ppermute | solution.py:61
  67.6 18.9 %collective-permute-start.7 = (bf16[4,64,768]{2,1,0:T(8,128)(2,1)S(1)}, bf16[4,64,768]{2,1,0:T(8,128)(2,1)S(1)}, u32[]{:S(2)}, u32[]{:S(2)}) collective-permute-start(bf16[4,64,768]{2,1,0:T(8,128)(2,1)S(1)} %slice_bitcast_fusion), channel_id=1, source_target_pairs={{0,60},{1,5},{2,62},{3,7},{4,0},{5,9},{6,2},{7,11},{8,4},{9,13},{1... | collective-permute-start | bytes 1179656 | tf_op jit(solution)/shard_map/ppermute | solution.py:61
  74.7 11.9 %collective-permute-start.5 = (bf16[4,64,768]{2,1,0:T(8,128)(2,1)S(1)}, bf16[4,64,768]{2,1,0:T(8,128)(2,1)S(1)}, u32[]{:S(2)}, u32[]{:S(2)}) collective-permute-start(bf16[4,64,768]{2,1,0:T(8,128)(2,1)S(1)} %get-tuple-element.62), channel_id=1, source_target_pairs={{0,61},{1,4},{2,63},{3,6},{4,1},{5,8},{6,3},{7,10},{8,5},{9,12},{1... | collective-permute-start | bytes 1179656 | tf_op jit(solution)/shard_map/ppermute | solution.py:61
  76.7 11.4 %collective-permute-start.4 = (bf16[4,64,768]{2,1,0:T(8,128)(2,1)S(1)}, bf16[4,64,768]{2,1,0:T(8,128)(2,1)S(1)}, u32[]{:S(2)}, u32[]{:S(2)}) collective-permute-start(bf16[4,64,768]{2,1,0:T(8,128)(2,1)S(1)} %get-tuple-element.63), channel_id=1, source_target_pairs={{0,4},{1,61},{2,6},{3,63},{4,8},{5,1},{6,10},{7,3},{8,12},{9,5},{1... | collective-permute-start | bytes 1179656 | tf_op jit(solution)/shard_map/ppermute | solution.py:61
  82.3 4.3 %collective-permute-start.6 = (bf16[3,64,768]{2,1,0:T(8,128)(2,1)S(1)}, bf16[3,64,768]{2,1,0:T(8,128)(2,1)S(1)}, u32[]{:S(2)}, u32[]{:S(2)}) collective-permute-start(bf16[3,64,768]{2,1,0:T(8,128)(2,1)S(1)} %slice.160), channel_id=1, source_target_pairs={{0,1},{1,0},{2,3},{3,2},{4,5},{5,4},{6,7},{7,6},{8,9},{9,8},{10,11... | collective-permute-start | bytes 884744 | tf_op jit(solution)/shard_map/ppermute | solution.py:52
  88.3 17.2 %collective-permute-start.11 = (bf16[2,2,64,768]{3,2,1,0:T(8,128)(2,1)S(1)}, bf16[2,2,64,768]{3,2,1,0:T(8,128)(2,1)S(1)}, u32[]{:S(2)}, u32[]{:S(2)}) collective-permute-start(bf16[2,2,64,768]{3,2,1,0:T(8,128)(2,1)S(1)} %pad_maximum_fusion.3), channel_id=1, source_target_pairs={{0,8},{1,57},{2,10},{3,59},{4,12},{5,61},{6,14},{7,63},{8,16},{9,1... | collective-permute-start | bytes 1179656 | tf_op jit(solution)/shard_map/ppermute | solution.py:61
  92.0 13.5 %collective-permute-start.12 = (bf16[64,768]{1,0:T(8,128)(2,1)S(1)}, bf16[64,768]{1,0:T(8,128)(2,1)S(1)}, u32[]{:S(2)}, u32[]{:S(2)}) collective-permute-start(bf16[64,768]{1,0:T(8,128)(2,1)S(1)} %slice_bitcast_fusion.5), channel_id=1, source_target_pairs={{0,16},{1,49},{2,18},{3,51},{4,20},{5,53},{6,22},{7,55},{8,24},{9,... | collective-permute-start | bytes 294920 | tf_op jit(solution)/shard_map/ppermute | solution.py:61
  105.5 20.6 %collective-permute-start.14 = (bf16[384,1536]{1,0:T(8,128)(2,1)S(1)}, bf16[384,1536]{1,0:T(8,128)(2,1)S(1)}, u32[]{:S(2)}, u32[]{:S(2)}) collective-permute-start(bf16[384,1536]{1,0:T(8,128)(2,1)S(1)} %shard_map.61), channel_id=1, source_target_pairs={{0,1},{1,0},{2,3},{3,2},{4,5},{5,4},{6,7},{7,6},{8,9},{9,8},{10,11... | collective-permute-start | bytes 3538952 | tf_op jit(solution)/shard_map/ppermute | solution.py:52
  107.9 18.2 %collective-permute-start.16 = (bf16[2,64,384]{2,1,0:T(8,128)(2,1)S(1)}, bf16[2,64,384]{2,1,0:T(8,128)(2,1)S(1)}, u32[]{:S(2)}, u32[]{:S(2)}) collective-permute-start(bf16[2,64,384]{2,1,0:T(8,128)(2,1)S(1)} %slice.210), channel_id=1, source_target_pairs={{0,1},{1,0},{2,3},{3,2},{4,5},{5,4},{6,7},{7,6},{8,9},{9,8},{10,11... | collective-permute-start | bytes 294920 | tf_op jit(solution)/shard_map/ppermute | solution.py:52
  110.1 16.0 %collective-permute-start.15 = (bf16[2,64,384]{2,1,0:T(8,128)(2,1)S(1)}, bf16[2,64,384]{2,1,0:T(8,128)(2,1)S(1)}, u32[]{:S(2)}, u32[]{:S(2)}) collective-permute-start(bf16[2,64,384]{2,1,0:T(8,128)(2,1)S(1)} %get-tuple-element.74), channel_id=1, source_target_pairs={{0,17},{1,48},{2,19},{3,50},{4,21},{5,52},{6,23},{7,54},{8,25},{9,... | collective-permute-start | bytes 294920 | tf_op jit(solution)/shard_map/ppermute | solution.py:61
  121.2 12.8 %collective-permute-start.13 = (bf16[2,64,384]{2,1,0:T(8,128)(2,1)S(1)}, bf16[2,64,384]{2,1,0:T(8,128)(2,1)S(1)}, u32[]{:S(2)}, u32[]{:S(2)}) collective-permute-start(bf16[2,64,384]{2,1,0:T(8,128)(2,1)S(1)} %get-tuple-element.73), channel_id=1, source_target_pairs={{0,16},{1,49},{2,18},{3,51},{4,20},{5,53},{6,22},{7,55},{8,24},{9,... | collective-permute-start | bytes 294920 | tf_op jit(solution)/shard_map/ppermute | solution.py:61

commit v4 on v3

v4 whole, which is shorter than its diff:
```python
import functools
import math

import jax
import jax.numpy as jnp
from jax import lax
from jax.experimental import pallas as pl
from jax.experimental.pallas import tpu as pltpu
from jax.sharding import PartitionSpec as P

cubic_term = 0.044715
plane = ("row", "rep")
ring = ("col", "rep")


def gelu_slope(values):
    scale = math.sqrt(2.0 / math.pi)
    inner = scale * (values + cubic_term * values * values * values)
    tangent = jnp.tanh(inner)
    return 0.5 * (1.0 + tangent) + 0.5 * values * (1.0 - tangent * tangent) * scale * (
        1.0 + 3.0 * cubic_term * values * values
    )


def index(x, y, core):
    return ((x * 2 + y % 2) * 2 + y // 2) * 2 + core


y_order = (0, 2, 1, 3)
along_x = [[[index(x, y, core) for x in range(4)] for y in y_order] for core in range(2)]
along_y = [[[index(x, y, core) for y in y_order] for x in range(4)] for core in range(2)]


early_steps = (7, 5, 3, 1, -7, -5, -3, -1, 8)
late_steps = (6, 4, 2, 0, -6, -4, -2)


def place(step):
    core = lax.rem(lax.axis_index("rep"), 2)
    chip = lax.rem(lax.axis_index("col") + (1 - 2 * core) * step + 16, 16)
    return jnp.where(core == 0, lax.rem(chip, 4) * 4 + lax.div(chip, 4), chip)


def gather(values, groups):
    copies = jnp.broadcast_to(values[None], (4,) + values.shape)
    parts = lax.all_to_all(copies, plane, 0, 0, axis_index_groups=groups)
    return parts.reshape((4 * values.shape[0],) + values.shape[1:])


def swap_cores(values):
    return lax.ppermute(values, "rep", [(0, 1), (1, 0), (2, 3), (3, 2)])


def gather_plane(gelu_grad, weight):
    line = gather(gelu_grad, along_x[0] + along_y[1])
    grad_tokens = gather(line, along_y[0] + along_x[1])
    return grad_tokens, swap_cores(weight)


def send(values, distance, cross=False):
    pairs = []
    for z in range(16):
        for rep in range(4):
            target = (z + (-distance if rep % 2 else distance)) % 16
            pairs.append((z * 4 + rep, target * 4 + (rep ^ 1 if cross else rep)))
    return lax.ppermute(values, ring, pairs)


def matmul_nt(a, b):
    return lax.dot_general(a, b, (((1,), (1,)), ((), ())), preferred_element_type=jnp.float32)


def matmul_tn(a, b):
    return lax.dot_general(a, b, (((0,), (0,)), ((), ())), preferred_element_type=jnp.float32)


def partial_kernel(steps, groups, grad_ref, own_ref, other_ref, out_ref):
    width = own_ref.shape[0]
    for start, count, flipped in groups:
        rows = jnp.concatenate([grad_ref[place(steps[start + i])] for i in range(count)], axis=0)
        for side, ref in enumerate((other_ref, own_ref) if flipped else (own_ref, other_ref)):
            part = matmul_nt(rows, ref[...]).astype(out_ref.dtype)
            out_ref[start : start + count, :, side * width : (side + 1) * width] = part.reshape(
                count, -1, width
            )


def partials(steps, grad_blocks, weight_own, weight_other, groups):
    count = len(steps)
    rows, depth = grad_blocks.shape[1:]
    width = weight_own.shape[0]
    vmem = pl.BlockSpec(memory_space=pltpu.VMEM)
    return pl.pallas_call(
        functools.partial(partial_kernel, steps, groups),
        out_shape=jax.ShapeDtypeStruct((count, rows, 2 * width), jnp.bfloat16),
        in_specs=[vmem] * 3,
        out_specs=vmem,
        compiler_params=pltpu.CompilerParams(vmem_limit_bytes=32 * 1024 * 1024),
        cost_estimate=pl.CostEstimate(
            flops=4 * count * rows * depth * width,
            bytes_accessed=2 * (grad_blocks.size + 2 * width * depth + 2 * count * rows * width),
            transcendentals=0,
        ),
    )(grad_blocks, weight_own, weight_other)


def weight_kernel(input_ref, grad_ref, other_ref, out_ref, rows_ref):
    half, depth = grad_ref.shape[1:]
    core = lax.rem(lax.axis_index("rep"), 2)
    for chip in range(16):
        turned = (chip % 4) * 4 + chip // 4
        own_at = jnp.where(core == 0, turned, chip)
        other_at = jnp.where(core == 0, chip, turned) + 16
        for at, tokens in ((own_at, core), (other_at, 1 - core)):
            rows = pl.ds(pl.multiple_of(at * half, half), half)
            rows_ref[rows, :] = input_ref[chip, tokens]
    tile = 256
    for start in range(0, depth, tile):
        out_ref[:, start : start + tile] = sum(
            matmul_tn(
                rows_ref[16 * half * i : 16 * half * (i + 1), :],
                ref[:, :, start : start + tile].reshape(16 * half, tile),
            )
            for i, ref in enumerate((grad_ref, other_ref))
        )


def weight_gradient(input_whole, grad_blocks, grad_other):
    tokens, width = input_whole.shape
    half, depth = grad_blocks.shape[1:]
    vmem = pl.BlockSpec(memory_space=pltpu.VMEM)
    return pl.pallas_call(
        weight_kernel,
        out_shape=jax.ShapeDtypeStruct((width, depth), jnp.float32),
        in_specs=[vmem] * 3,
        out_specs=vmem,
        scratch_shapes=[pltpu.VMEM((tokens, width), jnp.bfloat16)],
        compiler_params=pltpu.CompilerParams(vmem_limit_bytes=40 * 1024 * 1024),
        cost_estimate=pl.CostEstimate(
            flops=2 * tokens * width * depth,
            bytes_accessed=2 * tokens * (width + depth) + 4 * width * depth,
            transcendentals=0,
        ),
    )(input_whole.reshape(16, 2, half, width), grad_blocks, grad_other)


def local(layer_input, weight, gelu_input, upstream):
    first = lax.axis_index("rep") % 2 == 0
    tokens, width = layer_input.shape
    half = tokens // 2
    f32, bf16 = jnp.float32, jnp.bfloat16

    input_whole = lax.all_gather(layer_input, "col", axis=0, tiled=True)
    gelu_grad = (upstream.astype(f32) * gelu_slope(gelu_input.astype(f32))).astype(bf16)

    grad_tokens, weight_other = lax.cond(
        lax.axis_index("col") < 16,
        gather_plane,
        lambda g, w: (jnp.zeros((16 * half, g.shape[1]), g.dtype), jnp.zeros_like(w)),
        gelu_grad,
        weight,
    )
    grad_blocks = grad_tokens.reshape((16, half) + grad_tokens.shape[1:])
    grad_other = swap_cores(grad_blocks)

    ahead = partials(
        early_steps, grad_blocks, weight, weight_other, ((0, 4, False), (4, 4, True), (8, 1, False))
    )
    ahead, later_blocks = lax.optimization_barrier((ahead, grad_blocks))
    moved = (send(ahead[:4], 1), send(ahead[4:8], -1, cross=True))
    moved_far = send(ahead[8], 2)
    rest = partials(late_steps, later_blocks, weight, weight_other, ((0, 4, False), (4, 3, True)))
    rest_sibling = swap_cores(rest[4:])
    moved, moved_far, rest, rest_sibling = lax.optimization_barrier(
        (moved, moved_far, rest, rest_sibling)
    )

    sums = [
        jnp.stack([m[i].astype(f32) + r[i].astype(f32) for m, r in zip(moved, (rest, rest_sibling))])
        for i in range(3)
    ]
    sums[0] = sums[0].at[0].add(moved_far.astype(f32))
    here = jnp.stack([moved[0][3].astype(f32) + rest[3].astype(f32), moved[1][3].astype(f32)])
    moved = send(jnp.stack([sums[0], sums[2]]).astype(bf16), 2)
    moved, input_whole = lax.optimization_barrier((moved, input_whole))
    here = here + moved[1].astype(f32)
    last = (sums[1] + moved[0].astype(f32)).astype(bf16)
    moved = send(last[:, :, :width], 4)
    moved_cross = send(last[:, :, width:], 4, cross=True)
    here_cross = swap_cores(here[:, :, width:].astype(bf16))

    grad_weight = weight_gradient(input_whole, grad_blocks, grad_other)
    moved, grad_weight = lax.optimization_barrier((moved, grad_weight))
    cross = moved_cross.astype(f32) + here_cross.astype(f32)
    summed = here[:, :, :width] + moved.astype(f32) + cross[::-1]
    own, other = summed[0], summed[1]
    grad_input = jnp.where(
        first, jnp.concatenate([own, other]), jnp.concatenate([other, own])
    ).astype(bf16)
    return (grad_input, grad_weight)


def solution(mesh):
    in_specs = (
        P("col", ("row", "rep")),
        P(("row", "rep"), "col"),
        P(("row", "rep"), "col"),
        P(("row", "rep"), "col"),
    )
    out_specs = (P("col", ("row", "rep")), P(("row", "rep"), "col"))
    return jax.shard_map(local, mesh=mesh, in_specs=in_specs, out_specs=out_specs, check_vma=False)
```

time: 136 us -> 142 us (1.044)
  the two profiles are of different devices: /device:TPU:34 before, /device:TPU:1 now
where the time goes in v4:
time: 142 us
  starting transfers between devices  59 us (42%)
  waiting for transfers between devices  29.4 us (21%)
  Pallas kernels  15.1 us (11%)
  between operations  14.2 us (10%)
  blocking collectives  12.9 us (9%)
  other arithmetic  6.05 us (4%)
  local copies, waits for them, and re-layouts  4.78 us (3%)
    ppermute x6, starting transfers between devices, send(): return lax.ppermute(values, ring, pairs)  30 us
    ppermute x4, starting transfers between devices, swap_cores(): return lax.ppermute(values, 'rep', [(0, 1), (1, 0), (2, 3), (3, 2)])  24.1 us
    ppermute x6, waiting for transfers between devices, send(): return lax.ppermute(values, ring, pairs)  15.5 us
    all_to_all x1, blocking collectives, gather(): parts = lax.all_to_all(copies, plane, 0, 0, axis_index_groups=groups)  12.9 us
    all_to_all x1, waiting for transfers between devices, gather(): parts = lax.all_to_all(copies, plane, 0, 0, axis_index_groups=groups)  10.6 us
    pallas_call x2, Pallas kernels, partials(): pl.pallas_call(functools.partial(partial_kernel, steps, groups), out_shap...  9 us
    pallas_call x1, Pallas kernels, weight_gradient(): pl.pallas_call(weight_kernel, out_shape=jax.ShapeDtypeStruct((width, dept...  6.12 us
    all_to_all x1, starting transfers between devices, gather(): parts = lax.all_to_all(copies, plane, 0, 0, axis_index_groups=groups)  4.78 us
  transfers between devices with their start and end apart: 12, of which 5 were waited for; matrix products, arithmetic and copies ran while one was open for 6% of the time, Pallas kernels for 11%

profile of v4, /device:TPU:1, one launch (start us, length us, event | category | flops | bytes accessed | tf_op | source)
XLA Modules:
  0.0 141.5 jit_solution(4974983766301379651)
XLA Ops:
  9.2 40.6 %conditional.1 = (bf16[384,1536]{1,0:T(8,128)(2,1)}, bf16[16,64,1536]{2,1,0:T(8,128)(2,1)}) conditional(s32[]{:T(128)} %convert_element_type.102, () %tuple.26, (bf16[384,1536]{1,0:T(8,128)(2,1)}, bf16[64,1536]{1,0:T(8,128)(2,1)S(1)}) %tuple.27), branch_computations={%region_0.1_spmd, %region_1.2_spmd} | conditional | bytes 25362548 | solution.py:156
  9.3 12.9 %all_to_all.8 = bf16[4,64,1536]{2,1,0:T(8,128)(2,1)S(1)} all-to-all(bf16[4,64,1536]{2,1,0:T(8,128)(2,1)S(1)} %broadcast_in_dim.0), channel_id=1, replica_groups={{0,128,256,384},{2,130,258,386},{64,192,320,448},{66,194,322,450},{1,3,..., dimensions={0} | all-to-all | bytes 1572864 | tf_op jit(solution)/shard_map/cond/branch_1_fun/all_to_all | solution.py:46
  22.1 1.9 %broadcast_in_dim.2 = bf16[4,256,1536]{2,1,0:T(8,128)(2,1)} broadcast(bf16[256,1536]{1,0:T(8,128)(2,1)S(1)} %bitcast.27), dimensions={1,2} | broadcast | bytes 3932160 | tf_op jit(solution)/shard_map/cond/branch_1_fun/broadcast_in_dim | solution.py:45
  24.0 4.8 %all-to-all-start.1 = ((bf16[4,256,1536]{2,1,0:T(8,128)(2,1)}), bf16[4,256,1536]{2,1,0:T(8,128)(2,1)}, u32[]{:S(2)}, u32[]{:S(2)}) async-start(bf16[4,256,1536]{2,1,0:T(8,128)(2,1)} %broadcast_in_dim.2), calls=%async_computation.1 | async-start | bytes 6291456 | tf_op jit(solution)/shard_map/cond/branch_1_fun/all_to_all | solution.py:46
  28.8 7.8 %collective-permute-start = (bf16[384,1536]{1,0:T(8,128)(2,1)S(1)}, bf16[384,1536]{1,0:T(8,128)(2,1)}, u32[]{:S(2)}, u32[]{:S(2)}) collective-permute-start(bf16[384,1536]{1,0:T(8,128)(2,1)S(1)} %copy-done.2), channel_id=1, source_target_pairs={{0,1},{1,0},{2,3},{3,2},{4,5},{5,4},{6,7},{7,6},{8,9},{9,8},{10,11... | collective-permute-start | bytes 3538952 | tf_op jit(solution)/shard_map/cond/branch_1_fun/ppermute | solution.py:51
  36.6 2.6 %collective-permute-done = bf16[384,1536]{1,0:T(8,128)(2,1)} collective-permute-done((bf16[384,1536]{1,0:T(8,128)(2,1)S(1)}, bf16[384,1536]{1,0:T(8,128)(2,1)}, u32[]{:S(2)}, u32[]{:S(2)}) %collective-permute-start) | collective-permute-done | bytes 1179680 | tf_op jit(solution)/shard_map/cond/branch_1_fun/ppermute | solution.py:51
  39.2 10.6 %all-to-all-done.1 = bf16[4,256,1536]{2,1,0:T(8,128)(2,1)} async-done(((bf16[4,256,1536]{2,1,0:T(8,128)(2,1)}), bf16[4,256,1536]{2,1,0:T(8,128)(2,1)}, u32[]{:S(2)}, u32[]{:S(2)}) %all-to-all-start.1) | async-done | bytes 3145760 | tf_op jit(solution)/shard_map/cond/branch_1_fun/all_to_all | solution.py:46
  49.8 8.7 %collective-permute-start.7 = (bf16[16,64,1536]{2,1,0:T(8,128)(2,1)}, bf16[16,64,1536]{2,1,0:T(8,128)(2,1)S(1)}, u32[]{:S(2)}, u32[]{:S(2)}) collective-permute-start(bf16[16,64,1536]{2,1,0:T(8,128)(2,1)} %get-tuple-element.37.grad_ref), channel_id=1, source_target_pairs={{0,1},{1,0},{2,3},{3,2},{4,5},{5,4},{6,7},{7,6},{8,9},{9,8},{10,11... | collective-permute-start | bytes 9437192 | tf_op jit(solution)/shard_map/ppermute | solution.py:51
  58.5 5.0 %shard_map.59 = bf16[9,64,768]{2,1,0:T(8,128)(2,1)S(1)} custom-call(bf16[16,64,1536]{2,1,0:T(8,128)(2,1)} %get-tuple-element.37.grad_ref, bf16[384,1536]{1,0:T(8,128)(2,1)} %own_ref.3, bf16[384,1536]{1,0:T(8,128)(2,1)} %get-tuple-element.35.other_ref), custom_call_target="tpu_custom_call" | custom-call | flops 1358954496 | bytes 6389760 | tf_op jit(solution)/shard_map/pallas_call | solution.py:93
  63.6 2.1 %collective-permute-start.2 = (bf16[4,64,768]{2,1,0:T(8,128)(2,1)S(1)}, bf16[4,64,768]{2,1,0:T(8,128)(2,1)S(1)}, u32[]{:S(2)}, u32[]{:S(2)}) collective-permute-start(bf16[4,64,768]{2,1,0:T(8,128)(2,1)S(1)} %get-tuple-element.50), channel_id=1, source_target_pairs={{0,61},{1,4},{2,63},{3,6},{4,1},{5,8},{6,3},{7,10},{8,5},{9,12},{1... | collective-permute-start | bytes 1179656 | tf_op jit(solution)/shard_map/ppermute | solution.py:66
  65.7 7.4 %collective-permute-start.1 = (bf16[4,64,768]{2,1,0:T(8,128)(2,1)S(1)}, bf16[4,64,768]{2,1,0:T(8,128)(2,1)S(1)}, u32[]{:S(2)}, u32[]{:S(2)}) collective-permute-start(bf16[4,64,768]{2,1,0:T(8,128)(2,1)S(1)} %get-tuple-element.51), channel_id=1, source_target_pairs={{0,4},{1,61},{2,6},{3,63},{4,8},{5,1},{6,10},{7,3},{8,12},{9,5},{1... | collective-permute-start | bytes 1179656 | tf_op jit(solution)/shard_map/ppermute | solution.py:66
  73.1 4.0 %shard_map.60 = bf16[7,64,768]{2,1,0:T(8,128)(2,1)S(1)} custom-call(bf16[16,64,1536]{2,1,0:T(8,128)(2,1)} %get-tuple-element.37.grad_ref, bf16[384,1536]{1,0:T(8,128)(2,1)S(1)} %copy-done.1, bf16[384,1536]{1,0:T(8,128)(2,1)} %get-tuple-element.35.other_ref), custom_call_target="tpu_custom_call" | custom-call | flops 1056964608 | bytes 6193152 | tf_op jit(solution)/shard_map/pallas_call | solution.py:93
  77.1 2.3 %collective-permute-start.4 = (bf16[3,64,768]{2,1,0:T(8,128)(2,1)S(1)}, bf16[3,64,768]{2,1,0:T(8,128)(2,1)S(1)}, u32[]{:S(2)}, u32[]{:S(2)}) collective-permute-start(bf16[3,64,768]{2,1,0:T(8,128)(2,1)S(1)} %slice.129), channel_id=1, source_target_pairs={{0,1},{1,0},{2,3},{3,2},{4,5},{5,4},{6,7},{7,6},{8,9},{9,8},{10,11... | collective-permute-start | bytes 884744 | tf_op jit(solution)/shard_map/ppermute | solution.py:51
  79.5 4.1 %collective-permute-start.3 = (bf16[64,768]{1,0:T(8,128)(2,1)S(1)}, bf16[64,768]{1,0:T(8,128)(2,1)S(1)}, u32[]{:S(2)}, u32[]{:S(2)}) collective-permute-start(bf16[64,768]{1,0:T(8,128)(2,1)S(1)} %slice_bitcast_fusion.2), channel_id=1, source_target_pairs={{0,8},{1,57},{2,10},{3,59},{4,12},{5,61},{6,14},{7,63},{8,16},{9,1... | collective-permute-start | bytes 294920 | tf_op jit(solution)/shard_map/ppermute | solution.py:66
  83.6 2.7 %collective-permute-done.3 = bf16[64,768]{1,0:T(8,128)(2,1)S(1)} collective-permute-done((bf16[64,768]{1,0:T(8,128)(2,1)S(1)}, bf16[64,768]{1,0:T(8,128)(2,1)S(1)}, u32[]{:S(2)}, u32[]{:S(2)}) %collective-permute-start.3) | collective-permute-done | bytes 98336 | tf_op jit(solution)/shard_map/ppermute | solution.py:66
  88.0 4.9 %collective-permute-start.5 = (bf16[2,2,64,768]{3,2,1,0:T(8,128)(2,1)S(1)}, bf16[2,2,64,768]{3,2,1,0:T(8,128)(2,1)}, u32[]{:S(2)}, u32[]{:S(2)}) collective-permute-start(bf16[2,2,64,768]{3,2,1,0:T(8,128)(2,1)S(1)} %pad_maximum_fusion), channel_id=1, source_target_pairs={{0,8},{1,57},{2,10},{3,59},{4,12},{5,61},{6,14},{7,63},{8,16},{9,1... | collective-permute-start | bytes 1179656 | tf_op jit(solution)/shard_map/ppermute | solution.py:66
  92.9 9.0 %collective-permute-done.5 = bf16[2,2,64,768]{3,2,1,0:T(8,128)(2,1)} collective-permute-done((bf16[2,2,64,768]{3,2,1,0:T(8,128)(2,1)S(1)}, bf16[2,2,64,768]{3,2,1,0:T(8,128)(2,1)}, u32[]{:S(2)}, u32[]{:S(2)}) %collective-permute-start.5) | collective-permute-done | bytes 393248 | tf_op jit(solution)/shard_map/ppermute | solution.py:66
  101.9 1.4 fusion.9
  103.9 5.3 %collective-permute-start.9 = (bf16[2,64,384]{2,1,0:T(8,128)(2,1)}, bf16[2,64,384]{2,1,0:T(8,128)(2,1)}, u32[]{:S(2)}, u32[]{:S(2)}) collective-permute-start(bf16[2,64,384]{2,1,0:T(8,128)(2,1)} %slice.164), channel_id=1, source_target_pairs={{0,1},{1,0},{2,3},{3,2},{4,5},{5,4},{6,7},{7,6},{8,9},{9,8},{10,11... | collective-permute-start | bytes 294920 | tf_op jit(solution)/shard_map/ppermute | solution.py:51
  110.0 6.7 %collective-permute-start.8 = (bf16[2,64,384]{2,1,0:T(8,128)(2,1)}, bf16[2,64,384]{2,1,0:T(8,128)(2,1)}, u32[]{:S(2)}, u32[]{:S(2)}) collective-permute-start(bf16[2,64,384]{2,1,0:T(8,128)(2,1)} %get-tuple-element.59), channel_id=1, source_target_pairs={{0,17},{1,48},{2,19},{3,50},{4,21},{5,52},{6,23},{7,54},{8,25},{9,... | collective-permute-start | bytes 294920 | tf_op jit(solution)/shard_map/ppermute | solution.py:66
  116.7 4.9 %collective-permute-start.6 = (bf16[2,64,384]{2,1,0:T(8,128)(2,1)}, bf16[2,64,384]{2,1,0:T(8,128)(2,1)S(1)}, u32[]{:S(2)}, u32[]{:S(2)}) collective-permute-start(bf16[2,64,384]{2,1,0:T(8,128)(2,1)} %get-tuple-element.58), channel_id=1, source_target_pairs={{0,16},{1,49},{2,18},{3,51},{4,20},{5,53},{6,22},{7,55},{8,24},{9,... | collective-permute-start | bytes 294920 | tf_op jit(solution)/shard_map/ppermute | solution.py:66
  121.6 3.8 %collective-permute-done.8 = bf16[2,64,384]{2,1,0:T(8,128)(2,1)} collective-permute-done((bf16[2,64,384]{2,1,0:T(8,128)(2,1)}, bf16[2,64,384]{2,1,0:T(8,128)(2,1)}, u32[]{:S(2)}, u32[]{:S(2)}) %collective-permute-start.8) | collective-permute-done | bytes 98336 | tf_op jit(solution)/shard_map/ppermute | solution.py:66
  126.4 1.4 copy-done
  127.8 6.1 %shard_map.61 = f32[384,1536]{1,0:T(8,128)} custom-call(bf16[16,2,64,384]{3,2,1,0:T(8,128)(2,1)S(1)} %bitcast.26, bf16[16,64,1536]{2,1,0:T(8,128)(2,1)} %get-tuple-element.37.grad_ref, bf16[16,64,1536]{2,1,0:T(8,128)(2,1)S(1)} %collective-permute-done.7.other_ref), custom_call_target="tpu_custom_call" | custom-call | flops 2415919104 | bytes 10223616 | tf_op jit(solution)/shard_map/pallas_call | solution.py:132
  (32 shorter events, 6.9 us)
Async XLA Ops:
  7.2 94.7 %all-gather.2.cloned.1.call-start = ((), (), s32[]{:S(2)}) async-start(), calls=%async_computation.2 | async-start | bytes 1671168 | tf_op jit(solution)/shard_map/all_gather | solution.py:153
  24.0 4.8 %copy-start.2 = (bf16[384,1536]{1,0:T(8,128)(2,1)S(1)}, bf16[384,1536]{1,0:T(8,128)(2,1)}, u32[]{:S(2)}) copy-start(bf16[384,1536]{1,0:T(8,128)(2,1)} %get-tuple-element.17) | copy-start | bytes 3538948 | tf_op jit(solution)/shard_map/cond
  24.0 25.8 %all-to-all-start.1 = ((bf16[4,256,1536]{2,1,0:T(8,128)(2,1)}), bf16[4,256,1536]{2,1,0:T(8,128)(2,1)}, u32[]{:S(2)}, u32[]{:S(2)}) async-start(bf16[4,256,1536]{2,1,0:T(8,128)(2,1)} %broadcast_in_dim.2), calls=%async_computation.1 | async-start | bytes 6291456 | tf_op jit(solution)/shard_map/cond/branch_1_fun/all_to_all | solution.py:46
  28.8 10.4 %collective-permute-start = (bf16[384,1536]{1,0:T(8,128)(2,1)S(1)}, bf16[384,1536]{1,0:T(8,128)(2,1)}, u32[]{:S(2)}, u32[]{:S(2)}) collective-permute-start(bf16[384,1536]{1,0:T(8,128)(2,1)S(1)} %copy-done.2), channel_id=1, source_target_pairs={{0,1},{1,0},{2,3},{3,2},{4,5},{5,4},{6,7},{7,6},{8,9},{9,8},{10,11... | collective-permute-start | bytes 3538952 | tf_op jit(solution)/shard_map/cond/branch_1_fun/ppermute | solution.py:51
  49.8 76.6 %collective-permute-start.7 = (bf16[16,64,1536]{2,1,0:T(8,128)(2,1)}, bf16[16,64,1536]{2,1,0:T(8,128)(2,1)S(1)}, u32[]{:S(2)}, u32[]{:S(2)}) collective-permute-start(bf16[16,64,1536]{2,1,0:T(8,128)(2,1)} %get-tuple-element.37.grad_ref), channel_id=1, source_target_pairs={{0,1},{1,0},{2,3},{3,2},{4,5},{5,4},{6,7},{7,6},{8,9},{9,8},{10,11... | collective-permute-start | bytes 9437192 | tf_op jit(solution)/shard_map/ppermute | solution.py:51
  63.6 9.6 %copy-start.1 = (bf16[384,1536]{1,0:T(8,128)(2,1)S(1)}, bf16[384,1536]{1,0:T(8,128)(2,1)}, u32[]{:S(2)}) copy-start(bf16[384,1536]{1,0:T(8,128)(2,1)} %own_ref.3) | copy-start | bytes 3538948
  63.6 22.6 %collective-permute-start.2 = (bf16[4,64,768]{2,1,0:T(8,128)(2,1)S(1)}, bf16[4,64,768]{2,1,0:T(8,128)(2,1)S(1)}, u32[]{:S(2)}, u32[]{:S(2)}) collective-permute-start(bf16[4,64,768]{2,1,0:T(8,128)(2,1)S(1)} %get-tuple-element.50), channel_id=1, source_target_pairs={{0,61},{1,4},{2,63},{3,6},{4,1},{5,8},{6,3},{7,10},{8,5},{9,12},{1... | collective-permute-start | bytes 1179656 | tf_op jit(solution)/shard_map/ppermute | solution.py:66
  65.7 20.6 %collective-permute-start.1 = (bf16[4,64,768]{2,1,0:T(8,128)(2,1)S(1)}, bf16[4,64,768]{2,1,0:T(8,128)(2,1)S(1)}, u32[]{:S(2)}, u32[]{:S(2)}) collective-permute-start(bf16[4,64,768]{2,1,0:T(8,128)(2,1)S(1)} %get-tuple-element.51), channel_id=1, source_target_pairs={{0,4},{1,61},{2,6},{3,63},{4,8},{5,1},{6,10},{7,3},{8,12},{9,5},{1... | collective-permute-start | bytes 1179656 | tf_op jit(solution)/shard_map/ppermute | solution.py:66
  77.1 9.1 %collective-permute-start.4 = (bf16[3,64,768]{2,1,0:T(8,128)(2,1)S(1)}, bf16[3,64,768]{2,1,0:T(8,128)(2,1)S(1)}, u32[]{:S(2)}, u32[]{:S(2)}) collective-permute-start(bf16[3,64,768]{2,1,0:T(8,128)(2,1)S(1)} %slice.129), channel_id=1, source_target_pairs={{0,1},{1,0},{2,3},{3,2},{4,5},{5,4},{6,7},{7,6},{8,9},{9,8},{10,11... | collective-permute-start | bytes 884744 | tf_op jit(solution)/shard_map/ppermute | solution.py:51
  79.5 6.8 %collective-permute-start.3 = (bf16[64,768]{1,0:T(8,128)(2,1)S(1)}, bf16[64,768]{1,0:T(8,128)(2,1)S(1)}, u32[]{:S(2)}, u32[]{:S(2)}) collective-permute-start(bf16[64,768]{1,0:T(8,128)(2,1)S(1)} %slice_bitcast_fusion.2), channel_id=1, source_target_pairs={{0,8},{1,57},{2,10},{3,59},{4,12},{5,61},{6,14},{7,63},{8,16},{9,1... | collective-permute-start | bytes 294920 | tf_op jit(solution)/shard_map/ppermute | solution.py:66
  88.0 13.9 %collective-permute-start.5 = (bf16[2,2,64,768]{3,2,1,0:T(8,128)(2,1)S(1)}, bf16[2,2,64,768]{3,2,1,0:T(8,128)(2,1)}, u32[]{:S(2)}, u32[]{:S(2)}) collective-permute-start(bf16[2,2,64,768]{3,2,1,0:T(8,128)(2,1)S(1)} %pad_maximum_fusion), channel_id=1, source_target_pairs={{0,8},{1,57},{2,10},{3,59},{4,12},{5,61},{6,14},{7,63},{8,16},{9,1... | collective-permute-start | bytes 1179656 | tf_op jit(solution)/shard_map/ppermute | solution.py:66
  103.9 17.7 %collective-permute-start.9 = (bf16[2,64,384]{2,1,0:T(8,128)(2,1)}, bf16[2,64,384]{2,1,0:T(8,128)(2,1)}, u32[]{:S(2)}, u32[]{:S(2)}) collective-permute-start(bf16[2,64,384]{2,1,0:T(8,128)(2,1)} %slice.164), channel_id=1, source_target_pairs={{0,1},{1,0},{2,3},{3,2},{4,5},{5,4},{6,7},{7,6},{8,9},{9,8},{10,11... | collective-permute-start | bytes 294920 | tf_op jit(solution)/shard_map/ppermute | solution.py:51
  110.0 15.5 %collective-permute-start.8 = (bf16[2,64,384]{2,1,0:T(8,128)(2,1)}, bf16[2,64,384]{2,1,0:T(8,128)(2,1)}, u32[]{:S(2)}, u32[]{:S(2)}) collective-permute-start(bf16[2,64,384]{2,1,0:T(8,128)(2,1)} %get-tuple-element.59), channel_id=1, source_target_pairs={{0,17},{1,48},{2,19},{3,50},{4,21},{5,52},{6,23},{7,54},{8,25},{9,... | collective-permute-start | bytes 294920 | tf_op jit(solution)/shard_map/ppermute | solution.py:66
  116.7 17.2 %collective-permute-start.6 = (bf16[2,64,384]{2,1,0:T(8,128)(2,1)}, bf16[2,64,384]{2,1,0:T(8,128)(2,1)S(1)}, u32[]{:S(2)}, u32[]{:S(2)}) collective-permute-start(bf16[2,64,384]{2,1,0:T(8,128)(2,1)} %get-tuple-element.58), channel_id=1, source_target_pairs={{0,16},{1,49},{2,18},{3,51},{4,20},{5,53},{6,22},{7,55},{8,24},{9,... | collective-permute-start | bytes 294920 | tf_op jit(solution)/shard_map/ppermute | solution.py:66
  126.4 1.4 copy-start
Sparse Core Ops, SparseCore 0:
  10.1 69.7 all-gather.1

commit v5 on v4

--- a/solution.py
+++ b/solution.py
@@ -31,8 +31,8 @@
 along_y = [[[index(x, y, core) for y in y_order] for x in range(4)] for core in range(2)]
 
 
-early_steps = (7, 5, 3, 1, -7, -5, -3, -1, 8)
-late_steps = (6, 4, 2, 0, -6, -4, -2)
+early_groups = (((7, 5, 3, 1), False), ((-7, -5, -3, -1), True), ((8,), False))
+late_groups = (((6, 4, 2, 0), False), ((-6, -4, -2), True))
 
 
 def place(step):
@@ -51,10 +51,28 @@
     return lax.ppermute(values, "rep", [(0, 1), (1, 0), (2, 3), (3, 2)])
 
 
-def gather_plane(gelu_grad, weight):
+def first_round(gelu_grad, weight):
     line = gather(gelu_grad, along_x[0] + along_y[1])
     grad_tokens = gather(line, along_y[0] + along_x[1])
-    return grad_tokens, swap_cores(weight)
+    weight_other = swap_cores(weight)
+    grad_blocks = grad_tokens.reshape((16, gelu_grad.shape[0], gelu_grad.shape[1]))
+
+    ahead = partials(early_groups, grad_blocks, weight, weight_other)
+    ahead, later_blocks = lax.optimization_barrier((ahead, grad_blocks))
+    moved = send(ahead[0], 1), send(ahead[1], -1, cross=True), send(ahead[2], 2)
+    rest, for_sibling = partials(late_groups, later_blocks, weight, weight_other)
+    rest_sibling = swap_cores(for_sibling)
+    rest, later_blocks = lax.optimization_barrier((rest, later_blocks))
+    grad_other = swap_cores(later_blocks)
+
+    both = (2,) + rest.shape[1:]
+    outs = [
+        jax.ShapeDtypeStruct((2,) + both, jnp.bfloat16),
+        jax.ShapeDtypeStruct(both, jnp.float32),
+        jax.ShapeDtypeStruct(both, jnp.float32),
+    ]
+    sums = call(first_kernel, outs, (*moved, rest, rest_sibling))
+    return (*sums, grad_blocks, grad_other)
 
 
 def send(values, distance, cross=False):
@@ -74,34 +92,73 @@
     return lax.dot_general(a, b, (((0,), (0,)), ((), ())), preferred_element_type=jnp.float32)
 
 
-def partial_kernel(steps, groups, grad_ref, own_ref, other_ref, out_ref):
+def call(kernel, outs, args, flops=0):
+    vmem = pl.BlockSpec(memory_space=pltpu.VMEM)
+    moved = sum(v.size * v.dtype.itemsize for v in tuple(args) + tuple(outs))
+    return pl.pallas_call(
+        kernel,
+        out_shape=outs,
+        in_specs=[vmem] * len(args),
+        out_specs=tuple(vmem for _ in outs),
+        compiler_params=pltpu.CompilerParams(vmem_limit_bytes=32 * 1024 * 1024),
+        cost_estimate=pl.CostEstimate(flops=flops, bytes_accessed=moved, transcendentals=0),
+    )(*args)
+
+
+def partial_kernel(groups, grad_ref, own_ref, other_ref, *outs):
     width = own_ref.shape[0]
-    for start, count, flipped in groups:
-        rows = jnp.concatenate([grad_ref[place(steps[start + i])] for i in range(count)], axis=0)
+    for (steps, flipped), out_ref in zip(groups, outs):
+        rows = jnp.concatenate([grad_ref[place(step)] for step in steps], axis=0)
         for side, ref in enumerate((other_ref, own_ref) if flipped else (own_ref, other_ref)):
             part = matmul_nt(rows, ref[...]).astype(out_ref.dtype)
-            out_ref[start : start + count, :, side * width : (side + 1) * width] = part.reshape(
-                count, -1, width
-            )
-
-
-def partials(steps, grad_blocks, weight_own, weight_other, groups):
-    count = len(steps)
+            out_ref[:, :, side * width : (side + 1) * width] = part.reshape(len(steps), -1, width)
+
+
+def partials(groups, grad_blocks, weight_own, weight_other):
     rows, depth = grad_blocks.shape[1:]
     width = weight_own.shape[0]
-    vmem = pl.BlockSpec(memory_space=pltpu.VMEM)
-    return pl.pallas_call(
-        functools.partial(partial_kernel, steps, groups),
-        out_shape=jax.ShapeDtypeStruct((count, rows, 2 * width), jnp.bfloat16),
-        in_specs=[vmem] * 3,
-        out_specs=vmem,
-        compiler_params=pltpu.CompilerParams(vmem_limit_bytes=32 * 1024 * 1024),
-        cost_estimate=pl.CostEstimate(
-            flops=4 * count * rows * depth * width,
-            bytes_accessed=2 * (grad_blocks.size + 2 * width * depth + 2 * count * rows * width),
-            transcendentals=0,
-        ),
-    )(grad_blocks, weight_own, weight_other)
+    outs = [jax.ShapeDtypeStruct((len(g[0]), rows, 2 * width), jnp.bfloat16) for g in groups]
+    return call(
+        functools.partial(partial_kernel, groups),
+        outs,
+        (grad_blocks, weight_own, weight_other),
+        flops=4 * sum(len(g[0]) for g in groups) * rows * depth * width,
+    )
+
+
+def first_kernel(own_ref, cross_ref, far_ref, rest_ref, other_ref, send_ref, middle_ref, here_ref):
+    def total(i, *refs):
+        return sum(ref[i].astype(jnp.float32) for ref in refs)
+
+    dtype = send_ref.dtype
+    send_ref[0, 0] = (total(0, own_ref, rest_ref) + far_ref[0].astype(jnp.float32)).astype(dtype)
+    send_ref[0, 1] = total(0, cross_ref, other_ref).astype(dtype)
+    send_ref[1, 0] = total(2, own_ref, rest_ref).astype(dtype)
+    send_ref[1, 1] = total(2, cross_ref, other_ref).astype(dtype)
+    middle_ref[0] = total(1, own_ref, rest_ref)
+    middle_ref[1] = total(1, cross_ref, other_ref)
+    here_ref[0] = total(3, own_ref, rest_ref)
+    here_ref[1] = total(3, cross_ref)
+
+
+def second_kernel(moved_ref, middle_ref, here_ref, own_ref, cross_ref, stay_ref, swap_ref):
+    width = own_ref.shape[2]
+    ahead = (middle_ref[...] + moved_ref[0].astype(jnp.float32)).astype(own_ref.dtype)
+    own_ref[...] = ahead[:, :, :width]
+    cross_ref[...] = ahead[:, :, width:]
+    here = here_ref[...] + moved_ref[1].astype(jnp.float32)
+    stay_ref[...] = here[:, :, :width]
+    swap_ref[...] = here[:, :, width:].astype(swap_ref.dtype)
+
+
+def third_kernel(own_ref, cross_ref, stay_ref, swap_ref, out_ref):
+    half = own_ref.shape[1]
+    core = lax.rem(lax.axis_index("rep"), 2)
+    for i, place_of in enumerate((core, 1 - core)):
+        other = cross_ref[1 - i].astype(jnp.float32) + swap_ref[1 - i].astype(jnp.float32)
+        part = stay_ref[i] + own_ref[i].astype(jnp.float32) + other
+        rows = pl.ds(pl.multiple_of(place_of * half, half), half)
+        out_ref[rows, :] = part.astype(out_ref.dtype)
 
 
 def weight_kernel(input_ref, grad_ref, other_ref, out_ref, rows_ref):
@@ -145,7 +202,6 @@
 
 
 def local(layer_input, weight, gelu_input, upstream):
-    first = lax.axis_index("rep") % 2 == 0
     tokens, width = layer_input.shape
     half = tokens // 2
     f32, bf16 = jnp.float32, jnp.bfloat16
@@ -153,50 +209,25 @@
     input_whole = lax.all_gather(layer_input, "col", axis=0, tiled=True)
     gelu_grad = (upstream.astype(f32) * gelu_slope(gelu_input.astype(f32))).astype(bf16)
 
-    grad_tokens, weight_other = lax.cond(
+    both, blocks = (2, half, 2 * width), (16, half, gelu_grad.shape[1])
+    shapes = (((2,) + both, bf16), (both, f32), (both, f32), (blocks, bf16), (blocks, bf16))
+    to_send, middle, here, grad_blocks, grad_other = lax.cond(
         lax.axis_index("col") < 16,
-        gather_plane,
-        lambda g, w: (jnp.zeros((16 * half, g.shape[1]), g.dtype), jnp.zeros_like(w)),
+        first_round,
+        lambda g, w: tuple(jnp.zeros(*v) for v in shapes),
         gelu_grad,
         weight,
     )
-    grad_blocks = grad_tokens.reshape((16, half) + grad_tokens.shape[1:])
-    grad_other = swap_cores(grad_blocks)
-
-    ahead = partials(
-        early_steps, grad_blocks, weight, weight_other, ((0, 4, False), (4, 4, True), (8, 1, False))
-    )
-    ahead, later_blocks = lax.optimization_barrier((ahead, grad_blocks))
-    moved = (send(ahead[:4], 1), send(ahead[4:8], -1, cross=True))
-    moved_far = send(ahead[8], 2)
-    rest = partials(late_steps, later_blocks, weight, weight_other, ((0, 4, False), (4, 3, True)))
-    rest_sibling = swap_cores(rest[4:])
-    moved, moved_far, rest, rest_sibling = lax.optimization_barrier(
-        (moved, moved_far, rest, rest_sibling)
-    )
-
-    sums = [
-        jnp.stack([m[i].astype(f32) + r[i].astype(f32) for m, r in zip(moved, (rest, rest_sibling))])
-        for i in range(3)
-    ]
-    sums[0] = sums[0].at[0].add(moved_far.astype(f32))
-    here = jnp.stack([moved[0][3].astype(f32) + rest[3].astype(f32), moved[1][3].astype(f32)])
-    moved = send(jnp.stack([sums[0], sums[2]]).astype(bf16), 2)
-    moved, input_whole = lax.optimization_barrier((moved, input_whole))
-    here = here + moved[1].astype(f32)
-    last = (sums[1] + moved[0].astype(f32)).astype(bf16)
-    moved = send(last[:, :, :width], 4)
-    moved_cross = send(last[:, :, width:], 4, cross=True)
-    here_cross = swap_cores(here[:, :, width:].astype(bf16))
-
+
+    moved = send(to_send, 2)
     grad_weight = weight_gradient(input_whole, grad_blocks, grad_other)
     moved, grad_weight = lax.optimization_barrier((moved, grad_weight))
-    cross = moved_cross.astype(f32) + here_cross.astype(f32)
-    summed = here[:, :, :width] + moved.astype(f32) + cross[::-1]
-    own, other = summed[0], summed[1]
-    grad_input = jnp.where(
-        first, jnp.concatenate([own, other]), jnp.concatenate([other, own])
-    ).astype(bf16)
+    part = (2, half, width)
+    outs = [jax.ShapeDtypeStruct(part, t) for t in (bf16, bf16, f32, bf16)]
+    own, cross, stay, swapped = call(second_kernel, outs, (moved, middle, here))
+    last = send(own, 4), send(cross, 4, cross=True), stay, swap_cores(swapped)
+    outs = [jax.ShapeDtypeStruct((tokens, width), bf16)]
+    grad_input = call(third_kernel, outs, last)[0]
     return (grad_input, grad_weight)
 
 

time: 142 us -> 127 us (0.89)
  waiting for transfers between devices: 29.4 us -> 21.6 us
  other arithmetic: 6.05 us -> 1.3 us
  starting transfers between devices: 59 us -> 55.6 us
  Pallas kernels: 15.1 us -> 16.7 us
    ppermute x6, waiting for transfers between devices: 15.5 us -> 7.69 us  [send(): return lax.ppermute(values, ring, pairs)]
    ppermute x4, starting transfers between devices: 24.1 us -> 21.5 us  [swap_cores(): return lax.ppermute(values, 'rep', [(0, 1), (1, 0), (2, 3), (3, 2)])]
    add x5 -> x0, other arithmetic: 2.57 us -> none  [the longest x3 1.58 us: local(): m[i].astype(f32) + r[i].astype(f32)]
    convert_element_type x2 -> x0, other arithmetic: 2.06 us -> none  [the longest x1 1.4 us: local(): last = (sums[1] + moved[0].astype(f32)).astype(bf16)]
    slice x4 -> x0, local copies, waits for them, and re-layouts: 1.42 us -> none  [the longest x1 0.69 us: local(): moved = send(last[:, :, :width], 4)]
    pallas_call x2 -> x5, Pallas kernels: 9 us -> 9.6 us  [call(): pl.pallas_call(kernel, out_shape=outs, in_specs=[vmem] * len(args), out_s...]
  transfers between devices with their start and end apart: 12 -> 12, of which waited for: 5 -> 4; matrix products, arithmetic and copies ran while one was open for 6% -> 3% of each run, Pallas kernels for 11% -> 13%
where the time goes in v5:
time: 127 us; the launch traced here: 126 us
  starting transfers between devices  55.6 us (44%)
  waiting for transfers between devices  21.6 us (17%)
  Pallas kernels  16.7 us (13%)
  between operations  14.1 us (11%)
  blocking collectives  12.9 us (10%)
  local copies, waits for them, and re-layouts  3.37 us (3%)
  other arithmetic  1.3 us (1%)
    ppermute x6, starting transfers between devices, send(): return lax.ppermute(values, ring, pairs)  29.3 us
    ppermute x4, starting transfers between devices, swap_cores(): return lax.ppermute(values, 'rep', [(0, 1), (1, 0), (2, 3), (3, 2)])  21.5 us
    all_to_all x1, blocking collectives, gather(): parts = lax.all_to_all(copies, plane, 0, 0, axis_index_groups=groups)  12.9 us
    all_to_all x1, waiting for transfers between devices, gather(): parts = lax.all_to_all(copies, plane, 0, 0, axis_index_groups=groups)  10.7 us
    pallas_call x5, Pallas kernels, call(): pl.pallas_call(kernel, out_shape=outs, in_specs=[vmem] * len(args), out_s...  9.6 us
    ppermute x6, waiting for transfers between devices, send(): return lax.ppermute(values, ring, pairs)  7.69 us
    pallas_call x1, Pallas kernels, weight_gradient(): pl.pallas_call(weight_kernel, out_shape=jax.ShapeDtypeStruct((width, dept...  7.07 us
    all_to_all x1, starting transfers between devices, gather(): parts = lax.all_to_all(copies, plane, 0, 0, axis_index_groups=groups)  4.78 us
  transfers between devices with their start and end apart: 12, of which 4 were waited for; matrix products, arithmetic and copies ran while one was open for 3% of the time, Pallas kernels for 13%

profile of v5, /device:TPU:1, one launch (start us, length us, event | category | flops | bytes accessed | tf_op | source)
XLA Modules:
  0.0 125.5 jit_solution(16267762216226895780)
XLA Ops:
  7.9 1.3 %fusion.7 = bf16[64,1536]{1,0:T(8,128)(2,1)S(1)} fusion(bf16[64,1536]{1,0:T(8,128)(2,1)} %param.8, bf16[64,1536]{1,0:T(8,128)(2,1)} %param.9), kind=kLoop, calls=%fused_computation.14 | loop fusion | flops 2064384 | bytes 589824 | tf_op jit(solution)/shard_map/convert_element_type | solution.py:210
  9.2 78.7 %conditional.1 = (bf16[2,2,64,768]{3,2,1,0:T(8,128)(2,1)}, f32[2,64,768]{2,1,0:T(8,128)S(1)}, f32[2,64,768]{2,1,0:T(8,128)S(1)}, bf16[16,64,1536]{2,1,0:T(8,128)(2,1)}, bf16[16,64,1536]{2,1,0:T(8,128)(2,1)}) conditional(s32[]{:T(128)} %convert_element_type.12, () %tuple.19, (bf16[64,1536]{1,0:T(8,128)(2,1)S(1)}, bf16[384,1536]{1,0:T(8,128)(2,1)}) %tuple.20), branch_computations={%region_0.0_spmd, %region_1.0_spmd} | conditional | flops 2415919104 | bytes 57999700 | solution.py:214
  9.3 12.9 %all_to_all.8 = bf16[4,64,1536]{2,1,0:T(8,128)(2,1)S(1)} all-to-all(bf16[4,64,1536]{2,1,0:T(8,128)(2,1)S(1)} %broadcast_in_dim.0), channel_id=1, replica_groups={{0,128,256,384},{2,130,258,386},{64,192,320,448},{66,194,322,450},{1,3,..., dimensions={0} | all-to-all | bytes 1572864 | tf_op jit(solution)/shard_map/cond/branch_1_fun/all_to_all | solution.py:46
  22.1 1.9 %broadcast_in_dim.2 = bf16[4,256,1536]{2,1,0:T(8,128)(2,1)} broadcast(bf16[256,1536]{1,0:T(8,128)(2,1)S(1)} %bitcast.4), dimensions={1,2} | broadcast | bytes 3932160 | tf_op jit(solution)/shard_map/cond/branch_1_fun/broadcast_in_dim | solution.py:45
  24.0 4.8 %all-to-all-start.1 = ((bf16[4,256,1536]{2,1,0:T(8,128)(2,1)}), bf16[4,256,1536]{2,1,0:T(8,128)(2,1)}, u32[]{:S(2)}, u32[]{:S(2)}) async-start(bf16[4,256,1536]{2,1,0:T(8,128)(2,1)} %broadcast_in_dim.2), calls=%async_computation.1 | async-start | bytes 6291456 | tf_op jit(solution)/shard_map/cond/branch_1_fun/all_to_all | solution.py:46
  28.8 7.8 %collective-permute-start = (bf16[384,1536]{1,0:T(8,128)(2,1)S(1)}, bf16[384,1536]{1,0:T(8,128)(2,1)S(1)}, u32[]{:S(2)}, u32[]{:S(2)}) collective-permute-start(bf16[384,1536]{1,0:T(8,128)(2,1)S(1)} %copy-done.1), channel_id=1, source_target_pairs={{0,1},{1,0},{2,3},{3,2},{4,5},{5,4},{6,7},{7,6},{8,9},{9,8},{10,11... | collective-permute-start | bytes 3538952 | tf_op jit(solution)/shard_map/cond/branch_1_fun/ppermute | solution.py:51
  36.7 2.5 %collective-permute-done.other_ref = bf16[384,1536]{1,0:T(8,128)(2,1)S(1)} collective-permute-done((bf16[384,1536]{1,0:T(8,128)(2,1)S(1)}, bf16[384,1536]{1,0:T(8,128)(2,1)S(1)}, u32[]{:S(2)}, u32[]{:S(2)}) %collective-permute-start) | collective-permute-done | bytes 1179680 | tf_op jit(solution)/shard_map/cond/branch_1_fun/ppermute | solution.py:51
  39.1 10.7 %all-to-all-done.1 = bf16[4,256,1536]{2,1,0:T(8,128)(2,1)} async-done(((bf16[4,256,1536]{2,1,0:T(8,128)(2,1)}), bf16[4,256,1536]{2,1,0:T(8,128)(2,1)}, u32[]{:S(2)}, u32[]{:S(2)}) %all-to-all-start.1) | async-done | bytes 3145760 | tf_op jit(solution)/shard_map/cond/branch_1_fun/all_to_all | solution.py:46
  49.9 4.3 %branch_1_fun.3 = (bf16[4,64,768]{2,1,0:T(8,128)(2,1)S(1)}, bf16[4,64,768]{2,1,0:T(8,128)(2,1)S(1)}, bf16[1,64,768]{2,1,0:T(8,128)(2,1)S(1)}) custom-call(bf16[16,64,1536]{2,1,0:T(8,128)(2,1)} %bitcast.1.grad_ref, bf16[384,1536]{1,0:T(8,128)(2,1)S(1)} %copy-done.1, bf16[384,1536]{1,0:T(8,128)(2,1)S(1)} %collective-permute-done.other_ref), custom_call_target="tpu_custom_call" | custom-call | flops 1358954496 | bytes 6389760 | tf_op jit(solution)/shard_map/cond/branch_1_fun/pallas_call | solution.py:98
  54.2 3.6 %branch_1_fun.4 = (bf16[4,64,768]{2,1,0:T(8,128)(2,1)S(1)}, bf16[3,64,768]{2,1,0:T(8,128)(2,1)S(1)}) custom-call(bf16[16,64,1536]{2,1,0:T(8,128)(2,1)} %bitcast.1.grad_ref, bf16[384,1536]{1,0:T(8,128)(2,1)S(1)} %copy-done.1, bf16[384,1536]{1,0:T(8,128)(2,1)S(1)} %collective-permute-done.other_ref), custom_call_target="tpu_custom_call" | custom-call | flops 1056964608 | bytes 6193152 | tf_op jit(solution)/shard_map/cond/branch_1_fun/pallas_call | solution.py:98
  57.8 8.7 %collective-permute-start.5 = (bf16[16,64,1536]{2,1,0:T(8,128)(2,1)}, bf16[16,64,1536]{2,1,0:T(8,128)(2,1)}, u32[]{:S(2)}, u32[]{:S(2)}) collective-permute-start(bf16[16,64,1536]{2,1,0:T(8,128)(2,1)} %bitcast.1.grad_ref), channel_id=1, source_target_pairs={{0,1},{1,0},{2,3},{3,2},{4,5},{5,4},{6,7},{7,6},{8,9},{9,8},{10,11... | collective-permute-start | bytes 9437192 | tf_op jit(solution)/shard_map/cond/branch_1_fun/ppermute | solution.py:51
  66.5 7.4 %collective-permute-start.1 = (bf16[4,64,768]{2,1,0:T(8,128)(2,1)S(1)}, bf16[4,64,768]{2,1,0:T(8,128)(2,1)S(1)}, u32[]{:S(2)}, u32[]{:S(2)}) collective-permute-start(bf16[4,64,768]{2,1,0:T(8,128)(2,1)S(1)} %get-tuple-element.9), channel_id=1, source_target_pairs={{0,4},{1,61},{2,6},{3,63},{4,8},{5,1},{6,10},{7,3},{8,12},{9,5},{1... | collective-permute-start | bytes 1179656 | tf_op jit(solution)/shard_map/cond/branch_1_fun/ppermute | solution.py:84
  74.0 1.9 %collective-permute-start.2 = (bf16[4,64,768]{2,1,0:T(8,128)(2,1)S(1)}, bf16[4,64,768]{2,1,0:T(8,128)(2,1)S(1)}, u32[]{:S(2)}, u32[]{:S(2)}) collective-permute-start(bf16[4,64,768]{2,1,0:T(8,128)(2,1)S(1)} %get-tuple-element.10), channel_id=1, source_target_pairs={{0,61},{1,4},{2,63},{3,6},{4,1},{5,8},{6,3},{7,10},{8,5},{9,12},{1... | collective-permute-start | bytes 1179656 | tf_op jit(solution)/shard_map/cond/branch_1_fun/ppermute | solution.py:84
  75.9 3.0 %collective-permute-start.4 = (bf16[3,64,768]{2,1,0:T(8,128)(2,1)S(1)}, bf16[3,64,768]{2,1,0:T(8,128)(2,1)S(1)}, u32[]{:S(2)}, u32[]{:S(2)}) collective-permute-start(bf16[3,64,768]{2,1,0:T(8,128)(2,1)S(1)} %get-tuple-element.15), channel_id=1, source_target_pairs={{0,1},{1,0},{2,3},{3,2},{4,5},{5,4},{6,7},{7,6},{8,9},{9,8},{10,11... | collective-permute-start | bytes 884744 | tf_op jit(solution)/shard_map/cond/branch_1_fun/ppermute | solution.py:51
  78.9 3.1 %collective-permute-start.3 = (bf16[1,64,768]{2,1,0:T(8,128)(2,1)S(1)}, bf16[1,64,768]{2,1,0:T(8,128)(2,1)S(1)}, u32[]{:S(2)}, u32[]{:S(2)}) collective-permute-start(bf16[1,64,768]{2,1,0:T(8,128)(2,1)S(1)} %get-tuple-element.11), channel_id=1, source_target_pairs={{0,8},{1,57},{2,10},{3,59},{4,12},{5,61},{6,14},{7,63},{8,16},{9,1... | collective-permute-start | bytes 294920 | tf_op jit(solution)/shard_map/cond/branch_1_fun/ppermute | solution.py:84
  82.0 5.0 %collective-permute-done.3.far_ref = bf16[1,64,768]{2,1,0:T(8,128)(2,1)S(1)} collective-permute-done((bf16[1,64,768]{2,1,0:T(8,128)(2,1)S(1)}, bf16[1,64,768]{2,1,0:T(8,128)(2,1)S(1)}, u32[]{:S(2)}, u32[]{:S(2)}) %collective-permute-start.3) | collective-permute-done | bytes 98336 | tf_op jit(solution)/shard_map/cond/branch_1_fun/ppermute | solution.py:84
  87.0 0.9 branch_1_fun.5
  87.9 5.0 %collective-permute-start.6 = (bf16[2,2,64,768]{3,2,1,0:T(8,128)(2,1)}, bf16[2,2,64,768]{3,2,1,0:T(8,128)(2,1)S(1)}, u32[]{:S(2)}, u32[]{:S(2)}) collective-permute-start(bf16[2,2,64,768]{3,2,1,0:T(8,128)(2,1)} %get-tuple-element.33), channel_id=1, source_target_pairs={{0,8},{1,57},{2,10},{3,59},{4,12},{5,61},{6,14},{7,63},{8,16},{9,1... | collective-permute-start | bytes 1179656 | tf_op jit(solution)/shard_map/ppermute | solution.py:84
  93.0 1.4 %copy-done = bf16[2048,384]{1,0:T(8,128)(2,1)S(1)} copy-done((bf16[2048,384]{1,0:T(8,128)(2,1)S(1)}, bf16[2048,384]{1,0:T(8,128)(2,1)}, u32[]{:S(2)}) %copy-start) | copy-done | bytes 1572888
  94.4 7.1 %shard_map.60 = f32[384,1536]{1,0:T(8,128)} custom-call(bf16[16,2,64,384]{3,2,1,0:T(8,128)(2,1)S(1)} %bitcast.3, bf16[16,64,1536]{2,1,0:T(8,128)(2,1)} %get-tuple-element.34.grad_ref, bf16[16,64,1536]{2,1,0:T(8,128)(2,1)} %get-tuple-element.35.other_ref), custom_call_target="tpu_custom_call" | custom-call | flops 2415919104 | bytes 10223616 | tf_op jit(solution)/shard_map/pallas_call | solution.py:189
  101.5 6.4 %collective-permute-start.7 = (bf16[2,64,384]{2,1,0:T(8,128)(2,1)S(1)}, bf16[2,64,384]{2,1,0:T(8,128)(2,1)S(1)}, u32[]{:S(2)}, u32[]{:S(2)}) collective-permute-start(bf16[2,64,384]{2,1,0:T(8,128)(2,1)S(1)} %get-tuple-element.39), channel_id=1, source_target_pairs={{0,16},{1,49},{2,18},{3,51},{4,20},{5,53},{6,22},{7,55},{8,24},{9,... | collective-permute-start | bytes 294920 | tf_op jit(solution)/shard_map/ppermute | solution.py:84
  107.9 5.4 %collective-permute-start.8 = (bf16[2,64,384]{2,1,0:T(8,128)(2,1)S(1)}, bf16[2,64,384]{2,1,0:T(8,128)(2,1)S(1)}, u32[]{:S(2)}, u32[]{:S(2)}) collective-permute-start(bf16[2,64,384]{2,1,0:T(8,128)(2,1)S(1)} %get-tuple-element.40), channel_id=1, source_target_pairs={{0,17},{1,48},{2,19},{3,50},{4,21},{5,52},{6,23},{7,54},{8,25},{9,... | collective-permute-start | bytes 294920 | tf_op jit(solution)/shard_map/ppermute | solution.py:84
  113.3 1.9 %collective-permute-start.9 = (bf16[2,64,384]{2,1,0:T(8,128)(2,1)S(1)}, bf16[2,64,384]{2,1,0:T(8,128)(2,1)S(1)}, u32[]{:S(2)}, u32[]{:S(2)}) collective-permute-start(bf16[2,64,384]{2,1,0:T(8,128)(2,1)S(1)} %get-tuple-element.42), channel_id=1, source_target_pairs={{0,1},{1,0},{2,3},{3,2},{4,5},{5,4},{6,7},{7,6},{8,9},{9,8},{10,11... | collective-permute-start | bytes 294920 | tf_op jit(solution)/shard_map/ppermute | solution.py:51
  115.3 2.7 %collective-permute-done.8.cross_ref = bf16[2,64,384]{2,1,0:T(8,128)(2,1)S(1)} collective-permute-done((bf16[2,64,384]{2,1,0:T(8,128)(2,1)S(1)}, bf16[2,64,384]{2,1,0:T(8,128)(2,1)S(1)}, u32[]{:S(2)}, u32[]{:S(2)}) %collective-permute-start.8) | collective-permute-done | bytes 98336 | tf_op jit(solution)/shard_map/ppermute | solution.py:84
  (16 shorter events, 1.6 us)
Async XLA Ops:
  7.2 85.8 %all-gather.2.cloned.1.call-start = ((), (), s32[]{:S(2)}) async-start(), calls=%async_computation.2 | async-start | bytes 1671168 | tf_op jit(solution)/shard_map/all_gather | solution.py:209
  24.0 4.8 %copy-start.1 = (bf16[384,1536]{1,0:T(8,128)(2,1)S(1)}, bf16[384,1536]{1,0:T(8,128)(2,1)}, u32[]{:S(2)}) copy-start(bf16[384,1536]{1,0:T(8,128)(2,1)} %get-tuple-element.45.own_ref) | copy-start | bytes 3538948 | tf_op jit(solution)/shard_map/cond
  24.0 25.8 %all-to-all-start.1 = ((bf16[4,256,1536]{2,1,0:T(8,128)(2,1)}), bf16[4,256,1536]{2,1,0:T(8,128)(2,1)}, u32[]{:S(2)}, u32[]{:S(2)}) async-start(bf16[4,256,1536]{2,1,0:T(8,128)(2,1)} %broadcast_in_dim.2), calls=%async_computation.1 | async-start | bytes 6291456 | tf_op jit(solution)/shard_map/cond/branch_1_fun/all_to_all | solution.py:46
  28.8 10.3 %collective-permute-start = (bf16[384,1536]{1,0:T(8,128)(2,1)S(1)}, bf16[384,1536]{1,0:T(8,128)(2,1)S(1)}, u32[]{:S(2)}, u32[]{:S(2)}) collective-permute-start(bf16[384,1536]{1,0:T(8,128)(2,1)S(1)} %copy-done.1), channel_id=1, source_target_pairs={{0,1},{1,0},{2,3},{3,2},{4,5},{5,4},{6,7},{7,6},{8,9},{9,8},{10,11... | collective-permute-start | bytes 3538952 | tf_op jit(solution)/shard_map/cond/branch_1_fun/ppermute | solution.py:51
  57.8 30.1 %collective-permute-start.5 = (bf16[16,64,1536]{2,1,0:T(8,128)(2,1)}, bf16[16,64,1536]{2,1,0:T(8,128)(2,1)}, u32[]{:S(2)}, u32[]{:S(2)}) collective-permute-start(bf16[16,64,1536]{2,1,0:T(8,128)(2,1)} %bitcast.1.grad_ref), channel_id=1, source_target_pairs={{0,1},{1,0},{2,3},{3,2},{4,5},{5,4},{6,7},{7,6},{8,9},{9,8},{10,11... | collective-permute-start | bytes 9437192 | tf_op jit(solution)/shard_map/cond/branch_1_fun/ppermute | solution.py:51
  66.5 20.5 %collective-permute-start.1 = (bf16[4,64,768]{2,1,0:T(8,128)(2,1)S(1)}, bf16[4,64,768]{2,1,0:T(8,128)(2,1)S(1)}, u32[]{:S(2)}, u32[]{:S(2)}) collective-permute-start(bf16[4,64,768]{2,1,0:T(8,128)(2,1)S(1)} %get-tuple-element.9), channel_id=1, source_target_pairs={{0,4},{1,61},{2,6},{3,63},{4,8},{5,1},{6,10},{7,3},{8,12},{9,5},{1... | collective-permute-start | bytes 1179656 | tf_op jit(solution)/shard_map/cond/branch_1_fun/ppermute | solution.py:84
  74.0 13.0 %collective-permute-start.2 = (bf16[4,64,768]{2,1,0:T(8,128)(2,1)S(1)}, bf16[4,64,768]{2,1,0:T(8,128)(2,1)S(1)}, u32[]{:S(2)}, u32[]{:S(2)}) collective-permute-start(bf16[4,64,768]{2,1,0:T(8,128)(2,1)S(1)} %get-tuple-element.10), channel_id=1, source_target_pairs={{0,61},{1,4},{2,63},{3,6},{4,1},{5,8},{6,3},{7,10},{8,5},{9,12},{1... | collective-permute-start | bytes 1179656 | tf_op jit(solution)/shard_map/cond/branch_1_fun/ppermute | solution.py:84
  75.9 11.1 %collective-permute-start.4 = (bf16[3,64,768]{2,1,0:T(8,128)(2,1)S(1)}, bf16[3,64,768]{2,1,0:T(8,128)(2,1)S(1)}, u32[]{:S(2)}, u32[]{:S(2)}) collective-permute-start(bf16[3,64,768]{2,1,0:T(8,128)(2,1)S(1)} %get-tuple-element.15), channel_id=1, source_target_pairs={{0,1},{1,0},{2,3},{3,2},{4,5},{5,4},{6,7},{7,6},{8,9},{9,8},{10,11... | collective-permute-start | bytes 884744 | tf_op jit(solution)/shard_map/cond/branch_1_fun/ppermute | solution.py:51
  78.9 8.1 %collective-permute-start.3 = (bf16[1,64,768]{2,1,0:T(8,128)(2,1)S(1)}, bf16[1,64,768]{2,1,0:T(8,128)(2,1)S(1)}, u32[]{:S(2)}, u32[]{:S(2)}) collective-permute-start(bf16[1,64,768]{2,1,0:T(8,128)(2,1)S(1)} %get-tuple-element.11), channel_id=1, source_target_pairs={{0,8},{1,57},{2,10},{3,59},{4,12},{5,61},{6,14},{7,63},{8,16},{9,1... | collective-permute-start | bytes 294920 | tf_op jit(solution)/shard_map/cond/branch_1_fun/ppermute | solution.py:84
  87.9 13.5 %collective-permute-start.6 = (bf16[2,2,64,768]{3,2,1,0:T(8,128)(2,1)}, bf16[2,2,64,768]{3,2,1,0:T(8,128)(2,1)S(1)}, u32[]{:S(2)}, u32[]{:S(2)}) collective-permute-start(bf16[2,2,64,768]{3,2,1,0:T(8,128)(2,1)} %get-tuple-element.33), channel_id=1, source_target_pairs={{0,8},{1,57},{2,10},{3,59},{4,12},{5,61},{6,14},{7,63},{8,16},{9,1... | collective-permute-start | bytes 1179656 | tf_op jit(solution)/shard_map/ppermute | solution.py:84
  93.0 1.4 %copy-start = (bf16[2048,384]{1,0:T(8,128)(2,1)S(1)}, bf16[2048,384]{1,0:T(8,128)(2,1)}, u32[]{:S(2)}) copy-start(bf16[2048,384]{1,0:T(8,128)(2,1)} %all-gather.2.cloned.1.call-done) | copy-start | bytes 4718596
  101.5 13.8 %collective-permute-start.7 = (bf16[2,64,384]{2,1,0:T(8,128)(2,1)S(1)}, bf16[2,64,384]{2,1,0:T(8,128)(2,1)S(1)}, u32[]{:S(2)}, u32[]{:S(2)}) collective-permute-start(bf16[2,64,384]{2,1,0:T(8,128)(2,1)S(1)} %get-tuple-element.39), channel_id=1, source_target_pairs={{0,16},{1,49},{2,18},{3,51},{4,20},{5,53},{6,22},{7,55},{8,24},{9,... | collective-permute-start | bytes 294920 | tf_op jit(solution)/shard_map/ppermute | solution.py:84
  107.9 10.1 %collective-permute-start.8 = (bf16[2,64,384]{2,1,0:T(8,128)(2,1)S(1)}, bf16[2,64,384]{2,1,0:T(8,128)(2,1)S(1)}, u32[]{:S(2)}, u32[]{:S(2)}) collective-permute-start(bf16[2,64,384]{2,1,0:T(8,128)(2,1)S(1)} %get-tuple-element.40), channel_id=1, source_target_pairs={{0,17},{1,48},{2,19},{3,50},{4,21},{5,52},{6,23},{7,54},{8,25},{9,... | collective-permute-start | bytes 294920 | tf_op jit(solution)/shard_map/ppermute | solution.py:84
  113.3 4.7 %collective-permute-start.9 = (bf16[2,64,384]{2,1,0:T(8,128)(2,1)S(1)}, bf16[2,64,384]{2,1,0:T(8,128)(2,1)S(1)}, u32[]{:S(2)}, u32[]{:S(2)}) collective-permute-start(bf16[2,64,384]{2,1,0:T(8,128)(2,1)S(1)} %get-tuple-element.42), channel_id=1, source_target_pairs={{0,1},{1,0},{2,3},{3,2},{4,5},{5,4},{6,7},{7,6},{8,9},{9,8},{10,11... | collective-permute-start | bytes 294920 | tf_op jit(solution)/shard_map/ppermute | solution.py:51
Sparse Core Ops, SparseCore 0:
  10.1 69.0 all-gather.1

commit v6 on v5

--- a/solution.py
+++ b/solution.py
@@ -62,7 +62,6 @@
     moved = send(ahead[0], 1), send(ahead[1], -1, cross=True), send(ahead[2], 2)
     rest, for_sibling = partials(late_groups, later_blocks, weight, weight_other)
     rest_sibling = swap_cores(for_sibling)
-    rest, later_blocks = lax.optimization_barrier((rest, later_blocks))
     grad_other = swap_cores(later_blocks)
 
     both = (2,) + rest.shape[1:]

time: 127 us -> 128 us (level)
  transfers between devices with their start and end apart: 12 -> 12, of which waited for: 4 -> 5; matrix products, arithmetic and copies ran while one was open for 3% -> 3% of each run, Pallas kernels for 13% -> 13%
where the time goes in v6:
time: 128 us; the launch traced here: 126 us
  starting transfers between devices  56.6 us (44%)
  waiting for transfers between devices  21.4 us (17%)
  Pallas kernels  16.7 us (13%)
  between operations  14.1 us (11%)
  blocking collectives  12.9 us (10%)
  local copies, waits for them, and re-layouts  3.37 us (3%)
  other arithmetic  1.3 us (1%)
    ppermute x6, starting transfers between devices, send(): return lax.ppermute(values, ring, pairs)  30.3 us
    ppermute x4, starting transfers between devices, swap_cores(): return lax.ppermute(values, 'rep', [(0, 1), (1, 0), (2, 3), (3, 2)])  21.5 us
    all_to_all x1, blocking collectives, gather(): parts = lax.all_to_all(copies, plane, 0, 0, axis_index_groups=groups)  12.9 us
    all_to_all x1, waiting for transfers between devices, gather(): parts = lax.all_to_all(copies, plane, 0, 0, axis_index_groups=groups)  10.7 us
    pallas_call x5, Pallas kernels, call(): pl.pallas_call(kernel, out_shape=outs, in_specs=[vmem] * len(args), out_s...  9.6 us
    ppermute x6, waiting for transfers between devices, send(): return lax.ppermute(values, ring, pairs)  7.47 us
    pallas_call x1, Pallas kernels, weight_gradient(): pl.pallas_call(weight_kernel, out_shape=jax.ShapeDtypeStruct((width, dept...  7.07 us
    all_to_all x1, starting transfers between devices, gather(): parts = lax.all_to_all(copies, plane, 0, 0, axis_index_groups=groups)  4.78 us
  transfers between devices with their start and end apart: 12, of which 5 were waited for; matrix products, arithmetic and copies ran while one was open for 3% of the time, Pallas kernels for 13%

profile of v6, /device:TPU:1, one launch (start us, length us, event | category | flops | bytes accessed | tf_op | source)
XLA Modules:
  0.0 126.3 jit_solution(11102061002890419142)
XLA Ops:
  7.9 1.3 %fusion.7 = bf16[64,1536]{1,0:T(8,128)(2,1)S(1)} fusion(bf16[64,1536]{1,0:T(8,128)(2,1)} %param.8, bf16[64,1536]{1,0:T(8,128)(2,1)} %param.9), kind=kLoop, calls=%fused_computation.14 | loop fusion | flops 2064384 | bytes 589824 | tf_op jit(solution)/shard_map/convert_element_type | solution.py:209
  9.2 78.8 %conditional.1 = (bf16[2,2,64,768]{3,2,1,0:T(8,128)(2,1)}, f32[2,64,768]{2,1,0:T(8,128)S(1)}, f32[2,64,768]{2,1,0:T(8,128)S(1)}, bf16[16,64,1536]{2,1,0:T(8,128)(2,1)}, bf16[16,64,1536]{2,1,0:T(8,128)(2,1)}) conditional(s32[]{:T(128)} %convert_element_type.12, () %tuple.18, (bf16[64,1536]{1,0:T(8,128)(2,1)S(1)}, bf16[384,1536]{1,0:T(8,128)(2,1)}) %tuple.19), branch_computations={%region_0.0_spmd, %region_1.0_spmd} | conditional | flops 2415919104 | bytes 57999700 | solution.py:213
  9.3 12.9 %all_to_all.8 = bf16[4,64,1536]{2,1,0:T(8,128)(2,1)S(1)} all-to-all(bf16[4,64,1536]{2,1,0:T(8,128)(2,1)S(1)} %broadcast_in_dim.0), channel_id=1, replica_groups={{0,128,256,384},{2,130,258,386},{64,192,320,448},{66,194,322,450},{1,3,..., dimensions={0} | all-to-all | bytes 1572864 | tf_op jit(solution)/shard_map/cond/branch_1_fun/all_to_all | solution.py:46
  22.1 1.9 %broadcast_in_dim.2 = bf16[4,256,1536]{2,1,0:T(8,128)(2,1)} broadcast(bf16[256,1536]{1,0:T(8,128)(2,1)S(1)} %bitcast.4), dimensions={1,2} | broadcast | bytes 3932160 | tf_op jit(solution)/shard_map/cond/branch_1_fun/broadcast_in_dim | solution.py:45
  24.0 4.8 %all-to-all-start.1 = ((bf16[4,256,1536]{2,1,0:T(8,128)(2,1)}), bf16[4,256,1536]{2,1,0:T(8,128)(2,1)}, u32[]{:S(2)}, u32[]{:S(2)}) async-start(bf16[4,256,1536]{2,1,0:T(8,128)(2,1)} %broadcast_in_dim.2), calls=%async_computation.1 | async-start | bytes 6291456 | tf_op jit(solution)/shard_map/cond/branch_1_fun/all_to_all | solution.py:46
  28.8 7.8 %collective-permute-start = (bf16[384,1536]{1,0:T(8,128)(2,1)S(1)}, bf16[384,1536]{1,0:T(8,128)(2,1)S(1)}, u32[]{:S(2)}, u32[]{:S(2)}) collective-permute-start(bf16[384,1536]{1,0:T(8,128)(2,1)S(1)} %copy-done.1), channel_id=1, source_target_pairs={{0,1},{1,0},{2,3},{3,2},{4,5},{5,4},{6,7},{7,6},{8,9},{9,8},{10,11... | collective-permute-start | bytes 3538952 | tf_op jit(solution)/shard_map/cond/branch_1_fun/ppermute | solution.py:51
  36.7 2.5 %collective-permute-done.other_ref = bf16[384,1536]{1,0:T(8,128)(2,1)S(1)} collective-permute-done((bf16[384,1536]{1,0:T(8,128)(2,1)S(1)}, bf16[384,1536]{1,0:T(8,128)(2,1)S(1)}, u32[]{:S(2)}, u32[]{:S(2)}) %collective-permute-start) | collective-permute-done | bytes 1179680 | tf_op jit(solution)/shard_map/cond/branch_1_fun/ppermute | solution.py:51
  39.1 10.7 %all-to-all-done.1 = bf16[4,256,1536]{2,1,0:T(8,128)(2,1)} async-done(((bf16[4,256,1536]{2,1,0:T(8,128)(2,1)}), bf16[4,256,1536]{2,1,0:T(8,128)(2,1)}, u32[]{:S(2)}, u32[]{:S(2)}) %all-to-all-start.1) | async-done | bytes 3145760 | tf_op jit(solution)/shard_map/cond/branch_1_fun/all_to_all | solution.py:46
  49.9 4.3 %branch_1_fun.3 = (bf16[4,64,768]{2,1,0:T(8,128)(2,1)S(1)}, bf16[4,64,768]{2,1,0:T(8,128)(2,1)S(1)}, bf16[1,64,768]{2,1,0:T(8,128)(2,1)S(1)}) custom-call(bf16[16,64,1536]{2,1,0:T(8,128)(2,1)} %bitcast.1.grad_ref, bf16[384,1536]{1,0:T(8,128)(2,1)S(1)} %copy-done.1, bf16[384,1536]{1,0:T(8,128)(2,1)S(1)} %collective-permute-done.other_ref), custom_call_target="tpu_custom_call" | custom-call | flops 1358954496 | bytes 6389760 | tf_op jit(solution)/shard_map/cond/branch_1_fun/pallas_call | solution.py:97
  54.2 8.7 %collective-permute-start.5 = (bf16[16,64,1536]{2,1,0:T(8,128)(2,1)}, bf16[16,64,1536]{2,1,0:T(8,128)(2,1)}, u32[]{:S(2)}, u32[]{:S(2)}) collective-permute-start(bf16[16,64,1536]{2,1,0:T(8,128)(2,1)} %bitcast.1.grad_ref), channel_id=1, source_target_pairs={{0,1},{1,0},{2,3},{3,2},{4,5},{5,4},{6,7},{7,6},{8,9},{9,8},{10,11... | collective-permute-start | bytes 9437192 | tf_op jit(solution)/shard_map/cond/branch_1_fun/ppermute | solution.py:51
  62.9 7.4 %collective-permute-start.1 = (bf16[4,64,768]{2,1,0:T(8,128)(2,1)S(1)}, bf16[4,64,768]{2,1,0:T(8,128)(2,1)S(1)}, u32[]{:S(2)}, u32[]{:S(2)}) collective-permute-start(bf16[4,64,768]{2,1,0:T(8,128)(2,1)S(1)} %get-tuple-element.9), channel_id=1, source_target_pairs={{0,4},{1,61},{2,6},{3,63},{4,8},{5,1},{6,10},{7,3},{8,12},{9,5},{1... | collective-permute-start | bytes 1179656 | tf_op jit(solution)/shard_map/cond/branch_1_fun/ppermute | solution.py:83
  70.3 1.9 %collective-permute-start.2 = (bf16[4,64,768]{2,1,0:T(8,128)(2,1)S(1)}, bf16[4,64,768]{2,1,0:T(8,128)(2,1)S(1)}, u32[]{:S(2)}, u32[]{:S(2)}) collective-permute-start(bf16[4,64,768]{2,1,0:T(8,128)(2,1)S(1)} %get-tuple-element.10), channel_id=1, source_target_pairs={{0,61},{1,4},{2,63},{3,6},{4,1},{5,8},{6,3},{7,10},{8,5},{9,12},{1... | collective-permute-start | bytes 1179656 | tf_op jit(solution)/shard_map/cond/branch_1_fun/ppermute | solution.py:83
  72.3 3.6 %branch_1_fun.4 = (bf16[4,64,768]{2,1,0:T(8,128)(2,1)S(1)}, bf16[3,64,768]{2,1,0:T(8,128)(2,1)S(1)}) custom-call(bf16[16,64,1536]{2,1,0:T(8,128)(2,1)} %bitcast.1.grad_ref, bf16[384,1536]{1,0:T(8,128)(2,1)S(1)} %copy-done.1, bf16[384,1536]{1,0:T(8,128)(2,1)S(1)} %collective-permute-done.other_ref), custom_call_target="tpu_custom_call" | custom-call | flops 1056964608 | bytes 6193152 | tf_op jit(solution)/shard_map/cond/branch_1_fun/pallas_call | solution.py:97
  75.9 3.0 %collective-permute-start.4 = (bf16[3,64,768]{2,1,0:T(8,128)(2,1)S(1)}, bf16[3,64,768]{2,1,0:T(8,128)(2,1)S(1)}, u32[]{:S(2)}, u32[]{:S(2)}) collective-permute-start(bf16[3,64,768]{2,1,0:T(8,128)(2,1)S(1)} %get-tuple-element.14), channel_id=1, source_target_pairs={{0,1},{1,0},{2,3},{3,2},{4,5},{5,4},{6,7},{7,6},{8,9},{9,8},{10,11... | collective-permute-start | bytes 884744 | tf_op jit(solution)/shard_map/cond/branch_1_fun/ppermute | solution.py:51
  78.9 3.1 %collective-permute-start.3 = (bf16[1,64,768]{2,1,0:T(8,128)(2,1)S(1)}, bf16[1,64,768]{2,1,0:T(8,128)(2,1)S(1)}, u32[]{:S(2)}, u32[]{:S(2)}) collective-permute-start(bf16[1,64,768]{2,1,0:T(8,128)(2,1)S(1)} %get-tuple-element.11), channel_id=1, source_target_pairs={{0,8},{1,57},{2,10},{3,59},{4,12},{5,61},{6,14},{7,63},{8,16},{9,1... | collective-permute-start | bytes 294920 | tf_op jit(solution)/shard_map/cond/branch_1_fun/ppermute | solution.py:83
  82.0 5.0 %collective-permute-done.3.far_ref = bf16[1,64,768]{2,1,0:T(8,128)(2,1)S(1)} collective-permute-done((bf16[1,64,768]{2,1,0:T(8,128)(2,1)S(1)}, bf16[1,64,768]{2,1,0:T(8,128)(2,1)S(1)}, u32[]{:S(2)}, u32[]{:S(2)}) %collective-permute-start.3) | collective-permute-done | bytes 98336 | tf_op jit(solution)/shard_map/cond/branch_1_fun/ppermute | solution.py:83
  87.1 0.9 branch_1_fun.5
  88.0 3.8 %collective-permute-start.6 = (bf16[2,2,64,768]{3,2,1,0:T(8,128)(2,1)}, bf16[2,2,64,768]{3,2,1,0:T(8,128)(2,1)S(1)}, u32[]{:S(2)}, u32[]{:S(2)}) collective-permute-start(bf16[2,2,64,768]{3,2,1,0:T(8,128)(2,1)} %get-tuple-element.31), channel_id=1, source_target_pairs={{0,8},{1,57},{2,10},{3,59},{4,12},{5,61},{6,14},{7,63},{8,16},{9,1... | collective-permute-start | bytes 1179656 | tf_op jit(solution)/shard_map/ppermute | solution.py:83
  91.8 1.4 %copy-done = bf16[2048,384]{1,0:T(8,128)(2,1)S(1)} copy-done((bf16[2048,384]{1,0:T(8,128)(2,1)S(1)}, bf16[2048,384]{1,0:T(8,128)(2,1)}, u32[]{:S(2)}) %copy-start) | copy-done | bytes 1572888
  93.2 7.1 %shard_map.60 = f32[384,1536]{1,0:T(8,128)} custom-call(bf16[16,2,64,384]{3,2,1,0:T(8,128)(2,1)S(1)} %bitcast.3, bf16[16,64,1536]{2,1,0:T(8,128)(2,1)} %get-tuple-element.32.grad_ref, bf16[16,64,1536]{2,1,0:T(8,128)(2,1)} %get-tuple-element.33.other_ref), custom_call_target="tpu_custom_call" | custom-call | flops 2415919104 | bytes 10223616 | tf_op jit(solution)/shard_map/pallas_call | solution.py:188
  100.9 5.9 %collective-permute-start.7 = (bf16[2,64,384]{2,1,0:T(8,128)(2,1)S(1)}, bf16[2,64,384]{2,1,0:T(8,128)(2,1)S(1)}, u32[]{:S(2)}, u32[]{:S(2)}) collective-permute-start(bf16[2,64,384]{2,1,0:T(8,128)(2,1)S(1)} %get-tuple-element.37), channel_id=1, source_target_pairs={{0,16},{1,49},{2,18},{3,51},{4,20},{5,53},{6,22},{7,55},{8,24},{9,... | collective-permute-start | bytes 294920 | tf_op jit(solution)/shard_map/ppermute | solution.py:83
  106.8 8.2 %collective-permute-start.8 = (bf16[2,64,384]{2,1,0:T(8,128)(2,1)S(1)}, bf16[2,64,384]{2,1,0:T(8,128)(2,1)S(1)}, u32[]{:S(2)}, u32[]{:S(2)}) collective-permute-start(bf16[2,64,384]{2,1,0:T(8,128)(2,1)S(1)} %get-tuple-element.38), channel_id=1, source_target_pairs={{0,17},{1,48},{2,19},{3,50},{4,21},{5,52},{6,23},{7,54},{8,25},{9,... | collective-permute-start | bytes 294920 | tf_op jit(solution)/shard_map/ppermute | solution.py:83
  115.0 1.9 %collective-permute-start.9 = (bf16[2,64,384]{2,1,0:T(8,128)(2,1)S(1)}, bf16[2,64,384]{2,1,0:T(8,128)(2,1)S(1)}, u32[]{:S(2)}, u32[]{:S(2)}) collective-permute-start(bf16[2,64,384]{2,1,0:T(8,128)(2,1)S(1)} %get-tuple-element.40), channel_id=1, source_target_pairs={{0,1},{1,0},{2,3},{3,2},{4,5},{5,4},{6,7},{7,6},{8,9},{9,8},{10,11... | collective-permute-start | bytes 294920 | tf_op jit(solution)/shard_map/ppermute | solution.py:51
  116.9 1.9 %collective-permute-done.8.cross_ref = bf16[2,64,384]{2,1,0:T(8,128)(2,1)S(1)} collective-permute-done((bf16[2,64,384]{2,1,0:T(8,128)(2,1)S(1)}, bf16[2,64,384]{2,1,0:T(8,128)(2,1)S(1)}, u32[]{:S(2)}, u32[]{:S(2)}) %collective-permute-start.8) | collective-permute-done | bytes 98336 | tf_op jit(solution)/shard_map/ppermute | solution.py:83
  (16 shorter events, 2.1 us)
Async XLA Ops:
  7.2 84.6 %all-gather.2.cloned.1.call-start = ((), (), s32[]{:S(2)}) async-start(), calls=%async_computation.2 | async-start | bytes 1671168 | tf_op jit(solution)/shard_map/all_gather | solution.py:208
  24.0 4.8 %copy-start.1 = (bf16[384,1536]{1,0:T(8,128)(2,1)S(1)}, bf16[384,1536]{1,0:T(8,128)(2,1)}, u32[]{:S(2)}) copy-start(bf16[384,1536]{1,0:T(8,128)(2,1)} %get-tuple-element.43.own_ref) | copy-start | bytes 3538948 | tf_op jit(solution)/shard_map/cond
  24.0 25.8 %all-to-all-start.1 = ((bf16[4,256,1536]{2,1,0:T(8,128)(2,1)}), bf16[4,256,1536]{2,1,0:T(8,128)(2,1)}, u32[]{:S(2)}, u32[]{:S(2)}) async-start(bf16[4,256,1536]{2,1,0:T(8,128)(2,1)} %broadcast_in_dim.2), calls=%async_computation.1 | async-start | bytes 6291456 | tf_op jit(solution)/shard_map/cond/branch_1_fun/all_to_all | solution.py:46
  28.8 10.3 %collective-permute-start = (bf16[384,1536]{1,0:T(8,128)(2,1)S(1)}, bf16[384,1536]{1,0:T(8,128)(2,1)S(1)}, u32[]{:S(2)}, u32[]{:S(2)}) collective-permute-start(bf16[384,1536]{1,0:T(8,128)(2,1)S(1)} %copy-done.1), channel_id=1, source_target_pairs={{0,1},{1,0},{2,3},{3,2},{4,5},{5,4},{6,7},{7,6},{8,9},{9,8},{10,11... | collective-permute-start | bytes 3538952 | tf_op jit(solution)/shard_map/cond/branch_1_fun/ppermute | solution.py:51
  54.2 33.7 %collective-permute-start.5 = (bf16[16,64,1536]{2,1,0:T(8,128)(2,1)}, bf16[16,64,1536]{2,1,0:T(8,128)(2,1)}, u32[]{:S(2)}, u32[]{:S(2)}) collective-permute-start(bf16[16,64,1536]{2,1,0:T(8,128)(2,1)} %bitcast.1.grad_ref), channel_id=1, source_target_pairs={{0,1},{1,0},{2,3},{3,2},{4,5},{5,4},{6,7},{7,6},{8,9},{9,8},{10,11... | collective-permute-start | bytes 9437192 | tf_op jit(solution)/shard_map/cond/branch_1_fun/ppermute | solution.py:51
  62.9 24.1 %collective-permute-start.1 = (bf16[4,64,768]{2,1,0:T(8,128)(2,1)S(1)}, bf16[4,64,768]{2,1,0:T(8,128)(2,1)S(1)}, u32[]{:S(2)}, u32[]{:S(2)}) collective-permute-start(bf16[4,64,768]{2,1,0:T(8,128)(2,1)S(1)} %get-tuple-element.9), channel_id=1, source_target_pairs={{0,4},{1,61},{2,6},{3,63},{4,8},{5,1},{6,10},{7,3},{8,12},{9,5},{1... | collective-permute-start | bytes 1179656 | tf_op jit(solution)/shard_map/cond/branch_1_fun/ppermute | solution.py:83
  70.3 16.7 %collective-permute-start.2 = (bf16[4,64,768]{2,1,0:T(8,128)(2,1)S(1)}, bf16[4,64,768]{2,1,0:T(8,128)(2,1)S(1)}, u32[]{:S(2)}, u32[]{:S(2)}) collective-permute-start(bf16[4,64,768]{2,1,0:T(8,128)(2,1)S(1)} %get-tuple-element.10), channel_id=1, source_target_pairs={{0,61},{1,4},{2,63},{3,6},{4,1},{5,8},{6,3},{7,10},{8,5},{9,12},{1... | collective-permute-start | bytes 1179656 | tf_op jit(solution)/shard_map/cond/branch_1_fun/ppermute | solution.py:83
  75.9 11.1 %collective-permute-start.4 = (bf16[3,64,768]{2,1,0:T(8,128)(2,1)S(1)}, bf16[3,64,768]{2,1,0:T(8,128)(2,1)S(1)}, u32[]{:S(2)}, u32[]{:S(2)}) collective-permute-start(bf16[3,64,768]{2,1,0:T(8,128)(2,1)S(1)} %get-tuple-element.14), channel_id=1, source_target_pairs={{0,1},{1,0},{2,3},{3,2},{4,5},{5,4},{6,7},{7,6},{8,9},{9,8},{10,11... | collective-permute-start | bytes 884744 | tf_op jit(solution)/shard_map/cond/branch_1_fun/ppermute | solution.py:51
  78.9 8.1 %collective-permute-start.3 = (bf16[1,64,768]{2,1,0:T(8,128)(2,1)S(1)}, bf16[1,64,768]{2,1,0:T(8,128)(2,1)S(1)}, u32[]{:S(2)}, u32[]{:S(2)}) collective-permute-start(bf16[1,64,768]{2,1,0:T(8,128)(2,1)S(1)} %get-tuple-element.11), channel_id=1, source_target_pairs={{0,8},{1,57},{2,10},{3,59},{4,12},{5,61},{6,14},{7,63},{8,16},{9,1... | collective-permute-start | bytes 294920 | tf_op jit(solution)/shard_map/cond/branch_1_fun/ppermute | solution.py:83
  88.0 12.9 %collective-permute-start.6 = (bf16[2,2,64,768]{3,2,1,0:T(8,128)(2,1)}, bf16[2,2,64,768]{3,2,1,0:T(8,128)(2,1)S(1)}, u32[]{:S(2)}, u32[]{:S(2)}) collective-permute-start(bf16[2,2,64,768]{3,2,1,0:T(8,128)(2,1)} %get-tuple-element.31), channel_id=1, source_target_pairs={{0,8},{1,57},{2,10},{3,59},{4,12},{5,61},{6,14},{7,63},{8,16},{9,1... | collective-permute-start | bytes 1179656 | tf_op jit(solution)/shard_map/ppermute | solution.py:83
  91.8 1.4 %copy-start = (bf16[2048,384]{1,0:T(8,128)(2,1)S(1)}, bf16[2048,384]{1,0:T(8,128)(2,1)}, u32[]{:S(2)}) copy-start(bf16[2048,384]{1,0:T(8,128)(2,1)} %all-gather.2.cloned.1.call-done) | copy-start | bytes 4718596
  100.9 16.0 %collective-permute-start.7 = (bf16[2,64,384]{2,1,0:T(8,128)(2,1)S(1)}, bf16[2,64,384]{2,1,0:T(8,128)(2,1)S(1)}, u32[]{:S(2)}, u32[]{:S(2)}) collective-permute-start(bf16[2,64,384]{2,1,0:T(8,128)(2,1)S(1)} %get-tuple-element.37), channel_id=1, source_target_pairs={{0,16},{1,49},{2,18},{3,51},{4,20},{5,53},{6,22},{7,55},{8,24},{9,... | collective-permute-start | bytes 294920 | tf_op jit(solution)/shard_map/ppermute | solution.py:83
  106.8 12.0 %collective-permute-start.8 = (bf16[2,64,384]{2,1,0:T(8,128)(2,1)S(1)}, bf16[2,64,384]{2,1,0:T(8,128)(2,1)S(1)}, u32[]{:S(2)}, u32[]{:S(2)}) collective-permute-start(bf16[2,64,384]{2,1,0:T(8,128)(2,1)S(1)} %get-tuple-element.38), channel_id=1, source_target_pairs={{0,17},{1,48},{2,19},{3,50},{4,21},{5,52},{6,23},{7,54},{8,25},{9,... | collective-permute-start | bytes 294920 | tf_op jit(solution)/shard_map/ppermute | solution.py:83
  115.0 3.8 %collective-permute-start.9 = (bf16[2,64,384]{2,1,0:T(8,128)(2,1)S(1)}, bf16[2,64,384]{2,1,0:T(8,128)(2,1)S(1)}, u32[]{:S(2)}, u32[]{:S(2)}) collective-permute-start(bf16[2,64,384]{2,1,0:T(8,128)(2,1)S(1)} %get-tuple-element.40), channel_id=1, source_target_pairs={{0,1},{1,0},{2,3},{3,2},{4,5},{5,4},{6,7},{7,6},{8,9},{9,8},{10,11... | collective-permute-start | bytes 294920 | tf_op jit(solution)/shard_map/ppermute | solution.py:51
Sparse Core Ops, SparseCore 0:
  10.1 69.5 all-gather.1

commit v7 on v6

v7 whole, which is shorter than its diff:
```python
import functools
import math

import jax
import jax.numpy as jnp
from jax import lax
from jax.experimental import pallas as pl
from jax.experimental.pallas import tpu as pltpu
from jax.sharding import PartitionSpec as P

cubic_term = 0.044715
plane = ("row", "rep")
ring = ("col", "rep")


def gelu_slope(values):
    scale = math.sqrt(2.0 / math.pi)
    inner = scale * (values + cubic_term * values * values * values)
    tangent = jnp.tanh(inner)
    return 0.5 * (1.0 + tangent) + 0.5 * values * (1.0 - tangent * tangent) * scale * (
        1.0 + 3.0 * cubic_term * values * values
    )


def index(x, y, core):
    return ((x * 2 + y % 2) * 2 + y // 2) * 2 + core


y_order = (0, 2, 1, 3)
along_x = [[[index(x, y, core) for x in range(4)] for y in y_order] for core in range(2)]
along_y = [[[index(x, y, core) for y in y_order] for x in range(4)] for core in range(2)]


first_groups = (((8,), False), ((7, 5, 3, 1), False))
early_groups = (((-7, -5, -3, -1), True),)
late_groups = (((6, 4, 2, 0), False), ((-6, -4, -2), True))


def place(step):
    core = lax.rem(lax.axis_index("rep"), 2)
    chip = lax.rem(lax.axis_index("col") + (1 - 2 * core) * step + 16, 16)
    return jnp.where(core == 0, lax.rem(chip, 4) * 4 + lax.div(chip, 4), chip)


def gather(values, groups):
    copies = jnp.broadcast_to(values[None], (4,) + values.shape)
    parts = lax.all_to_all(copies, plane, 0, 0, axis_index_groups=groups)
    return parts.reshape((4 * values.shape[0],) + values.shape[1:])


def swap_cores(values):
    return lax.ppermute(values, "rep", [(0, 1), (1, 0), (2, 3), (3, 2)])


def send(values, distance, cross=False):
    pairs = []
    for z in range(16):
        for rep in range(4):
            target = (z + (-distance if rep % 2 else distance)) % 16
            pairs.append((z * 4 + rep, target * 4 + (rep ^ 1 if cross else rep)))
    return lax.ppermute(values, ring, pairs)


def matmul_nt(a, b):
    return lax.dot_general(a, b, (((1,), (1,)), ((), ())), preferred_element_type=jnp.float32)


def matmul_tn(a, b):
    return lax.dot_general(a, b, (((0,), (0,)), ((), ())), preferred_element_type=jnp.float32)


def call(kernel, outs, args, flops=0, scratch=()):
    vmem = pl.BlockSpec(memory_space=pltpu.VMEM)
    moved = sum(v.size * v.dtype.itemsize for v in tuple(args) + tuple(outs))
    return pl.pallas_call(
        kernel,
        out_shape=outs,
        in_specs=[vmem] * len(args),
        out_specs=tuple(vmem for _ in outs),
        scratch_shapes=scratch,
        compiler_params=pltpu.CompilerParams(vmem_limit_bytes=32 * 1024 * 1024),
        cost_estimate=pl.CostEstimate(flops=flops, bytes_accessed=moved, transcendentals=0),
    )(*args)


def partial_kernel(groups, add, grad_ref, own_ref, other_ref, *refs):
    width = own_ref.shape[0]
    first_ref, outs = (refs[0], refs[1:]) if add else (None, refs)
    for (steps, flipped), out_ref in zip(groups, outs):
        rows = jnp.concatenate([grad_ref[place(step)] for step in steps], axis=0)
        for side, ref in enumerate((other_ref, own_ref) if flipped else (own_ref, other_ref)):
            part = matmul_nt(rows, ref[...]).reshape(len(steps), -1, width)
            columns = slice(side * width, (side + 1) * width)
            out_ref[:, :, columns] = part.astype(out_ref.dtype)
            if first_ref is not None and out_ref is outs[0]:
                first = part[0] + first_ref[0, :, columns].astype(jnp.float32)
                out_ref[0, :, columns] = first.astype(out_ref.dtype)


def partials(groups, grad_blocks, weight_own, weight_other, *add):
    rows, depth = grad_blocks.shape[1:]
    width = weight_own.shape[0]
    outs = [jax.ShapeDtypeStruct((len(g[0]), rows, 2 * width), jnp.bfloat16) for g in groups]
    return call(
        functools.partial(partial_kernel, groups, bool(add)),
        outs,
        (grad_blocks, weight_own, weight_other, *add),
        flops=4 * sum(len(g[0]) for g in groups) * rows * depth * width,
    )


def first_kernel(own_ref, cross_ref, rest_ref, other_ref, send_ref, middle_ref, here_ref):
    def total(i, *refs):
        return sum(ref[i].astype(jnp.float32) for ref in refs)

    dtype = send_ref.dtype
    send_ref[0, 0] = total(0, own_ref, rest_ref).astype(dtype)
    send_ref[0, 1] = total(0, cross_ref, other_ref).astype(dtype)
    send_ref[1, 0] = total(2, own_ref, rest_ref).astype(dtype)
    send_ref[1, 1] = total(2, cross_ref, other_ref).astype(dtype)
    middle_ref[0] = total(1, own_ref, rest_ref)
    middle_ref[1] = total(1, cross_ref, other_ref)
    here_ref[0] = total(3, own_ref, rest_ref)
    here_ref[1] = total(3, cross_ref)


def second_kernel(moved_ref, middle_ref, here_ref, own_ref, cross_ref, stay_ref, swap_ref):
    width = own_ref.shape[2]
    ahead = (middle_ref[...] + moved_ref[0].astype(jnp.float32)).astype(own_ref.dtype)
    own_ref[...] = ahead[:, :, :width]
    cross_ref[...] = ahead[:, :, width:]
    here = here_ref[...] + moved_ref[1].astype(jnp.float32)
    stay_ref[...] = here[:, :, :width]
    swap_ref[...] = here[:, :, width:].astype(swap_ref.dtype)


def third_kernel(own_ref, cross_ref, stay_ref, swap_ref, out_ref):
    half = own_ref.shape[1]
    core = lax.rem(lax.axis_index("rep"), 2)
    for i, place_of in enumerate((core, 1 - core)):
        other = cross_ref[1 - i].astype(jnp.float32) + swap_ref[1 - i].astype(jnp.float32)
        part = stay_ref[i] + own_ref[i].astype(jnp.float32) + other
        rows = pl.ds(pl.multiple_of(place_of * half, half), half)
        out_ref[rows, :] = part.astype(out_ref.dtype)


def taken(step, *args):
    return lax.cond(
        lax.axis_index("col") < 16,
        step,
        lambda *a: jax.tree.map(lambda v: jnp.zeros(v.shape, v.dtype), jax.eval_shape(step, *a)),
        *args,
    )


def first_round(grad_blocks, weight, weight_other):
    far, ahead = partials(first_groups, grad_blocks, weight, weight_other)
    far = send(far, 2)
    own = send(ahead, 1)
    ahead, next_blocks = lax.optimization_barrier((ahead, grad_blocks))
    behind = partials(early_groups, next_blocks, weight, weight_other)[0]
    cross = send(behind, -1, cross=True)
    behind, later_blocks = lax.optimization_barrier((behind, next_blocks))
    rest, for_sibling = partials(late_groups, later_blocks, weight, weight_other, far)
    rest_sibling = swap_cores(for_sibling)

    both = (2,) + rest.shape[1:]
    outs = [
        jax.ShapeDtypeStruct((2,) + both, jnp.bfloat16),
        jax.ShapeDtypeStruct(both, jnp.float32),
        jax.ShapeDtypeStruct(both, jnp.float32),
    ]
    return call(first_kernel, outs, (own, cross, rest, rest_sibling))


def gather_plane(gelu_grad, weight):
    line = gather(gelu_grad, along_x[0] + along_y[1])
    grad_tokens = gather(line, along_y[0] + along_x[1])
    return grad_tokens.reshape((16,) + gelu_grad.shape), swap_cores(weight)


def gather_and_round(gelu_grad, weight):
    grad_blocks, weight_other = taken(gather_plane, gelu_grad, weight)
    grad_other = swap_cores(grad_blocks)
    return (*taken(first_round, grad_blocks, weight, weight_other), grad_blocks, grad_other)


def weight_kernel(sibling, input_ref, grad_ref, *refs):
    first_ref = refs[0] if len(refs) == 3 else None
    out_ref, rows_ref = refs[-2:]
    half, depth = grad_ref.shape[1:]
    core = lax.rem(lax.axis_index("rep"), 2)
    core = 1 - core if sibling else core
    for chip in range(16):
        at = jnp.where(core == 0, (chip % 4) * 4 + chip // 4, chip)
        rows = pl.ds(pl.multiple_of(at * half, half), half)
        rows_ref[rows, :] = input_ref[chip, core]
    tile = 256
    for start in range(0, depth, tile):
        grad = grad_ref[:, :, start : start + tile].reshape(16 * half, tile)
        part = matmul_tn(rows_ref[...], grad)
        if first_ref is not None:
            part = part + first_ref[:, start : start + tile]
        out_ref[:, start : start + tile] = part


def weight_gradient(sibling, input_whole, grad_blocks, *first):
    tokens, width = input_whole.shape
    half, depth = grad_blocks.shape[1:]
    out = jax.ShapeDtypeStruct((width, depth), jnp.float32)
    return call(
        functools.partial(weight_kernel, sibling),
        [out],
        (input_whole.reshape(16, 2, half, width), grad_blocks, *first),
        flops=tokens * width * depth,
        scratch=[pltpu.VMEM((tokens // 2, width), jnp.bfloat16)],
    )[0]


def local(layer_input, weight, gelu_input, upstream):
    tokens, width = layer_input.shape
    half = tokens // 2
    f32, bf16 = jnp.float32, jnp.bfloat16

    input_whole = lax.all_gather(layer_input, "col", axis=0, tiled=True)
    gelu_grad = (upstream.astype(f32) * gelu_slope(gelu_input.astype(f32))).astype(bf16)

    to_send, middle, here, grad_blocks, grad_other = taken(gather_and_round, gelu_grad, weight)

    moved = send(to_send, 2)
    grad_weight = weight_gradient(False, input_whole, grad_blocks)
    grad_weight = weight_gradient(True, input_whole, grad_other, grad_weight)
    moved, grad_weight = lax.optimization_barrier((moved, grad_weight))
    part = (2, half, width)
    outs = [jax.ShapeDtypeStruct(part, t) for t in (bf16, bf16, f32, bf16)]
    own, cross, stay, swapped = call(second_kernel, outs, (moved, middle, here))
    last = send(own, 4), send(cross, 4, cross=True), stay, swap_cores(swapped)
    outs = [jax.ShapeDtypeStruct((tokens, width), bf16)]
    grad_input = call(third_kernel, outs, last)[0]
    return (grad_input, grad_weight)


def solution(mesh):
    in_specs = (
        P("col", ("row", "rep")),
        P(("row", "rep"), "col"),
        P(("row", "rep"), "col"),
        P(("row", "rep"), "col"),
    )
    out_specs = (P("col", ("row", "rep")), P(("row", "rep"), "col"))
    return jax.shard_map(local, mesh=mesh, in_specs=in_specs, out_specs=out_specs, check_vma=False)
```

time: 128 us -> 129 us (level)
  Pallas kernels: 16.7 us -> 22.7 us
  starting transfers between devices: 56.6 us -> 52.6 us
  waiting for transfers between devices: 21.4 us -> 19.4 us
    pallas_call x5 -> x8, Pallas kernels: 9.6 us -> 22.7 us  [call(): pl.pallas_call(kernel, out_shape=outs, in_specs=[vmem] * len(args), out_s...]
    pallas_call x1 -> x0, Pallas kernels: 7.07 us -> none  [weight_gradient(): pl.pallas_call(weight_kernel, out_shape=jax.ShapeDtypeStruct((width, dept...]
    ppermute x6, starting transfers between devices: 30.3 us -> 25.7 us  [send(): return lax.ppermute(values, ring, pairs)]
    ppermute x6, waiting for transfers between devices: 7.47 us -> 4.34 us  [send(): return lax.ppermute(values, ring, pairs)]
    ppermute x4, waiting for transfers between devices: 2.46 us -> 3.78 us  [swap_cores(): return lax.ppermute(values, 'rep', [(0, 1), (1, 0), (2, 3), (3, 2)])]
  transfers between devices with their start and end apart: 12 -> 12, of which waited for: 5 -> 6; matrix products, arithmetic and copies ran while one was open for 3% -> 3% of each run, Pallas kernels for 13% -> 16%
where the time goes in v7:
time: 129 us; the launch traced here: 126 us
  starting transfers between devices  52.6 us (41%)
  Pallas kernels  22.7 us (18%)
  waiting for transfers between devices  19.4 us (15%)
  between operations  14.1 us (11%)
  blocking collectives  12.9 us (10%)
  local copies, waits for them, and re-layouts  3.38 us (3%)
  other arithmetic  1.3 us (1%)
    ppermute x6, starting transfers between devices, send(): return lax.ppermute(values, ring, pairs)  25.7 us
    pallas_call x8, Pallas kernels, call(): pl.pallas_call(kernel, out_shape=outs, in_specs=[vmem] * len(args), out_s...  22.7 us
    ppermute x4, starting transfers between devices, swap_cores(): return lax.ppermute(values, 'rep', [(0, 1), (1, 0), (2, 3), (3, 2)])  22 us
    all_to_all x1, blocking collectives, gather(): parts = lax.all_to_all(copies, plane, 0, 0, axis_index_groups=groups)  12.9 us
    all_to_all x1, waiting for transfers between devices, gather(): parts = lax.all_to_all(copies, plane, 0, 0, axis_index_groups=groups)  10.6 us
    all_to_all x1, starting transfers between devices, gather(): parts = lax.all_to_all(copies, plane, 0, 0, axis_index_groups=groups)  4.78 us
    ppermute x6, waiting for transfers between devices, send(): return lax.ppermute(values, ring, pairs)  4.34 us
    ppermute x4, waiting for transfers between devices, swap_cores(): return lax.ppermute(values, 'rep', [(0, 1), (1, 0), (2, 3), (3, 2)])  3.78 us
  transfers between devices with their start and end apart: 12, of which 6 were waited for; matrix products, arithmetic and copies ran while one was open for 3% of the time, Pallas kernels for 16%

profile of v7, /device:TPU:1, one launch (start us, length us, event | category | flops | bytes accessed | tf_op | source)
XLA Modules:
  0.0 126.5 jit_solution(8401656150317250664)
XLA Ops:
  9.2 78.9 %conditional.3 = (bf16[2,2,64,768]{3,2,1,0:T(8,128)(2,1)}, f32[2,64,768]{2,1,0:T(8,128)}, f32[2,64,768]{2,1,0:T(8,128)}, bf16[16,64,1536]{2,1,0:T(8,128)(2,1)}, bf16[16,64,1536]{2,1,0:T(8,128)(2,1)}) conditional(s32[]{:T(128)} %convert_element_type.16, () %tuple.33, (bf16[64,1536]{1,0:T(8,128)(2,1)S(1)}, bf16[384,1536]{1,0:T(8,128)(2,1)}) %tuple.34), branch_computations={%region_0.0_spmd, %region_1.0_spmd} | conditional | flops 2415919104 | bytes 68223440 | solution.py:148
  9.2 40.7 %conditional = (bf16[16,64,1536]{2,1,0:T(8,128)(2,1)}, bf16[384,1536]{1,0:T(8,128)(2,1)}) conditional(s32[]{:T(128)} %convert_element_type.4, () %tuple.25, (bf16[64,1536]{1,0:T(8,128)(2,1)S(1)}, bf16[384,1536]{1,0:T(8,128)(2,1)}) %param.5), branch_computations={%region_2.0_spmd, %region_3.0_spmd} | conditional | bytes 25362548 | solution.py:148
  9.3 12.9 %all_to_all.8 = bf16[4,64,1536]{2,1,0:T(8,128)(2,1)S(1)} all-to-all(bf16[4,64,1536]{2,1,0:T(8,128)(2,1)S(1)} %broadcast_in_dim.0), channel_id=1, replica_groups={{0,128,256,384},{2,130,258,386},{64,192,320,448},{66,194,322,450},{1,3,..., dimensions={0} | all-to-all | bytes 1572864 | tf_op jit(solution)/shard_map/cond/branch_1_fun/cond/branch_1_fun/all_to_all | solution.py:47
  22.1 1.9 %broadcast_in_dim.2 = bf16[4,256,1536]{2,1,0:T(8,128)(2,1)} broadcast(bf16[256,1536]{1,0:T(8,128)(2,1)S(1)} %bitcast.5), dimensions={1,2} | broadcast | bytes 3932160 | tf_op jit(solution)/shard_map/cond/branch_1_fun/cond/branch_1_fun/broadcast_in_dim | solution.py:46
  24.1 4.8 %all-to-all-start.1 = ((bf16[4,256,1536]{2,1,0:T(8,128)(2,1)}), bf16[4,256,1536]{2,1,0:T(8,128)(2,1)}, u32[]{:S(2)}, u32[]{:S(2)}) async-start(bf16[4,256,1536]{2,1,0:T(8,128)(2,1)} %broadcast_in_dim.2), calls=%async_computation.1 | async-start | bytes 6291456 | tf_op jit(solution)/shard_map/cond/branch_1_fun/cond/branch_1_fun/all_to_all | solution.py:47
  28.9 7.8 %collective-permute-start = (bf16[384,1536]{1,0:T(8,128)(2,1)S(1)}, bf16[384,1536]{1,0:T(8,128)(2,1)}, u32[]{:S(2)}, u32[]{:S(2)}) collective-permute-start(bf16[384,1536]{1,0:T(8,128)(2,1)S(1)} %copy-done.1), channel_id=1, source_target_pairs={{0,1},{1,0},{2,3},{3,2},{4,5},{5,4},{6,7},{7,6},{8,9},{9,8},{10,11... | collective-permute-start | bytes 3538952 | tf_op jit(solution)/shard_map/cond/branch_1_fun/cond/branch_1_fun/ppermute | solution.py:52
  36.7 2.6 %collective-permute-done = bf16[384,1536]{1,0:T(8,128)(2,1)} collective-permute-done((bf16[384,1536]{1,0:T(8,128)(2,1)S(1)}, bf16[384,1536]{1,0:T(8,128)(2,1)}, u32[]{:S(2)}, u32[]{:S(2)}) %collective-permute-start) | collective-permute-done | bytes 1179680 | tf_op jit(solution)/shard_map/cond/branch_1_fun/cond/branch_1_fun/ppermute | solution.py:52
  39.3 10.6 %all-to-all-done.1 = bf16[4,256,1536]{2,1,0:T(8,128)(2,1)} async-done(((bf16[4,256,1536]{2,1,0:T(8,128)(2,1)}), bf16[4,256,1536]{2,1,0:T(8,128)(2,1)}, u32[]{:S(2)}, u32[]{:S(2)}) %all-to-all-start.1) | async-done | bytes 3145760 | tf_op jit(solution)/shard_map/cond/branch_1_fun/cond/branch_1_fun/all_to_all | solution.py:47
  49.9 8.7 %collective-permute-start.5 = (bf16[16,64,1536]{2,1,0:T(8,128)(2,1)}, bf16[16,64,1536]{2,1,0:T(8,128)(2,1)}, u32[]{:S(2)}, u32[]{:S(2)}) collective-permute-start(bf16[16,64,1536]{2,1,0:T(8,128)(2,1)} %get-tuple-element.76), channel_id=1, source_target_pairs={{0,1},{1,0},{2,3},{3,2},{4,5},{5,4},{6,7},{7,6},{8,9},{9,8},{10,11... | collective-permute-start | bytes 9437192 | tf_op jit(solution)/shard_map/cond/branch_1_fun/ppermute | solution.py:52
  58.6 29.5 %conditional.1 = ((bf16[2,2,64,768]{3,2,1,0:T(8,128)(2,1)}, f32[2,64,768]{2,1,0:T(8,128)}, f32[2,64,768]{2,1,0:T(8,128)})) conditional(s32[]{:T(128)} %convert_element_type.4, () %tuple.24, (bf16[16,64,1536]{2,1,0:T(8,128)(2,1)}, bf16[384,1536]{1,0:T(8,128)(2,1)}, bf16[384,1536]{1,0:T(8,128)(2,1)}) %tuple.26), branch_computations={%region_4.0_spmd, %region_5.0_spmd} | conditional | flops 2415919104 | bytes 30277828 | solution.py:148
  58.6 4.4 %branch_1_fun.4 = (bf16[1,64,768]{2,1,0:T(8,128)(2,1)S(1)}, bf16[4,64,768]{2,1,0:T(8,128)(2,1)S(1)}) custom-call(bf16[16,64,1536]{2,1,0:T(8,128)(2,1)} %get-tuple-element.21.grad_ref, bf16[384,1536]{1,0:T(8,128)(2,1)} %get-tuple-element.17.own_ref, bf16[384,1536]{1,0:T(8,128)(2,1)} %get-tuple-element.18.other_ref), custom_call_target="tpu_custom_call" | custom-call | flops 754974720 | bytes 5996544 | tf_op jit(solution)/shard_map/cond/branch_1_fun/cond/branch_1_fun/pallas_call | solution.py:75
  63.0 7.9 %collective-permute-start.3 = (bf16[1,64,768]{2,1,0:T(8,128)(2,1)S(1)}, bf16[1,64,768]{2,1,0:T(8,128)(2,1)S(1)}, u32[]{:S(2)}, u32[]{:S(2)}) collective-permute-start(bf16[1,64,768]{2,1,0:T(8,128)(2,1)S(1)} %get-tuple-element.22), channel_id=1, source_target_pairs={{0,8},{1,57},{2,10},{3,59},{4,12},{5,61},{6,14},{7,63},{8,16},{9,1... | collective-permute-start | bytes 294920 | tf_op jit(solution)/shard_map/cond/branch_1_fun/cond/branch_1_fun/ppermute | solution.py:61
  70.8 2.6 %collective-permute-start.1 = (bf16[4,64,768]{2,1,0:T(8,128)(2,1)S(1)}, bf16[4,64,768]{2,1,0:T(8,128)(2,1)S(1)}, u32[]{:S(2)}, u32[]{:S(2)}) collective-permute-start(bf16[4,64,768]{2,1,0:T(8,128)(2,1)S(1)} %get-tuple-element.19), channel_id=1, source_target_pairs={{0,4},{1,61},{2,6},{3,63},{4,8},{5,1},{6,10},{7,3},{8,12},{9,5},{1... | collective-permute-start | bytes 1179656 | tf_op jit(solution)/shard_map/cond/branch_1_fun/cond/branch_1_fun/ppermute | solution.py:61
  73.5 3.2 %branch_1_fun.5 = bf16[4,64,768]{2,1,0:T(8,128)(2,1)S(1)} custom-call(bf16[16,64,1536]{2,1,0:T(8,128)(2,1)} %get-tuple-element.21.grad_ref, bf16[384,1536]{1,0:T(8,128)(2,1)S(1)} %copy-done.2, bf16[384,1536]{1,0:T(8,128)(2,1)} %get-tuple-element.18.other_ref), custom_call_target="tpu_custom_call" | custom-call | flops 603979776 | bytes 5898240 | tf_op jit(solution)/shard_map/cond/branch_1_fun/cond/branch_1_fun/pallas_call | solution.py:75
  76.7 1.9 %collective-permute-start.2 = (bf16[4,64,768]{2,1,0:T(8,128)(2,1)S(1)}, bf16[4,64,768]{2,1,0:T(8,128)(2,1)S(1)}, u32[]{:S(2)}, u32[]{:S(2)}) collective-permute-start(bf16[4,64,768]{2,1,0:T(8,128)(2,1)S(1)} %branch_1_fun.5), channel_id=1, source_target_pairs={{0,61},{1,4},{2,63},{3,6},{4,1},{5,8},{6,3},{7,10},{8,5},{9,12},{1... | collective-permute-start | bytes 1179656 | tf_op jit(solution)/shard_map/cond/branch_1_fun/cond/branch_1_fun/ppermute | solution.py:61
  78.7 3.9 %branch_1_fun.6 = (bf16[4,64,768]{2,1,0:T(8,128)(2,1)S(1)}, bf16[3,64,768]{2,1,0:T(8,128)(2,1)S(1)}) custom-call(bf16[16,64,1536]{2,1,0:T(8,128)(2,1)} %get-tuple-element.21.grad_ref, bf16[384,1536]{1,0:T(8,128)(2,1)S(1)} %copy-done.2, bf16[384,1536]{1,0:T(8,128)(2,1)} %get-tuple-element.18.other_ref, bf16[1,64,768]{2,1,0:T(8,128)(2,1)S(1)} %collective-permute-done.3.refs_0_), custom_call_target="tpu_custom_call" | custom-call | flops 1056964608 | bytes 6291456 | tf_op jit(solution)/shard_map/cond/branch_1_fun/cond/branch_1_fun/pallas_call | solution.py:75
  82.6 3.0 %collective-permute-start.4 = (bf16[3,64,768]{2,1,0:T(8,128)(2,1)S(1)}, bf16[3,64,768]{2,1,0:T(8,128)(2,1)S(1)}, u32[]{:S(2)}, u32[]{:S(2)}) collective-permute-start(bf16[3,64,768]{2,1,0:T(8,128)(2,1)S(1)} %get-tuple-element.24), channel_id=1, source_target_pairs={{0,1},{1,0},{2,3},{3,2},{4,5},{5,4},{6,7},{7,6},{8,9},{9,8},{10,11... | collective-permute-start | bytes 884744 | tf_op jit(solution)/shard_map/cond/branch_1_fun/cond/branch_1_fun/ppermute | solution.py:52
  88.1 4.2 %collective-permute-start.6 = (bf16[2,2,64,768]{3,2,1,0:T(8,128)(2,1)}, bf16[2,2,64,768]{3,2,1,0:T(8,128)(2,1)S(1)}, u32[]{:S(2)}, u32[]{:S(2)}) collective-permute-start(bf16[2,2,64,768]{3,2,1,0:T(8,128)(2,1)} %get-tuple-element.44), channel_id=1, source_target_pairs={{0,8},{1,57},{2,10},{3,59},{4,12},{5,61},{6,14},{7,63},{8,16},{9,1... | collective-permute-start | bytes 1179656 | tf_op jit(solution)/shard_map/ppermute | solution.py:61
  93.8 3.4 %shard_map.60.refs_0_ = f32[384,1536]{1,0:T(8,128)S(1)} custom-call(bf16[16,2,64,384]{3,2,1,0:T(8,128)(2,1)S(1)} %bitcast.3, bf16[16,64,1536]{2,1,0:T(8,128)(2,1)} %get-tuple-element.46.grad_ref), custom_call_target="tpu_custom_call" | custom-call | flops 1207959552 | bytes 7077888 | tf_op jit(solution)/shard_map/pallas_call | solution.py:75
  97.2 4.8 %shard_map.61 = f32[384,1536]{1,0:T(8,128)} custom-call(bf16[16,2,64,384]{3,2,1,0:T(8,128)(2,1)S(1)} %bitcast.4, bf16[16,64,1536]{2,1,0:T(8,128)(2,1)} %get-tuple-element.45.grad_ref, f32[384,1536]{1,0:T(8,128)S(1)} %shard_map.60.refs_0_), custom_call_target="tpu_custom_call" | custom-call | flops 1207959552 | bytes 9437184 | tf_op jit(solution)/shard_map/pallas_call | solution.py:75
  103.2 5.6 %collective-permute-start.7 = (bf16[2,64,384]{2,1,0:T(8,128)(2,1)S(1)}, bf16[2,64,384]{2,1,0:T(8,128)(2,1)S(1)}, u32[]{:S(2)}, u32[]{:S(2)}) collective-permute-start(bf16[2,64,384]{2,1,0:T(8,128)(2,1)S(1)} %get-tuple-element.50), channel_id=1, source_target_pairs={{0,16},{1,49},{2,18},{3,51},{4,20},{5,53},{6,22},{7,55},{8,24},{9,... | collective-permute-start | bytes 294920 | tf_op jit(solution)/shard_map/ppermute | solution.py:61
  108.8 3.5 %collective-permute-start.8 = (bf16[2,64,384]{2,1,0:T(8,128)(2,1)S(1)}, bf16[2,64,384]{2,1,0:T(8,128)(2,1)S(1)}, u32[]{:S(2)}, u32[]{:S(2)}) collective-permute-start(bf16[2,64,384]{2,1,0:T(8,128)(2,1)S(1)} %get-tuple-element.51), channel_id=1, source_target_pairs={{0,17},{1,48},{2,19},{3,50},{4,21},{5,52},{6,23},{7,54},{8,25},{9,... | collective-permute-start | bytes 294920 | tf_op jit(solution)/shard_map/ppermute | solution.py:61
  112.3 2.5 %collective-permute-start.9 = (bf16[2,64,384]{2,1,0:T(8,128)(2,1)S(1)}, bf16[2,64,384]{2,1,0:T(8,128)(2,1)S(1)}, u32[]{:S(2)}, u32[]{:S(2)}) collective-permute-start(bf16[2,64,384]{2,1,0:T(8,128)(2,1)S(1)} %get-tuple-element.53), channel_id=1, source_target_pairs={{0,1},{1,0},{2,3},{3,2},{4,5},{5,4},{6,7},{7,6},{8,9},{9,8},{10,11... | collective-permute-start | bytes 294920 | tf_op jit(solution)/shard_map/ppermute | solution.py:52
  115.0 3.9 %collective-permute-done.8.cross_ref = bf16[2,64,384]{2,1,0:T(8,128)(2,1)S(1)} collective-permute-done((bf16[2,64,384]{2,1,0:T(8,128)(2,1)S(1)}, bf16[2,64,384]{2,1,0:T(8,128)(2,1)S(1)}, u32[]{:S(2)}, u32[]{:S(2)}) %collective-permute-start.8) | collective-permute-done | bytes 98336 | tf_op jit(solution)/shard_map/ppermute | solution.py:61
  (22 shorter events, 8.1 us)
Async XLA Ops:
  7.2 85.2 %all-gather.2.cloned.1.call-start = ((), (), s32[]{:S(2)}) async-start(), calls=%async_computation.2 | async-start | bytes 1671168 | tf_op jit(solution)/shard_map/all_gather | solution.py:225
  24.1 4.8 %copy-start.1 = (bf16[384,1536]{1,0:T(8,128)(2,1)S(1)}, bf16[384,1536]{1,0:T(8,128)(2,1)}, u32[]{:S(2)}) copy-start(bf16[384,1536]{1,0:T(8,128)(2,1)} %get-tuple-element.15) | copy-start | bytes 3538948 | tf_op jit(solution)/shard_map/cond/branch_1_fun/cond
  24.1 25.8 %all-to-all-start.1 = ((bf16[4,256,1536]{2,1,0:T(8,128)(2,1)}), bf16[4,256,1536]{2,1,0:T(8,128)(2,1)}, u32[]{:S(2)}, u32[]{:S(2)}) async-start(bf16[4,256,1536]{2,1,0:T(8,128)(2,1)} %broadcast_in_dim.2), calls=%async_computation.1 | async-start | bytes 6291456 | tf_op jit(solution)/shard_map/cond/branch_1_fun/cond/branch_1_fun/all_to_all | solution.py:47
  28.9 10.4 %collective-permute-start = (bf16[384,1536]{1,0:T(8,128)(2,1)S(1)}, bf16[384,1536]{1,0:T(8,128)(2,1)}, u32[]{:S(2)}, u32[]{:S(2)}) collective-permute-start(bf16[384,1536]{1,0:T(8,128)(2,1)S(1)} %copy-done.1), channel_id=1, source_target_pairs={{0,1},{1,0},{2,3},{3,2},{4,5},{5,4},{6,7},{7,6},{8,9},{9,8},{10,11... | collective-permute-start | bytes 3538952 | tf_op jit(solution)/shard_map/cond/branch_1_fun/cond/branch_1_fun/ppermute | solution.py:52
  49.9 38.2 %collective-permute-start.5 = (bf16[16,64,1536]{2,1,0:T(8,128)(2,1)}, bf16[16,64,1536]{2,1,0:T(8,128)(2,1)}, u32[]{:S(2)}, u32[]{:S(2)}) collective-permute-start(bf16[16,64,1536]{2,1,0:T(8,128)(2,1)} %get-tuple-element.76), channel_id=1, source_target_pairs={{0,1},{1,0},{2,3},{3,2},{4,5},{5,4},{6,7},{7,6},{8,9},{9,8},{10,11... | collective-permute-start | bytes 9437192 | tf_op jit(solution)/shard_map/cond/branch_1_fun/ppermute | solution.py:52
  58.6 14.9 %copy-start.2 = (bf16[384,1536]{1,0:T(8,128)(2,1)S(1)}, bf16[384,1536]{1,0:T(8,128)(2,1)}, u32[]{:S(2)}) copy-start(bf16[384,1536]{1,0:T(8,128)(2,1)} %get-tuple-element.17.own_ref) | copy-start | bytes 3538948 | tf_op jit(solution)/shard_map/cond/branch_1_fun/cond
  63.0 15.7 %collective-permute-start.3 = (bf16[1,64,768]{2,1,0:T(8,128)(2,1)S(1)}, bf16[1,64,768]{2,1,0:T(8,128)(2,1)S(1)}, u32[]{:S(2)}, u32[]{:S(2)}) collective-permute-start(bf16[1,64,768]{2,1,0:T(8,128)(2,1)S(1)} %get-tuple-element.22), channel_id=1, source_target_pairs={{0,8},{1,57},{2,10},{3,59},{4,12},{5,61},{6,14},{7,63},{8,16},{9,1... | collective-permute-start | bytes 294920 | tf_op jit(solution)/shard_map/cond/branch_1_fun/cond/branch_1_fun/ppermute | solution.py:61
  70.8 16.2 %collective-permute-start.1 = (bf16[4,64,768]{2,1,0:T(8,128)(2,1)S(1)}, bf16[4,64,768]{2,1,0:T(8,128)(2,1)S(1)}, u32[]{:S(2)}, u32[]{:S(2)}) collective-permute-start(bf16[4,64,768]{2,1,0:T(8,128)(2,1)S(1)} %get-tuple-element.19), channel_id=1, source_target_pairs={{0,4},{1,61},{2,6},{3,63},{4,8},{5,1},{6,10},{7,3},{8,12},{9,5},{1... | collective-permute-start | bytes 1179656 | tf_op jit(solution)/shard_map/cond/branch_1_fun/cond/branch_1_fun/ppermute | solution.py:61
  76.7 10.3 %collective-permute-start.2 = (bf16[4,64,768]{2,1,0:T(8,128)(2,1)S(1)}, bf16[4,64,768]{2,1,0:T(8,128)(2,1)S(1)}, u32[]{:S(2)}, u32[]{:S(2)}) collective-permute-start(bf16[4,64,768]{2,1,0:T(8,128)(2,1)S(1)} %branch_1_fun.5), channel_id=1, source_target_pairs={{0,61},{1,4},{2,63},{3,6},{4,1},{5,8},{6,3},{7,10},{8,5},{9,12},{1... | collective-permute-start | bytes 1179656 | tf_op jit(solution)/shard_map/cond/branch_1_fun/cond/branch_1_fun/ppermute | solution.py:61
  82.6 4.2 %collective-permute-start.4 = (bf16[3,64,768]{2,1,0:T(8,128)(2,1)S(1)}, bf16[3,64,768]{2,1,0:T(8,128)(2,1)S(1)}, u32[]{:S(2)}, u32[]{:S(2)}) collective-permute-start(bf16[3,64,768]{2,1,0:T(8,128)(2,1)S(1)} %get-tuple-element.24), channel_id=1, source_target_pairs={{0,1},{1,0},{2,3},{3,2},{4,5},{5,4},{6,7},{7,6},{8,9},{9,8},{10,11... | collective-permute-start | bytes 884744 | tf_op jit(solution)/shard_map/cond/branch_1_fun/cond/branch_1_fun/ppermute | solution.py:52
  88.1 13.9 %collective-permute-start.6 = (bf16[2,2,64,768]{3,2,1,0:T(8,128)(2,1)}, bf16[2,2,64,768]{3,2,1,0:T(8,128)(2,1)S(1)}, u32[]{:S(2)}, u32[]{:S(2)}) collective-permute-start(bf16[2,2,64,768]{3,2,1,0:T(8,128)(2,1)} %get-tuple-element.44), channel_id=1, source_target_pairs={{0,8},{1,57},{2,10},{3,59},{4,12},{5,61},{6,14},{7,63},{8,16},{9,1... | collective-permute-start | bytes 1179656 | tf_op jit(solution)/shard_map/ppermute | solution.py:61
  92.4 1.4 %copy-start = (bf16[2048,384]{1,0:T(8,128)(2,1)S(1)}, bf16[2048,384]{1,0:T(8,128)(2,1)}, u32[]{:S(2)}) copy-start(bf16[2048,384]{1,0:T(8,128)(2,1)} %all-gather.2.cloned.1.call-done) | copy-start | bytes 4718596
  103.2 11.8 %collective-permute-start.7 = (bf16[2,64,384]{2,1,0:T(8,128)(2,1)S(1)}, bf16[2,64,384]{2,1,0:T(8,128)(2,1)S(1)}, u32[]{:S(2)}, u32[]{:S(2)}) collective-permute-start(bf16[2,64,384]{2,1,0:T(8,128)(2,1)S(1)} %get-tuple-element.50), channel_id=1, source_target_pairs={{0,16},{1,49},{2,18},{3,51},{4,20},{5,53},{6,22},{7,55},{8,24},{9,... | collective-permute-start | bytes 294920 | tf_op jit(solution)/shard_map/ppermute | solution.py:61
  108.8 10.1 %collective-permute-start.8 = (bf16[2,64,384]{2,1,0:T(8,128)(2,1)S(1)}, bf16[2,64,384]{2,1,0:T(8,128)(2,1)S(1)}, u32[]{:S(2)}, u32[]{:S(2)}) collective-permute-start(bf16[2,64,384]{2,1,0:T(8,128)(2,1)S(1)} %get-tuple-element.51), channel_id=1, source_target_pairs={{0,17},{1,48},{2,19},{3,50},{4,21},{5,52},{6,23},{7,54},{8,25},{9,... | collective-permute-start | bytes 294920 | tf_op jit(solution)/shard_map/ppermute | solution.py:61
  112.3 6.7 %collective-permute-start.9 = (bf16[2,64,384]{2,1,0:T(8,128)(2,1)S(1)}, bf16[2,64,384]{2,1,0:T(8,128)(2,1)S(1)}, u32[]{:S(2)}, u32[]{:S(2)}) collective-permute-start(bf16[2,64,384]{2,1,0:T(8,128)(2,1)S(1)} %get-tuple-element.53), channel_id=1, source_target_pairs={{0,1},{1,0},{2,3},{3,2},{4,5},{5,4},{6,7},{7,6},{8,9},{9,8},{10,11... | collective-permute-start | bytes 294920 | tf_op jit(solution)/shard_map/ppermute | solution.py:52
Sparse Core Ops, SparseCore 0:
  10.1 70.1 all-gather.1

commit v8 on v7

--- a/solution.py
+++ b/solution.py
@@ -31,15 +31,20 @@
 along_y = [[[index(x, y, core) for y in y_order] for x in range(4)] for core in range(2)]
 
 
-first_groups = (((8,), False), ((7, 5, 3, 1), False))
-early_groups = (((-7, -5, -3, -1), True),)
-late_groups = (((6, 4, 2, 0), False), ((-6, -4, -2), True))
-
-
-def place(step):
-    core = lax.rem(lax.axis_index("rep"), 2)
-    chip = lax.rem(lax.axis_index("col") + (1 - 2 * core) * step + 16, 16)
-    return jnp.where(core == 0, lax.rem(chip, 4) * 4 + lax.div(chip, 4), chip)
+early_groups = (
+    (((8, 0),), False),
+    (((7, 0), (5, 0), (3, 0), (1, 0)), False),
+    (((-7, 0), (-5, 0), (-3, 0), (-1, 0)), True),
+)
+late_groups = (
+    (((6, 0), (4, 0), (2, 0), (0, 0)), False),
+    (((6, 1), (4, 1), (2, 1)), False),
+)
+
+
+def place(chip, core):
+    turned = lax.rem(chip, 4) * 4 + lax.div(chip, 4)
+    return jnp.where(core == 0, turned, chip)
 
 
 def gather(values, groups):
@@ -69,43 +74,86 @@
     return lax.dot_general(a, b, (((0,), (0,)), ((), ())), preferred_element_type=jnp.float32)
 
 
-def call(kernel, outs, args, flops=0, scratch=()):
-    vmem = pl.BlockSpec(memory_space=pltpu.VMEM)
+def call(kernel, outs, args, flops=0, scratch=(), space=pltpu.VMEM, out_space=pltpu.VMEM):
     moved = sum(v.size * v.dtype.itemsize for v in tuple(args) + tuple(outs))
     return pl.pallas_call(
         kernel,
         out_shape=outs,
-        in_specs=[vmem] * len(args),
-        out_specs=tuple(vmem for _ in outs),
+        in_specs=[pl.BlockSpec(memory_space=space) for _ in args],
+        out_specs=tuple(pl.BlockSpec(memory_space=out_space) for _ in outs),
         scratch_shapes=scratch,
-        compiler_params=pltpu.CompilerParams(vmem_limit_bytes=32 * 1024 * 1024),
+        compiler_params=pltpu.CompilerParams(vmem_limit_bytes=40 * 1024 * 1024),
         cost_estimate=pl.CostEstimate(flops=flops, bytes_accessed=moved, transcendentals=0),
     )(*args)
 
 
-def partial_kernel(groups, add, grad_ref, own_ref, other_ref, *refs):
-    width = own_ref.shape[0]
-    first_ref, outs = (refs[0], refs[1:]) if add else (None, refs)
-    for (steps, flipped), out_ref in zip(groups, outs):
-        rows = jnp.concatenate([grad_ref[place(step)] for step in steps], axis=0)
-        for side, ref in enumerate((other_ref, own_ref) if flipped else (own_ref, other_ref)):
-            part = matmul_nt(rows, ref[...]).reshape(len(steps), -1, width)
-            columns = slice(side * width, (side + 1) * width)
+def partial_kernel(groups, n_grads, n_in, *refs):
+    grad_refs, weight_refs = refs[:n_grads], refs[n_grads : n_grads + 2]
+    add_refs = refs[n_grads + 2 : n_in]
+    outs = refs[n_in : n_in + len(groups)]
+    blocks_ref, weights_ref, add_ref, block_sems, weight_sems, add_sem = refs[n_in + len(groups) :]
+    core = lax.rem(lax.axis_index("rep"), 2)
+    z = lax.axis_index("col")
+    width = weights_ref.shape[1]
+
+    weight_copies = [
+        pltpu.make_async_copy(ref, weights_ref.at[i], weight_sems.at[i])
+        for i, ref in enumerate(weight_refs)
+    ]
+    block_copies = []
+    for items, _ in groups:
+        for step, whose in items:
+            chip = lax.rem(z + (1 - 2 * core) * step + 16, 16)
+            at = place(chip, 1 - core if whose else core)
+            i = len(block_copies)
+            block_copies.append(
+                pltpu.make_async_copy(grad_refs[whose].at[at], blocks_ref.at[i], block_sems.at[i])
+            )
+    add_copies = [pltpu.make_async_copy(ref, add_ref, add_sem) for ref in add_refs]
+    for copy in weight_copies[:1] + block_copies + weight_copies[1:] + add_copies:
+        copy.start()
+
+    start = 0
+    for number, ((items, flipped), out_ref) in enumerate(zip(groups, outs)):
+        count = len(items)
+        for copy in block_copies[start : start + count]:
+            copy.wait()
+        rows = blocks_ref[start : start + count].reshape(count * blocks_ref.shape[1], -1)
+        start += count
+        for side in range(2):
+            if number == 0:
+                weight_copies[side].wait()
+            part = matmul_nt(rows, weights_ref[side]).reshape(count, -1, width)
+            at = (1 - side if flipped else side) * width
+            columns = slice(at, at + width)
             out_ref[:, :, columns] = part.astype(out_ref.dtype)
-            if first_ref is not None and out_ref is outs[0]:
-                first = part[0] + first_ref[0, :, columns].astype(jnp.float32)
+            if add_copies and number == 0:
+                if side == 0:
+                    add_copies[0].wait()
+                first = part[0] + add_ref[0, :, columns].astype(jnp.float32)
                 out_ref[0, :, columns] = first.astype(out_ref.dtype)
 
 
-def partials(groups, grad_blocks, weight_own, weight_other, *add):
-    rows, depth = grad_blocks.shape[1:]
-    width = weight_own.shape[0]
-    outs = [jax.ShapeDtypeStruct((len(g[0]), rows, 2 * width), jnp.bfloat16) for g in groups]
+def partials(groups, grads, weights, *add):
+    rows, depth = grads[0].shape[1:]
+    width = weights[0].shape[0]
+    count = sum(len(items) for items, _ in groups)
+    bf16 = jnp.bfloat16
+    args = (*grads, *weights, *add)
     return call(
-        functools.partial(partial_kernel, groups, bool(add)),
-        outs,
-        (grad_blocks, weight_own, weight_other, *add),
-        flops=4 * sum(len(g[0]) for g in groups) * rows * depth * width,
+        functools.partial(partial_kernel, groups, len(grads), len(args)),
+        [jax.ShapeDtypeStruct((len(items), rows, 2 * width), bf16) for items, _ in groups],
+        args,
+        flops=4 * count * rows * depth * width,
+        scratch=[
+            pltpu.VMEM((count, rows, depth), bf16),
+            pltpu.VMEM((2, width, depth), bf16),
+            pltpu.VMEM((1, rows, 2 * width), bf16),
+            pltpu.SemaphoreType.DMA((count,)),
+            pltpu.SemaphoreType.DMA((2,)),
+            pltpu.SemaphoreType.DMA,
+        ],
+        space=pl.ANY,
     )
 
 
@@ -154,15 +202,12 @@
 
 
 def first_round(grad_blocks, weight, weight_other):
-    far, ahead = partials(first_groups, grad_blocks, weight, weight_other)
+    grad_other = swap_cores(grad_blocks)
+    weights = weight, weight_other
+    far, ahead, behind = partials(early_groups, (grad_blocks,), weights)
     far = send(far, 2)
-    own = send(ahead, 1)
-    ahead, next_blocks = lax.optimization_barrier((ahead, grad_blocks))
-    behind = partials(early_groups, next_blocks, weight, weight_other)[0]
-    cross = send(behind, -1, cross=True)
-    behind, later_blocks = lax.optimization_barrier((behind, next_blocks))
-    rest, for_sibling = partials(late_groups, later_blocks, weight, weight_other, far)
-    rest_sibling = swap_cores(for_sibling)
+    own, cross = send(ahead, 1), send(behind, -1, cross=True)
+    rest, rest_other = partials(late_groups, (grad_blocks, grad_other), weights, far)
 
     both = (2,) + rest.shape[1:]
     outs = [
@@ -170,7 +215,7 @@
         jax.ShapeDtypeStruct(both, jnp.float32),
         jax.ShapeDtypeStruct(both, jnp.float32),
     ]
-    return call(first_kernel, outs, (own, cross, rest, rest_sibling))
+    return (*call(first_kernel, outs, (own, cross, rest, rest_other)), grad_other)
 
 
 def gather_plane(gelu_grad, weight):
@@ -181,39 +226,76 @@
 
 def gather_and_round(gelu_grad, weight):
     grad_blocks, weight_other = taken(gather_plane, gelu_grad, weight)
-    grad_other = swap_cores(grad_blocks)
-    return (*taken(first_round, grad_blocks, weight, weight_other), grad_blocks, grad_other)
-
-
-def weight_kernel(sibling, input_ref, grad_ref, *refs):
-    first_ref = refs[0] if len(refs) == 3 else None
-    out_ref, rows_ref = refs[-2:]
-    half, depth = grad_ref.shape[1:]
+    return (*taken(first_round, grad_blocks, weight, weight_other), grad_blocks)
+
+
+def weight_kernel(input_ref, *refs):
+    grad_refs, out_ref = refs[:2], refs[2]
+    rows_ref, grads_ref, parts_ref, row_sems, grad_sems, out_sems = refs[3:]
+    half, tiles, tile = input_ref.shape[2], grads_ref.shape[1], grads_ref.shape[4]
     core = lax.rem(lax.axis_index("rep"), 2)
-    core = 1 - core if sibling else core
-    for chip in range(16):
-        at = jnp.where(core == 0, (chip % 4) * 4 + chip // 4, chip)
-        rows = pl.ds(pl.multiple_of(at * half, half), half)
-        rows_ref[rows, :] = input_ref[chip, core]
-    tile = 256
-    for start in range(0, depth, tile):
-        grad = grad_ref[:, :, start : start + tile].reshape(16 * half, tile)
-        part = matmul_tn(rows_ref[...], grad)
-        if first_ref is not None:
-            part = part + first_ref[:, start : start + tile]
-        out_ref[:, start : start + tile] = part
-
-
-def weight_gradient(sibling, input_whole, grad_blocks, *first):
+    row_copies, grad_copies, out_copies = [], [], []
+    for whose in range(2):
+        holder = 1 - core if whose else core
+        for chip in range(16):
+            at = jnp.where(holder == 0, (chip % 4) * 4 + chip // 4, chip)
+            rows = pl.ds(pl.multiple_of(at * half, half), half)
+            row_copies.append(
+                pltpu.make_async_copy(
+                    input_ref.at[chip, holder],
+                    rows_ref.at[whose, rows],
+                    row_sems.at[whose * 16 + chip],
+                )
+            )
+    for i in range(tiles):
+        columns = pl.ds(i * tile, tile)
+        for whose, ref in enumerate(grad_refs):
+            grad_copies.append(
+                pltpu.make_async_copy(
+                    ref.at[:, :, columns], grads_ref.at[whose, i], grad_sems.at[2 * i + whose]
+                )
+            )
+        out_copies.append(
+            pltpu.make_async_copy(parts_ref.at[i], out_ref.at[:, columns], out_sems.at[i])
+        )
+    for copy in row_copies + grad_copies:
+        copy.start()
+    for copy in row_copies:
+        copy.wait()
+    for i in range(tiles):
+        part = None
+        for whose in range(2):
+            grad_copies[2 * i + whose].wait()
+            grad = grads_ref[whose, i].reshape(16 * half, tile)
+            product = matmul_tn(rows_ref[whose], grad)
+            part = product if part is None else part + product
+        parts_ref[i] = part
+        out_copies[i].start()
+    for copy in out_copies:
+        copy.wait()
+
+
+def weight_gradient(input_whole, grad_blocks, grad_other):
     tokens, width = input_whole.shape
     half, depth = grad_blocks.shape[1:]
-    out = jax.ShapeDtypeStruct((width, depth), jnp.float32)
+    tile = 256
+    tiles = depth // tile
+    bf16 = jnp.bfloat16
     return call(
-        functools.partial(weight_kernel, sibling),
-        [out],
-        (input_whole.reshape(16, 2, half, width), grad_blocks, *first),
-        flops=tokens * width * depth,
-        scratch=[pltpu.VMEM((tokens // 2, width), jnp.bfloat16)],
+        weight_kernel,
+        [jax.ShapeDtypeStruct((width, depth), jnp.float32)],
+        (input_whole.reshape(16, 2, half, width), grad_blocks, grad_other),
+        flops=2 * tokens * width * depth,
+        scratch=[
+            pltpu.VMEM((2, tokens // 2, width), bf16),
+            pltpu.VMEM((2, tiles, 16, half, tile), bf16),
+            pltpu.VMEM((tiles, width, tile), jnp.float32),
+            pltpu.SemaphoreType.DMA((32,)),
+            pltpu.SemaphoreType.DMA((2 * tiles,)),
+            pltpu.SemaphoreType.DMA((tiles,)),
+        ],
+        space=pl.ANY,
+        out_space=pl.ANY,
     )[0]
 
 
@@ -225,11 +307,10 @@
     input_whole = lax.all_gather(layer_input, "col", axis=0, tiled=True)
     gelu_grad = (upstream.astype(f32) * gelu_slope(gelu_input.astype(f32))).astype(bf16)
 
-    to_send, middle, here, grad_blocks, grad_other = taken(gather_and_round, gelu_grad, weight)
+    to_send, middle, here, grad_other, grad_blocks = taken(gather_and_round, gelu_grad, weight)
 
     moved = send(to_send, 2)
-    grad_weight = weight_gradient(False, input_whole, grad_blocks)
-    grad_weight = weight_gradient(True, input_whole, grad_other, grad_weight)
+    grad_weight = weight_gradient(input_whole, grad_blocks, grad_other)
     moved, grad_weight = lax.optimization_barrier((moved, grad_weight))
     part = (2, half, width)
     outs = [jax.ShapeDtypeStruct(part, t) for t in (bf16, bf16, f32, bf16)]

time: 129 us -> 133 us (1.031); the launches traced: 126 us -> 133 us
  waiting for transfers between devices: 19.4 us -> 26.6 us
    ppermute x6, waiting for transfers between devices: 4.34 us -> 12.8 us  [send(): return lax.ppermute(values, ring, pairs)]
    ppermute x4 -> x3, starting transfers between devices: 22 us -> 18.6 us  [swap_cores(): return lax.ppermute(values, 'rep', [(0, 1), (1, 0), (2, 3), (3, 2)])]
    ppermute x6, starting transfers between devices: 25.7 us -> 28.3 us  [send(): return lax.ppermute(values, ring, pairs)]
    ppermute x4 -> x3, waiting for transfers between devices: 3.78 us -> 2.59 us  [swap_cores(): return lax.ppermute(values, 'rep', [(0, 1), (1, 0), (2, 3), (3, 2)])]
    pallas_call x8 -> x6, Pallas kernels: 22.7 us -> 22.7 us  [call(): pl.pallas_call(kernel, out_shape=outs, in_specs=[pl.BlockSpec(memory_spac...]
  transfers between devices with their start and end apart: 12 -> 11, of which waited for: 6 -> 4; matrix products, arithmetic and copies ran while one was open for 3% -> 2% of each run, Pallas kernels for 16% -> 16%
where the time goes in v8:
time: 133 us
  starting transfers between devices  51.7 us (39%)
  waiting for transfers between devices  26.6 us (20%)
  Pallas kernels  22.7 us (17%)
  between operations  14.1 us (11%)
  blocking collectives  12.9 us (10%)
  local copies, waits for them, and re-layouts  3.34 us (3%)
    ppermute x6, starting transfers between devices, send(): return lax.ppermute(values, ring, pairs)  28.3 us
    pallas_call x6, Pallas kernels, call(): pl.pallas_call(kernel, out_shape=outs, in_specs=[pl.BlockSpec(memory_spac...  22.7 us
    ppermute x3, starting transfers between devices, swap_cores(): return lax.ppermute(values, 'rep', [(0, 1), (1, 0), (2, 3), (3, 2)])  18.6 us
    all_to_all x1, blocking collectives, gather(): parts = lax.all_to_all(copies, plane, 0, 0, axis_index_groups=groups)  12.9 us
    ppermute x6, waiting for transfers between devices, send(): return lax.ppermute(values, ring, pairs)  12.8 us
    all_to_all x1, waiting for transfers between devices, gather(): parts = lax.all_to_all(copies, plane, 0, 0, axis_index_groups=groups)  10.6 us
    all_to_all x1, starting transfers between devices, gather(): parts = lax.all_to_all(copies, plane, 0, 0, axis_index_groups=groups)  4.78 us
  transfers between devices with their start and end apart: 11, of which 4 were waited for; matrix products, arithmetic and copies ran while one was open for 2% of the time, Pallas kernels for 16%

profile of v8, /device:TPU:1, one launch (start us, length us, event | category | flops | bytes accessed | tf_op | source)
XLA Modules:
  0.0 132.7 jit_solution(10898086515180979249)
XLA Ops:
  7.9 1.3 fusion.7
  9.2 79.6 %conditional.3 = (bf16[2,2,64,768]{3,2,1,0:T(8,128)(2,1)}, f32[2,64,768]{2,1,0:T(8,128)}, f32[2,64,768]{2,1,0:T(8,128)}, bf16[16,64,1536]{2,1,0:T(8,128)(2,1)}, bf16[16,64,1536]{2,1,0:T(8,128)(2,1)}) conditional(s32[]{:T(128)} %convert_element_type.16, () %tuple.32, (bf16[64,1536]{1,0:T(8,128)(2,1)S(1)}, bf16[384,1536]{1,0:T(8,128)(2,1)}) %tuple.33), branch_computations={%region_0.0_spmd, %region_1.0_spmd} | conditional | flops 2415919104 | bytes 64684480 | solution.py:196
  9.2 40.6 %conditional = (bf16[16,64,1536]{2,1,0:T(8,128)(2,1)}, bf16[384,1536]{1,0:T(8,128)(2,1)}) conditional(s32[]{:T(128)} %convert_element_type.4, () %tuple.24, (bf16[64,1536]{1,0:T(8,128)(2,1)S(1)}, bf16[384,1536]{1,0:T(8,128)(2,1)}) %param.5), branch_computations={%region_2.0_spmd, %region_3.0_spmd} | conditional | bytes 25362548 | solution.py:196
  9.3 12.9 %all_to_all.8 = bf16[4,64,1536]{2,1,0:T(8,128)(2,1)S(1)} all-to-all(bf16[4,64,1536]{2,1,0:T(8,128)(2,1)S(1)} %broadcast_in_dim.0), channel_id=1, replica_groups={{0,128,256,384},{2,130,258,386},{64,192,320,448},{66,194,322,450},{1,3,..., dimensions={0} | all-to-all | bytes 1572864 | tf_op jit(solution)/shard_map/cond/branch_1_fun/cond/branch_1_fun/all_to_all | solution.py:52
  22.1 1.9 %broadcast_in_dim.2 = bf16[4,256,1536]{2,1,0:T(8,128)(2,1)} broadcast(bf16[256,1536]{1,0:T(8,128)(2,1)S(1)} %bitcast.4), dimensions={1,2} | broadcast | bytes 3932160 | tf_op jit(solution)/shard_map/cond/branch_1_fun/cond/branch_1_fun/broadcast_in_dim | solution.py:51
  24.0 4.8 %all-to-all-start.1 = ((bf16[4,256,1536]{2,1,0:T(8,128)(2,1)}), bf16[4,256,1536]{2,1,0:T(8,128)(2,1)}, u32[]{:S(2)}, u32[]{:S(2)}) async-start(bf16[4,256,1536]{2,1,0:T(8,128)(2,1)} %broadcast_in_dim.2), calls=%async_computation.1 | async-start | bytes 6291456 | tf_op jit(solution)/shard_map/cond/branch_1_fun/cond/branch_1_fun/all_to_all | solution.py:52
  28.8 7.8 %collective-permute-start = (bf16[384,1536]{1,0:T(8,128)(2,1)S(1)}, bf16[384,1536]{1,0:T(8,128)(2,1)}, u32[]{:S(2)}, u32[]{:S(2)}) collective-permute-start(bf16[384,1536]{1,0:T(8,128)(2,1)S(1)} %copy-done.1), channel_id=1, source_target_pairs={{0,1},{1,0},{2,3},{3,2},{4,5},{5,4},{6,7},{7,6},{8,9},{9,8},{10,11... | collective-permute-start | bytes 3538952 | tf_op jit(solution)/shard_map/cond/branch_1_fun/cond/branch_1_fun/ppermute | solution.py:57
  36.6 2.6 %collective-permute-done = bf16[384,1536]{1,0:T(8,128)(2,1)} collective-permute-done((bf16[384,1536]{1,0:T(8,128)(2,1)S(1)}, bf16[384,1536]{1,0:T(8,128)(2,1)}, u32[]{:S(2)}, u32[]{:S(2)}) %collective-permute-start) | collective-permute-done | bytes 1179680 | tf_op jit(solution)/shard_map/cond/branch_1_fun/cond/branch_1_fun/ppermute | solution.py:57
  39.2 10.6 %all-to-all-done.1 = bf16[4,256,1536]{2,1,0:T(8,128)(2,1)} async-done(((bf16[4,256,1536]{2,1,0:T(8,128)(2,1)}), bf16[4,256,1536]{2,1,0:T(8,128)(2,1)}, u32[]{:S(2)}, u32[]{:S(2)}) %all-to-all-start.1) | async-done | bytes 3145760 | tf_op jit(solution)/shard_map/cond/branch_1_fun/cond/branch_1_fun/all_to_all | solution.py:52
  49.8 38.9 %conditional.1 = (bf16[2,2,64,768]{3,2,1,0:T(8,128)(2,1)}, f32[2,64,768]{2,1,0:T(8,128)}, f32[2,64,768]{2,1,0:T(8,128)}, bf16[16,64,1536]{2,1,0:T(8,128)(2,1)}) conditional(s32[]{:T(128)} %convert_element_type.4, () %tuple.23, (bf16[16,64,1536]{2,1,0:T(8,128)(2,1)}, bf16[384,1536]{1,0:T(8,128)(2,1)}, bf16[384,1536]{1,0:T(8,128)(2,1)}) %tuple.25), branch_computations={%region_4.0_spmd, %region_5.0_spmd} | conditional | flops 2415919104 | bytes 39321820 | solution.py:196
  49.8 8.8 %collective-permute-start.3 = (bf16[16,64,1536]{2,1,0:T(8,128)(2,1)}, bf16[16,64,1536]{2,1,0:T(8,128)(2,1)}, u32[]{:S(2)}, u32[]{:S(2)}) collective-permute-start(bf16[16,64,1536]{2,1,0:T(8,128)(2,1)} %get-tuple-element.16.refs_0_), channel_id=1, source_target_pairs={{0,1},{1,0},{2,3},{3,2},{4,5},{5,4},{6,7},{7,6},{8,9},{9,8},{10,11... | collective-permute-start | bytes 9437192 | tf_op jit(solution)/shard_map/cond/branch_1_fun/cond/branch_1_fun/ppermute | solution.py:57
  58.7 5.1 %branch_1_fun.3 = (bf16[1,64,768]{2,1,0:T(8,128)(2,1)S(1)}, bf16[4,64,768]{2,1,0:T(8,128)(2,1)S(1)}, bf16[4,64,768]{2,1,0:T(8,128)(2,1)S(1)}) custom-call(bf16[16,64,1536]{2,1,0:T(8,128)(2,1)} %get-tuple-element.16.refs_0_, bf16[384,1536]{1,0:T(8,128)(2,1)} %get-tuple-element.17.refs_1_.refs_2_, bf16[384,1536]{1,0:T(8,128)(2,1)} %get-tuple-element.18.refs_2_.refs_3_), custom_call_target="tpu_custom_call" | custom-call | flops 1358954496 | bytes 6389760 | tf_op jit(solution)/shard_map/cond/branch_1_fun/cond/branch_1_fun/pallas_call | solution.py:79
  63.7 7.4 %collective-permute-start.1 = (bf16[4,64,768]{2,1,0:T(8,128)(2,1)S(1)}, bf16[4,64,768]{2,1,0:T(8,128)(2,1)S(1)}, u32[]{:S(2)}, u32[]{:S(2)}) collective-permute-start(bf16[4,64,768]{2,1,0:T(8,128)(2,1)S(1)} %get-tuple-element.19), channel_id=1, source_target_pairs={{0,4},{1,61},{2,6},{3,63},{4,8},{5,1},{6,10},{7,3},{8,12},{9,5},{1... | collective-permute-start | bytes 1179656 | tf_op jit(solution)/shard_map/cond/branch_1_fun/cond/branch_1_fun/ppermute | solution.py:66
  71.2 1.9 %collective-permute-start.2 = (bf16[4,64,768]{2,1,0:T(8,128)(2,1)S(1)}, bf16[4,64,768]{2,1,0:T(8,128)(2,1)S(1)}, u32[]{:S(2)}, u32[]{:S(2)}) collective-permute-start(bf16[4,64,768]{2,1,0:T(8,128)(2,1)S(1)} %get-tuple-element.20), channel_id=1, source_target_pairs={{0,61},{1,4},{2,63},{3,6},{4,1},{5,8},{6,3},{7,10},{8,5},{9,12},{1... | collective-permute-start | bytes 1179656 | tf_op jit(solution)/shard_map/cond/branch_1_fun/cond/branch_1_fun/ppermute | solution.py:66
  73.1 3.1 %collective-permute-start.4 = (bf16[1,64,768]{2,1,0:T(8,128)(2,1)S(1)}, bf16[1,64,768]{2,1,0:T(8,128)(2,1)S(1)}, u32[]{:S(2)}, u32[]{:S(2)}) collective-permute-start(bf16[1,64,768]{2,1,0:T(8,128)(2,1)S(1)} %get-tuple-element.21), channel_id=1, source_target_pairs={{0,8},{1,57},{2,10},{3,59},{4,12},{5,61},{6,14},{7,63},{8,16},{9,1... | collective-permute-start | bytes 294920 | tf_op jit(solution)/shard_map/cond/branch_1_fun/cond/branch_1_fun/ppermute | solution.py:66
  76.2 7.7 %collective-permute-done.4.refs_4_ = bf16[1,64,768]{2,1,0:T(8,128)(2,1)S(1)} collective-permute-done((bf16[1,64,768]{2,1,0:T(8,128)(2,1)S(1)}, bf16[1,64,768]{2,1,0:T(8,128)(2,1)S(1)}, u32[]{:S(2)}, u32[]{:S(2)}) %collective-permute-start.4) | collective-permute-done | bytes 98336 | tf_op jit(solution)/shard_map/cond/branch_1_fun/cond/branch_1_fun/ppermute | solution.py:66
  83.9 3.8 %branch_1_fun.4 = (bf16[4,64,768]{2,1,0:T(8,128)(2,1)S(1)}, bf16[3,64,768]{2,1,0:T(8,128)(2,1)S(1)}) custom-call(bf16[16,64,1536]{2,1,0:T(8,128)(2,1)} %get-tuple-element.16.refs_0_, bf16[16,64,1536]{2,1,0:T(8,128)(2,1)} %collective-permute-done.3.refs_1_, bf16[384,1536]{1,0:T(8,128)(2,1)S(1)} %copy-done.2, ...), custom_call_target="tpu_custom_call" | custom-call | flops 1056964608 | bytes 9437184 | tf_op jit(solution)/shard_map/cond/branch_1_fun/cond/branch_1_fun/pallas_call | solution.py:79
  88.8 5.9 %collective-permute-start.5 = (bf16[2,2,64,768]{3,2,1,0:T(8,128)(2,1)}, bf16[2,2,64,768]{3,2,1,0:T(8,128)(2,1)S(1)}, u32[]{:S(2)}, u32[]{:S(2)}) collective-permute-start(bf16[2,2,64,768]{3,2,1,0:T(8,128)(2,1)} %get-tuple-element.47), channel_id=1, source_target_pairs={{0,8},{1,57},{2,10},{3,59},{4,12},{5,61},{6,14},{7,63},{8,16},{9,1... | collective-permute-start | bytes 1179656 | tf_op jit(solution)/shard_map/ppermute | solution.py:66
  94.8 1.4 %copy-done = bf16[2048,384]{1,0:T(8,128)(2,1)S(1)} copy-done((bf16[2048,384]{1,0:T(8,128)(2,1)S(1)}, bf16[2048,384]{1,0:T(8,128)(2,1)}, u32[]{:S(2)}) %copy-start) | copy-done | bytes 1572888
  96.2 10.9 %shard_map.60 = f32[384,1536]{1,0:T(8,128)} custom-call(bf16[16,2,64,384]{3,2,1,0:T(8,128)(2,1)S(1)} %bitcast.3, bf16[16,64,1536]{2,1,0:T(8,128)(2,1)} %get-tuple-element.48.refs_0_, bf16[16,64,1536]{2,1,0:T(8,128)(2,1)} %get-tuple-element.49.refs_1_), custom_call_target="tpu_custom_call" | custom-call | flops 2415919104 | bytes 10223616 | tf_op jit(solution)/shard_map/pallas_call | solution.py:79
  108.3 5.4 %collective-permute-start.6 = (bf16[2,64,384]{2,1,0:T(8,128)(2,1)S(1)}, bf16[2,64,384]{2,1,0:T(8,128)(2,1)S(1)}, u32[]{:S(2)}, u32[]{:S(2)}) collective-permute-start(bf16[2,64,384]{2,1,0:T(8,128)(2,1)S(1)} %get-tuple-element.53), channel_id=1, source_target_pairs={{0,16},{1,49},{2,18},{3,51},{4,20},{5,53},{6,22},{7,55},{8,24},{9,... | collective-permute-start | bytes 294920 | tf_op jit(solution)/shard_map/ppermute | solution.py:66
  113.7 4.5 %collective-permute-start.7 = (bf16[2,64,384]{2,1,0:T(8,128)(2,1)S(1)}, bf16[2,64,384]{2,1,0:T(8,128)(2,1)S(1)}, u32[]{:S(2)}, u32[]{:S(2)}) collective-permute-start(bf16[2,64,384]{2,1,0:T(8,128)(2,1)S(1)} %get-tuple-element.54), channel_id=1, source_target_pairs={{0,17},{1,48},{2,19},{3,50},{4,21},{5,52},{6,23},{7,54},{8,25},{9,... | collective-permute-start | bytes 294920 | tf_op jit(solution)/shard_map/ppermute | solution.py:66
  118.2 1.9 %collective-permute-start.8 = (bf16[2,64,384]{2,1,0:T(8,128)(2,1)S(1)}, bf16[2,64,384]{2,1,0:T(8,128)(2,1)S(1)}, u32[]{:S(2)}, u32[]{:S(2)}) collective-permute-start(bf16[2,64,384]{2,1,0:T(8,128)(2,1)S(1)} %get-tuple-element.56), channel_id=1, source_target_pairs={{0,1},{1,0},{2,3},{3,2},{4,5},{5,4},{6,7},{7,6},{8,9},{9,8},{10,11... | collective-permute-start | bytes 294920 | tf_op jit(solution)/shard_map/ppermute | solution.py:57
  120.1 5.1 %collective-permute-done.7.cross_ref = bf16[2,64,384]{2,1,0:T(8,128)(2,1)S(1)} collective-permute-done((bf16[2,64,384]{2,1,0:T(8,128)(2,1)S(1)}, bf16[2,64,384]{2,1,0:T(8,128)(2,1)S(1)}, u32[]{:S(2)}, u32[]{:S(2)}) %collective-permute-start.7) | collective-permute-done | bytes 98336 | tf_op jit(solution)/shard_map/ppermute | solution.py:66
  (18 shorter events, 3.8 us)
Async XLA Ops:
  7.2 87.6 %all-gather.2.cloned.1.call-start = ((), (), s32[]{:S(2)}) async-start(), calls=%async_computation.2 | async-start | bytes 1671168 | tf_op jit(solution)/shard_map/all_gather | solution.py:307
  24.0 4.8 %copy-start.1 = (bf16[384,1536]{1,0:T(8,128)(2,1)S(1)}, bf16[384,1536]{1,0:T(8,128)(2,1)}, u32[]{:S(2)}) copy-start(bf16[384,1536]{1,0:T(8,128)(2,1)} %get-tuple-element.15) | copy-start | bytes 3538948 | tf_op jit(solution)/shard_map/cond/branch_1_fun/cond
  24.0 25.8 %all-to-all-start.1 = ((bf16[4,256,1536]{2,1,0:T(8,128)(2,1)}), bf16[4,256,1536]{2,1,0:T(8,128)(2,1)}, u32[]{:S(2)}, u32[]{:S(2)}) async-start(bf16[4,256,1536]{2,1,0:T(8,128)(2,1)} %broadcast_in_dim.2), calls=%async_computation.1 | async-start | bytes 6291456 | tf_op jit(solution)/shard_map/cond/branch_1_fun/cond/branch_1_fun/all_to_all | solution.py:52
  28.8 10.4 %collective-permute-start = (bf16[384,1536]{1,0:T(8,128)(2,1)S(1)}, bf16[384,1536]{1,0:T(8,128)(2,1)}, u32[]{:S(2)}, u32[]{:S(2)}) collective-permute-start(bf16[384,1536]{1,0:T(8,128)(2,1)S(1)} %copy-done.1), channel_id=1, source_target_pairs={{0,1},{1,0},{2,3},{3,2},{4,5},{5,4},{6,7},{7,6},{8,9},{9,8},{10,11... | collective-permute-start | bytes 3538952 | tf_op jit(solution)/shard_map/cond/branch_1_fun/cond/branch_1_fun/ppermute | solution.py:57
  49.8 34.0 %copy-start.2 = (bf16[384,1536]{1,0:T(8,128)(2,1)S(1)}, bf16[384,1536]{1,0:T(8,128)(2,1)}, u32[]{:S(2)}) copy-start(bf16[384,1536]{1,0:T(8,128)(2,1)} %get-tuple-element.17.refs_1_.refs_2_) | copy-start | bytes 3538948 | tf_op jit(solution)/shard_map/cond/branch_1_fun/cond
  49.8 34.0 %collective-permute-start.3 = (bf16[16,64,1536]{2,1,0:T(8,128)(2,1)}, bf16[16,64,1536]{2,1,0:T(8,128)(2,1)}, u32[]{:S(2)}, u32[]{:S(2)}) collective-permute-start(bf16[16,64,1536]{2,1,0:T(8,128)(2,1)} %get-tuple-element.16.refs_0_), channel_id=1, source_target_pairs={{0,1},{1,0},{2,3},{3,2},{4,5},{5,4},{6,7},{7,6},{8,9},{9,8},{10,11... | collective-permute-start | bytes 9437192 | tf_op jit(solution)/shard_map/cond/branch_1_fun/cond/branch_1_fun/ppermute | solution.py:57
  63.7 23.9 %collective-permute-start.1 = (bf16[4,64,768]{2,1,0:T(8,128)(2,1)S(1)}, bf16[4,64,768]{2,1,0:T(8,128)(2,1)S(1)}, u32[]{:S(2)}, u32[]{:S(2)}) collective-permute-start(bf16[4,64,768]{2,1,0:T(8,128)(2,1)S(1)} %get-tuple-element.19), channel_id=1, source_target_pairs={{0,4},{1,61},{2,6},{3,63},{4,8},{5,1},{6,10},{7,3},{8,12},{9,5},{1... | collective-permute-start | bytes 1179656 | tf_op jit(solution)/shard_map/cond/branch_1_fun/cond/branch_1_fun/ppermute | solution.py:66
  71.2 16.5 %collective-permute-start.2 = (bf16[4,64,768]{2,1,0:T(8,128)(2,1)S(1)}, bf16[4,64,768]{2,1,0:T(8,128)(2,1)S(1)}, u32[]{:S(2)}, u32[]{:S(2)}) collective-permute-start(bf16[4,64,768]{2,1,0:T(8,128)(2,1)S(1)} %get-tuple-element.20), channel_id=1, source_target_pairs={{0,61},{1,4},{2,63},{3,6},{4,1},{5,8},{6,3},{7,10},{8,5},{9,12},{1... | collective-permute-start | bytes 1179656 | tf_op jit(solution)/shard_map/cond/branch_1_fun/cond/branch_1_fun/ppermute | solution.py:66
  73.1 10.8 %collective-permute-start.4 = (bf16[1,64,768]{2,1,0:T(8,128)(2,1)S(1)}, bf16[1,64,768]{2,1,0:T(8,128)(2,1)S(1)}, u32[]{:S(2)}, u32[]{:S(2)}) collective-permute-start(bf16[1,64,768]{2,1,0:T(8,128)(2,1)S(1)} %get-tuple-element.21), channel_id=1, source_target_pairs={{0,8},{1,57},{2,10},{3,59},{4,12},{5,61},{6,14},{7,63},{8,16},{9,1... | collective-permute-start | bytes 294920 | tf_op jit(solution)/shard_map/cond/branch_1_fun/cond/branch_1_fun/ppermute | solution.py:66
  88.8 18.3 %collective-permute-start.5 = (bf16[2,2,64,768]{3,2,1,0:T(8,128)(2,1)}, bf16[2,2,64,768]{3,2,1,0:T(8,128)(2,1)S(1)}, u32[]{:S(2)}, u32[]{:S(2)}) collective-permute-start(bf16[2,2,64,768]{3,2,1,0:T(8,128)(2,1)} %get-tuple-element.47), channel_id=1, source_target_pairs={{0,8},{1,57},{2,10},{3,59},{4,12},{5,61},{6,14},{7,63},{8,16},{9,1... | collective-permute-start | bytes 1179656 | tf_op jit(solution)/shard_map/ppermute | solution.py:66
  94.8 1.4 %copy-start = (bf16[2048,384]{1,0:T(8,128)(2,1)S(1)}, bf16[2048,384]{1,0:T(8,128)(2,1)}, u32[]{:S(2)}) copy-start(bf16[2048,384]{1,0:T(8,128)(2,1)} %all-gather.2.cloned.1.call-done) | copy-start | bytes 4718596
  108.3 11.9 %collective-permute-start.6 = (bf16[2,64,384]{2,1,0:T(8,128)(2,1)S(1)}, bf16[2,64,384]{2,1,0:T(8,128)(2,1)S(1)}, u32[]{:S(2)}, u32[]{:S(2)}) collective-permute-start(bf16[2,64,384]{2,1,0:T(8,128)(2,1)S(1)} %get-tuple-element.53), channel_id=1, source_target_pairs={{0,16},{1,49},{2,18},{3,51},{4,20},{5,53},{6,22},{7,55},{8,24},{9,... | collective-permute-start | bytes 294920 | tf_op jit(solution)/shard_map/ppermute | solution.py:66
  113.7 11.5 %collective-permute-start.7 = (bf16[2,64,384]{2,1,0:T(8,128)(2,1)S(1)}, bf16[2,64,384]{2,1,0:T(8,128)(2,1)S(1)}, u32[]{:S(2)}, u32[]{:S(2)}) collective-permute-start(bf16[2,64,384]{2,1,0:T(8,128)(2,1)S(1)} %get-tuple-element.54), channel_id=1, source_target_pairs={{0,17},{1,48},{2,19},{3,50},{4,21},{5,52},{6,23},{7,54},{8,25},{9,... | collective-permute-start | bytes 294920 | tf_op jit(solution)/shard_map/ppermute | solution.py:66
  118.2 7.0 %collective-permute-start.8 = (bf16[2,64,384]{2,1,0:T(8,128)(2,1)S(1)}, bf16[2,64,384]{2,1,0:T(8,128)(2,1)S(1)}, u32[]{:S(2)}, u32[]{:S(2)}) collective-permute-start(bf16[2,64,384]{2,1,0:T(8,128)(2,1)S(1)} %get-tuple-element.56), channel_id=1, source_target_pairs={{0,1},{1,0},{2,3},{3,2},{4,5},{5,4},{6,7},{7,6},{8,9},{9,8},{10,11... | collective-permute-start | bytes 294920 | tf_op jit(solution)/shard_map/ppermute | solution.py:57
Sparse Core Ops, SparseCore 0:
  10.1 69.7 all-gather.1

commit v9 on v7

--- a/solution.py
+++ b/solution.py
@@ -31,15 +31,13 @@
 along_y = [[[index(x, y, core) for y in y_order] for x in range(4)] for core in range(2)]
 
 
-first_groups = (((8,), False), ((7, 5, 3, 1), False))
-early_groups = (((-7, -5, -3, -1), True),)
+early_groups = (((8,), False), ((7, 5, 3, 1), False), ((-7, -5, -3, -1), True))
 late_groups = (((6, 4, 2, 0), False), ((-6, -4, -2), True))
 
 
-def place(step):
-    core = lax.rem(lax.axis_index("rep"), 2)
-    chip = lax.rem(lax.axis_index("col") + (1 - 2 * core) * step + 16, 16)
-    return jnp.where(core == 0, lax.rem(chip, 4) * 4 + lax.div(chip, 4), chip)
+def place(chip, core):
+    turned = lax.rem(chip, 4) * 4 + lax.div(chip, 4)
+    return jnp.where(core == 0, turned, chip)
 
 
 def gather(values, groups):
@@ -78,34 +76,45 @@
         in_specs=[vmem] * len(args),
         out_specs=tuple(vmem for _ in outs),
         scratch_shapes=scratch,
-        compiler_params=pltpu.CompilerParams(vmem_limit_bytes=32 * 1024 * 1024),
+        compiler_params=pltpu.CompilerParams(vmem_limit_bytes=40 * 1024 * 1024),
         cost_estimate=pl.CostEstimate(flops=flops, bytes_accessed=moved, transcendentals=0),
     )(*args)
 
 
-def partial_kernel(groups, add, grad_ref, own_ref, other_ref, *refs):
+def partial_kernel(groups, dots, grad_ref, own_ref, other_ref, *refs):
+    outs = refs[-len(groups) :]
+    add_ref = refs[0] if len(refs) > len(groups) else None
+    core = lax.rem(lax.axis_index("rep"), 2)
+    z = lax.axis_index("col")
     width = own_ref.shape[0]
-    first_ref, outs = (refs[0], refs[1:]) if add else (None, refs)
-    for (steps, flipped), out_ref in zip(groups, outs):
-        rows = jnp.concatenate([grad_ref[place(step)] for step in steps], axis=0)
-        for side, ref in enumerate((other_ref, own_ref) if flipped else (own_ref, other_ref)):
-            part = matmul_nt(rows, ref[...]).reshape(len(steps), -1, width)
-            columns = slice(side * width, (side + 1) * width)
-            out_ref[:, :, columns] = part.astype(out_ref.dtype)
-            if first_ref is not None and out_ref is outs[0]:
-                first = part[0] + first_ref[0, :, columns].astype(jnp.float32)
-                out_ref[0, :, columns] = first.astype(out_ref.dtype)
-
-
-def partials(groups, grad_blocks, weight_own, weight_other, *add):
+    blocks = [
+        (out_ref, i, flipped, lax.rem(z + (1 - 2 * core) * step + 16, 16))
+        for (steps, flipped), out_ref in zip(groups, outs)
+        for i, step in enumerate(steps)
+    ]
+    start = 0
+    for count in dots:
+        taken_now = blocks[start : start + count]
+        rows = jnp.concatenate([grad_ref[place(chip, core)] for _, _, _, chip in taken_now], axis=0)
+        for side, ref in enumerate((own_ref, other_ref)):
+            part = matmul_nt(rows, ref[...]).reshape(count, -1, width)
+            for j, (out_ref, i, flipped, _) in enumerate(taken_now):
+                at = (1 - side if flipped else side) * width
+                value = part[j]
+                if add_ref is not None and start + j == 0:
+                    value = value + add_ref[0, :, at : at + width].astype(jnp.float32)
+                out_ref[i, :, at : at + width] = value.astype(out_ref.dtype)
+        start += count
+
+
+def partials(groups, dots, grad_blocks, weights, *add):
     rows, depth = grad_blocks.shape[1:]
-    width = weight_own.shape[0]
-    outs = [jax.ShapeDtypeStruct((len(g[0]), rows, 2 * width), jnp.bfloat16) for g in groups]
+    width = weights[0].shape[0]
     return call(
-        functools.partial(partial_kernel, groups, bool(add)),
-        outs,
-        (grad_blocks, weight_own, weight_other, *add),
-        flops=4 * sum(len(g[0]) for g in groups) * rows * depth * width,
+        functools.partial(partial_kernel, groups, dots),
+        [jax.ShapeDtypeStruct((len(g[0]), rows, 2 * width), jnp.bfloat16) for g in groups],
+        (grad_blocks, *weights, *add),
+        flops=12 * sum(dots) * rows * depth * width,
     )
 
 
@@ -154,15 +163,13 @@
 
 
 def first_round(grad_blocks, weight, weight_other):
-    far, ahead = partials(first_groups, grad_blocks, weight, weight_other)
+    weights = weight, weight_other
+    far, ahead, behind = partials(early_groups, (5, 4), grad_blocks, weights)
+    far, later_blocks = lax.optimization_barrier((far, grad_blocks))
     far = send(far, 2)
-    own = send(ahead, 1)
-    ahead, next_blocks = lax.optimization_barrier((ahead, grad_blocks))
-    behind = partials(early_groups, next_blocks, weight, weight_other)[0]
-    cross = send(behind, -1, cross=True)
-    behind, later_blocks = lax.optimization_barrier((behind, next_blocks))
-    rest, for_sibling = partials(late_groups, later_blocks, weight, weight_other, far)
-    rest_sibling = swap_cores(for_sibling)
+    own, cross = send(ahead, 1), send(behind, -1, cross=True)
+    rest, for_sibling = partials(late_groups, (7,), later_blocks, weights, far)
+    rest_other = swap_cores(for_sibling)
 
     both = (2,) + rest.shape[1:]
     outs = [
@@ -170,7 +177,7 @@
         jax.ShapeDtypeStruct(both, jnp.float32),
         jax.ShapeDtypeStruct(both, jnp.float32),
     ]
-    return call(first_kernel, outs, (own, cross, rest, rest_sibling))
+    return call(first_kernel, outs, (own, cross, rest, rest_other))
 
 
 def gather_plane(gelu_grad, weight):
@@ -181,8 +188,7 @@
 
 def gather_and_round(gelu_grad, weight):
     grad_blocks, weight_other = taken(gather_plane, gelu_grad, weight)
-    grad_other = swap_cores(grad_blocks)
-    return (*taken(first_round, grad_blocks, weight, weight_other), grad_blocks, grad_other)
+    return (*taken(first_round, grad_blocks, weight, weight_other), grad_blocks)
 
 
 def weight_kernel(sibling, input_ref, grad_ref, *refs):
@@ -212,7 +218,7 @@
         functools.partial(weight_kernel, sibling),
         [out],
         (input_whole.reshape(16, 2, half, width), grad_blocks, *first),
-        flops=tokens * width * depth,
+        flops=(1 if sibling else 40) * tokens * width * depth,
         scratch=[pltpu.VMEM((tokens // 2, width), jnp.bfloat16)],
     )[0]
 
@@ -225,9 +231,10 @@
     input_whole = lax.all_gather(layer_input, "col", axis=0, tiled=True)
     gelu_grad = (upstream.astype(f32) * gelu_slope(gelu_input.astype(f32))).astype(bf16)
 
-    to_send, middle, here, grad_blocks, grad_other = taken(gather_and_round, gelu_grad, weight)
+    to_send, middle, here, grad_blocks = taken(gather_and_round, gelu_grad, weight)
 
     moved = send(to_send, 2)
+    grad_other = swap_cores(grad_blocks)
     grad_weight = weight_gradient(False, input_whole, grad_blocks)
     grad_weight = weight_gradient(True, input_whole, grad_other, grad_weight)
     moved, grad_weight = lax.optimization_barrier((moved, grad_weight))

time: 129 us -> 126 us (0.977)
  the two profiles are of different devices: /device:TPU:1 before, /device:TPU:2 now
where the time goes in v9:
time: 126 us
  waiting for transfers between devices  36.8 us (29%)
  starting transfers between devices  35.7 us (28%)
  Pallas kernels  17.8 us (14%)
  blocking collectives  16.3 us (13%)
  between operations  14.1 us (11%)
  local copies, waits for them, and re-layouts  3.39 us (3%)
  other arithmetic  1.3 us (1%)
    ppermute x6, starting transfers between devices, send(): return lax.ppermute(values, ring, pairs)  19.4 us
    pallas_call x7, Pallas kernels, call(): pl.pallas_call(kernel, out_shape=outs, in_specs=[vmem] * len(args), out_s...  17.8 us
    all_to_all x1, waiting for transfers between devices, gather(): parts = lax.all_to_all(copies, plane, 0, 0, axis_index_groups=groups)  17 us
    all_to_all x1, blocking collectives, gather(): parts = lax.all_to_all(copies, plane, 0, 0, axis_index_groups=groups)  16.3 us
    ppermute x6, waiting for transfers between devices, send(): return lax.ppermute(values, ring, pairs)  14.8 us
    ppermute x4, starting transfers between devices, swap_cores(): return lax.ppermute(values, 'rep', [(0, 1), (1, 0), (2, 3), (3, 2)])  11.5 us
    all_to_all x1, starting transfers between devices, gather(): parts = lax.all_to_all(copies, plane, 0, 0, axis_index_groups=groups)  4.78 us
    ppermute x4, waiting for transfers between devices, swap_cores(): return lax.ppermute(values, 'rep', [(0, 1), (1, 0), (2, 3), (3, 2)])  2.95 us
  transfers between devices with their start and end apart: 12, of which 7 were waited for; matrix products, arithmetic and copies ran while one was open for 3% of the time, Pallas kernels for 13%

profile of v9, /device:TPU:2, one launch (start us, length us, event | category | flops | bytes accessed | tf_op | source)
XLA Modules:
  0.0 125.5 jit_solution(14875096689152938418)
XLA Ops:
  9.2 74.7 %conditional.3 = (bf16[2,2,64,768]{3,2,1,0:T(8,128)(2,1)}, f32[2,64,768]{2,1,0:T(8,128)}, f32[2,64,768]{2,1,0:T(8,128)}, bf16[16,64,1536]{2,1,0:T(8,128)(2,1)}) conditional(s32[]{:T(128)} %convert_element_type.16, () %tuple.32, (bf16[64,1536]{1,0:T(8,128)(2,1)S(1)}, bf16[384,1536]{1,0:T(8,128)(2,1)}) %tuple.33), branch_computations={%region_0.0_spmd, %region_1.0_spmd} | conditional | flops 7247757312 | bytes 50135456 | solution.py:157
  9.2 45.0 %conditional = (bf16[16,64,1536]{2,1,0:T(8,128)(2,1)}, bf16[384,1536]{1,0:T(8,128)(2,1)}) conditional(s32[]{:T(128)} %convert_element_type.4, () %tuple.24, (bf16[64,1536]{1,0:T(8,128)(2,1)S(1)}, bf16[384,1536]{1,0:T(8,128)(2,1)}) %param.5), branch_computations={%region_2.0_spmd, %region_3.0_spmd} | conditional | bytes 25362548 | solution.py:157
  9.3 16.3 %all_to_all.8 = bf16[4,64,1536]{2,1,0:T(8,128)(2,1)S(1)} all-to-all(bf16[4,64,1536]{2,1,0:T(8,128)(2,1)S(1)} %broadcast_in_dim.0), channel_id=1, replica_groups={{0,128,256,384},{2,130,258,386},{64,192,320,448},{66,194,322,450},{1,3,..., dimensions={0} | all-to-all | bytes 1572864 | tf_op jit(solution)/shard_map/cond/branch_1_fun/cond/branch_1_fun/all_to_all | solution.py:45
  25.6 1.9 %broadcast_in_dim.2 = bf16[4,256,1536]{2,1,0:T(8,128)(2,1)} broadcast(bf16[256,1536]{1,0:T(8,128)(2,1)S(1)} %bitcast.5), dimensions={1,2} | broadcast | bytes 3932160 | tf_op jit(solution)/shard_map/cond/branch_1_fun/cond/branch_1_fun/broadcast_in_dim | solution.py:44
  27.5 4.8 %all-to-all-start.1 = ((bf16[4,256,1536]{2,1,0:T(8,128)(2,1)}), bf16[4,256,1536]{2,1,0:T(8,128)(2,1)}, u32[]{:S(2)}, u32[]{:S(2)}) async-start(bf16[4,256,1536]{2,1,0:T(8,128)(2,1)} %broadcast_in_dim.2), calls=%async_computation.1 | async-start | bytes 6291456 | tf_op jit(solution)/shard_map/cond/branch_1_fun/cond/branch_1_fun/all_to_all | solution.py:45
  32.3 1.9 %collective-permute-start = (bf16[384,1536]{1,0:T(8,128)(2,1)S(1)}, bf16[384,1536]{1,0:T(8,128)(2,1)}, u32[]{:S(2)}, u32[]{:S(2)}) collective-permute-start(bf16[384,1536]{1,0:T(8,128)(2,1)S(1)} %copy-done.1), channel_id=1, source_target_pairs={{0,1},{1,0},{2,3},{3,2},{4,5},{5,4},{6,7},{7,6},{8,9},{9,8},{10,11... | collective-permute-start | bytes 3538952 | tf_op jit(solution)/shard_map/cond/branch_1_fun/cond/branch_1_fun/ppermute | solution.py:50
  34.3 2.9 %collective-permute-done = bf16[384,1536]{1,0:T(8,128)(2,1)} collective-permute-done((bf16[384,1536]{1,0:T(8,128)(2,1)S(1)}, bf16[384,1536]{1,0:T(8,128)(2,1)}, u32[]{:S(2)}, u32[]{:S(2)}) %collective-permute-start) | collective-permute-done | bytes 1179680 | tf_op jit(solution)/shard_map/cond/branch_1_fun/cond/branch_1_fun/ppermute | solution.py:50
  37.2 17.0 %all-to-all-done.1 = bf16[4,256,1536]{2,1,0:T(8,128)(2,1)} async-done(((bf16[4,256,1536]{2,1,0:T(8,128)(2,1)}), bf16[4,256,1536]{2,1,0:T(8,128)(2,1)}, u32[]{:S(2)}, u32[]{:S(2)}) %all-to-all-start.1) | async-done | bytes 3145760 | tf_op jit(solution)/shard_map/cond/branch_1_fun/cond/branch_1_fun/all_to_all | solution.py:45
  54.2 29.6 %conditional.1 = ((bf16[2,2,64,768]{3,2,1,0:T(8,128)(2,1)}, f32[2,64,768]{2,1,0:T(8,128)}, f32[2,64,768]{2,1,0:T(8,128)})) conditional(s32[]{:T(128)} %convert_element_type.4, () %tuple.23, (bf16[16,64,1536]{2,1,0:T(8,128)(2,1)}, bf16[384,1536]{1,0:T(8,128)(2,1)}, bf16[384,1536]{1,0:T(8,128)(2,1)}) %tuple.25), branch_computations={%region_4.0_spmd, %region_5.0_spmd} | conditional | flops 7247757312 | bytes 24772804 | solution.py:157
  54.2 4.7 %branch_1_fun.3 = (bf16[1,64,768]{2,1,0:T(8,128)(2,1)S(1)}, bf16[4,64,768]{2,1,0:T(8,128)(2,1)S(1)}, bf16[4,64,768]{2,1,0:T(8,128)(2,1)S(1)}) custom-call(bf16[16,64,1536]{2,1,0:T(8,128)(2,1)} %get-tuple-element.22.grad_ref, bf16[384,1536]{1,0:T(8,128)(2,1)} %get-tuple-element.17.own_ref, bf16[384,1536]{1,0:T(8,128)(2,1)} %get-tuple-element.18.other_ref), custom_call_target="tpu_custom_call" | custom-call | flops 4076863488 | bytes 6389760 | tf_op jit(solution)/shard_map/cond/branch_1_fun/cond/branch_1_fun/pallas_call | solution.py:73
  58.9 1.9 %collective-permute-start.3 = (bf16[1,64,768]{2,1,0:T(8,128)(2,1)S(1)}, bf16[1,64,768]{2,1,0:T(8,128)(2,1)S(1)}, u32[]{:S(2)}, u32[]{:S(2)}) collective-permute-start(bf16[1,64,768]{2,1,0:T(8,128)(2,1)S(1)} %get-tuple-element.23), channel_id=1, source_target_pairs={{0,8},{1,57},{2,10},{3,59},{4,12},{5,61},{6,14},{7,63},{8,16},{9,1... | collective-permute-start | bytes 294920 | tf_op jit(solution)/shard_map/cond/branch_1_fun/cond/branch_1_fun/ppermute | solution.py:59
  60.9 3.4 %collective-permute-start.1 = (bf16[4,64,768]{2,1,0:T(8,128)(2,1)S(1)}, bf16[4,64,768]{2,1,0:T(8,128)(2,1)S(1)}, u32[]{:S(2)}, u32[]{:S(2)}) collective-permute-start(bf16[4,64,768]{2,1,0:T(8,128)(2,1)S(1)} %get-tuple-element.19), channel_id=1, source_target_pairs={{0,4},{1,61},{2,6},{3,63},{4,8},{5,1},{6,10},{7,3},{8,12},{9,5},{1... | collective-permute-start | bytes 1179656 | tf_op jit(solution)/shard_map/cond/branch_1_fun/cond/branch_1_fun/ppermute | solution.py:59
  64.2 5.7 %collective-permute-start.2 = (bf16[4,64,768]{2,1,0:T(8,128)(2,1)S(1)}, bf16[4,64,768]{2,1,0:T(8,128)(2,1)S(1)}, u32[]{:S(2)}, u32[]{:S(2)}) collective-permute-start(bf16[4,64,768]{2,1,0:T(8,128)(2,1)S(1)} %get-tuple-element.20), channel_id=1, source_target_pairs={{0,61},{1,4},{2,63},{3,6},{4,1},{5,8},{6,3},{7,10},{8,5},{9,12},{1... | collective-permute-start | bytes 1179656 | tf_op jit(solution)/shard_map/cond/branch_1_fun/cond/branch_1_fun/ppermute | solution.py:59
  70.0 3.8 %branch_1_fun.4 = (bf16[4,64,768]{2,1,0:T(8,128)(2,1)S(1)}, bf16[3,64,768]{2,1,0:T(8,128)(2,1)S(1)}) custom-call(bf16[16,64,1536]{2,1,0:T(8,128)(2,1)} %get-tuple-element.22.grad_ref, bf16[384,1536]{1,0:T(8,128)(2,1)S(1)} %copy-done.2, bf16[384,1536]{1,0:T(8,128)(2,1)} %get-tuple-element.18.other_ref, bf16[1,64,768]{2,1,0:T(8,128)(2,1)S(1)} %collective-permute-done.3.refs_0_), custom_call_target="tpu_custom_call" | custom-call | flops 3170893824 | bytes 6291456 | tf_op jit(solution)/shard_map/cond/branch_1_fun/cond/branch_1_fun/pallas_call | solution.py:73
  73.8 1.9 %collective-permute-start.4 = (bf16[3,64,768]{2,1,0:T(8,128)(2,1)S(1)}, bf16[3,64,768]{2,1,0:T(8,128)(2,1)S(1)}, u32[]{:S(2)}, u32[]{:S(2)}) collective-permute-start(bf16[3,64,768]{2,1,0:T(8,128)(2,1)S(1)} %get-tuple-element.25), channel_id=1, source_target_pairs={{0,1},{1,0},{2,3},{3,2},{4,5},{5,4},{6,7},{7,6},{8,9},{9,8},{10,11... | collective-permute-start | bytes 884744 | tf_op jit(solution)/shard_map/cond/branch_1_fun/cond/branch_1_fun/ppermute | solution.py:50
  75.8 7.0 %collective-permute-done.1.own_ref = bf16[4,64,768]{2,1,0:T(8,128)(2,1)S(1)} collective-permute-done((bf16[4,64,768]{2,1,0:T(8,128)(2,1)S(1)}, bf16[4,64,768]{2,1,0:T(8,128)(2,1)S(1)}, u32[]{:S(2)}, u32[]{:S(2)}) %collective-permute-start.1) | collective-permute-done | bytes 393248 | tf_op jit(solution)/shard_map/cond/branch_1_fun/cond/branch_1_fun/ppermute | solution.py:59
  85.8 2.3 %collective-permute-start.6 = (bf16[16,64,1536]{2,1,0:T(8,128)(2,1)}, bf16[16,64,1536]{2,1,0:T(8,128)(2,1)S(1)}, u32[]{:S(2)}, u32[]{:S(2)}) collective-permute-start(bf16[16,64,1536]{2,1,0:T(8,128)(2,1)} %get-tuple-element.45.grad_ref), channel_id=1, source_target_pairs={{0,1},{1,0},{2,3},{3,2},{4,5},{5,4},{6,7},{7,6},{8,9},{9,8},{10,11... | collective-permute-start | bytes 9437192 | tf_op jit(solution)/shard_map/ppermute | solution.py:50
  90.9 3.4 %shard_map.60.refs_0_ = f32[384,1536]{1,0:T(8,128)S(1)} custom-call(bf16[16,2,64,384]{3,2,1,0:T(8,128)(2,1)S(1)} %bitcast.3, bf16[16,64,1536]{2,1,0:T(8,128)(2,1)} %get-tuple-element.45.grad_ref), custom_call_target="tpu_custom_call" | custom-call | flops 48318382080 | bytes 7077888 | tf_op jit(solution)/shard_map/pallas_call | solution.py:73
  94.3 2.9 %shard_map.61 = f32[384,1536]{1,0:T(8,128)} custom-call(bf16[16,2,64,384]{3,2,1,0:T(8,128)(2,1)S(1)} %bitcast.4, bf16[16,64,1536]{2,1,0:T(8,128)(2,1)S(1)} %collective-permute-done.6.grad_ref, f32[384,1536]{1,0:T(8,128)S(1)} %shard_map.60.refs_0_), custom_call_target="tpu_custom_call" | custom-call | flops 1207959552 | bytes 9437184 | tf_op jit(solution)/shard_map/pallas_call | solution.py:73
  97.2 2.7 %collective-permute-done.5.moved_ref = bf16[2,2,64,768]{3,2,1,0:T(8,128)(2,1)S(1)} collective-permute-done((bf16[2,2,64,768]{3,2,1,0:T(8,128)(2,1)}, bf16[2,2,64,768]{3,2,1,0:T(8,128)(2,1)S(1)}, u32[]{:S(2)}, u32[]{:S(2)}) %collective-permute-start.5) | collective-permute-done | bytes 393248 | tf_op jit(solution)/shard_map/ppermute | solution.py:59
  101.1 4.5 %collective-permute-start.7 = (bf16[2,64,384]{2,1,0:T(8,128)(2,1)S(1)}, bf16[2,64,384]{2,1,0:T(8,128)(2,1)S(1)}, u32[]{:S(2)}, u32[]{:S(2)}) collective-permute-start(bf16[2,64,384]{2,1,0:T(8,128)(2,1)S(1)} %get-tuple-element.49), channel_id=1, source_target_pairs={{0,16},{1,49},{2,18},{3,51},{4,20},{5,53},{6,22},{7,55},{8,24},{9,... | collective-permute-start | bytes 294920 | tf_op jit(solution)/shard_map/ppermute | solution.py:59
  105.6 1.9 %collective-permute-start.8 = (bf16[2,64,384]{2,1,0:T(8,128)(2,1)S(1)}, bf16[2,64,384]{2,1,0:T(8,128)(2,1)S(1)}, u32[]{:S(2)}, u32[]{:S(2)}) collective-permute-start(bf16[2,64,384]{2,1,0:T(8,128)(2,1)S(1)} %get-tuple-element.50), channel_id=1, source_target_pairs={{0,17},{1,48},{2,19},{3,50},{4,21},{5,52},{6,23},{7,54},{8,25},{9,... | collective-permute-start | bytes 294920 | tf_op jit(solution)/shard_map/ppermute | solution.py:59
  107.6 5.3 %collective-permute-start.9 = (bf16[2,64,384]{2,1,0:T(8,128)(2,1)S(1)}, bf16[2,64,384]{2,1,0:T(8,128)(2,1)S(1)}, u32[]{:S(2)}, u32[]{:S(2)}) collective-permute-start(bf16[2,64,384]{2,1,0:T(8,128)(2,1)S(1)} %get-tuple-element.52), channel_id=1, source_target_pairs={{0,1},{1,0},{2,3},{3,2},{4,5},{5,4},{6,7},{7,6},{8,9},{9,8},{10,11... | collective-permute-start | bytes 294920 | tf_op jit(solution)/shard_map/ppermute | solution.py:50
  114.2 3.8 %collective-permute-done.8.cross_ref = bf16[2,64,384]{2,1,0:T(8,128)(2,1)S(1)} collective-permute-done((bf16[2,64,384]{2,1,0:T(8,128)(2,1)S(1)}, bf16[2,64,384]{2,1,0:T(8,128)(2,1)S(1)}, u32[]{:S(2)}, u32[]{:S(2)}) %collective-permute-start.8) | collective-permute-done | bytes 98336 | tf_op jit(solution)/shard_map/ppermute | solution.py:59
  (21 shorter events, 11.1 us)
Async XLA Ops:
  7.2 82.3 %all-gather.2.cloned.1.call-start = ((), (), s32[]{:S(2)}) async-start(), calls=%async_computation.2 | async-start | bytes 1671168 | tf_op jit(solution)/shard_map/all_gather | solution.py:231
  27.5 4.8 %copy-start.1 = (bf16[384,1536]{1,0:T(8,128)(2,1)S(1)}, bf16[384,1536]{1,0:T(8,128)(2,1)}, u32[]{:S(2)}) copy-start(bf16[384,1536]{1,0:T(8,128)(2,1)} %get-tuple-element.15) | copy-start | bytes 3538948 | tf_op jit(solution)/shard_map/cond/branch_1_fun/cond
  27.5 26.7 %all-to-all-start.1 = ((bf16[4,256,1536]{2,1,0:T(8,128)(2,1)}), bf16[4,256,1536]{2,1,0:T(8,128)(2,1)}, u32[]{:S(2)}, u32[]{:S(2)}) async-start(bf16[4,256,1536]{2,1,0:T(8,128)(2,1)} %broadcast_in_dim.2), calls=%async_computation.1 | async-start | bytes 6291456 | tf_op jit(solution)/shard_map/cond/branch_1_fun/cond/branch_1_fun/all_to_all | solution.py:45
  32.3 4.9 %collective-permute-start = (bf16[384,1536]{1,0:T(8,128)(2,1)S(1)}, bf16[384,1536]{1,0:T(8,128)(2,1)}, u32[]{:S(2)}, u32[]{:S(2)}) collective-permute-start(bf16[384,1536]{1,0:T(8,128)(2,1)S(1)} %copy-done.1), channel_id=1, source_target_pairs={{0,1},{1,0},{2,3},{3,2},{4,5},{5,4},{6,7},{7,6},{8,9},{9,8},{10,11... | collective-permute-start | bytes 3538952 | tf_op jit(solution)/shard_map/cond/branch_1_fun/cond/branch_1_fun/ppermute | solution.py:50
  54.2 15.8 %copy-start.2 = (bf16[384,1536]{1,0:T(8,128)(2,1)S(1)}, bf16[384,1536]{1,0:T(8,128)(2,1)}, u32[]{:S(2)}) copy-start(bf16[384,1536]{1,0:T(8,128)(2,1)} %get-tuple-element.17.own_ref) | copy-start | bytes 3538948 | tf_op jit(solution)/shard_map/cond/branch_1_fun/cond
  58.9 11.1 %collective-permute-start.3 = (bf16[1,64,768]{2,1,0:T(8,128)(2,1)S(1)}, bf16[1,64,768]{2,1,0:T(8,128)(2,1)S(1)}, u32[]{:S(2)}, u32[]{:S(2)}) collective-permute-start(bf16[1,64,768]{2,1,0:T(8,128)(2,1)S(1)} %get-tuple-element.23), channel_id=1, source_target_pairs={{0,8},{1,57},{2,10},{3,59},{4,12},{5,61},{6,14},{7,63},{8,16},{9,1... | collective-permute-start | bytes 294920 | tf_op jit(solution)/shard_map/cond/branch_1_fun/cond/branch_1_fun/ppermute | solution.py:59
  60.9 21.9 %collective-permute-start.1 = (bf16[4,64,768]{2,1,0:T(8,128)(2,1)S(1)}, bf16[4,64,768]{2,1,0:T(8,128)(2,1)S(1)}, u32[]{:S(2)}, u32[]{:S(2)}) collective-permute-start(bf16[4,64,768]{2,1,0:T(8,128)(2,1)S(1)} %get-tuple-element.19), channel_id=1, source_target_pairs={{0,4},{1,61},{2,6},{3,63},{4,8},{5,1},{6,10},{7,3},{8,12},{9,5},{1... | collective-permute-start | bytes 1179656 | tf_op jit(solution)/shard_map/cond/branch_1_fun/cond/branch_1_fun/ppermute | solution.py:59
  64.2 18.5 %collective-permute-start.2 = (bf16[4,64,768]{2,1,0:T(8,128)(2,1)S(1)}, bf16[4,64,768]{2,1,0:T(8,128)(2,1)S(1)}, u32[]{:S(2)}, u32[]{:S(2)}) collective-permute-start(bf16[4,64,768]{2,1,0:T(8,128)(2,1)S(1)} %get-tuple-element.20), channel_id=1, source_target_pairs={{0,61},{1,4},{2,63},{3,6},{4,1},{5,8},{6,3},{7,10},{8,5},{9,12},{1... | collective-permute-start | bytes 1179656 | tf_op jit(solution)/shard_map/cond/branch_1_fun/cond/branch_1_fun/ppermute | solution.py:59
  73.8 8.9 %collective-permute-start.4 = (bf16[3,64,768]{2,1,0:T(8,128)(2,1)S(1)}, bf16[3,64,768]{2,1,0:T(8,128)(2,1)S(1)}, u32[]{:S(2)}, u32[]{:S(2)}) collective-permute-start(bf16[3,64,768]{2,1,0:T(8,128)(2,1)S(1)} %get-tuple-element.25), channel_id=1, source_target_pairs={{0,1},{1,0},{2,3},{3,2},{4,5},{5,4},{6,7},{7,6},{8,9},{9,8},{10,11... | collective-permute-start | bytes 884744 | tf_op jit(solution)/shard_map/cond/branch_1_fun/cond/branch_1_fun/ppermute | solution.py:50
  83.9 16.0 %collective-permute-start.5 = (bf16[2,2,64,768]{3,2,1,0:T(8,128)(2,1)}, bf16[2,2,64,768]{3,2,1,0:T(8,128)(2,1)S(1)}, u32[]{:S(2)}, u32[]{:S(2)}) collective-permute-start(bf16[2,2,64,768]{3,2,1,0:T(8,128)(2,1)} %get-tuple-element.44), channel_id=1, source_target_pairs={{0,8},{1,57},{2,10},{3,59},{4,12},{5,61},{6,14},{7,63},{8,16},{9,1... | collective-permute-start | bytes 1179656 | tf_op jit(solution)/shard_map/ppermute | solution.py:59
  85.8 8.5 %collective-permute-start.6 = (bf16[16,64,1536]{2,1,0:T(8,128)(2,1)}, bf16[16,64,1536]{2,1,0:T(8,128)(2,1)S(1)}, u32[]{:S(2)}, u32[]{:S(2)}) collective-permute-start(bf16[16,64,1536]{2,1,0:T(8,128)(2,1)} %get-tuple-element.45.grad_ref), channel_id=1, source_target_pairs={{0,1},{1,0},{2,3},{3,2},{4,5},{5,4},{6,7},{7,6},{8,9},{9,8},{10,11... | collective-permute-start | bytes 9437192 | tf_op jit(solution)/shard_map/ppermute | solution.py:50
  89.5 1.4 %copy-start = (bf16[2048,384]{1,0:T(8,128)(2,1)S(1)}, bf16[2048,384]{1,0:T(8,128)(2,1)}, u32[]{:S(2)}) copy-start(bf16[2048,384]{1,0:T(8,128)(2,1)} %all-gather.2.cloned.1.call-done) | copy-start | bytes 4718596
  101.1 13.1 %collective-permute-start.7 = (bf16[2,64,384]{2,1,0:T(8,128)(2,1)S(1)}, bf16[2,64,384]{2,1,0:T(8,128)(2,1)S(1)}, u32[]{:S(2)}, u32[]{:S(2)}) collective-permute-start(bf16[2,64,384]{2,1,0:T(8,128)(2,1)S(1)} %get-tuple-element.49), channel_id=1, source_target_pairs={{0,16},{1,49},{2,18},{3,51},{4,20},{5,53},{6,22},{7,55},{8,24},{9,... | collective-permute-start | bytes 294920 | tf_op jit(solution)/shard_map/ppermute | solution.py:59
  105.6 12.3 %collective-permute-start.8 = (bf16[2,64,384]{2,1,0:T(8,128)(2,1)S(1)}, bf16[2,64,384]{2,1,0:T(8,128)(2,1)S(1)}, u32[]{:S(2)}, u32[]{:S(2)}) collective-permute-start(bf16[2,64,384]{2,1,0:T(8,128)(2,1)S(1)} %get-tuple-element.50), channel_id=1, source_target_pairs={{0,17},{1,48},{2,19},{3,50},{4,21},{5,52},{6,23},{7,54},{8,25},{9,... | collective-permute-start | bytes 294920 | tf_op jit(solution)/shard_map/ppermute | solution.py:59
  107.6 10.4 %collective-permute-start.9 = (bf16[2,64,384]{2,1,0:T(8,128)(2,1)S(1)}, bf16[2,64,384]{2,1,0:T(8,128)(2,1)S(1)}, u32[]{:S(2)}, u32[]{:S(2)}) collective-permute-start(bf16[2,64,384]{2,1,0:T(8,128)(2,1)S(1)} %get-tuple-element.52), channel_id=1, source_target_pairs={{0,1},{1,0},{2,3},{3,2},{4,5},{5,4},{6,7},{7,6},{8,9},{9,8},{10,11... | collective-permute-start | bytes 294920 | tf_op jit(solution)/shard_map/ppermute | solution.py:50
Sparse Core Ops, SparseCore 0:
  10.1 79.3 all-gather.1

commit v10 on v9

--- a/solution.py
+++ b/solution.py
@@ -31,7 +31,8 @@
 along_y = [[[index(x, y, core) for y in y_order] for x in range(4)] for core in range(2)]
 
 
-early_groups = (((8,), False), ((7, 5, 3, 1), False), ((-7, -5, -3, -1), True))
+first_groups = (((8,), False), ((7, 5, 3, 1), False))
+early_groups = (((-7, -5, -3, -1), True),)
 late_groups = (((6, 4, 2, 0), False), ((-6, -4, -2), True))
 
 
@@ -162,13 +163,22 @@
     )
 
 
-def first_round(grad_blocks, weight, weight_other):
+def gather_and_round(gelu_grad, weight):
+    line = gather(gelu_grad, along_x[0] + along_y[1])
+    weight_other = swap_cores(weight)
+    grad_tokens = gather(line, along_y[0] + along_x[1])
+    grad_blocks = grad_tokens.reshape((16,) + gelu_grad.shape)
+
     weights = weight, weight_other
-    far, ahead, behind = partials(early_groups, (5, 4), grad_blocks, weights)
-    far, later_blocks = lax.optimization_barrier((far, grad_blocks))
-    far = send(far, 2)
-    own, cross = send(ahead, 1), send(behind, -1, cross=True)
+    far, ahead = partials(first_groups, (5,), grad_blocks, weights)
+    far, next_blocks = lax.optimization_barrier((far, grad_blocks))
+    far, own = send(far, 2), send(ahead, 1)
+    behind = partials(early_groups, (4,), next_blocks, weights)[0]
+    behind, later_blocks = lax.optimization_barrier((behind, next_blocks))
+    cross = send(behind, -1, cross=True)
     rest, for_sibling = partials(late_groups, (7,), later_blocks, weights, far)
+    rest, last_blocks = lax.optimization_barrier((rest, later_blocks))
+    kept = jnp.where(lax.axis_index("col") < 16, last_blocks, jnp.zeros_like(last_blocks))
     rest_other = swap_cores(for_sibling)
 
     both = (2,) + rest.shape[1:]
@@ -177,18 +187,7 @@
         jax.ShapeDtypeStruct(both, jnp.float32),
         jax.ShapeDtypeStruct(both, jnp.float32),
     ]
-    return call(first_kernel, outs, (own, cross, rest, rest_other))
-
-
-def gather_plane(gelu_grad, weight):
-    line = gather(gelu_grad, along_x[0] + along_y[1])
-    grad_tokens = gather(line, along_y[0] + along_x[1])
-    return grad_tokens.reshape((16,) + gelu_grad.shape), swap_cores(weight)
-
-
-def gather_and_round(gelu_grad, weight):
-    grad_blocks, weight_other = taken(gather_plane, gelu_grad, weight)
-    return (*taken(first_round, grad_blocks, weight, weight_other), grad_blocks)
+    return (*call(first_kernel, outs, (own, cross, rest, rest_other)), kept)
 
 
 def weight_kernel(sibling, input_ref, grad_ref, *refs):

time: 126 us -> 127 us (level)
  the two profiles are of different devices: /device:TPU:2 before, /device:TPU:1 now
where the time goes in v10:
time: 127 us
  starting transfers between devices  54.1 us (43%)
  waiting for transfers between devices  22.7 us (18%)
  Pallas kernels  16.2 us (13%)
  between operations  14.1 us (11%)
  blocking collectives  12.9 us (10%)
  local copies, waits for them, and re-layouts  3.35 us (3%)
  other arithmetic  3.14 us (2%)
    ppermute x6, starting transfers between devices, send(): return lax.ppermute(values, ring, pairs)  29.9 us
    ppermute x4, starting transfers between devices, swap_cores(): return lax.ppermute(values, 'rep', [(0, 1), (1, 0), (2, 3), (3, 2)])  20 us
    pallas_call x8, Pallas kernels, call(): pl.pallas_call(kernel, out_shape=outs, in_specs=[vmem] * len(args), out_s...  16.2 us
    all_to_all x1, blocking collectives, gather(): parts = lax.all_to_all(copies, plane, 0, 0, axis_index_groups=groups)  12.9 us
    all_to_all x1, waiting for transfers between devices, gather(): parts = lax.all_to_all(copies, plane, 0, 0, axis_index_groups=groups)  10.8 us
    ppermute x6, waiting for transfers between devices, send(): return lax.ppermute(values, ring, pairs)  7.46 us
    all_to_all x1, starting transfers between devices, gather(): parts = lax.all_to_all(copies, plane, 0, 0, axis_index_groups=groups)  4.15 us
    ppermute x4, waiting for transfers between devices, swap_cores(): return lax.ppermute(values, 'rep', [(0, 1), (1, 0), (2, 3), (3, 2)])  3.77 us
  transfers between devices with their start and end apart: 12, of which 7 were waited for; matrix products, arithmetic and copies ran while one was open for 4% of the time, Pallas kernels for 12%

profile of v10, /device:TPU:1, one launch (start us, length us, event | category | flops | bytes accessed | tf_op | source)
XLA Modules:
  0.0 126.5 jit_solution(14200703975297588930)
XLA Ops:
  9.2 79.5 %conditional.1 = (bf16[2,2,64,768]{3,2,1,0:T(8,128)(2,1)}, f32[2,64,768]{2,1,0:T(8,128)}, f32[2,64,768]{2,1,0:T(8,128)}, bf16[16,64,1536]{2,1,0:T(8,128)(2,1)}) conditional(s32[]{:T(128)} %convert_element_type.12, () %tuple.20, (bf16[64,1536]{1,0:T(8,128)(2,1)S(1)}, bf16[384,1536]{1,0:T(8,128)(2,1)}) %tuple.21), branch_computations={%region_0.0_spmd, %region_1.2_spmd} | conditional | flops 7249330176 | bytes 57213260 | solution.py:158
  9.3 12.9 %all_to_all.8 = bf16[4,64,1536]{2,1,0:T(8,128)(2,1)S(1)} all-to-all(bf16[4,64,1536]{2,1,0:T(8,128)(2,1)S(1)} %broadcast_in_dim.0), channel_id=1, replica_groups={{0,128,256,384},{2,130,258,386},{64,192,320,448},{66,194,322,450},{1,3,..., dimensions={0} | all-to-all | bytes 1572864 | tf_op jit(solution)/shard_map/cond/branch_1_fun/all_to_all | solution.py:46
  22.1 1.9 %broadcast_in_dim.2 = bf16[4,256,1536]{2,1,0:T(8,128)(2,1)} broadcast(bf16[256,1536]{1,0:T(8,128)(2,1)S(1)} %bitcast.9), dimensions={1,2} | broadcast | bytes 3932160 | tf_op jit(solution)/shard_map/cond/branch_1_fun/broadcast_in_dim | solution.py:45
  24.0 4.2 %all-to-all-start.1 = ((bf16[4,256,1536]{2,1,0:T(8,128)(2,1)}), bf16[4,256,1536]{2,1,0:T(8,128)(2,1)S(1)}, u32[]{:S(2)}, u32[]{:S(2)}) async-start(bf16[4,256,1536]{2,1,0:T(8,128)(2,1)} %broadcast_in_dim.2), calls=%async_computation.1 | async-start | bytes 6291456 | tf_op jit(solution)/shard_map/cond/branch_1_fun/all_to_all | solution.py:46
  28.2 7.4 %collective-permute-start = (bf16[384,1536]{1,0:T(8,128)(2,1)}, bf16[384,1536]{1,0:T(8,128)(2,1)}, u32[]{:S(2)}, u32[]{:S(2)}) collective-permute-start(bf16[384,1536]{1,0:T(8,128)(2,1)} %get-tuple-element.42.own_ref), channel_id=1, source_target_pairs={{0,1},{1,0},{2,3},{3,2},{4,5},{5,4},{6,7},{7,6},{8,9},{9,8},{10,11... | collective-permute-start | bytes 3538952 | tf_op jit(solution)/shard_map/cond/branch_1_fun/ppermute | solution.py:51
  35.6 2.8 %collective-permute-done.other_ref = bf16[384,1536]{1,0:T(8,128)(2,1)} collective-permute-done((bf16[384,1536]{1,0:T(8,128)(2,1)}, bf16[384,1536]{1,0:T(8,128)(2,1)}, u32[]{:S(2)}, u32[]{:S(2)}) %collective-permute-start) | collective-permute-done | bytes 1179680 | tf_op jit(solution)/shard_map/cond/branch_1_fun/ppermute | solution.py:51
  38.3 10.8 %all-to-all-done.1 = bf16[4,256,1536]{2,1,0:T(8,128)(2,1)S(1)} async-done(((bf16[4,256,1536]{2,1,0:T(8,128)(2,1)}), bf16[4,256,1536]{2,1,0:T(8,128)(2,1)S(1)}, u32[]{:S(2)}, u32[]{:S(2)}) %all-to-all-start.1) | async-done | bytes 3145760 | tf_op jit(solution)/shard_map/cond/branch_1_fun/all_to_all | solution.py:46
  49.1 2.9 %branch_1_fun.4 = (bf16[1,64,768]{2,1,0:T(8,128)(2,1)S(1)}, bf16[4,64,768]{2,1,0:T(8,128)(2,1)S(1)}) custom-call(bf16[16,64,1536]{2,1,0:T(8,128)(2,1)S(1)} %bitcast.3, bf16[384,1536]{1,0:T(8,128)(2,1)} %get-tuple-element.42.own_ref, bf16[384,1536]{1,0:T(8,128)(2,1)} %collective-permute-done.other_ref), custom_call_target="tpu_custom_call" | custom-call | flops 2264924160 | bytes 5996544 | tf_op jit(solution)/shard_map/cond/branch_1_fun/pallas_call | solution.py:74
  52.1 11.0 %collective-permute-start.1 = (bf16[4,64,768]{2,1,0:T(8,128)(2,1)S(1)}, bf16[4,64,768]{2,1,0:T(8,128)(2,1)S(1)}, u32[]{:S(2)}, u32[]{:S(2)}) collective-permute-start(bf16[4,64,768]{2,1,0:T(8,128)(2,1)S(1)} %get-tuple-element.6), channel_id=1, source_target_pairs={{0,4},{1,61},{2,6},{3,63},{4,8},{5,1},{6,10},{7,3},{8,12},{9,5},{1... | collective-permute-start | bytes 1179656 | tf_op jit(solution)/shard_map/cond/branch_1_fun/ppermute | solution.py:60
  63.0 3.1 %collective-permute-start.3 = (bf16[1,64,768]{2,1,0:T(8,128)(2,1)S(1)}, bf16[1,64,768]{2,1,0:T(8,128)(2,1)S(1)}, u32[]{:S(2)}, u32[]{:S(2)}) collective-permute-start(bf16[1,64,768]{2,1,0:T(8,128)(2,1)S(1)} %get-tuple-element.11), channel_id=1, source_target_pairs={{0,8},{1,57},{2,10},{3,59},{4,12},{5,61},{6,14},{7,63},{8,16},{9,1... | collective-permute-start | bytes 294920 | tf_op jit(solution)/shard_map/cond/branch_1_fun/ppermute | solution.py:60
  66.1 2.3 %branch_1_fun.5 = bf16[4,64,768]{2,1,0:T(8,128)(2,1)S(1)} custom-call(bf16[16,64,1536]{2,1,0:T(8,128)(2,1)S(1)} %bitcast.4, bf16[384,1536]{1,0:T(8,128)(2,1)S(1)} %copy-done.3, bf16[384,1536]{1,0:T(8,128)(2,1)} %collective-permute-done.other_ref), custom_call_target="tpu_custom_call" | custom-call | flops 1811939328 | bytes 5898240 | tf_op jit(solution)/shard_map/cond/branch_1_fun/pallas_call | solution.py:74
  68.4 3.0 %collective-permute-start.2 = (bf16[4,64,768]{2,1,0:T(8,128)(2,1)S(1)}, bf16[4,64,768]{2,1,0:T(8,128)(2,1)S(1)}, u32[]{:S(2)}, u32[]{:S(2)}) collective-permute-start(bf16[4,64,768]{2,1,0:T(8,128)(2,1)S(1)} %branch_1_fun.5), channel_id=1, source_target_pairs={{0,61},{1,4},{2,63},{3,6},{4,1},{5,8},{6,3},{7,10},{8,5},{9,12},{1... | collective-permute-start | bytes 1179656 | tf_op jit(solution)/shard_map/cond/branch_1_fun/ppermute | solution.py:60
  71.4 2.7 %collective-permute-done.3.refs_0_ = bf16[1,64,768]{2,1,0:T(8,128)(2,1)S(1)} collective-permute-done((bf16[1,64,768]{2,1,0:T(8,128)(2,1)S(1)}, bf16[1,64,768]{2,1,0:T(8,128)(2,1)S(1)}, u32[]{:S(2)}, u32[]{:S(2)}) %collective-permute-start.3) | collective-permute-done | bytes 98336 | tf_op jit(solution)/shard_map/cond/branch_1_fun/ppermute | solution.py:60
  74.1 2.9 %branch_1_fun.6 = (bf16[4,64,768]{2,1,0:T(8,128)(2,1)S(1)}, bf16[3,64,768]{2,1,0:T(8,128)(2,1)S(1)}) custom-call(bf16[16,64,1536]{2,1,0:T(8,128)(2,1)S(1)} %bitcast.5, bf16[384,1536]{1,0:T(8,128)(2,1)S(1)} %copy-done.3, bf16[384,1536]{1,0:T(8,128)(2,1)} %collective-permute-done.other_ref, bf16[1,64,768]{2,1,0:T(8,128)(2,1)S(1)} %collective-permute-done.3.refs_0_), custom_call_target="tpu_custom_call" | custom-call | flops 3170893824 | bytes 6291456 | tf_op jit(solution)/shard_map/cond/branch_1_fun/pallas_call | solution.py:74
  77.0 8.8 %collective-permute-start.4 = (bf16[3,64,768]{2,1,0:T(8,128)(2,1)S(1)}, bf16[3,64,768]{2,1,0:T(8,128)(2,1)S(1)}, u32[]{:S(2)}, u32[]{:S(2)}) collective-permute-start(bf16[3,64,768]{2,1,0:T(8,128)(2,1)S(1)} %get-tuple-element.14), channel_id=1, source_target_pairs={{0,1},{1,0},{2,3},{3,2},{4,5},{5,4},{6,7},{7,6},{8,9},{9,8},{10,11... | collective-permute-start | bytes 884744 | tf_op jit(solution)/shard_map/cond/branch_1_fun/ppermute | solution.py:51
  85.8 1.8 %broadcast_select_fusion = bf16[16,64,1536]{2,1,0:T(8,128)(2,1)} fusion(bf16[16,64,1536]{2,1,0:T(8,128)(2,1)S(1)} %bitcast.6, pred[]{:T(512)S(6)} %lt.4), kind=kLoop, calls=%fused_computation | loop fusion | flops 1572864 | bytes 6291457 | tf_op jit(solution)/shard_map/cond/branch_1_fun/jit(_where)/select_n | solution.py:181
  88.7 1.9 %collective-permute-start.5 = (bf16[2,2,64,768]{3,2,1,0:T(8,128)(2,1)}, bf16[2,2,64,768]{3,2,1,0:T(8,128)(2,1)S(1)}, u32[]{:S(2)}, u32[]{:S(2)}) collective-permute-start(bf16[2,2,64,768]{3,2,1,0:T(8,128)(2,1)} %get-tuple-element.31), channel_id=1, source_target_pairs={{0,8},{1,57},{2,10},{3,59},{4,12},{5,61},{6,14},{7,63},{8,16},{9,1... | collective-permute-start | bytes 1179656 | tf_op jit(solution)/shard_map/ppermute | solution.py:60
  90.7 1.9 %collective-permute-start.6 = (bf16[16,64,1536]{2,1,0:T(8,128)(2,1)}, bf16[16,64,1536]{2,1,0:T(8,128)(2,1)S(1)}, u32[]{:S(2)}, u32[]{:S(2)}) collective-permute-start(bf16[16,64,1536]{2,1,0:T(8,128)(2,1)} %get-tuple-element.32.grad_ref), channel_id=1, source_target_pairs={{0,1},{1,0},{2,3},{3,2},{4,5},{5,4},{6,7},{7,6},{8,9},{9,8},{10,11... | collective-permute-start | bytes 9437192 | tf_op jit(solution)/shard_map/ppermute | solution.py:51
  94.0 3.4 %shard_map.60.refs_0_ = f32[384,1536]{1,0:T(8,128)S(1)} custom-call(bf16[16,2,64,384]{3,2,1,0:T(8,128)(2,1)S(1)} %bitcast.7, bf16[16,64,1536]{2,1,0:T(8,128)(2,1)} %get-tuple-element.32.grad_ref), custom_call_target="tpu_custom_call" | custom-call | flops 48318382080 | bytes 7077888 | tf_op jit(solution)/shard_map/pallas_call | solution.py:74
  98.4 2.9 %shard_map.61 = f32[384,1536]{1,0:T(8,128)} custom-call(bf16[16,2,64,384]{3,2,1,0:T(8,128)(2,1)S(1)} %bitcast.8, bf16[16,64,1536]{2,1,0:T(8,128)(2,1)S(1)} %collective-permute-done.6.grad_ref, f32[384,1536]{1,0:T(8,128)S(1)} %shard_map.60.refs_0_), custom_call_target="tpu_custom_call" | custom-call | flops 1207959552 | bytes 9437184 | tf_op jit(solution)/shard_map/pallas_call | solution.py:74
  102.9 3.3 %collective-permute-start.7 = (bf16[2,64,384]{2,1,0:T(8,128)(2,1)S(1)}, bf16[2,64,384]{2,1,0:T(8,128)(2,1)S(1)}, u32[]{:S(2)}, u32[]{:S(2)}) collective-permute-start(bf16[2,64,384]{2,1,0:T(8,128)(2,1)S(1)} %get-tuple-element.36), channel_id=1, source_target_pairs={{0,16},{1,49},{2,18},{3,51},{4,20},{5,53},{6,22},{7,55},{8,24},{9,... | collective-permute-start | bytes 294920 | tf_op jit(solution)/shard_map/ppermute | solution.py:60
  106.2 7.7 %collective-permute-start.8 = (bf16[2,64,384]{2,1,0:T(8,128)(2,1)S(1)}, bf16[2,64,384]{2,1,0:T(8,128)(2,1)S(1)}, u32[]{:S(2)}, u32[]{:S(2)}) collective-permute-start(bf16[2,64,384]{2,1,0:T(8,128)(2,1)S(1)} %get-tuple-element.37), channel_id=1, source_target_pairs={{0,17},{1,48},{2,19},{3,50},{4,21},{5,52},{6,23},{7,54},{8,25},{9,... | collective-permute-start | bytes 294920 | tf_op jit(solution)/shard_map/ppermute | solution.py:60
  113.9 1.9 %collective-permute-start.9 = (bf16[2,64,384]{2,1,0:T(8,128)(2,1)S(1)}, bf16[2,64,384]{2,1,0:T(8,128)(2,1)S(1)}, u32[]{:S(2)}, u32[]{:S(2)}) collective-permute-start(bf16[2,64,384]{2,1,0:T(8,128)(2,1)S(1)} %get-tuple-element.39), channel_id=1, source_target_pairs={{0,1},{1,0},{2,3},{3,2},{4,5},{5,4},{6,7},{7,6},{8,9},{9,8},{10,11... | collective-permute-start | bytes 294920 | tf_op jit(solution)/shard_map/ppermute | solution.py:51
  115.8 1.8 %collective-permute-done.7.own_ref = bf16[2,64,384]{2,1,0:T(8,128)(2,1)S(1)} collective-permute-done((bf16[2,64,384]{2,1,0:T(8,128)(2,1)S(1)}, bf16[2,64,384]{2,1,0:T(8,128)(2,1)S(1)}, u32[]{:S(2)}, u32[]{:S(2)}) %collective-permute-start.7) | collective-permute-done | bytes 98336 | tf_op jit(solution)/shard_map/ppermute | solution.py:60
  (23 shorter events, 9.2 us)
Async XLA Ops:
  7.2 85.4 %all-gather.2.cloned.1.call-start = ((), (), s32[]{:S(2)}) async-start(), calls=%async_computation.2 | async-start | bytes 1671168 | tf_op jit(solution)/shard_map/all_gather | solution.py:230
  24.0 25.1 %all-to-all-start.1 = ((bf16[4,256,1536]{2,1,0:T(8,128)(2,1)}), bf16[4,256,1536]{2,1,0:T(8,128)(2,1)S(1)}, u32[]{:S(2)}, u32[]{:S(2)}) async-start(bf16[4,256,1536]{2,1,0:T(8,128)(2,1)} %broadcast_in_dim.2), calls=%async_computation.1 | async-start | bytes 6291456 | tf_op jit(solution)/shard_map/cond/branch_1_fun/all_to_all | solution.py:46
  28.2 10.2 %collective-permute-start = (bf16[384,1536]{1,0:T(8,128)(2,1)}, bf16[384,1536]{1,0:T(8,128)(2,1)}, u32[]{:S(2)}, u32[]{:S(2)}) collective-permute-start(bf16[384,1536]{1,0:T(8,128)(2,1)} %get-tuple-element.42.own_ref), channel_id=1, source_target_pairs={{0,1},{1,0},{2,3},{3,2},{4,5},{5,4},{6,7},{7,6},{8,9},{9,8},{10,11... | collective-permute-start | bytes 3538952 | tf_op jit(solution)/shard_map/cond/branch_1_fun/ppermute | solution.py:51
  49.1 17.0 %copy-start.3 = (bf16[384,1536]{1,0:T(8,128)(2,1)S(1)}, bf16[384,1536]{1,0:T(8,128)(2,1)}, u32[]{:S(2)}) copy-start(bf16[384,1536]{1,0:T(8,128)(2,1)} %get-tuple-element.42.own_ref) | copy-start | bytes 3538948 | tf_op jit(solution)/shard_map/cond
  52.1 35.6 %collective-permute-start.1 = (bf16[4,64,768]{2,1,0:T(8,128)(2,1)S(1)}, bf16[4,64,768]{2,1,0:T(8,128)(2,1)S(1)}, u32[]{:S(2)}, u32[]{:S(2)}) collective-permute-start(bf16[4,64,768]{2,1,0:T(8,128)(2,1)S(1)} %get-tuple-element.6), channel_id=1, source_target_pairs={{0,4},{1,61},{2,6},{3,63},{4,8},{5,1},{6,10},{7,3},{8,12},{9,5},{1... | collective-permute-start | bytes 1179656 | tf_op jit(solution)/shard_map/cond/branch_1_fun/ppermute | solution.py:60
  63.0 11.1 %collective-permute-start.3 = (bf16[1,64,768]{2,1,0:T(8,128)(2,1)S(1)}, bf16[1,64,768]{2,1,0:T(8,128)(2,1)S(1)}, u32[]{:S(2)}, u32[]{:S(2)}) collective-permute-start(bf16[1,64,768]{2,1,0:T(8,128)(2,1)S(1)} %get-tuple-element.11), channel_id=1, source_target_pairs={{0,8},{1,57},{2,10},{3,59},{4,12},{5,61},{6,14},{7,63},{8,16},{9,1... | collective-permute-start | bytes 294920 | tf_op jit(solution)/shard_map/cond/branch_1_fun/ppermute | solution.py:60
  68.4 19.2 %collective-permute-start.2 = (bf16[4,64,768]{2,1,0:T(8,128)(2,1)S(1)}, bf16[4,64,768]{2,1,0:T(8,128)(2,1)S(1)}, u32[]{:S(2)}, u32[]{:S(2)}) collective-permute-start(bf16[4,64,768]{2,1,0:T(8,128)(2,1)S(1)} %branch_1_fun.5), channel_id=1, source_target_pairs={{0,61},{1,4},{2,63},{3,6},{4,1},{5,8},{6,3},{7,10},{8,5},{9,12},{1... | collective-permute-start | bytes 1179656 | tf_op jit(solution)/shard_map/cond/branch_1_fun/ppermute | solution.py:60
  77.0 10.6 %collective-permute-start.4 = (bf16[3,64,768]{2,1,0:T(8,128)(2,1)S(1)}, bf16[3,64,768]{2,1,0:T(8,128)(2,1)S(1)}, u32[]{:S(2)}, u32[]{:S(2)}) collective-permute-start(bf16[3,64,768]{2,1,0:T(8,128)(2,1)S(1)} %get-tuple-element.14), channel_id=1, source_target_pairs={{0,1},{1,0},{2,3},{3,2},{4,5},{5,4},{6,7},{7,6},{8,9},{9,8},{10,11... | collective-permute-start | bytes 884744 | tf_op jit(solution)/shard_map/cond/branch_1_fun/ppermute | solution.py:51
  88.7 14.1 %collective-permute-start.5 = (bf16[2,2,64,768]{3,2,1,0:T(8,128)(2,1)}, bf16[2,2,64,768]{3,2,1,0:T(8,128)(2,1)S(1)}, u32[]{:S(2)}, u32[]{:S(2)}) collective-permute-start(bf16[2,2,64,768]{3,2,1,0:T(8,128)(2,1)} %get-tuple-element.31), channel_id=1, source_target_pairs={{0,8},{1,57},{2,10},{3,59},{4,12},{5,61},{6,14},{7,63},{8,16},{9,1... | collective-permute-start | bytes 1179656 | tf_op jit(solution)/shard_map/ppermute | solution.py:60
  90.7 7.8 %collective-permute-start.6 = (bf16[16,64,1536]{2,1,0:T(8,128)(2,1)}, bf16[16,64,1536]{2,1,0:T(8,128)(2,1)S(1)}, u32[]{:S(2)}, u32[]{:S(2)}) collective-permute-start(bf16[16,64,1536]{2,1,0:T(8,128)(2,1)} %get-tuple-element.32.grad_ref), channel_id=1, source_target_pairs={{0,1},{1,0},{2,3},{3,2},{4,5},{5,4},{6,7},{7,6},{8,9},{9,8},{10,11... | collective-permute-start | bytes 9437192 | tf_op jit(solution)/shard_map/ppermute | solution.py:51
  92.6 1.4 %copy-start = (bf16[2048,384]{1,0:T(8,128)(2,1)S(1)}, bf16[2048,384]{1,0:T(8,128)(2,1)}, u32[]{:S(2)}) copy-start(bf16[2048,384]{1,0:T(8,128)(2,1)} %all-gather.2.cloned.1.call-done) | copy-start | bytes 4718596
  97.4 5.4 %copy-start.1 = (f32[2,64,768]{2,1,0:T(8,128)S(1)}, f32[2,64,768]{2,1,0:T(8,128)}, u32[]{:S(2)}) copy-start(f32[2,64,768]{2,1,0:T(8,128)} %get-tuple-element.34.middle_ref) | copy-start | bytes 1179652
  97.4 5.4 %copy-start.2 = (f32[2,64,768]{2,1,0:T(8,128)S(1)}, f32[2,64,768]{2,1,0:T(8,128)}, u32[]{:S(2)}) copy-start(f32[2,64,768]{2,1,0:T(8,128)} %get-tuple-element.35.here_ref) | copy-start | bytes 1179652
  102.9 14.7 %collective-permute-start.7 = (bf16[2,64,384]{2,1,0:T(8,128)(2,1)S(1)}, bf16[2,64,384]{2,1,0:T(8,128)(2,1)S(1)}, u32[]{:S(2)}, u32[]{:S(2)}) collective-permute-start(bf16[2,64,384]{2,1,0:T(8,128)(2,1)S(1)} %get-tuple-element.36), channel_id=1, source_target_pairs={{0,16},{1,49},{2,18},{3,51},{4,20},{5,53},{6,22},{7,55},{8,24},{9,... | collective-permute-start | bytes 294920 | tf_op jit(solution)/shard_map/ppermute | solution.py:60
  106.2 12.8 %collective-permute-start.8 = (bf16[2,64,384]{2,1,0:T(8,128)(2,1)S(1)}, bf16[2,64,384]{2,1,0:T(8,128)(2,1)S(1)}, u32[]{:S(2)}, u32[]{:S(2)}) collective-permute-start(bf16[2,64,384]{2,1,0:T(8,128)(2,1)S(1)} %get-tuple-element.37), channel_id=1, source_target_pairs={{0,17},{1,48},{2,19},{3,50},{4,21},{5,52},{6,23},{7,54},{8,25},{9,... | collective-permute-start | bytes 294920 | tf_op jit(solution)/shard_map/ppermute | solution.py:60
  113.9 5.1 %collective-permute-start.9 = (bf16[2,64,384]{2,1,0:T(8,128)(2,1)S(1)}, bf16[2,64,384]{2,1,0:T(8,128)(2,1)S(1)}, u32[]{:S(2)}, u32[]{:S(2)}) collective-permute-start(bf16[2,64,384]{2,1,0:T(8,128)(2,1)S(1)} %get-tuple-element.39), channel_id=1, source_target_pairs={{0,1},{1,0},{2,3},{3,2},{4,5},{5,4},{6,7},{7,6},{8,9},{9,8},{10,11... | collective-permute-start | bytes 294920 | tf_op jit(solution)/shard_map/ppermute | solution.py:51
Sparse Core Ops, SparseCore 0:
  10.1 71.1 all-gather.1

commit v11 on v10

--- a/solution.py
+++ b/solution.py
@@ -163,11 +163,19 @@
     )
 
 
-def gather_and_round(gelu_grad, weight):
-    line = gather(gelu_grad, along_x[0] + along_y[1])
+def first_gather(gelu_grad, block):
+    return gather(gelu_grad, along_x[0] + along_y[1]), send(block, -4)
+
+
+def gather_and_round(line, weight, block, input_4):
     weight_other = swap_cores(weight)
     grad_tokens = gather(line, along_y[0] + along_x[1])
-    grad_blocks = grad_tokens.reshape((16,) + gelu_grad.shape)
+    input_8 = send(input_4[0], -4)
+    input_2_6 = send(jnp.stack([block, input_4]), -2)
+    grad_tokens, input_2_6 = lax.optimization_barrier((grad_tokens, input_2_6))
+    evens = jnp.stack([block, input_2_6[0], input_4, input_2_6[1]])
+    odds = send(evens, -1)
+    grad_blocks = grad_tokens.reshape((16,) + (line.shape[0] // 4, line.shape[1]))
 
     weights = weight, weight_other
     far, ahead = partials(first_groups, (5,), grad_blocks, weights)
@@ -181,25 +189,39 @@
     kept = jnp.where(lax.axis_index("col") < 16, last_blocks, jnp.zeros_like(last_blocks))
     rest_other = swap_cores(for_sibling)
 
+    width = weight.shape[0]
+    half = block.shape[1]
+    parts = [v[..., width:].reshape(-1, half, width) for v in (evens[1:], odds, input_8)]
+    gathered = evens, odds, input_8, jnp.concatenate(parts)
+
     both = (2,) + rest.shape[1:]
     outs = [
         jax.ShapeDtypeStruct((2,) + both, jnp.bfloat16),
         jax.ShapeDtypeStruct(both, jnp.float32),
         jax.ShapeDtypeStruct(both, jnp.float32),
     ]
-    return (*call(first_kernel, outs, (own, cross, rest, rest_other)), kept)
-
-
-def weight_kernel(sibling, input_ref, grad_ref, *refs):
+    return (*call(first_kernel, outs, (own, cross, rest, rest_other)), kept, *gathered)
+
+
+def weight_kernel(sibling, evens_ref, odds_ref, far_ref, other_ref, grad_ref, *refs):
     first_ref = refs[0] if len(refs) == 3 else None
     out_ref, rows_ref = refs[-2:]
     half, depth = grad_ref.shape[1:]
+    width = out_ref.shape[0]
     core = lax.rem(lax.axis_index("rep"), 2)
-    core = 1 - core if sibling else core
-    for chip in range(16):
-        at = jnp.where(core == 0, (chip % 4) * 4 + chip // 4, chip)
-        rows = pl.ds(pl.multiple_of(at * half, half), half)
-        rows_ref[rows, :] = input_ref[chip, core]
+    z = lax.axis_index("col")
+    holder = 1 - core if sibling else core
+    whose = 1 if sibling else 0
+    blocks = [(2 * i, evens_ref[i, whose, :, :width]) for i in range(4)]
+    blocks += [(2 * i + 1, odds_ref[i, whose, :, :width]) for i in range(4)]
+    blocks += [(8, other_ref[14] if sibling else far_ref[:, :width])]
+    blocks += [
+        (-step, other_ref[2 * i + 1 - whose]) for i, step in enumerate((2, 4, 6, 1, 3, 5, 7))
+    ]
+    for step, block in blocks:
+        chip = lax.rem(z + (1 - 2 * core) * step + 16, 16)
+        rows = pl.ds(pl.multiple_of(place(chip, holder) * half, half), half)
+        rows_ref[rows, :] = block
     tile = 256
     for start in range(0, depth, tile):
         grad = grad_ref[:, :, start : start + tile].reshape(16 * half, tile)
@@ -209,16 +231,16 @@
         out_ref[:, start : start + tile] = part
 
 
-def weight_gradient(sibling, input_whole, grad_blocks, *first):
-    tokens, width = input_whole.shape
+def weight_gradient(sibling, gathered, grad_blocks, *first):
     half, depth = grad_blocks.shape[1:]
+    width = gathered[3].shape[2]
     out = jax.ShapeDtypeStruct((width, depth), jnp.float32)
     return call(
         functools.partial(weight_kernel, sibling),
         [out],
-        (input_whole.reshape(16, 2, half, width), grad_blocks, *first),
-        flops=(1 if sibling else 40) * tokens * width * depth,
-        scratch=[pltpu.VMEM((tokens // 2, width), jnp.bfloat16)],
+        (*gathered, grad_blocks, *first),
+        flops=(1 if sibling else 40) * 32 * half * width * depth,
+        scratch=[pltpu.VMEM((16 * half, width), jnp.bfloat16)],
     )[0]
 
 
@@ -227,15 +249,23 @@
     half = tokens // 2
     f32, bf16 = jnp.float32, jnp.bfloat16
 
-    input_whole = lax.all_gather(layer_input, "col", axis=0, tiled=True)
+    block = jnp.concatenate(
+        [v.reshape(2, half, width) for v in (layer_input, swap_cores(layer_input))], axis=2
+    )
+    block = jnp.where(lax.axis_index("rep") % 2 == 0, block, block[::-1])
     gelu_grad = (upstream.astype(f32) * gelu_slope(gelu_input.astype(f32))).astype(bf16)
-
-    to_send, middle, here, grad_blocks = taken(gather_and_round, gelu_grad, weight)
+    gelu_grad, block = lax.optimization_barrier((gelu_grad, block))
+
+    line, input_4 = taken(first_gather, gelu_grad, block)
+    to_send, middle, here, grad_blocks, *gathered, for_sibling = taken(
+        gather_and_round, line, weight, block, input_4
+    )
 
     moved = send(to_send, 2)
     grad_other = swap_cores(grad_blocks)
-    grad_weight = weight_gradient(False, input_whole, grad_blocks)
-    grad_weight = weight_gradient(True, input_whole, grad_other, grad_weight)
+    gathered = (*gathered, swap_cores(for_sibling))
+    grad_weight = weight_gradient(False, gathered, grad_blocks)
+    grad_weight = weight_gradient(True, gathered, grad_other, grad_weight)
     moved, grad_weight = lax.optimization_barrier((moved, grad_weight))
     part = (2, half, width)
     outs = [jax.ShapeDtypeStruct(part, t) for t in (bf16, bf16, f32, bf16)]

time: 127 us -> 138 us (1.087)
  the two profiles are of different devices: /device:TPU:1 before, /device:TPU:51 now
where the time goes in v11:
time: 138 us; the launch traced here: 137 us
  starting transfers between devices  72 us (52%)
  waiting for transfers between devices  30.7 us (22%)
  Pallas kernels  17.9 us (13%)
  other arithmetic  8.74 us (6%)
  local copies, waits for them, and re-layouts  7 us (5%)
    ppermute x10, starting transfers between devices, send(): return lax.ppermute(values, ring, pairs)  43.8 us
    ppermute x10, waiting for transfers between devices, send(): return lax.ppermute(values, ring, pairs)  28.9 us
    ppermute x6, starting transfers between devices, swap_cores(): return lax.ppermute(values, 'rep', [(0, 1), (1, 0), (2, 3), (3, 2)])  19.7 us
    pallas_call x8, Pallas kernels, call(): pl.pallas_call(kernel, out_shape=outs, in_specs=[vmem] * len(args), out_s...  17.9 us
    all_to_all x2, starting transfers between devices, gather(): parts = lax.all_to_all(copies, plane, 0, 0, axis_index_groups=groups)  8.5 us
    broadcast_in_dim x2, local copies, waits for them, and re-layouts, gather(): copies = jnp.broadcast_to(values[None], (4,) + values.shape)  3.95 us
  transfers between devices with their start and end apart: 18, of which 5 were waited for; matrix products, arithmetic and copies ran while one was open for 6% of the time, Pallas kernels for 10%

profile of v11, /device:TPU:51, one launch (start us, length us, event | category | flops | bytes accessed | tf_op | source)
XLA Modules:
  0.0 137.3 jit_solution(16090704915711078350)
XLA Ops:
  0.6 2.6 %collective-permute-start.9 = (bf16[128,384]{1,0:T(8,128)(2,1)}, bf16[128,384]{1,0:T(8,128)(2,1)S(1)}, u32[]{:S(2)}, u32[]{:S(2)}) collective-permute-start(bf16[128,384]{1,0:T(8,128)(2,1)} %param.8), channel_id=1, source_target_pairs={{0,1},{1,0},{2,3},{3,2},{4,5},{5,4},{6,7},{7,6},{8,9},{9,8},{10,11... | collective-permute-start | bytes 294920 | tf_op jit(solution)/shard_map/ppermute | solution.py:51
  5.5 23.2 %conditional.2 = (bf16[256,1536]{1,0:T(8,128)(2,1)}, bf16[2,64,768]{2,1,0:T(8,128)(2,1)}) conditional(s32[]{:T(128)} %convert_element_type.13, () %tuple.30, (bf16[64,1536]{1,0:T(8,128)(2,1)S(1)}, bf16[2,64,768]{2,1,0:T(8,128)(2,1)S(1)}) %tuple.31), branch_computations={%region_0.1_spmd, %region_1.2_spmd} | conditional | bytes 4128856 | solution.py:158
  6.5 4.2 %all-to-all-start = ((bf16[4,64,1536]{2,1,0:T(8,128)(2,1)}), bf16[4,64,1536]{2,1,0:T(8,128)(2,1)}, u32[]{:S(2)}, u32[]{:S(2)}) async-start(bf16[4,64,1536]{2,1,0:T(8,128)(2,1)} %broadcast_in_dim.0), calls=%async_computation | async-start | bytes 1572864 | tf_op jit(solution)/shard_map/cond/branch_1_fun/all_to_all | solution.py:46
  10.7 8.8 %collective-permute-start = (bf16[2,64,768]{2,1,0:T(8,128)(2,1)S(1)}, bf16[2,64,768]{2,1,0:T(8,128)(2,1)}, u32[]{:S(2)}, u32[]{:S(2)}) collective-permute-start(bf16[2,64,768]{2,1,0:T(8,128)(2,1)S(1)} %get-tuple-element.13), channel_id=1, source_target_pairs={{0,48},{1,17},{2,50},{3,19},{4,52},{5,21},{6,54},{7,23},{8,56},{9,... | collective-permute-start | bytes 589832 | tf_op jit(solution)/shard_map/cond/branch_1_fun/ppermute | solution.py:60
  19.5 9.2 %collective-permute-done = bf16[2,64,768]{2,1,0:T(8,128)(2,1)} collective-permute-done((bf16[2,64,768]{2,1,0:T(8,128)(2,1)S(1)}, bf16[2,64,768]{2,1,0:T(8,128)(2,1)}, u32[]{:S(2)}, u32[]{:S(2)}) %collective-permute-start) | collective-permute-done | bytes 196640 | tf_op jit(solution)/shard_map/cond/branch_1_fun/ppermute | solution.py:60
  28.7 69.8 %conditional.3 = (bf16[2,2,64,768]{3,2,1,0:T(8,128)(2,1)}, f32[2,64,768]{2,1,0:T(8,128)S(1)}, f32[2,64,768]{2,1,0:T(8,128)}, bf16[16,64,1536]{2,1,0:T(8,128)(2,1...) conditional(s32[]{:T(128)} %convert_element_type.13, () %tuple.29, ...), branch_computations={%region_2.3_spmd, %region_3.4_spmd} | conditional | flops 7252328448 | bytes 70287928 | solution.py:158
  28.7 3.0 %broadcast_in_dim.2 = bf16[4,256,1536]{2,1,0:T(8,128)(2,1)} broadcast(bf16[256,1536]{1,0:T(8,128)(2,1)} %get-tuple-element.14), dimensions={1,2} | broadcast | bytes 3932160 | tf_op jit(solution)/shard_map/cond/branch_1_fun/broadcast_in_dim | solution.py:45
  31.7 4.3 %all-to-all-start.1 = ((bf16[4,256,1536]{2,1,0:T(8,128)(2,1)}), bf16[4,256,1536]{2,1,0:T(8,128)(2,1)S(1)}, u32[]{:S(2)}, u32[]{:S(2)}) async-start(bf16[4,256,1536]{2,1,0:T(8,128)(2,1)} %broadcast_in_dim.2), calls=%async_computation.1 | async-start | bytes 6291456 | tf_op jit(solution)/shard_map/cond/branch_1_fun/all_to_all | solution.py:46
  36.0 5.7 %collective-permute-start.2 = (bf16[384,1536]{1,0:T(8,128)(2,1)}, bf16[384,1536]{1,0:T(8,128)(2,1)}, u32[]{:S(2)}, u32[]{:S(2)}) collective-permute-start(bf16[384,1536]{1,0:T(8,128)(2,1)} %get-tuple-element.70.own_ref), channel_id=1, source_target_pairs={{0,1},{1,0},{2,3},{3,2},{4,5},{5,4},{6,7},{7,6},{8,9},{9,8},{10,11... | collective-permute-start | bytes 3538952 | tf_op jit(solution)/shard_map/cond/branch_1_fun/ppermute | solution.py:51
  43.3 2.4 %collective-permute-start.1 = (bf16[2,2,64,768]{3,2,1,0:T(8,128)(2,1)}, bf16[2,2,64,768]{3,2,1,0:T(8,128)(2,1)}, u32[]{:S(2)}, u32[]{:S(2)}) collective-permute-start(bf16[2,2,64,768]{3,2,1,0:T(8,128)(2,1)} %pad_maximum_fusion.2), channel_id=1, source_target_pairs={{0,56},{1,9},{2,58},{3,11},{4,60},{5,13},{6,62},{7,15},{8,0},{9,17... | collective-permute-start | bytes 1179656 | tf_op jit(solution)/shard_map/cond/branch_1_fun/ppermute | solution.py:60
  46.6 5.1 %collective-permute-start.8 = (bf16[64,768]{1,0:T(8,128)(2,1)S(1)}, bf16[64,768]{1,0:T(8,128)(2,1)S(1)}, u32[]{:S(2)}, u32[]{:S(2)}) collective-permute-start(bf16[64,768]{1,0:T(8,128)(2,1)S(1)} %slice_bitcast_fusion), channel_id=1, source_target_pairs={{0,48},{1,17},{2,50},{3,19},{4,52},{5,21},{6,54},{7,23},{8,56},{9,... | collective-permute-start | bytes 294920 | tf_op jit(solution)/shard_map/cond/branch_1_fun/ppermute | solution.py:60
  51.7 11.6 %collective-permute-done.8 = bf16[64,768]{1,0:T(8,128)(2,1)S(1)} collective-permute-done((bf16[64,768]{1,0:T(8,128)(2,1)S(1)}, bf16[64,768]{1,0:T(8,128)(2,1)S(1)}, u32[]{:S(2)}, u32[]{:S(2)}) %collective-permute-start.8) | collective-permute-done | bytes 98336 | tf_op jit(solution)/shard_map/cond/branch_1_fun/ppermute | solution.py:60
  64.4 2.9 %branch_1_fun.4 = (bf16[1,64,768]{2,1,0:T(8,128)(2,1)S(1)}, bf16[4,64,768]{2,1,0:T(8,128)(2,1)S(1)}) custom-call(bf16[16,64,1536]{2,1,0:T(8,128)(2,1)S(1)} %bitcast.13, bf16[384,1536]{1,0:T(8,128)(2,1)} %get-tuple-element.70.own_ref, bf16[384,1536]{1,0:T(8,128)(2,1)} %collective-permute-done.2.other_ref), custom_call_target="tpu_custom_call" | custom-call | flops 2264924160 | bytes 5996544 | tf_op jit(solution)/shard_map/cond/branch_1_fun/pallas_call | solution.py:74
  67.3 7.5 %collective-permute-start.5 = (bf16[1,64,768]{2,1,0:T(8,128)(2,1)S(1)}, bf16[1,64,768]{2,1,0:T(8,128)(2,1)S(1)}, u32[]{:S(2)}, u32[]{:S(2)}) collective-permute-start(bf16[1,64,768]{2,1,0:T(8,128)(2,1)S(1)} %get-tuple-element.24), channel_id=1, source_target_pairs={{0,8},{1,57},{2,10},{3,59},{4,12},{5,61},{6,14},{7,63},{8,16},{9,1... | collective-permute-start | bytes 294920 | tf_op jit(solution)/shard_map/cond/branch_1_fun/ppermute | solution.py:60
  81.9 3.4 %collective-permute-start.7 = (bf16[4,2,64,768]{3,2,1,0:T(8,128)(2,1)S(1)}, bf16[4,2,64,768]{3,2,1,0:T(8,128)(2,1)}, u32[]{:S(2)}, u32[]{:S(2)}) collective-permute-start(bf16[4,2,64,768]{3,2,1,0:T(8,128)(2,1)S(1)} %pad_maximum_fusion), channel_id=1, source_target_pairs={{0,60},{1,5},{2,62},{3,7},{4,0},{5,9},{6,2},{7,11},{8,4},{9,13},{1... | collective-permute-start | bytes 2359304 | tf_op jit(solution)/shard_map/cond/branch_1_fun/ppermute | solution.py:60
  86.3 2.9 %branch_1_fun.6 = (bf16[4,64,768]{2,1,0:T(8,128)(2,1)S(1)}, bf16[3,64,768]{2,1,0:T(8,128)(2,1)S(1)}) custom-call(bf16[16,64,1536]{2,1,0:T(8,128)(2,1)S(1)} %bitcast.15, bf16[384,1536]{1,0:T(8,128)(2,1)S(1)} %copy-done.7, bf16[384,1536]{1,0:T(8,128)(2,1)} %collective-permute-done.2.other_ref, bf16[1,64,768]{2,1,0:T(8,128)(2,1)S(1)} %collective-permute-done.5.refs_0_), custom_call_target="tpu_custom_call" | custom-call | flops 3170893824 | bytes 6291456 | tf_op jit(solution)/shard_map/cond/branch_1_fun/pallas_call | solution.py:74
  89.1 2.6 %collective-permute-start.6 = (bf16[3,64,768]{2,1,0:T(8,128)(2,1)S(1)}, bf16[3,64,768]{2,1,0:T(8,128)(2,1)S(1)}, u32[]{:S(2)}, u32[]{:S(2)}) collective-permute-start(bf16[3,64,768]{2,1,0:T(8,128)(2,1)S(1)} %get-tuple-element.27), channel_id=1, source_target_pairs={{0,1},{1,0},{2,3},{3,2},{4,5},{5,4},{6,7},{7,6},{8,9},{9,8},{10,11... | collective-permute-start | bytes 884744 | tf_op jit(solution)/shard_map/cond/branch_1_fun/ppermute | solution.py:51
  98.5 5.0 %collective-permute-start.11 = (bf16[15,64,384]{2,1,0:T(8,128)(2,1)}, bf16[15,64,384]{2,1,0:T(8,128)(2,1)S(1)}, u32[]{:S(2)}, u32[]{:S(2)}) collective-permute-start(bf16[15,64,384]{2,1,0:T(8,128)(2,1)} %get-tuple-element.59), channel_id=1, source_target_pairs={{0,1},{1,0},{2,3},{3,2},{4,5},{5,4},{6,7},{7,6},{8,9},{9,8},{10,11... | collective-permute-start | bytes 2211848 | tf_op jit(solution)/shard_map/ppermute | solution.py:51
  103.5 3.1 %collective-permute-start.10 = (bf16[2,2,64,768]{3,2,1,0:T(8,128)(2,1)}, bf16[2,2,64,768]{3,2,1,0:T(8,128)(2,1)S(1)}, u32[]{:S(2)}, u32[]{:S(2)}) collective-permute-start(bf16[2,2,64,768]{3,2,1,0:T(8,128)(2,1)} %get-tuple-element.55), channel_id=1, source_target_pairs={{0,8},{1,57},{2,10},{3,59},{4,12},{5,61},{6,14},{7,63},{8,16},{9,1... | collective-permute-start | bytes 1179656 | tf_op jit(solution)/shard_map/ppermute | solution.py:60
  108.6 4.0 %shard_map.60.refs_0_ = f32[384,1536]{1,0:T(8,128)S(1)} custom-call(bf16[4,2,64,768]{3,2,1,0:T(8,128)(2,1)} %get-tuple-element.56.evens_ref, bf16[4,2,64,768]{3,2,1,0:T(8,128)(2,1)} %get-tuple-element.57.odds_ref, bf16[64,768]{1,0:T(8,128)(2,1)S(1)} %get-tuple-element.58.far_ref, bf16[15,64,384]{2,1,0:T(8,128)(2,1)S(1)} %collective-permute-done.11.other_ref, ...), custom_call_target="tpu_custom_call" | custom-call | flops 48318382080 | bytes 7913472 | tf_op jit(solution)/shard_map/pallas_call | solution.py:74
  114.4 4.1 %shard_map.61 = f32[384,1536]{1,0:T(8,128)} custom-call(bf16[4,2,64,768]{3,2,1,0:T(8,128)(2,1)S(1)} %copy-done.1, bf16[4,2,64,768]{3,2,1,0:T(8,128)(2,1)} %get-tuple-element.57.odds_ref, bf16[64,768]{1,0:T(8,128)(2,1)S(1)} %get-tuple-element.58.far_ref, bf16[15,64,384]{2,1,0:T(8,128)(2,1)S(1)} %collective-permute-done.11.other_ref, ...), custom_call_target="tpu_custom_call" | custom-call | flops 1207959552 | bytes 10272768 | tf_op jit(solution)/shard_map/pallas_call | solution.py:74
  118.6 5.3 %collective-permute-start.13 = (bf16[2,64,384]{2,1,0:T(8,128)(2,1)S(1)}, bf16[2,64,384]{2,1,0:T(8,128)(2,1)S(1)}, u32[]{:S(2)}, u32[]{:S(2)}) collective-permute-start(bf16[2,64,384]{2,1,0:T(8,128)(2,1)S(1)} %get-tuple-element.64), channel_id=1, source_target_pairs={{0,16},{1,49},{2,18},{3,51},{4,20},{5,53},{6,22},{7,55},{8,24},{9,... | collective-permute-start | bytes 294920 | tf_op jit(solution)/shard_map/ppermute | solution.py:60
  123.9 4.5 %collective-permute-start.14 = (bf16[2,64,384]{2,1,0:T(8,128)(2,1)S(1)}, bf16[2,64,384]{2,1,0:T(8,128)(2,1)S(1)}, u32[]{:S(2)}, u32[]{:S(2)}) collective-permute-start(bf16[2,64,384]{2,1,0:T(8,128)(2,1)S(1)} %get-tuple-element.65), channel_id=1, source_target_pairs={{0,17},{1,48},{2,19},{3,50},{4,21},{5,52},{6,23},{7,54},{8,25},{9,... | collective-permute-start | bytes 294920 | tf_op jit(solution)/shard_map/ppermute | solution.py:60
  130.3 6.3 %collective-permute-done.14.cross_ref = bf16[2,64,384]{2,1,0:T(8,128)(2,1)S(1)} collective-permute-done((bf16[2,64,384]{2,1,0:T(8,128)(2,1)S(1)}, bf16[2,64,384]{2,1,0:T(8,128)(2,1)S(1)}, u32[]{:S(2)}, u32[]{:S(2)}) %collective-permute-start.14) | collective-permute-done | bytes 98336 | tf_op jit(solution)/shard_map/ppermute | solution.py:60
  (52 shorter events, 28.1 us)
Async XLA Ops:
  0.6 3.9 %collective-permute-start.9 = (bf16[128,384]{1,0:T(8,128)(2,1)}, bf16[128,384]{1,0:T(8,128)(2,1)S(1)}, u32[]{:S(2)}, u32[]{:S(2)}) collective-permute-start(bf16[128,384]{1,0:T(8,128)(2,1)} %param.8), channel_id=1, source_target_pairs={{0,1},{1,0},{2,3},{3,2},{4,5},{5,4},{6,7},{7,6},{8,9},{9,8},{10,11... | collective-permute-start | bytes 294920 | tf_op jit(solution)/shard_map/ppermute | solution.py:51
  6.5 22.2 %all-to-all-start = ((bf16[4,64,1536]{2,1,0:T(8,128)(2,1)}), bf16[4,64,1536]{2,1,0:T(8,128)(2,1)}, u32[]{:S(2)}, u32[]{:S(2)}) async-start(bf16[4,64,1536]{2,1,0:T(8,128)(2,1)} %broadcast_in_dim.0), calls=%async_computation | async-start | bytes 1572864 | tf_op jit(solution)/shard_map/cond/branch_1_fun/all_to_all | solution.py:46
  10.7 18.0 %collective-permute-start = (bf16[2,64,768]{2,1,0:T(8,128)(2,1)S(1)}, bf16[2,64,768]{2,1,0:T(8,128)(2,1)}, u32[]{:S(2)}, u32[]{:S(2)}) collective-permute-start(bf16[2,64,768]{2,1,0:T(8,128)(2,1)S(1)} %get-tuple-element.13), channel_id=1, source_target_pairs={{0,48},{1,17},{2,50},{3,19},{4,52},{5,21},{6,54},{7,23},{8,56},{9,... | collective-permute-start | bytes 589832 | tf_op jit(solution)/shard_map/cond/branch_1_fun/ppermute | solution.py:60
  31.7 31.6 %all-to-all-start.1 = ((bf16[4,256,1536]{2,1,0:T(8,128)(2,1)}), bf16[4,256,1536]{2,1,0:T(8,128)(2,1)S(1)}, u32[]{:S(2)}, u32[]{:S(2)}) async-start(bf16[4,256,1536]{2,1,0:T(8,128)(2,1)} %broadcast_in_dim.2), calls=%async_computation.1 | async-start | bytes 6291456 | tf_op jit(solution)/shard_map/cond/branch_1_fun/all_to_all | solution.py:46
  36.0 28.4 %collective-permute-start.2 = (bf16[384,1536]{1,0:T(8,128)(2,1)}, bf16[384,1536]{1,0:T(8,128)(2,1)}, u32[]{:S(2)}, u32[]{:S(2)}) collective-permute-start(bf16[384,1536]{1,0:T(8,128)(2,1)} %get-tuple-element.70.own_ref), channel_id=1, source_target_pairs={{0,1},{1,0},{2,3},{3,2},{4,5},{5,4},{6,7},{7,6},{8,9},{9,8},{10,11... | collective-permute-start | bytes 3538952 | tf_op jit(solution)/shard_map/cond/branch_1_fun/ppermute | solution.py:51
  43.3 19.9 %collective-permute-start.1 = (bf16[2,2,64,768]{3,2,1,0:T(8,128)(2,1)}, bf16[2,2,64,768]{3,2,1,0:T(8,128)(2,1)}, u32[]{:S(2)}, u32[]{:S(2)}) collective-permute-start(bf16[2,2,64,768]{3,2,1,0:T(8,128)(2,1)} %pad_maximum_fusion.2), channel_id=1, source_target_pairs={{0,56},{1,9},{2,58},{3,11},{4,60},{5,13},{6,62},{7,15},{8,0},{9,17... | collective-permute-start | bytes 1179656 | tf_op jit(solution)/shard_map/cond/branch_1_fun/ppermute | solution.py:60
  46.6 16.6 %collective-permute-start.8 = (bf16[64,768]{1,0:T(8,128)(2,1)S(1)}, bf16[64,768]{1,0:T(8,128)(2,1)S(1)}, u32[]{:S(2)}, u32[]{:S(2)}) collective-permute-start(bf16[64,768]{1,0:T(8,128)(2,1)S(1)} %slice_bitcast_fusion), channel_id=1, source_target_pairs={{0,48},{1,17},{2,50},{3,19},{4,52},{5,21},{6,54},{7,23},{8,56},{9,... | collective-permute-start | bytes 294920 | tf_op jit(solution)/shard_map/cond/branch_1_fun/ppermute | solution.py:60
  64.4 10.4 %copy-start.7 = (bf16[384,1536]{1,0:T(8,128)(2,1)S(1)}, bf16[384,1536]{1,0:T(8,128)(2,1)}, u32[]{:S(2)}) copy-start(bf16[384,1536]{1,0:T(8,128)(2,1)} %get-tuple-element.70.own_ref) | copy-start | bytes 3538948 | tf_op jit(solution)/shard_map/cond
  67.3 19.0 %collective-permute-start.5 = (bf16[1,64,768]{2,1,0:T(8,128)(2,1)S(1)}, bf16[1,64,768]{2,1,0:T(8,128)(2,1)S(1)}, u32[]{:S(2)}, u32[]{:S(2)}) collective-permute-start(bf16[1,64,768]{2,1,0:T(8,128)(2,1)S(1)} %get-tuple-element.24), channel_id=1, source_target_pairs={{0,8},{1,57},{2,10},{3,59},{4,12},{5,61},{6,14},{7,63},{8,16},{9,1... | collective-permute-start | bytes 294920 | tf_op jit(solution)/shard_map/cond/branch_1_fun/ppermute | solution.py:60
  77.0 16.5 %collective-permute-start.4 = (bf16[4,64,768]{2,1,0:T(8,128)(2,1)S(1)}, bf16[4,64,768]{2,1,0:T(8,128)(2,1)S(1)}, u32[]{:S(2)}, u32[]{:S(2)}) collective-permute-start(bf16[4,64,768]{2,1,0:T(8,128)(2,1)S(1)} %branch_1_fun.5), channel_id=1, source_target_pairs={{0,61},{1,4},{2,63},{3,6},{4,1},{5,8},{6,3},{7,10},{8,5},{9,12},{1... | collective-permute-start | bytes 1179656 | tf_op jit(solution)/shard_map/cond/branch_1_fun/ppermute | solution.py:60
  79.0 14.6 %collective-permute-start.3 = (bf16[4,64,768]{2,1,0:T(8,128)(2,1)S(1)}, bf16[4,64,768]{2,1,0:T(8,128)(2,1)S(1)}, u32[]{:S(2)}, u32[]{:S(2)}) collective-permute-start(bf16[4,64,768]{2,1,0:T(8,128)(2,1)S(1)} %get-tuple-element.19), channel_id=1, source_target_pairs={{0,4},{1,61},{2,6},{3,63},{4,8},{5,1},{6,10},{7,3},{8,12},{9,5},{1... | collective-permute-start | bytes 1179656 | tf_op jit(solution)/shard_map/cond/branch_1_fun/ppermute | solution.py:60
  81.9 11.6 %copy-start = (bf16[4,2,64,768]{3,2,1,0:T(8,128)(2,1)}, bf16[4,2,64,768]{3,2,1,0:T(8,128)(2,1)S(1)}, u32[]{:S(2)}) copy-start(bf16[4,2,64,768]{3,2,1,0:T(8,128)(2,1)S(1)} %pad_maximum_fusion) | copy-start | bytes 2359300 | tf_op jit(solution)/shard_map/cond
  81.9 14.5 %collective-permute-start.7 = (bf16[4,2,64,768]{3,2,1,0:T(8,128)(2,1)S(1)}, bf16[4,2,64,768]{3,2,1,0:T(8,128)(2,1)}, u32[]{:S(2)}, u32[]{:S(2)}) collective-permute-start(bf16[4,2,64,768]{3,2,1,0:T(8,128)(2,1)S(1)} %pad_maximum_fusion), channel_id=1, source_target_pairs={{0,60},{1,5},{2,62},{3,7},{4,0},{5,9},{6,2},{7,11},{8,4},{9,13},{1... | collective-permute-start | bytes 2359304 | tf_op jit(solution)/shard_map/cond/branch_1_fun/ppermute | solution.py:60
  89.1 4.4 %collective-permute-start.6 = (bf16[3,64,768]{2,1,0:T(8,128)(2,1)S(1)}, bf16[3,64,768]{2,1,0:T(8,128)(2,1)S(1)}, u32[]{:S(2)}, u32[]{:S(2)}) collective-permute-start(bf16[3,64,768]{2,1,0:T(8,128)(2,1)S(1)} %get-tuple-element.27), channel_id=1, source_target_pairs={{0,1},{1,0},{2,3},{3,2},{4,5},{5,4},{6,7},{7,6},{8,9},{9,8},{10,11... | collective-permute-start | bytes 884744 | tf_op jit(solution)/shard_map/cond/branch_1_fun/ppermute | solution.py:51
  98.5 5.0 %copy-start.3 = (f32[2,64,768]{2,1,0:T(8,128)}, f32[2,64,768]{2,1,0:T(8,128)S(1)}, u32[]{:S(2)}) copy-start(f32[2,64,768]{2,1,0:T(8,128)S(1)} %get-tuple-element.62.middle_ref) | copy-start | bytes 1179652
  98.5 10.1 %collective-permute-start.11 = (bf16[15,64,384]{2,1,0:T(8,128)(2,1)}, bf16[15,64,384]{2,1,0:T(8,128)(2,1)S(1)}, u32[]{:S(2)}, u32[]{:S(2)}) collective-permute-start(bf16[15,64,384]{2,1,0:T(8,128)(2,1)} %get-tuple-element.59), channel_id=1, source_target_pairs={{0,1},{1,0},{2,3},{3,2},{4,5},{5,4},{6,7},{7,6},{8,9},{9,8},{10,11... | collective-permute-start | bytes 2211848 | tf_op jit(solution)/shard_map/ppermute | solution.py:51
  103.5 15.0 %collective-permute-start.10 = (bf16[2,2,64,768]{3,2,1,0:T(8,128)(2,1)}, bf16[2,2,64,768]{3,2,1,0:T(8,128)(2,1)S(1)}, u32[]{:S(2)}, u32[]{:S(2)}) collective-permute-start(bf16[2,2,64,768]{3,2,1,0:T(8,128)(2,1)} %get-tuple-element.55), channel_id=1, source_target_pairs={{0,8},{1,57},{2,10},{3,59},{4,12},{5,61},{6,14},{7,63},{8,16},{9,1... | collective-permute-start | bytes 1179656 | tf_op jit(solution)/shard_map/ppermute | solution.py:60
  106.7 7.8 %collective-permute-start.12 = (bf16[16,64,1536]{2,1,0:T(8,128)(2,1)}, bf16[16,64,1536]{2,1,0:T(8,128)(2,1)S(1)}, u32[]{:S(2)}, u32[]{:S(2)}) collective-permute-start(bf16[16,64,1536]{2,1,0:T(8,128)(2,1)} %get-tuple-element.60.grad_ref), channel_id=1, source_target_pairs={{0,1},{1,0},{2,3},{3,2},{4,5},{5,4},{6,7},{7,6},{8,9},{9,8},{10,11... | collective-permute-start | bytes 9437192 | tf_op jit(solution)/shard_map/ppermute | solution.py:51
  108.6 5.8 %copy-start.1 = (bf16[4,2,64,768]{3,2,1,0:T(8,128)(2,1)S(1)}, bf16[4,2,64,768]{3,2,1,0:T(8,128)(2,1)}, u32[]{:S(2)}) copy-start(bf16[4,2,64,768]{3,2,1,0:T(8,128)(2,1)} %get-tuple-element.56.evens_ref) | copy-start | bytes 2359300
  112.6 5.9 %copy-start.2 = (f32[2,64,768]{2,1,0:T(8,128)S(1)}, f32[2,64,768]{2,1,0:T(8,128)}, u32[]{:S(2)}) copy-start(f32[2,64,768]{2,1,0:T(8,128)} %get-tuple-element.63.here_ref) | copy-start | bytes 1179652
  112.6 5.9 %copy-start.4 = (f32[2,64,768]{2,1,0:T(8,128)S(1)}, f32[2,64,768]{2,1,0:T(8,128)}, u32[]{:S(2)}) copy-start(f32[2,64,768]{2,1,0:T(8,128)} %copy-done.3) | copy-start | bytes 1179652
  118.6 11.7 %collective-permute-start.13 = (bf16[2,64,384]{2,1,0:T(8,128)(2,1)S(1)}, bf16[2,64,384]{2,1,0:T(8,128)(2,1)S(1)}, u32[]{:S(2)}, u32[]{:S(2)}) collective-permute-start(bf16[2,64,384]{2,1,0:T(8,128)(2,1)S(1)} %get-tuple-element.64), channel_id=1, source_target_pairs={{0,16},{1,49},{2,18},{3,51},{4,20},{5,53},{6,22},{7,55},{8,24},{9,... | collective-permute-start | bytes 294920 | tf_op jit(solution)/shard_map/ppermute | solution.py:60
  123.9 12.7 %collective-permute-start.14 = (bf16[2,64,384]{2,1,0:T(8,128)(2,1)S(1)}, bf16[2,64,384]{2,1,0:T(8,128)(2,1)S(1)}, u32[]{:S(2)}, u32[]{:S(2)}) collective-permute-start(bf16[2,64,384]{2,1,0:T(8,128)(2,1)S(1)} %get-tuple-element.65), channel_id=1, source_target_pairs={{0,17},{1,48},{2,19},{3,50},{4,21},{5,52},{6,23},{7,54},{8,25},{9,... | collective-permute-start | bytes 294920 | tf_op jit(solution)/shard_map/ppermute | solution.py:60
  128.4 8.2 %collective-permute-start.15 = (bf16[2,64,384]{2,1,0:T(8,128)(2,1)S(1)}, bf16[2,64,384]{2,1,0:T(8,128)(2,1)S(1)}, u32[]{:S(2)}, u32[]{:S(2)}) collective-permute-start(bf16[2,64,384]{2,1,0:T(8,128)(2,1)S(1)} %get-tuple-element.67), channel_id=1, source_target_pairs={{0,1},{1,0},{2,3},{3,2},{4,5},{5,4},{6,7},{7,6},{8,9},{9,8},{10,11... | collective-permute-start | bytes 294920 | tf_op jit(solution)/shard_map/ppermute | solution.py:51
  (2 other events, 9.0 us)

commit v12 on v9

--- a/solution.py
+++ b/solution.py
@@ -162,7 +162,12 @@
     )
 
 
-def first_round(grad_blocks, weight, weight_other):
+def gather_and_round(gelu_grad, weight):
+    line = gather(gelu_grad, along_x[0] + along_y[1])
+    weight_other = swap_cores(weight)
+    grad_tokens = gather(line, along_y[0] + along_x[1])
+    grad_blocks = grad_tokens.reshape((16,) + gelu_grad.shape)
+
     weights = weight, weight_other
     far, ahead, behind = partials(early_groups, (5, 4), grad_blocks, weights)
     far, later_blocks = lax.optimization_barrier((far, grad_blocks))
@@ -177,18 +182,7 @@
         jax.ShapeDtypeStruct(both, jnp.float32),
         jax.ShapeDtypeStruct(both, jnp.float32),
     ]
-    return call(first_kernel, outs, (own, cross, rest, rest_other))
-
-
-def gather_plane(gelu_grad, weight):
-    line = gather(gelu_grad, along_x[0] + along_y[1])
-    grad_tokens = gather(line, along_y[0] + along_x[1])
-    return grad_tokens.reshape((16,) + gelu_grad.shape), swap_cores(weight)
-
-
-def gather_and_round(gelu_grad, weight):
-    grad_blocks, weight_other = taken(gather_plane, gelu_grad, weight)
-    return (*taken(first_round, grad_blocks, weight, weight_other), grad_blocks)
+    return (*call(first_kernel, outs, (own, cross, rest, rest_other)), grad_blocks)
 
 
 def weight_kernel(sibling, input_ref, grad_ref, *refs):

time: 126 us -> 124 us (0.984)
  the two profiles are of different devices: /device:TPU:2 before, /device:TPU:1 now
where the time goes in v12:
time: 124 us; the launch traced here: 122 us
  starting transfers between devices  52 us (42%)
  waiting for transfers between devices  23.1 us (19%)
  Pallas kernels  15.6 us (13%)
  between operations  14.1 us (11%)
  blocking collectives  12.9 us (10%)
  local copies, waits for them, and re-layouts  3.4 us (3%)
  other arithmetic  1.3 us (1%)
    ppermute x6, starting transfers between devices, send(): return lax.ppermute(values, ring, pairs)  32.1 us
    pallas_call x7, Pallas kernels, call(): pl.pallas_call(kernel, out_shape=outs, in_specs=[vmem] * len(args), out_s...  15.6 us
    ppermute x4, starting transfers between devices, swap_cores(): return lax.ppermute(values, 'rep', [(0, 1), (1, 0), (2, 3), (3, 2)])  15 us
    all_to_all x1, blocking collectives, gather(): parts = lax.all_to_all(copies, plane, 0, 0, axis_index_groups=groups)  12.9 us
    all_to_all x1, waiting for transfers between devices, gather(): parts = lax.all_to_all(copies, plane, 0, 0, axis_index_groups=groups)  10.7 us
    ppermute x6, waiting for transfers between devices, send(): return lax.ppermute(values, ring, pairs)  8.24 us
    all_to_all x1, starting transfers between devices, gather(): parts = lax.all_to_all(copies, plane, 0, 0, axis_index_groups=groups)  4.77 us
    ppermute x4, waiting for transfers between devices, swap_cores(): return lax.ppermute(values, 'rep', [(0, 1), (1, 0), (2, 3), (3, 2)])  3.43 us
  transfers between devices with their start and end apart: 12, of which 6 were waited for; matrix products, arithmetic and copies ran while one was open for 3% of the time, Pallas kernels for 12%

profile of v12, /device:TPU:1, one launch (start us, length us, event | category | flops | bytes accessed | tf_op | source)
XLA Modules:
  0.0 122.4 jit_solution(2627251045085110991)
XLA Ops:
  9.2 74.2 %conditional.1 = (bf16[2,2,64,768]{3,2,1,0:T(8,128)(2,1)}, f32[2,64,768]{2,1,0:T(8,128)}, f32[2,64,768]{2,1,0:T(8,128)}, bf16[16,64,1536]{2,1,0:T(8,128)(2,1)}) conditional(s32[]{:T(128)} %convert_element_type.12, () %tuple.18, (bf16[64,1536]{1,0:T(8,128)(2,1)S(1)}, bf16[384,1536]{1,0:T(8,128)(2,1)}) %tuple.19), branch_computations={%region_0.0_spmd, %region_1.0_spmd} | conditional | flops 7247757312 | bytes 45416740 | solution.py:157
  9.3 12.9 %all_to_all.8 = bf16[4,64,1536]{2,1,0:T(8,128)(2,1)S(1)} all-to-all(bf16[4,64,1536]{2,1,0:T(8,128)(2,1)S(1)} %broadcast_in_dim.0), channel_id=1, replica_groups={{0,128,256,384},{2,130,258,386},{64,192,320,448},{66,194,322,450},{1,3,..., dimensions={0} | all-to-all | bytes 1572864 | tf_op jit(solution)/shard_map/cond/branch_1_fun/all_to_all | solution.py:45
  22.1 1.9 %broadcast_in_dim.2 = bf16[4,256,1536]{2,1,0:T(8,128)(2,1)} broadcast(bf16[256,1536]{1,0:T(8,128)(2,1)S(1)} %bitcast.5), dimensions={1,2} | broadcast | bytes 3932160 | tf_op jit(solution)/shard_map/cond/branch_1_fun/broadcast_in_dim | solution.py:44
  24.1 4.8 %all-to-all-start.1 = ((bf16[4,256,1536]{2,1,0:T(8,128)(2,1)}), bf16[4,256,1536]{2,1,0:T(8,128)(2,1)}, u32[]{:S(2)}, u32[]{:S(2)}) async-start(bf16[4,256,1536]{2,1,0:T(8,128)(2,1)} %broadcast_in_dim.2), calls=%async_computation.1 | async-start | bytes 6291456 | tf_op jit(solution)/shard_map/cond/branch_1_fun/all_to_all | solution.py:45
  28.9 7.8 %collective-permute-start = (bf16[384,1536]{1,0:T(8,128)(2,1)S(1)}, bf16[384,1536]{1,0:T(8,128)(2,1)S(1)}, u32[]{:S(2)}, u32[]{:S(2)}) collective-permute-start(bf16[384,1536]{1,0:T(8,128)(2,1)S(1)} %copy-done.3), channel_id=1, source_target_pairs={{0,1},{1,0},{2,3},{3,2},{4,5},{5,4},{6,7},{7,6},{8,9},{9,8},{10,11... | collective-permute-start | bytes 3538952 | tf_op jit(solution)/shard_map/cond/branch_1_fun/ppermute | solution.py:50
  36.7 2.5 %collective-permute-done.other_ref = bf16[384,1536]{1,0:T(8,128)(2,1)S(1)} collective-permute-done((bf16[384,1536]{1,0:T(8,128)(2,1)S(1)}, bf16[384,1536]{1,0:T(8,128)(2,1)S(1)}, u32[]{:S(2)}, u32[]{:S(2)}) %collective-permute-start) | collective-permute-done | bytes 1179680 | tf_op jit(solution)/shard_map/cond/branch_1_fun/ppermute | solution.py:50
  39.1 10.7 %all-to-all-done.1 = bf16[4,256,1536]{2,1,0:T(8,128)(2,1)} async-done(((bf16[4,256,1536]{2,1,0:T(8,128)(2,1)}), bf16[4,256,1536]{2,1,0:T(8,128)(2,1)}, u32[]{:S(2)}, u32[]{:S(2)}) %all-to-all-start.1) | async-done | bytes 3145760 | tf_op jit(solution)/shard_map/cond/branch_1_fun/all_to_all | solution.py:45
  49.9 3.9 %branch_1_fun.3 = (bf16[1,64,768]{2,1,0:T(8,128)(2,1)S(1)}, bf16[4,64,768]{2,1,0:T(8,128)(2,1)S(1)}, bf16[4,64,768]{2,1,0:T(8,128)(2,1)S(1)}) custom-call(bf16[16,64,1536]{2,1,0:T(8,128)(2,1)} %bitcast.1.grad_ref, bf16[384,1536]{1,0:T(8,128)(2,1)S(1)} %copy-done.3, bf16[384,1536]{1,0:T(8,128)(2,1)S(1)} %collective-permute-done.other_ref), custom_call_target="tpu_custom_call" | custom-call | flops 4076863488 | bytes 6389760 | tf_op jit(solution)/shard_map/cond/branch_1_fun/pallas_call | solution.py:73
  53.8 11.9 %collective-permute-start.3 = (bf16[1,64,768]{2,1,0:T(8,128)(2,1)S(1)}, bf16[1,64,768]{2,1,0:T(8,128)(2,1)S(1)}, u32[]{:S(2)}, u32[]{:S(2)}) collective-permute-start(bf16[1,64,768]{2,1,0:T(8,128)(2,1)S(1)} %get-tuple-element.10), channel_id=1, source_target_pairs={{0,8},{1,57},{2,10},{3,59},{4,12},{5,61},{6,14},{7,63},{8,16},{9,1... | collective-permute-start | bytes 294920 | tf_op jit(solution)/shard_map/cond/branch_1_fun/ppermute | solution.py:59
  65.7 2.6 %collective-permute-start.1 = (bf16[4,64,768]{2,1,0:T(8,128)(2,1)S(1)}, bf16[4,64,768]{2,1,0:T(8,128)(2,1)S(1)}, u32[]{:S(2)}, u32[]{:S(2)}) collective-permute-start(bf16[4,64,768]{2,1,0:T(8,128)(2,1)S(1)} %get-tuple-element.6), channel_id=1, source_target_pairs={{0,4},{1,61},{2,6},{3,63},{4,8},{5,1},{6,10},{7,3},{8,12},{9,5},{1... | collective-permute-start | bytes 1179656 | tf_op jit(solution)/shard_map/cond/branch_1_fun/ppermute | solution.py:59
  68.3 2.3 %collective-permute-start.2 = (bf16[4,64,768]{2,1,0:T(8,128)(2,1)S(1)}, bf16[4,64,768]{2,1,0:T(8,128)(2,1)S(1)}, u32[]{:S(2)}, u32[]{:S(2)}) collective-permute-start(bf16[4,64,768]{2,1,0:T(8,128)(2,1)S(1)} %get-tuple-element.7), channel_id=1, source_target_pairs={{0,61},{1,4},{2,63},{3,6},{4,1},{5,8},{6,3},{7,10},{8,5},{9,12},{1... | collective-permute-start | bytes 1179656 | tf_op jit(solution)/shard_map/cond/branch_1_fun/ppermute | solution.py:59
  70.6 3.5 %branch_1_fun.4 = (bf16[4,64,768]{2,1,0:T(8,128)(2,1)S(1)}, bf16[3,64,768]{2,1,0:T(8,128)(2,1)S(1)}) custom-call(bf16[16,64,1536]{2,1,0:T(8,128)(2,1)} %bitcast.1.grad_ref, bf16[384,1536]{1,0:T(8,128)(2,1)S(1)} %copy-done.3, bf16[384,1536]{1,0:T(8,128)(2,1)S(1)} %collective-permute-done.other_ref, bf16[1,64,768]{2,1,0:T(8,128)(2,1)S(1)} %collective-permute-done.3.refs_0_), custom_call_target="tpu_custom_call" | custom-call | flops 3170893824 | bytes 6291456 | tf_op jit(solution)/shard_map/cond/branch_1_fun/pallas_call | solution.py:73
  74.1 3.4 %collective-permute-start.4 = (bf16[3,64,768]{2,1,0:T(8,128)(2,1)S(1)}, bf16[3,64,768]{2,1,0:T(8,128)(2,1)S(1)}, u32[]{:S(2)}, u32[]{:S(2)}) collective-permute-start(bf16[3,64,768]{2,1,0:T(8,128)(2,1)S(1)} %get-tuple-element.12), channel_id=1, source_target_pairs={{0,1},{1,0},{2,3},{3,2},{4,5},{5,4},{6,7},{7,6},{8,9},{9,8},{10,11... | collective-permute-start | bytes 884744 | tf_op jit(solution)/shard_map/cond/branch_1_fun/ppermute | solution.py:50
  77.4 2.1 %collective-permute-done.1.own_ref = bf16[4,64,768]{2,1,0:T(8,128)(2,1)S(1)} collective-permute-done((bf16[4,64,768]{2,1,0:T(8,128)(2,1)S(1)}, bf16[4,64,768]{2,1,0:T(8,128)(2,1)S(1)}, u32[]{:S(2)}, u32[]{:S(2)}) %collective-permute-start.1) | collective-permute-done | bytes 393248 | tf_op jit(solution)/shard_map/cond/branch_1_fun/ppermute | solution.py:59
  79.6 2.7 %collective-permute-done.2.cross_ref = bf16[4,64,768]{2,1,0:T(8,128)(2,1)S(1)} collective-permute-done((bf16[4,64,768]{2,1,0:T(8,128)(2,1)S(1)}, bf16[4,64,768]{2,1,0:T(8,128)(2,1)S(1)}, u32[]{:S(2)}, u32[]{:S(2)}) %collective-permute-start.2) | collective-permute-done | bytes 393248 | tf_op jit(solution)/shard_map/cond/branch_1_fun/ppermute | solution.py:59
  83.4 4.0 %collective-permute-start.5 = (bf16[2,2,64,768]{3,2,1,0:T(8,128)(2,1)}, bf16[2,2,64,768]{3,2,1,0:T(8,128)(2,1)S(1)}, u32[]{:S(2)}, u32[]{:S(2)}) collective-permute-start(bf16[2,2,64,768]{3,2,1,0:T(8,128)(2,1)} %get-tuple-element.28), channel_id=1, source_target_pairs={{0,8},{1,57},{2,10},{3,59},{4,12},{5,61},{6,14},{7,63},{8,16},{9,1... | collective-permute-start | bytes 1179656 | tf_op jit(solution)/shard_map/ppermute | solution.py:59
  87.4 1.9 %collective-permute-start.6 = (bf16[16,64,1536]{2,1,0:T(8,128)(2,1)}, bf16[16,64,1536]{2,1,0:T(8,128)(2,1)S(1)}, u32[]{:S(2)}, u32[]{:S(2)}) collective-permute-start(bf16[16,64,1536]{2,1,0:T(8,128)(2,1)} %get-tuple-element.29.grad_ref), channel_id=1, source_target_pairs={{0,1},{1,0},{2,3},{3,2},{4,5},{5,4},{6,7},{7,6},{8,9},{9,8},{10,11... | collective-permute-start | bytes 9437192 | tf_op jit(solution)/shard_map/ppermute | solution.py:50
  89.4 1.4 %copy-done = bf16[2048,384]{1,0:T(8,128)(2,1)S(1)} copy-done((bf16[2048,384]{1,0:T(8,128)(2,1)S(1)}, bf16[2048,384]{1,0:T(8,128)(2,1)}, u32[]{:S(2)}) %copy-start) | copy-done | bytes 1572888
  90.8 3.4 %shard_map.60.refs_0_ = f32[384,1536]{1,0:T(8,128)S(1)} custom-call(bf16[16,2,64,384]{3,2,1,0:T(8,128)(2,1)S(1)} %bitcast.3, bf16[16,64,1536]{2,1,0:T(8,128)(2,1)} %get-tuple-element.29.grad_ref), custom_call_target="tpu_custom_call" | custom-call | flops 48318382080 | bytes 7077888 | tf_op jit(solution)/shard_map/pallas_call | solution.py:73
  95.1 2.9 %shard_map.61 = f32[384,1536]{1,0:T(8,128)} custom-call(bf16[16,2,64,384]{3,2,1,0:T(8,128)(2,1)S(1)} %bitcast.4, bf16[16,64,1536]{2,1,0:T(8,128)(2,1)S(1)} %collective-permute-done.6.grad_ref, f32[384,1536]{1,0:T(8,128)S(1)} %shard_map.60.refs_0_), custom_call_target="tpu_custom_call" | custom-call | flops 1207959552 | bytes 9437184 | tf_op jit(solution)/shard_map/pallas_call | solution.py:73
  98.2 6.3 %collective-permute-start.7 = (bf16[2,64,384]{2,1,0:T(8,128)(2,1)S(1)}, bf16[2,64,384]{2,1,0:T(8,128)(2,1)S(1)}, u32[]{:S(2)}, u32[]{:S(2)}) collective-permute-start(bf16[2,64,384]{2,1,0:T(8,128)(2,1)S(1)} %get-tuple-element.33), channel_id=1, source_target_pairs={{0,16},{1,49},{2,18},{3,51},{4,20},{5,53},{6,22},{7,55},{8,24},{9,... | collective-permute-start | bytes 294920 | tf_op jit(solution)/shard_map/ppermute | solution.py:59
  104.4 5.1 %collective-permute-start.8 = (bf16[2,64,384]{2,1,0:T(8,128)(2,1)S(1)}, bf16[2,64,384]{2,1,0:T(8,128)(2,1)S(1)}, u32[]{:S(2)}, u32[]{:S(2)}) collective-permute-start(bf16[2,64,384]{2,1,0:T(8,128)(2,1)S(1)} %get-tuple-element.34), channel_id=1, source_target_pairs={{0,17},{1,48},{2,19},{3,50},{4,21},{5,52},{6,23},{7,54},{8,25},{9,... | collective-permute-start | bytes 294920 | tf_op jit(solution)/shard_map/ppermute | solution.py:59
  109.6 1.9 %collective-permute-start.9 = (bf16[2,64,384]{2,1,0:T(8,128)(2,1)S(1)}, bf16[2,64,384]{2,1,0:T(8,128)(2,1)S(1)}, u32[]{:S(2)}, u32[]{:S(2)}) collective-permute-start(bf16[2,64,384]{2,1,0:T(8,128)(2,1)S(1)} %get-tuple-element.36), channel_id=1, source_target_pairs={{0,1},{1,0},{2,3},{3,2},{4,5},{5,4},{6,7},{7,6},{8,9},{9,8},{10,11... | collective-permute-start | bytes 294920 | tf_op jit(solution)/shard_map/ppermute | solution.py:50
  111.5 3.4 %collective-permute-done.8.cross_ref = bf16[2,64,384]{2,1,0:T(8,128)(2,1)S(1)} collective-permute-done((bf16[2,64,384]{2,1,0:T(8,128)(2,1)S(1)}, bf16[2,64,384]{2,1,0:T(8,128)(2,1)S(1)}, u32[]{:S(2)}, u32[]{:S(2)}) %collective-permute-start.8) | collective-permute-done | bytes 98336 | tf_op jit(solution)/shard_map/ppermute | solution.py:59
  (21 shorter events, 5.0 us)
Async XLA Ops:
  7.2 82.2 %all-gather.2.cloned.1.call-start = ((), (), s32[]{:S(2)}) async-start(), calls=%async_computation.2 | async-start | bytes 1671168 | tf_op jit(solution)/shard_map/all_gather | solution.py:225
  24.1 4.8 %copy-start.3 = (bf16[384,1536]{1,0:T(8,128)(2,1)S(1)}, bf16[384,1536]{1,0:T(8,128)(2,1)}, u32[]{:S(2)}) copy-start(bf16[384,1536]{1,0:T(8,128)(2,1)} %get-tuple-element.39.own_ref) | copy-start | bytes 3538948 | tf_op jit(solution)/shard_map/cond
  24.1 25.8 %all-to-all-start.1 = ((bf16[4,256,1536]{2,1,0:T(8,128)(2,1)}), bf16[4,256,1536]{2,1,0:T(8,128)(2,1)}, u32[]{:S(2)}, u32[]{:S(2)}) async-start(bf16[4,256,1536]{2,1,0:T(8,128)(2,1)} %broadcast_in_dim.2), calls=%async_computation.1 | async-start | bytes 6291456 | tf_op jit(solution)/shard_map/cond/branch_1_fun/all_to_all | solution.py:45
  28.9 10.3 %collective-permute-start = (bf16[384,1536]{1,0:T(8,128)(2,1)S(1)}, bf16[384,1536]{1,0:T(8,128)(2,1)S(1)}, u32[]{:S(2)}, u32[]{:S(2)}) collective-permute-start(bf16[384,1536]{1,0:T(8,128)(2,1)S(1)} %copy-done.3), channel_id=1, source_target_pairs={{0,1},{1,0},{2,3},{3,2},{4,5},{5,4},{6,7},{7,6},{8,9},{9,8},{10,11... | collective-permute-start | bytes 3538952 | tf_op jit(solution)/shard_map/cond/branch_1_fun/ppermute | solution.py:50
  53.8 16.8 %collective-permute-start.3 = (bf16[1,64,768]{2,1,0:T(8,128)(2,1)S(1)}, bf16[1,64,768]{2,1,0:T(8,128)(2,1)S(1)}, u32[]{:S(2)}, u32[]{:S(2)}) collective-permute-start(bf16[1,64,768]{2,1,0:T(8,128)(2,1)S(1)} %get-tuple-element.10), channel_id=1, source_target_pairs={{0,8},{1,57},{2,10},{3,59},{4,12},{5,61},{6,14},{7,63},{8,16},{9,1... | collective-permute-start | bytes 294920 | tf_op jit(solution)/shard_map/cond/branch_1_fun/ppermute | solution.py:59
  65.7 13.9 %collective-permute-start.1 = (bf16[4,64,768]{2,1,0:T(8,128)(2,1)S(1)}, bf16[4,64,768]{2,1,0:T(8,128)(2,1)S(1)}, u32[]{:S(2)}, u32[]{:S(2)}) collective-permute-start(bf16[4,64,768]{2,1,0:T(8,128)(2,1)S(1)} %get-tuple-element.6), channel_id=1, source_target_pairs={{0,4},{1,61},{2,6},{3,63},{4,8},{5,1},{6,10},{7,3},{8,12},{9,5},{1... | collective-permute-start | bytes 1179656 | tf_op jit(solution)/shard_map/cond/branch_1_fun/ppermute | solution.py:59
  68.3 14.0 %collective-permute-start.2 = (bf16[4,64,768]{2,1,0:T(8,128)(2,1)S(1)}, bf16[4,64,768]{2,1,0:T(8,128)(2,1)S(1)}, u32[]{:S(2)}, u32[]{:S(2)}) collective-permute-start(bf16[4,64,768]{2,1,0:T(8,128)(2,1)S(1)} %get-tuple-element.7), channel_id=1, source_target_pairs={{0,61},{1,4},{2,63},{3,6},{4,1},{5,8},{6,3},{7,10},{8,5},{9,12},{1... | collective-permute-start | bytes 1179656 | tf_op jit(solution)/shard_map/cond/branch_1_fun/ppermute | solution.py:59
  74.1 8.2 %collective-permute-start.4 = (bf16[3,64,768]{2,1,0:T(8,128)(2,1)S(1)}, bf16[3,64,768]{2,1,0:T(8,128)(2,1)S(1)}, u32[]{:S(2)}, u32[]{:S(2)}) collective-permute-start(bf16[3,64,768]{2,1,0:T(8,128)(2,1)S(1)} %get-tuple-element.12), channel_id=1, source_target_pairs={{0,1},{1,0},{2,3},{3,2},{4,5},{5,4},{6,7},{7,6},{8,9},{9,8},{10,11... | collective-permute-start | bytes 884744 | tf_op jit(solution)/shard_map/cond/branch_1_fun/ppermute | solution.py:50
  83.4 14.6 %collective-permute-start.5 = (bf16[2,2,64,768]{3,2,1,0:T(8,128)(2,1)}, bf16[2,2,64,768]{3,2,1,0:T(8,128)(2,1)S(1)}, u32[]{:S(2)}, u32[]{:S(2)}) collective-permute-start(bf16[2,2,64,768]{3,2,1,0:T(8,128)(2,1)} %get-tuple-element.28), channel_id=1, source_target_pairs={{0,8},{1,57},{2,10},{3,59},{4,12},{5,61},{6,14},{7,63},{8,16},{9,1... | collective-permute-start | bytes 1179656 | tf_op jit(solution)/shard_map/ppermute | solution.py:59
  87.4 7.8 %collective-permute-start.6 = (bf16[16,64,1536]{2,1,0:T(8,128)(2,1)}, bf16[16,64,1536]{2,1,0:T(8,128)(2,1)S(1)}, u32[]{:S(2)}, u32[]{:S(2)}) collective-permute-start(bf16[16,64,1536]{2,1,0:T(8,128)(2,1)} %get-tuple-element.29.grad_ref), channel_id=1, source_target_pairs={{0,1},{1,0},{2,3},{3,2},{4,5},{5,4},{6,7},{7,6},{8,9},{9,8},{10,11... | collective-permute-start | bytes 9437192 | tf_op jit(solution)/shard_map/ppermute | solution.py:50
  89.3 1.4 %copy-start = (bf16[2048,384]{1,0:T(8,128)(2,1)S(1)}, bf16[2048,384]{1,0:T(8,128)(2,1)}, u32[]{:S(2)}) copy-start(bf16[2048,384]{1,0:T(8,128)(2,1)} %all-gather.2.cloned.1.call-done) | copy-start | bytes 4718596
  94.2 3.9 %copy-start.1 = (f32[2,64,768]{2,1,0:T(8,128)S(1)}, f32[2,64,768]{2,1,0:T(8,128)}, u32[]{:S(2)}) copy-start(f32[2,64,768]{2,1,0:T(8,128)} %get-tuple-element.31.middle_ref) | copy-start | bytes 1179652
  94.2 3.9 %copy-start.2 = (f32[2,64,768]{2,1,0:T(8,128)S(1)}, f32[2,64,768]{2,1,0:T(8,128)}, u32[]{:S(2)}) copy-start(f32[2,64,768]{2,1,0:T(8,128)} %get-tuple-element.32.here_ref) | copy-start | bytes 1179652
  98.2 13.4 %collective-permute-start.7 = (bf16[2,64,384]{2,1,0:T(8,128)(2,1)S(1)}, bf16[2,64,384]{2,1,0:T(8,128)(2,1)S(1)}, u32[]{:S(2)}, u32[]{:S(2)}) collective-permute-start(bf16[2,64,384]{2,1,0:T(8,128)(2,1)S(1)} %get-tuple-element.33), channel_id=1, source_target_pairs={{0,16},{1,49},{2,18},{3,51},{4,20},{5,53},{6,22},{7,55},{8,24},{9,... | collective-permute-start | bytes 294920 | tf_op jit(solution)/shard_map/ppermute | solution.py:59
  104.4 10.4 %collective-permute-start.8 = (bf16[2,64,384]{2,1,0:T(8,128)(2,1)S(1)}, bf16[2,64,384]{2,1,0:T(8,128)(2,1)S(1)}, u32[]{:S(2)}, u32[]{:S(2)}) collective-permute-start(bf16[2,64,384]{2,1,0:T(8,128)(2,1)S(1)} %get-tuple-element.34), channel_id=1, source_target_pairs={{0,17},{1,48},{2,19},{3,50},{4,21},{5,52},{6,23},{7,54},{8,25},{9,... | collective-permute-start | bytes 294920 | tf_op jit(solution)/shard_map/ppermute | solution.py:59
  109.6 5.3 %collective-permute-start.9 = (bf16[2,64,384]{2,1,0:T(8,128)(2,1)S(1)}, bf16[2,64,384]{2,1,0:T(8,128)(2,1)S(1)}, u32[]{:S(2)}, u32[]{:S(2)}) collective-permute-start(bf16[2,64,384]{2,1,0:T(8,128)(2,1)S(1)} %get-tuple-element.36), channel_id=1, source_target_pairs={{0,1},{1,0},{2,3},{3,2},{4,5},{5,4},{6,7},{7,6},{8,9},{9,8},{10,11... | collective-permute-start | bytes 294920 | tf_op jit(solution)/shard_map/ppermute | solution.py:50
Sparse Core Ops, SparseCore 0:
  10.1 71.1 all-gather.1

commit v13 on v12

--- a/solution.py
+++ b/solution.py
@@ -229,13 +229,14 @@
 
     moved = send(to_send, 2)
     grad_other = swap_cores(grad_blocks)
-    grad_weight = weight_gradient(False, input_whole, grad_blocks)
-    grad_weight = weight_gradient(True, input_whole, grad_other, grad_weight)
-    moved, grad_weight = lax.optimization_barrier((moved, grad_weight))
+    own_weight = weight_gradient(False, input_whole, grad_blocks)
+    moved, own_weight = lax.optimization_barrier((moved, own_weight))
     part = (2, half, width)
     outs = [jax.ShapeDtypeStruct(part, t) for t in (bf16, bf16, f32, bf16)]
     own, cross, stay, swapped = call(second_kernel, outs, (moved, middle, here))
     last = send(own, 4), send(cross, 4, cross=True), stay, swap_cores(swapped)
+    grad_weight = weight_gradient(True, input_whole, grad_other, own_weight)
+    last, grad_weight = lax.optimization_barrier((last, grad_weight))
     outs = [jax.ShapeDtypeStruct((tokens, width), bf16)]
     grad_input = call(third_kernel, outs, last)[0]
     return (grad_input, grad_weight)

time: 124 us -> 125 us (level)
  waiting for transfers between devices: 23.1 us -> 24.5 us
  transfers between devices with their start and end apart: 12 -> 12, of which waited for: 6 -> 7; matrix products, arithmetic and copies ran while one was open for 3% -> 3% of each run, Pallas kernels for 12% -> 12%
where the time goes in v13:
time: 125 us; the launch traced here: 124 us
  starting transfers between devices  52.3 us (42%)
  waiting for transfers between devices  24.5 us (20%)
  Pallas kernels  15.7 us (13%)
  between operations  14.1 us (11%)
  blocking collectives  12.9 us (10%)
  local copies, waits for them, and re-layouts  3.38 us (3%)
  other arithmetic  1.3 us (1%)
    ppermute x6, starting transfers between devices, send(): return lax.ppermute(values, ring, pairs)  32.5 us
    pallas_call x7, Pallas kernels, call(): pl.pallas_call(kernel, out_shape=outs, in_specs=[vmem] * len(args), out_s...  15.7 us
    ppermute x4, starting transfers between devices, swap_cores(): return lax.ppermute(values, 'rep', [(0, 1), (1, 0), (2, 3), (3, 2)])  15 us
    all_to_all x1, blocking collectives, gather(): parts = lax.all_to_all(copies, plane, 0, 0, axis_index_groups=groups)  12.9 us
    all_to_all x1, waiting for transfers between devices, gather(): parts = lax.all_to_all(copies, plane, 0, 0, axis_index_groups=groups)  10.7 us
    ppermute x6, waiting for transfers between devices, send(): return lax.ppermute(values, ring, pairs)  9.39 us
    all_to_all x1, starting transfers between devices, gather(): parts = lax.all_to_all(copies, plane, 0, 0, axis_index_groups=groups)  4.77 us
    ppermute x4, waiting for transfers between devices, swap_cores(): return lax.ppermute(values, 'rep', [(0, 1), (1, 0), (2, 3), (3, 2)])  3.64 us
  transfers between devices with their start and end apart: 12, of which 7 were waited for; matrix products, arithmetic and copies ran while one was open for 3% of the time, Pallas kernels for 12%

profile of v13, /device:TPU:1, one launch (start us, length us, event | category | flops | bytes accessed | tf_op | source)
XLA Modules:
  0.0 124.2 jit_solution(7797765035988346908)
XLA Ops:
  9.2 74.2 %conditional.1 = (bf16[2,2,64,768]{3,2,1,0:T(8,128)(2,1)}, f32[2,64,768]{2,1,0:T(8,128)}, f32[2,64,768]{2,1,0:T(8,128)}, bf16[16,64,1536]{2,1,0:T(8,128)(2,1)}) conditional(s32[]{:T(128)} %convert_element_type.12, () %tuple.19, (bf16[64,1536]{1,0:T(8,128)(2,1)S(1)}, bf16[384,1536]{1,0:T(8,128)(2,1)}) %tuple.20), branch_computations={%region_0.0_spmd, %region_1.0_spmd} | conditional | flops 7247757312 | bytes 45416740 | solution.py:157
  9.3 12.9 %all_to_all.8 = bf16[4,64,1536]{2,1,0:T(8,128)(2,1)S(1)} all-to-all(bf16[4,64,1536]{2,1,0:T(8,128)(2,1)S(1)} %broadcast_in_dim.0), channel_id=1, replica_groups={{0,128,256,384},{2,130,258,386},{64,192,320,448},{66,194,322,450},{1,3,..., dimensions={0} | all-to-all | bytes 1572864 | tf_op jit(solution)/shard_map/cond/branch_1_fun/all_to_all | solution.py:45
  22.1 1.9 %broadcast_in_dim.2 = bf16[4,256,1536]{2,1,0:T(8,128)(2,1)} broadcast(bf16[256,1536]{1,0:T(8,128)(2,1)S(1)} %bitcast.5), dimensions={1,2} | broadcast | bytes 3932160 | tf_op jit(solution)/shard_map/cond/branch_1_fun/broadcast_in_dim | solution.py:44
  24.0 4.8 %all-to-all-start.1 = ((bf16[4,256,1536]{2,1,0:T(8,128)(2,1)}), bf16[4,256,1536]{2,1,0:T(8,128)(2,1)}, u32[]{:S(2)}, u32[]{:S(2)}) async-start(bf16[4,256,1536]{2,1,0:T(8,128)(2,1)} %broadcast_in_dim.2), calls=%async_computation.1 | async-start | bytes 6291456 | tf_op jit(solution)/shard_map/cond/branch_1_fun/all_to_all | solution.py:45
  28.8 7.8 %collective-permute-start = (bf16[384,1536]{1,0:T(8,128)(2,1)S(1)}, bf16[384,1536]{1,0:T(8,128)(2,1)S(1)}, u32[]{:S(2)}, u32[]{:S(2)}) collective-permute-start(bf16[384,1536]{1,0:T(8,128)(2,1)S(1)} %copy-done.4), channel_id=1, source_target_pairs={{0,1},{1,0},{2,3},{3,2},{4,5},{5,4},{6,7},{7,6},{8,9},{9,8},{10,11... | collective-permute-start | bytes 3538952 | tf_op jit(solution)/shard_map/cond/branch_1_fun/ppermute | solution.py:50
  36.7 2.5 %collective-permute-done.other_ref = bf16[384,1536]{1,0:T(8,128)(2,1)S(1)} collective-permute-done((bf16[384,1536]{1,0:T(8,128)(2,1)S(1)}, bf16[384,1536]{1,0:T(8,128)(2,1)S(1)}, u32[]{:S(2)}, u32[]{:S(2)}) %collective-permute-start) | collective-permute-done | bytes 1179680 | tf_op jit(solution)/shard_map/cond/branch_1_fun/ppermute | solution.py:50
  39.1 10.7 %all-to-all-done.1 = bf16[4,256,1536]{2,1,0:T(8,128)(2,1)} async-done(((bf16[4,256,1536]{2,1,0:T(8,128)(2,1)}), bf16[4,256,1536]{2,1,0:T(8,128)(2,1)}, u32[]{:S(2)}, u32[]{:S(2)}) %all-to-all-start.1) | async-done | bytes 3145760 | tf_op jit(solution)/shard_map/cond/branch_1_fun/all_to_all | solution.py:45
  49.9 3.9 %branch_1_fun.3 = (bf16[1,64,768]{2,1,0:T(8,128)(2,1)S(1)}, bf16[4,64,768]{2,1,0:T(8,128)(2,1)S(1)}, bf16[4,64,768]{2,1,0:T(8,128)(2,1)S(1)}) custom-call(bf16[16,64,1536]{2,1,0:T(8,128)(2,1)} %bitcast.1.grad_ref, bf16[384,1536]{1,0:T(8,128)(2,1)S(1)} %copy-done.4, bf16[384,1536]{1,0:T(8,128)(2,1)S(1)} %collective-permute-done.other_ref), custom_call_target="tpu_custom_call" | custom-call | flops 4076863488 | bytes 6389760 | tf_op jit(solution)/shard_map/cond/branch_1_fun/pallas_call | solution.py:73
  53.7 11.9 %collective-permute-start.3 = (bf16[1,64,768]{2,1,0:T(8,128)(2,1)S(1)}, bf16[1,64,768]{2,1,0:T(8,128)(2,1)S(1)}, u32[]{:S(2)}, u32[]{:S(2)}) collective-permute-start(bf16[1,64,768]{2,1,0:T(8,128)(2,1)S(1)} %get-tuple-element.10), channel_id=1, source_target_pairs={{0,8},{1,57},{2,10},{3,59},{4,12},{5,61},{6,14},{7,63},{8,16},{9,1... | collective-permute-start | bytes 294920 | tf_op jit(solution)/shard_map/cond/branch_1_fun/ppermute | solution.py:59
  65.6 2.6 %collective-permute-start.1 = (bf16[4,64,768]{2,1,0:T(8,128)(2,1)S(1)}, bf16[4,64,768]{2,1,0:T(8,128)(2,1)S(1)}, u32[]{:S(2)}, u32[]{:S(2)}) collective-permute-start(bf16[4,64,768]{2,1,0:T(8,128)(2,1)S(1)} %get-tuple-element.6), channel_id=1, source_target_pairs={{0,4},{1,61},{2,6},{3,63},{4,8},{5,1},{6,10},{7,3},{8,12},{9,5},{1... | collective-permute-start | bytes 1179656 | tf_op jit(solution)/shard_map/cond/branch_1_fun/ppermute | solution.py:59
  68.3 2.3 %collective-permute-start.2 = (bf16[4,64,768]{2,1,0:T(8,128)(2,1)S(1)}, bf16[4,64,768]{2,1,0:T(8,128)(2,1)S(1)}, u32[]{:S(2)}, u32[]{:S(2)}) collective-permute-start(bf16[4,64,768]{2,1,0:T(8,128)(2,1)S(1)} %get-tuple-element.7), channel_id=1, source_target_pairs={{0,61},{1,4},{2,63},{3,6},{4,1},{5,8},{6,3},{7,10},{8,5},{9,12},{1... | collective-permute-start | bytes 1179656 | tf_op jit(solution)/shard_map/cond/branch_1_fun/ppermute | solution.py:59
  70.5 3.5 %branch_1_fun.4 = (bf16[4,64,768]{2,1,0:T(8,128)(2,1)S(1)}, bf16[3,64,768]{2,1,0:T(8,128)(2,1)S(1)}) custom-call(bf16[16,64,1536]{2,1,0:T(8,128)(2,1)} %bitcast.1.grad_ref, bf16[384,1536]{1,0:T(8,128)(2,1)S(1)} %copy-done.4, bf16[384,1536]{1,0:T(8,128)(2,1)S(1)} %collective-permute-done.other_ref, bf16[1,64,768]{2,1,0:T(8,128)(2,1)S(1)} %collective-permute-done.3.refs_0_), custom_call_target="tpu_custom_call" | custom-call | flops 3170893824 | bytes 6291456 | tf_op jit(solution)/shard_map/cond/branch_1_fun/pallas_call | solution.py:73
  74.0 3.4 %collective-permute-start.4 = (bf16[3,64,768]{2,1,0:T(8,128)(2,1)S(1)}, bf16[3,64,768]{2,1,0:T(8,128)(2,1)S(1)}, u32[]{:S(2)}, u32[]{:S(2)}) collective-permute-start(bf16[3,64,768]{2,1,0:T(8,128)(2,1)S(1)} %get-tuple-element.12), channel_id=1, source_target_pairs={{0,1},{1,0},{2,3},{3,2},{4,5},{5,4},{6,7},{7,6},{8,9},{9,8},{10,11... | collective-permute-start | bytes 884744 | tf_op jit(solution)/shard_map/cond/branch_1_fun/ppermute | solution.py:50
  79.4 2.9 %collective-permute-done.2.cross_ref = bf16[4,64,768]{2,1,0:T(8,128)(2,1)S(1)} collective-permute-done((bf16[4,64,768]{2,1,0:T(8,128)(2,1)S(1)}, bf16[4,64,768]{2,1,0:T(8,128)(2,1)S(1)}, u32[]{:S(2)}, u32[]{:S(2)}) %collective-permute-start.2) | collective-permute-done | bytes 393248 | tf_op jit(solution)/shard_map/cond/branch_1_fun/ppermute | solution.py:59
  83.4 3.9 %collective-permute-start.5 = (bf16[2,2,64,768]{3,2,1,0:T(8,128)(2,1)}, bf16[2,2,64,768]{3,2,1,0:T(8,128)(2,1)S(1)}, u32[]{:S(2)}, u32[]{:S(2)}) collective-permute-start(bf16[2,2,64,768]{3,2,1,0:T(8,128)(2,1)} %get-tuple-element.33), channel_id=1, source_target_pairs={{0,8},{1,57},{2,10},{3,59},{4,12},{5,61},{6,14},{7,63},{8,16},{9,1... | collective-permute-start | bytes 1179656 | tf_op jit(solution)/shard_map/ppermute | solution.py:59
  87.3 1.9 %collective-permute-start.9 = (bf16[16,64,1536]{2,1,0:T(8,128)(2,1)}, bf16[16,64,1536]{2,1,0:T(8,128)(2,1)S(1)}, u32[]{:S(2)}, u32[]{:S(2)}) collective-permute-start(bf16[16,64,1536]{2,1,0:T(8,128)(2,1)} %get-tuple-element.34.grad_ref), channel_id=1, source_target_pairs={{0,1},{1,0},{2,3},{3,2},{4,5},{5,4},{6,7},{7,6},{8,9},{9,8},{10,11... | collective-permute-start | bytes 9437192 | tf_op jit(solution)/shard_map/ppermute | solution.py:50
  89.3 1.4 %copy-done = bf16[2048,384]{1,0:T(8,128)(2,1)S(1)} copy-done((bf16[2048,384]{1,0:T(8,128)(2,1)S(1)}, bf16[2048,384]{1,0:T(8,128)(2,1)}, u32[]{:S(2)}) %copy-start) | copy-done | bytes 1572888
  90.7 3.5 %shard_map.60.refs_0_ = f32[384,1536]{1,0:T(8,128)S(1)} custom-call(bf16[16,2,64,384]{3,2,1,0:T(8,128)(2,1)S(1)} %bitcast.3, bf16[16,64,1536]{2,1,0:T(8,128)(2,1)} %get-tuple-element.34.grad_ref), custom_call_target="tpu_custom_call" | custom-call | flops 48318382080 | bytes 7077888 | tf_op jit(solution)/shard_map/pallas_call | solution.py:73
  94.3 3.3 %collective-permute-done.5.moved_ref = bf16[2,2,64,768]{3,2,1,0:T(8,128)(2,1)S(1)} collective-permute-done((bf16[2,2,64,768]{3,2,1,0:T(8,128)(2,1)}, bf16[2,2,64,768]{3,2,1,0:T(8,128)(2,1)S(1)}, u32[]{:S(2)}, u32[]{:S(2)}) %collective-permute-start.5) | collective-permute-done | bytes 393248 | tf_op jit(solution)/shard_map/ppermute | solution.py:59
  97.6 5.9 %collective-permute-start.6 = (bf16[2,64,384]{2,1,0:T(8,128)(2,1)S(1)}, bf16[2,64,384]{2,1,0:T(8,128)(2,1)S(1)}, u32[]{:S(2)}, u32[]{:S(2)}) collective-permute-start(bf16[2,64,384]{2,1,0:T(8,128)(2,1)S(1)} %get-tuple-element.38), channel_id=1, source_target_pairs={{0,16},{1,49},{2,18},{3,51},{4,20},{5,53},{6,22},{7,55},{8,24},{9,... | collective-permute-start | bytes 294920 | tf_op jit(solution)/shard_map/ppermute | solution.py:59
  103.5 5.9 %collective-permute-start.7 = (bf16[2,64,384]{2,1,0:T(8,128)(2,1)S(1)}, bf16[2,64,384]{2,1,0:T(8,128)(2,1)S(1)}, u32[]{:S(2)}, u32[]{:S(2)}) collective-permute-start(bf16[2,64,384]{2,1,0:T(8,128)(2,1)S(1)} %get-tuple-element.39), channel_id=1, source_target_pairs={{0,17},{1,48},{2,19},{3,50},{4,21},{5,52},{6,23},{7,54},{8,25},{9,... | collective-permute-start | bytes 294920 | tf_op jit(solution)/shard_map/ppermute | solution.py:59
  109.4 1.9 %collective-permute-start.8 = (bf16[2,64,384]{2,1,0:T(8,128)(2,1)S(1)}, bf16[2,64,384]{2,1,0:T(8,128)(2,1)S(1)}, u32[]{:S(2)}, u32[]{:S(2)}) collective-permute-start(bf16[2,64,384]{2,1,0:T(8,128)(2,1)S(1)} %get-tuple-element.41), channel_id=1, source_target_pairs={{0,1},{1,0},{2,3},{3,2},{4,5},{5,4},{6,7},{7,6},{8,9},{9,8},{10,11... | collective-permute-start | bytes 294920 | tf_op jit(solution)/shard_map/ppermute | solution.py:50
  111.4 2.9 %shard_map.62 = f32[384,1536]{1,0:T(8,128)} custom-call(bf16[16,2,64,384]{3,2,1,0:T(8,128)(2,1)S(1)} %bitcast.4, bf16[16,64,1536]{2,1,0:T(8,128)(2,1)S(1)} %collective-permute-done.9.grad_ref, f32[384,1536]{1,0:T(8,128)S(1)} %shard_map.60.refs_0_), custom_call_target="tpu_custom_call" | custom-call | flops 1207959552 | bytes 9437184 | tf_op jit(solution)/shard_map/pallas_call | solution.py:73
  114.3 2.4 %collective-permute-done.7.cross_ref = bf16[2,64,384]{2,1,0:T(8,128)(2,1)S(1)} collective-permute-done((bf16[2,64,384]{2,1,0:T(8,128)(2,1)S(1)}, bf16[2,64,384]{2,1,0:T(8,128)(2,1)S(1)}, u32[]{:S(2)}, u32[]{:S(2)}) %collective-permute-start.7) | collective-permute-done | bytes 98336 | tf_op jit(solution)/shard_map/ppermute | solution.py:59
  (23 shorter events, 6.0 us)
Async XLA Ops:
  7.2 82.1 %all-gather.2.cloned.1.call-start = ((), (), s32[]{:S(2)}) async-start(), calls=%async_computation.2 | async-start | bytes 1671168 | tf_op jit(solution)/shard_map/all_gather | solution.py:225
  24.0 4.8 %copy-start.4 = (bf16[384,1536]{1,0:T(8,128)(2,1)S(1)}, bf16[384,1536]{1,0:T(8,128)(2,1)}, u32[]{:S(2)}) copy-start(bf16[384,1536]{1,0:T(8,128)(2,1)} %get-tuple-element.49.own_ref) | copy-start | bytes 3538948 | tf_op jit(solution)/shard_map/cond
  24.0 25.8 %all-to-all-start.1 = ((bf16[4,256,1536]{2,1,0:T(8,128)(2,1)}), bf16[4,256,1536]{2,1,0:T(8,128)(2,1)}, u32[]{:S(2)}, u32[]{:S(2)}) async-start(bf16[4,256,1536]{2,1,0:T(8,128)(2,1)} %broadcast_in_dim.2), calls=%async_computation.1 | async-start | bytes 6291456 | tf_op jit(solution)/shard_map/cond/branch_1_fun/all_to_all | solution.py:45
  28.8 10.3 %collective-permute-start = (bf16[384,1536]{1,0:T(8,128)(2,1)S(1)}, bf16[384,1536]{1,0:T(8,128)(2,1)S(1)}, u32[]{:S(2)}, u32[]{:S(2)}) collective-permute-start(bf16[384,1536]{1,0:T(8,128)(2,1)S(1)} %copy-done.4), channel_id=1, source_target_pairs={{0,1},{1,0},{2,3},{3,2},{4,5},{5,4},{6,7},{7,6},{8,9},{9,8},{10,11... | collective-permute-start | bytes 3538952 | tf_op jit(solution)/shard_map/cond/branch_1_fun/ppermute | solution.py:50
  53.7 16.8 %collective-permute-start.3 = (bf16[1,64,768]{2,1,0:T(8,128)(2,1)S(1)}, bf16[1,64,768]{2,1,0:T(8,128)(2,1)S(1)}, u32[]{:S(2)}, u32[]{:S(2)}) collective-permute-start(bf16[1,64,768]{2,1,0:T(8,128)(2,1)S(1)} %get-tuple-element.10), channel_id=1, source_target_pairs={{0,8},{1,57},{2,10},{3,59},{4,12},{5,61},{6,14},{7,63},{8,16},{9,1... | collective-permute-start | bytes 294920 | tf_op jit(solution)/shard_map/cond/branch_1_fun/ppermute | solution.py:59
  65.6 13.8 %collective-permute-start.1 = (bf16[4,64,768]{2,1,0:T(8,128)(2,1)S(1)}, bf16[4,64,768]{2,1,0:T(8,128)(2,1)S(1)}, u32[]{:S(2)}, u32[]{:S(2)}) collective-permute-start(bf16[4,64,768]{2,1,0:T(8,128)(2,1)S(1)} %get-tuple-element.6), channel_id=1, source_target_pairs={{0,4},{1,61},{2,6},{3,63},{4,8},{5,1},{6,10},{7,3},{8,12},{9,5},{1... | collective-permute-start | bytes 1179656 | tf_op jit(solution)/shard_map/cond/branch_1_fun/ppermute | solution.py:59
  68.3 14.0 %collective-permute-start.2 = (bf16[4,64,768]{2,1,0:T(8,128)(2,1)S(1)}, bf16[4,64,768]{2,1,0:T(8,128)(2,1)S(1)}, u32[]{:S(2)}, u32[]{:S(2)}) collective-permute-start(bf16[4,64,768]{2,1,0:T(8,128)(2,1)S(1)} %get-tuple-element.7), channel_id=1, source_target_pairs={{0,61},{1,4},{2,63},{3,6},{4,1},{5,8},{6,3},{7,10},{8,5},{9,12},{1... | collective-permute-start | bytes 1179656 | tf_op jit(solution)/shard_map/cond/branch_1_fun/ppermute | solution.py:59
  74.0 4.6 %collective-permute-start.4 = (bf16[3,64,768]{2,1,0:T(8,128)(2,1)S(1)}, bf16[3,64,768]{2,1,0:T(8,128)(2,1)S(1)}, u32[]{:S(2)}, u32[]{:S(2)}) collective-permute-start(bf16[3,64,768]{2,1,0:T(8,128)(2,1)S(1)} %get-tuple-element.12), channel_id=1, source_target_pairs={{0,1},{1,0},{2,3},{3,2},{4,5},{5,4},{6,7},{7,6},{8,9},{9,8},{10,11... | collective-permute-start | bytes 884744 | tf_op jit(solution)/shard_map/cond/branch_1_fun/ppermute | solution.py:50
  83.4 14.2 %collective-permute-start.5 = (bf16[2,2,64,768]{3,2,1,0:T(8,128)(2,1)}, bf16[2,2,64,768]{3,2,1,0:T(8,128)(2,1)S(1)}, u32[]{:S(2)}, u32[]{:S(2)}) collective-permute-start(bf16[2,2,64,768]{3,2,1,0:T(8,128)(2,1)} %get-tuple-element.33), channel_id=1, source_target_pairs={{0,8},{1,57},{2,10},{3,59},{4,12},{5,61},{6,14},{7,63},{8,16},{9,1... | collective-permute-start | bytes 1179656 | tf_op jit(solution)/shard_map/ppermute | solution.py:59
  87.3 24.0 %collective-permute-start.9 = (bf16[16,64,1536]{2,1,0:T(8,128)(2,1)}, bf16[16,64,1536]{2,1,0:T(8,128)(2,1)S(1)}, u32[]{:S(2)}, u32[]{:S(2)}) collective-permute-start(bf16[16,64,1536]{2,1,0:T(8,128)(2,1)} %get-tuple-element.34.grad_ref), channel_id=1, source_target_pairs={{0,1},{1,0},{2,3},{3,2},{4,5},{5,4},{6,7},{7,6},{8,9},{9,8},{10,11... | collective-permute-start | bytes 9437192 | tf_op jit(solution)/shard_map/ppermute | solution.py:50
  89.3 1.4 %copy-start = (bf16[2048,384]{1,0:T(8,128)(2,1)S(1)}, bf16[2048,384]{1,0:T(8,128)(2,1)}, u32[]{:S(2)}) copy-start(bf16[2048,384]{1,0:T(8,128)(2,1)} %all-gather.2.cloned.1.call-done) | copy-start | bytes 4718596
  90.7 6.9 %copy-start.2 = (f32[2,64,768]{2,1,0:T(8,128)S(1)}, f32[2,64,768]{2,1,0:T(8,128)}, u32[]{:S(2)}) copy-start(f32[2,64,768]{2,1,0:T(8,128)} %get-tuple-element.37.here_ref) | copy-start | bytes 1179652
  90.7 6.9 %copy-start.3 = (f32[2,64,768]{2,1,0:T(8,128)S(1)}, f32[2,64,768]{2,1,0:T(8,128)}, u32[]{:S(2)}) copy-start(f32[2,64,768]{2,1,0:T(8,128)} %get-tuple-element.36.middle_ref) | copy-start | bytes 1179652
  90.7 20.7 %copy-start.1 = (bf16[2048,384]{1,0:T(8,128)(2,1)S(1)}, bf16[2048,384]{1,0:T(8,128)(2,1)}, u32[]{:S(2)}) copy-start(bf16[2048,384]{1,0:T(8,128)(2,1)} %all-gather.2.cloned.1.call-done) | copy-start | bytes 4718596
  97.6 16.7 %collective-permute-start.6 = (bf16[2,64,384]{2,1,0:T(8,128)(2,1)S(1)}, bf16[2,64,384]{2,1,0:T(8,128)(2,1)S(1)}, u32[]{:S(2)}, u32[]{:S(2)}) collective-permute-start(bf16[2,64,384]{2,1,0:T(8,128)(2,1)S(1)} %get-tuple-element.38), channel_id=1, source_target_pairs={{0,16},{1,49},{2,18},{3,51},{4,20},{5,53},{6,22},{7,55},{8,24},{9,... | collective-permute-start | bytes 294920 | tf_op jit(solution)/shard_map/ppermute | solution.py:59
  103.5 13.1 %collective-permute-start.7 = (bf16[2,64,384]{2,1,0:T(8,128)(2,1)S(1)}, bf16[2,64,384]{2,1,0:T(8,128)(2,1)S(1)}, u32[]{:S(2)}, u32[]{:S(2)}) collective-permute-start(bf16[2,64,384]{2,1,0:T(8,128)(2,1)S(1)} %get-tuple-element.39), channel_id=1, source_target_pairs={{0,17},{1,48},{2,19},{3,50},{4,21},{5,52},{6,23},{7,54},{8,25},{9,... | collective-permute-start | bytes 294920 | tf_op jit(solution)/shard_map/ppermute | solution.py:59
  109.4 7.2 %collective-permute-start.8 = (bf16[2,64,384]{2,1,0:T(8,128)(2,1)S(1)}, bf16[2,64,384]{2,1,0:T(8,128)(2,1)S(1)}, u32[]{:S(2)}, u32[]{:S(2)}) collective-permute-start(bf16[2,64,384]{2,1,0:T(8,128)(2,1)S(1)} %get-tuple-element.41), channel_id=1, source_target_pairs={{0,1},{1,0},{2,3},{3,2},{4,5},{5,4},{6,7},{7,6},{8,9},{9,8},{10,11... | collective-permute-start | bytes 294920 | tf_op jit(solution)/shard_map/ppermute | solution.py:50
Sparse Core Ops, SparseCore 0:
  10.1 71.7 all-gather.1

commit v14 on v12

--- a/solution.py
+++ b/solution.py
@@ -118,12 +118,14 @@
     )
 
 
-def first_kernel(own_ref, cross_ref, rest_ref, other_ref, send_ref, middle_ref, here_ref):
+def first_kernel(own_ref, cross_ref, far_ref, rest_ref, other_ref, *outs):
+    send_ref, middle_ref, here_ref = outs
+
     def total(i, *refs):
         return sum(ref[i].astype(jnp.float32) for ref in refs)
 
     dtype = send_ref.dtype
-    send_ref[0, 0] = total(0, own_ref, rest_ref).astype(dtype)
+    send_ref[0, 0] = (total(0, own_ref, rest_ref) + far_ref[0].astype(jnp.float32)).astype(dtype)
     send_ref[0, 1] = total(0, cross_ref, other_ref).astype(dtype)
     send_ref[1, 0] = total(2, own_ref, rest_ref).astype(dtype)
     send_ref[1, 1] = total(2, cross_ref, other_ref).astype(dtype)
@@ -173,7 +175,7 @@
     far, later_blocks = lax.optimization_barrier((far, grad_blocks))
     far = send(far, 2)
     own, cross = send(ahead, 1), send(behind, -1, cross=True)
-    rest, for_sibling = partials(late_groups, (7,), later_blocks, weights, far)
+    rest, for_sibling = partials(late_groups, (7,), later_blocks, weights)
     rest_other = swap_cores(for_sibling)
 
     both = (2,) + rest.shape[1:]
@@ -182,7 +184,7 @@
         jax.ShapeDtypeStruct(both, jnp.float32),
         jax.ShapeDtypeStruct(both, jnp.float32),
     ]
-    return (*call(first_kernel, outs, (own, cross, rest, rest_other)), grad_blocks)
+    return (*call(first_kernel, outs, (own, cross, far, rest, rest_other)), grad_blocks)
 
 
 def weight_kernel(sibling, input_ref, grad_ref, *refs):

time: 124 us -> 125 us (level)
  starting transfers between devices: 52 us -> 56.5 us
  waiting for transfers between devices: 23.1 us -> 19.3 us
    ppermute x6, starting transfers between devices: 32.1 us -> 37 us  [send(): return lax.ppermute(values, ring, pairs)]
    ppermute x6, waiting for transfers between devices: 8.24 us -> 4.4 us  [send(): return lax.ppermute(values, ring, pairs)]
  transfers between devices with their start and end apart: 12 -> 12, of which waited for: 6 -> 5; matrix products, arithmetic and copies ran while one was open for 3% -> 3% of each run, Pallas kernels for 12% -> 12%
where the time goes in v14:
time: 125 us; the launch traced here: 123 us
  starting transfers between devices  56.5 us (45%)
  waiting for transfers between devices  19.3 us (15%)
  Pallas kernels  15.6 us (12%)
  between operations  14.1 us (11%)
  blocking collectives  12.9 us (10%)
  local copies, waits for them, and re-layouts  3.4 us (3%)
  other arithmetic  1.3 us (1%)
    ppermute x6, starting transfers between devices, send(): return lax.ppermute(values, ring, pairs)  37 us
    pallas_call x7, Pallas kernels, call(): pl.pallas_call(kernel, out_shape=outs, in_specs=[vmem] * len(args), out_s...  15.6 us
    ppermute x4, starting transfers between devices, swap_cores(): return lax.ppermute(values, 'rep', [(0, 1), (1, 0), (2, 3), (3, 2)])  14.7 us
    all_to_all x1, blocking collectives, gather(): parts = lax.all_to_all(copies, plane, 0, 0, axis_index_groups=groups)  12.9 us
    all_to_all x1, waiting for transfers between devices, gather(): parts = lax.all_to_all(copies, plane, 0, 0, axis_index_groups=groups)  10.7 us
    all_to_all x1, starting transfers between devices, gather(): parts = lax.all_to_all(copies, plane, 0, 0, axis_index_groups=groups)  4.77 us
    ppermute x6, waiting for transfers between devices, send(): return lax.ppermute(values, ring, pairs)  4.4 us
    ppermute x4, waiting for transfers between devices, swap_cores(): return lax.ppermute(values, 'rep', [(0, 1), (1, 0), (2, 3), (3, 2)])  3.43 us
  transfers between devices with their start and end apart: 12, of which 5 were waited for; matrix products, arithmetic and copies ran while one was open for 3% of the time, Pallas kernels for 12%

profile of v14, /device:TPU:1, one launch (start us, length us, event | category | flops | bytes accessed | tf_op | source)
XLA Modules:
  0.0 123.1 jit_solution(8802602100571916131)
XLA Ops:
  7.9 1.3 %fusion.7 = bf16[64,1536]{1,0:T(8,128)(2,1)S(1)} fusion(bf16[64,1536]{1,0:T(8,128)(2,1)} %param.8, bf16[64,1536]{1,0:T(8,128)(2,1)} %param.9), kind=kLoop, calls=%fused_computation.14 | loop fusion | flops 2064384 | bytes 589824 | tf_op jit(solution)/shard_map/convert_element_type | solution.py:228
  9.2 73.3 %conditional.1 = (bf16[2,2,64,768]{3,2,1,0:T(8,128)(2,1)}, f32[2,64,768]{2,1,0:T(8,128)}, f32[2,64,768]{2,1,0:T(8,128)}, bf16[16,64,1536]{2,1,0:T(8,128)(2,1)}) conditional(s32[]{:T(128)} %convert_element_type.12, () %tuple.18, (bf16[64,1536]{1,0:T(8,128)(2,1)S(1)}, bf16[384,1536]{1,0:T(8,128)(2,1)}) %tuple.19), branch_computations={%region_0.0_spmd, %region_1.0_spmd} | conditional | flops 7247757312 | bytes 45416740 | solution.py:159
  9.3 12.9 %all_to_all.8 = bf16[4,64,1536]{2,1,0:T(8,128)(2,1)S(1)} all-to-all(bf16[4,64,1536]{2,1,0:T(8,128)(2,1)S(1)} %broadcast_in_dim.0), channel_id=1, replica_groups={{0,128,256,384},{2,130,258,386},{64,192,320,448},{66,194,322,450},{1,3,..., dimensions={0} | all-to-all | bytes 1572864 | tf_op jit(solution)/shard_map/cond/branch_1_fun/all_to_all | solution.py:45
  22.1 1.9 %broadcast_in_dim.2 = bf16[4,256,1536]{2,1,0:T(8,128)(2,1)} broadcast(bf16[256,1536]{1,0:T(8,128)(2,1)S(1)} %bitcast.5), dimensions={1,2} | broadcast | bytes 3932160 | tf_op jit(solution)/shard_map/cond/branch_1_fun/broadcast_in_dim | solution.py:44
  24.1 4.8 %all-to-all-start.1 = ((bf16[4,256,1536]{2,1,0:T(8,128)(2,1)}), bf16[4,256,1536]{2,1,0:T(8,128)(2,1)}, u32[]{:S(2)}, u32[]{:S(2)}) async-start(bf16[4,256,1536]{2,1,0:T(8,128)(2,1)} %broadcast_in_dim.2), calls=%async_computation.1 | async-start | bytes 6291456 | tf_op jit(solution)/shard_map/cond/branch_1_fun/all_to_all | solution.py:45
  28.9 7.8 %collective-permute-start = (bf16[384,1536]{1,0:T(8,128)(2,1)S(1)}, bf16[384,1536]{1,0:T(8,128)(2,1)S(1)}, u32[]{:S(2)}, u32[]{:S(2)}) collective-permute-start(bf16[384,1536]{1,0:T(8,128)(2,1)S(1)} %copy-done.3), channel_id=1, source_target_pairs={{0,1},{1,0},{2,3},{3,2},{4,5},{5,4},{6,7},{7,6},{8,9},{9,8},{10,11... | collective-permute-start | bytes 3538952 | tf_op jit(solution)/shard_map/cond/branch_1_fun/ppermute | solution.py:50
  36.7 2.5 %collective-permute-done.other_ref = bf16[384,1536]{1,0:T(8,128)(2,1)S(1)} collective-permute-done((bf16[384,1536]{1,0:T(8,128)(2,1)S(1)}, bf16[384,1536]{1,0:T(8,128)(2,1)S(1)}, u32[]{:S(2)}, u32[]{:S(2)}) %collective-permute-start) | collective-permute-done | bytes 1179680 | tf_op jit(solution)/shard_map/cond/branch_1_fun/ppermute | solution.py:50
  39.1 10.7 %all-to-all-done.1 = bf16[4,256,1536]{2,1,0:T(8,128)(2,1)} async-done(((bf16[4,256,1536]{2,1,0:T(8,128)(2,1)}), bf16[4,256,1536]{2,1,0:T(8,128)(2,1)}, u32[]{:S(2)}, u32[]{:S(2)}) %all-to-all-start.1) | async-done | bytes 3145760 | tf_op jit(solution)/shard_map/cond/branch_1_fun/all_to_all | solution.py:45
  49.9 3.9 %branch_1_fun.3 = (bf16[1,64,768]{2,1,0:T(8,128)(2,1)S(1)}, bf16[4,64,768]{2,1,0:T(8,128)(2,1)S(1)}, bf16[4,64,768]{2,1,0:T(8,128)(2,1)S(1)}) custom-call(bf16[16,64,1536]{2,1,0:T(8,128)(2,1)} %bitcast.1.grad_ref, bf16[384,1536]{1,0:T(8,128)(2,1)S(1)} %copy-done.3, bf16[384,1536]{1,0:T(8,128)(2,1)S(1)} %collective-permute-done.other_ref), custom_call_target="tpu_custom_call" | custom-call | flops 4076863488 | bytes 6389760 | tf_op jit(solution)/shard_map/cond/branch_1_fun/pallas_call | solution.py:73
  53.8 11.4 %collective-permute-start.1 = (bf16[4,64,768]{2,1,0:T(8,128)(2,1)S(1)}, bf16[4,64,768]{2,1,0:T(8,128)(2,1)S(1)}, u32[]{:S(2)}, u32[]{:S(2)}) collective-permute-start(bf16[4,64,768]{2,1,0:T(8,128)(2,1)S(1)} %get-tuple-element.6), channel_id=1, source_target_pairs={{0,4},{1,61},{2,6},{3,63},{4,8},{5,1},{6,10},{7,3},{8,12},{9,5},{1... | collective-permute-start | bytes 1179656 | tf_op jit(solution)/shard_map/cond/branch_1_fun/ppermute | solution.py:59
  65.2 1.9 %collective-permute-start.2 = (bf16[4,64,768]{2,1,0:T(8,128)(2,1)S(1)}, bf16[4,64,768]{2,1,0:T(8,128)(2,1)S(1)}, u32[]{:S(2)}, u32[]{:S(2)}) collective-permute-start(bf16[4,64,768]{2,1,0:T(8,128)(2,1)S(1)} %get-tuple-element.7), channel_id=1, source_target_pairs={{0,61},{1,4},{2,63},{3,6},{4,1},{5,8},{6,3},{7,10},{8,5},{9,12},{1... | collective-permute-start | bytes 1179656 | tf_op jit(solution)/shard_map/cond/branch_1_fun/ppermute | solution.py:59
  67.1 3.5 %branch_1_fun.4 = (bf16[4,64,768]{2,1,0:T(8,128)(2,1)S(1)}, bf16[3,64,768]{2,1,0:T(8,128)(2,1)S(1)}) custom-call(bf16[16,64,1536]{2,1,0:T(8,128)(2,1)} %bitcast.1.grad_ref, bf16[384,1536]{1,0:T(8,128)(2,1)S(1)} %copy-done.3, bf16[384,1536]{1,0:T(8,128)(2,1)S(1)} %collective-permute-done.other_ref), custom_call_target="tpu_custom_call" | custom-call | flops 3170893824 | bytes 6193152 | tf_op jit(solution)/shard_map/cond/branch_1_fun/pallas_call | solution.py:73
  70.7 3.0 %collective-permute-start.4 = (bf16[3,64,768]{2,1,0:T(8,128)(2,1)S(1)}, bf16[3,64,768]{2,1,0:T(8,128)(2,1)S(1)}, u32[]{:S(2)}, u32[]{:S(2)}) collective-permute-start(bf16[3,64,768]{2,1,0:T(8,128)(2,1)S(1)} %get-tuple-element.12), channel_id=1, source_target_pairs={{0,1},{1,0},{2,3},{3,2},{4,5},{5,4},{6,7},{7,6},{8,9},{9,8},{10,11... | collective-permute-start | bytes 884744 | tf_op jit(solution)/shard_map/cond/branch_1_fun/ppermute | solution.py:50
  73.7 5.0 %collective-permute-start.3 = (bf16[1,64,768]{2,1,0:T(8,128)(2,1)S(1)}, bf16[1,64,768]{2,1,0:T(8,128)(2,1)S(1)}, u32[]{:S(2)}, u32[]{:S(2)}) collective-permute-start(bf16[1,64,768]{2,1,0:T(8,128)(2,1)S(1)} %get-tuple-element.9), channel_id=1, source_target_pairs={{0,8},{1,57},{2,10},{3,59},{4,12},{5,61},{6,14},{7,63},{8,16},{9,1... | collective-permute-start | bytes 294920 | tf_op jit(solution)/shard_map/cond/branch_1_fun/ppermute | solution.py:59
  78.7 2.6 %collective-permute-done.3.far_ref = bf16[1,64,768]{2,1,0:T(8,128)(2,1)S(1)} collective-permute-done((bf16[1,64,768]{2,1,0:T(8,128)(2,1)S(1)}, bf16[1,64,768]{2,1,0:T(8,128)(2,1)S(1)}, u32[]{:S(2)}, u32[]{:S(2)}) %collective-permute-start.3) | collective-permute-done | bytes 98336 | tf_op jit(solution)/shard_map/cond/branch_1_fun/ppermute | solution.py:59
  82.5 6.0 %collective-permute-start.5 = (bf16[2,2,64,768]{3,2,1,0:T(8,128)(2,1)}, bf16[2,2,64,768]{3,2,1,0:T(8,128)(2,1)S(1)}, u32[]{:S(2)}, u32[]{:S(2)}) collective-permute-start(bf16[2,2,64,768]{3,2,1,0:T(8,128)(2,1)} %get-tuple-element.28), channel_id=1, source_target_pairs={{0,8},{1,57},{2,10},{3,59},{4,12},{5,61},{6,14},{7,63},{8,16},{9,1... | collective-permute-start | bytes 1179656 | tf_op jit(solution)/shard_map/ppermute | solution.py:59
  88.5 1.9 %collective-permute-start.6 = (bf16[16,64,1536]{2,1,0:T(8,128)(2,1)}, bf16[16,64,1536]{2,1,0:T(8,128)(2,1)S(1)}, u32[]{:S(2)}, u32[]{:S(2)}) collective-permute-start(bf16[16,64,1536]{2,1,0:T(8,128)(2,1)} %get-tuple-element.29.grad_ref), channel_id=1, source_target_pairs={{0,1},{1,0},{2,3},{3,2},{4,5},{5,4},{6,7},{7,6},{8,9},{9,8},{10,11... | collective-permute-start | bytes 9437192 | tf_op jit(solution)/shard_map/ppermute | solution.py:50
  90.5 1.4 %copy-done = bf16[2048,384]{1,0:T(8,128)(2,1)S(1)} copy-done((bf16[2048,384]{1,0:T(8,128)(2,1)S(1)}, bf16[2048,384]{1,0:T(8,128)(2,1)}, u32[]{:S(2)}) %copy-start) | copy-done | bytes 1572888
  91.9 3.4 %shard_map.60.refs_0_ = f32[384,1536]{1,0:T(8,128)S(1)} custom-call(bf16[16,2,64,384]{3,2,1,0:T(8,128)(2,1)S(1)} %bitcast.3, bf16[16,64,1536]{2,1,0:T(8,128)(2,1)} %get-tuple-element.29.grad_ref), custom_call_target="tpu_custom_call" | custom-call | flops 48318382080 | bytes 7077888 | tf_op jit(solution)/shard_map/pallas_call | solution.py:73
  96.3 2.9 %shard_map.61 = f32[384,1536]{1,0:T(8,128)} custom-call(bf16[16,2,64,384]{3,2,1,0:T(8,128)(2,1)S(1)} %bitcast.4, bf16[16,64,1536]{2,1,0:T(8,128)(2,1)S(1)} %collective-permute-done.6.grad_ref, f32[384,1536]{1,0:T(8,128)S(1)} %shard_map.60.refs_0_), custom_call_target="tpu_custom_call" | custom-call | flops 1207959552 | bytes 9437184 | tf_op jit(solution)/shard_map/pallas_call | solution.py:73
  99.3 6.2 %collective-permute-start.7 = (bf16[2,64,384]{2,1,0:T(8,128)(2,1)S(1)}, bf16[2,64,384]{2,1,0:T(8,128)(2,1)S(1)}, u32[]{:S(2)}, u32[]{:S(2)}) collective-permute-start(bf16[2,64,384]{2,1,0:T(8,128)(2,1)S(1)} %get-tuple-element.33), channel_id=1, source_target_pairs={{0,16},{1,49},{2,18},{3,51},{4,20},{5,53},{6,22},{7,55},{8,24},{9,... | collective-permute-start | bytes 294920 | tf_op jit(solution)/shard_map/ppermute | solution.py:59
  105.4 6.4 %collective-permute-start.8 = (bf16[2,64,384]{2,1,0:T(8,128)(2,1)S(1)}, bf16[2,64,384]{2,1,0:T(8,128)(2,1)S(1)}, u32[]{:S(2)}, u32[]{:S(2)}) collective-permute-start(bf16[2,64,384]{2,1,0:T(8,128)(2,1)S(1)} %get-tuple-element.34), channel_id=1, source_target_pairs={{0,17},{1,48},{2,19},{3,50},{4,21},{5,52},{6,23},{7,54},{8,25},{9,... | collective-permute-start | bytes 294920 | tf_op jit(solution)/shard_map/ppermute | solution.py:59
  111.9 1.9 %collective-permute-start.9 = (bf16[2,64,384]{2,1,0:T(8,128)(2,1)S(1)}, bf16[2,64,384]{2,1,0:T(8,128)(2,1)S(1)}, u32[]{:S(2)}, u32[]{:S(2)}) collective-permute-start(bf16[2,64,384]{2,1,0:T(8,128)(2,1)S(1)} %get-tuple-element.36), channel_id=1, source_target_pairs={{0,1},{1,0},{2,3},{3,2},{4,5},{5,4},{6,7},{7,6},{8,9},{9,8},{10,11... | collective-permute-start | bytes 294920 | tf_op jit(solution)/shard_map/ppermute | solution.py:50
  113.8 1.7 %collective-permute-done.8.cross_ref = bf16[2,64,384]{2,1,0:T(8,128)(2,1)S(1)} collective-permute-done((bf16[2,64,384]{2,1,0:T(8,128)(2,1)S(1)}, bf16[2,64,384]{2,1,0:T(8,128)(2,1)S(1)}, u32[]{:S(2)}, u32[]{:S(2)}) %collective-permute-start.8) | collective-permute-done | bytes 98336 | tf_op jit(solution)/shard_map/ppermute | solution.py:59
  (21 shorter events, 3.7 us)
Async XLA Ops:
  7.2 83.3 %all-gather.2.cloned.1.call-start = ((), (), s32[]{:S(2)}) async-start(), calls=%async_computation.2 | async-start | bytes 1671168 | tf_op jit(solution)/shard_map/all_gather | solution.py:227
  24.1 4.8 %copy-start.3 = (bf16[384,1536]{1,0:T(8,128)(2,1)S(1)}, bf16[384,1536]{1,0:T(8,128)(2,1)}, u32[]{:S(2)}) copy-start(bf16[384,1536]{1,0:T(8,128)(2,1)} %get-tuple-element.39.own_ref) | copy-start | bytes 3538948 | tf_op jit(solution)/shard_map/cond
  24.1 25.8 %all-to-all-start.1 = ((bf16[4,256,1536]{2,1,0:T(8,128)(2,1)}), bf16[4,256,1536]{2,1,0:T(8,128)(2,1)}, u32[]{:S(2)}, u32[]{:S(2)}) async-start(bf16[4,256,1536]{2,1,0:T(8,128)(2,1)} %broadcast_in_dim.2), calls=%async_computation.1 | async-start | bytes 6291456 | tf_op jit(solution)/shard_map/cond/branch_1_fun/all_to_all | solution.py:45
  28.9 10.3 %collective-permute-start = (bf16[384,1536]{1,0:T(8,128)(2,1)S(1)}, bf16[384,1536]{1,0:T(8,128)(2,1)S(1)}, u32[]{:S(2)}, u32[]{:S(2)}) collective-permute-start(bf16[384,1536]{1,0:T(8,128)(2,1)S(1)} %copy-done.3), channel_id=1, source_target_pairs={{0,1},{1,0},{2,3},{3,2},{4,5},{5,4},{6,7},{7,6},{8,9},{9,8},{10,11... | collective-permute-start | bytes 3538952 | tf_op jit(solution)/shard_map/cond/branch_1_fun/ppermute | solution.py:50
  53.8 27.6 %collective-permute-start.1 = (bf16[4,64,768]{2,1,0:T(8,128)(2,1)S(1)}, bf16[4,64,768]{2,1,0:T(8,128)(2,1)S(1)}, u32[]{:S(2)}, u32[]{:S(2)}) collective-permute-start(bf16[4,64,768]{2,1,0:T(8,128)(2,1)S(1)} %get-tuple-element.6), channel_id=1, source_target_pairs={{0,4},{1,61},{2,6},{3,63},{4,8},{5,1},{6,10},{7,3},{8,12},{9,5},{1... | collective-permute-start | bytes 1179656 | tf_op jit(solution)/shard_map/cond/branch_1_fun/ppermute | solution.py:59
  65.2 16.1 %collective-permute-start.2 = (bf16[4,64,768]{2,1,0:T(8,128)(2,1)S(1)}, bf16[4,64,768]{2,1,0:T(8,128)(2,1)S(1)}, u32[]{:S(2)}, u32[]{:S(2)}) collective-permute-start(bf16[4,64,768]{2,1,0:T(8,128)(2,1)S(1)} %get-tuple-element.7), channel_id=1, source_target_pairs={{0,61},{1,4},{2,63},{3,6},{4,1},{5,8},{6,3},{7,10},{8,5},{9,12},{1... | collective-permute-start | bytes 1179656 | tf_op jit(solution)/shard_map/cond/branch_1_fun/ppermute | solution.py:59
  70.7 10.7 %collective-permute-start.4 = (bf16[3,64,768]{2,1,0:T(8,128)(2,1)S(1)}, bf16[3,64,768]{2,1,0:T(8,128)(2,1)S(1)}, u32[]{:S(2)}, u32[]{:S(2)}) collective-permute-start(bf16[3,64,768]{2,1,0:T(8,128)(2,1)S(1)} %get-tuple-element.12), channel_id=1, source_target_pairs={{0,1},{1,0},{2,3},{3,2},{4,5},{5,4},{6,7},{7,6},{8,9},{9,8},{10,11... | collective-permute-start | bytes 884744 | tf_op jit(solution)/shard_map/cond/branch_1_fun/ppermute | solution.py:50
  73.7 7.7 %collective-permute-start.3 = (bf16[1,64,768]{2,1,0:T(8,128)(2,1)S(1)}, bf16[1,64,768]{2,1,0:T(8,128)(2,1)S(1)}, u32[]{:S(2)}, u32[]{:S(2)}) collective-permute-start(bf16[1,64,768]{2,1,0:T(8,128)(2,1)S(1)} %get-tuple-element.9), channel_id=1, source_target_pairs={{0,8},{1,57},{2,10},{3,59},{4,12},{5,61},{6,14},{7,63},{8,16},{9,1... | collective-permute-start | bytes 294920 | tf_op jit(solution)/shard_map/cond/branch_1_fun/ppermute | solution.py:59
  82.5 16.7 %collective-permute-start.5 = (bf16[2,2,64,768]{3,2,1,0:T(8,128)(2,1)}, bf16[2,2,64,768]{3,2,1,0:T(8,128)(2,1)S(1)}, u32[]{:S(2)}, u32[]{:S(2)}) collective-permute-start(bf16[2,2,64,768]{3,2,1,0:T(8,128)(2,1)} %get-tuple-element.28), channel_id=1, source_target_pairs={{0,8},{1,57},{2,10},{3,59},{4,12},{5,61},{6,14},{7,63},{8,16},{9,1... | collective-permute-start | bytes 1179656 | tf_op jit(solution)/shard_map/ppermute | solution.py:59
  88.5 7.8 %collective-permute-start.6 = (bf16[16,64,1536]{2,1,0:T(8,128)(2,1)}, bf16[16,64,1536]{2,1,0:T(8,128)(2,1)S(1)}, u32[]{:S(2)}, u32[]{:S(2)}) collective-permute-start(bf16[16,64,1536]{2,1,0:T(8,128)(2,1)} %get-tuple-element.29.grad_ref), channel_id=1, source_target_pairs={{0,1},{1,0},{2,3},{3,2},{4,5},{5,4},{6,7},{7,6},{8,9},{9,8},{10,11... | collective-permute-start | bytes 9437192 | tf_op jit(solution)/shard_map/ppermute | solution.py:50
  90.5 1.4 %copy-start = (bf16[2048,384]{1,0:T(8,128)(2,1)S(1)}, bf16[2048,384]{1,0:T(8,128)(2,1)}, u32[]{:S(2)}) copy-start(bf16[2048,384]{1,0:T(8,128)(2,1)} %all-gather.2.cloned.1.call-done) | copy-start | bytes 4718596
  95.3 3.9 %copy-start.1 = (f32[2,64,768]{2,1,0:T(8,128)S(1)}, f32[2,64,768]{2,1,0:T(8,128)}, u32[]{:S(2)}) copy-start(f32[2,64,768]{2,1,0:T(8,128)} %get-tuple-element.31.middle_ref) | copy-start | bytes 1179652
  95.3 3.9 %copy-start.2 = (f32[2,64,768]{2,1,0:T(8,128)S(1)}, f32[2,64,768]{2,1,0:T(8,128)}, u32[]{:S(2)}) copy-start(f32[2,64,768]{2,1,0:T(8,128)} %get-tuple-element.32.here_ref) | copy-start | bytes 1179652
  99.3 14.5 %collective-permute-start.7 = (bf16[2,64,384]{2,1,0:T(8,128)(2,1)S(1)}, bf16[2,64,384]{2,1,0:T(8,128)(2,1)S(1)}, u32[]{:S(2)}, u32[]{:S(2)}) collective-permute-start(bf16[2,64,384]{2,1,0:T(8,128)(2,1)S(1)} %get-tuple-element.33), channel_id=1, source_target_pairs={{0,16},{1,49},{2,18},{3,51},{4,20},{5,53},{6,22},{7,55},{8,24},{9,... | collective-permute-start | bytes 294920 | tf_op jit(solution)/shard_map/ppermute | solution.py:59
  105.4 10.1 %collective-permute-start.8 = (bf16[2,64,384]{2,1,0:T(8,128)(2,1)S(1)}, bf16[2,64,384]{2,1,0:T(8,128)(2,1)S(1)}, u32[]{:S(2)}, u32[]{:S(2)}) collective-permute-start(bf16[2,64,384]{2,1,0:T(8,128)(2,1)S(1)} %get-tuple-element.34), channel_id=1, source_target_pairs={{0,17},{1,48},{2,19},{3,50},{4,21},{5,52},{6,23},{7,54},{8,25},{9,... | collective-permute-start | bytes 294920 | tf_op jit(solution)/shard_map/ppermute | solution.py:59
  111.9 3.7 %collective-permute-start.9 = (bf16[2,64,384]{2,1,0:T(8,128)(2,1)S(1)}, bf16[2,64,384]{2,1,0:T(8,128)(2,1)S(1)}, u32[]{:S(2)}, u32[]{:S(2)}) collective-permute-start(bf16[2,64,384]{2,1,0:T(8,128)(2,1)S(1)} %get-tuple-element.36), channel_id=1, source_target_pairs={{0,1},{1,0},{2,3},{3,2},{4,5},{5,4},{6,7},{7,6},{8,9},{9,8},{10,11... | collective-permute-start | bytes 294920 | tf_op jit(solution)/shard_map/ppermute | solution.py:50
Sparse Core Ops, SparseCore 0:
  10.1 70.3 all-gather.1

commit v15 on v12

--- a/solution.py
+++ b/solution.py
@@ -40,8 +40,26 @@
     return jnp.where(core == 0, turned, chip)
 
 
-def gather(values, groups):
-    copies = jnp.broadcast_to(values[None], (4,) + values.shape)
+def copy_kernel(values_ref, out_ref, sems):
+    copies = [pltpu.make_async_copy(values_ref, out_ref.at[i], sems.at[i]) for i in range(4)]
+    for copy in copies:
+        copy.start()
+    for copy in copies:
+        copy.wait()
+
+
+def four_copies(values):
+    return pl.pallas_call(
+        copy_kernel,
+        out_shape=jax.ShapeDtypeStruct((4,) + values.shape, values.dtype),
+        in_specs=[pl.BlockSpec(memory_space=pltpu.VMEM)],
+        out_specs=pl.BlockSpec(memory_space=pl.ANY),
+        scratch_shapes=[pltpu.SemaphoreType.DMA((4,))],
+    )(values)
+
+
+def gather(values, groups, copied=False):
+    copies = four_copies(values) if copied else jnp.broadcast_to(values[None], (4,) + values.shape)
     parts = lax.all_to_all(copies, plane, 0, 0, axis_index_groups=groups)
     return parts.reshape((4 * values.shape[0],) + values.shape[1:])
 
@@ -165,7 +183,7 @@
 def gather_and_round(gelu_grad, weight):
     line = gather(gelu_grad, along_x[0] + along_y[1])
     weight_other = swap_cores(weight)
-    grad_tokens = gather(line, along_y[0] + along_x[1])
+    grad_tokens = gather(line, along_y[0] + along_x[1], copied=True)
     grad_blocks = grad_tokens.reshape((16,) + gelu_grad.shape)
 
     weights = weight, weight_other

time: 124 us -> 126 us (1.016)
  the two profiles are of different devices: /device:TPU:1 before, /device:TPU:2 now
where the time goes in v15:
time: 126 us; the launch traced here: 125 us
  waiting for transfers between devices  36.6 us (29%)
  starting transfers between devices  36 us (29%)
  Pallas kernels  18.4 us (15%)
  blocking collectives  17.1 us (14%)
  between operations  14.1 us (11%)
  local copies, waits for them, and re-layouts  1.48 us (1%)
  other arithmetic  1.3 us (1%)
    ppermute x6, starting transfers between devices, send(): return lax.ppermute(values, ring, pairs)  21.3 us
    all_to_all x1, waiting for transfers between devices, gather(): parts = lax.all_to_all(copies, plane, 0, 0, axis_index_groups=groups)  17.1 us
    all_to_all x1, blocking collectives, gather(): parts = lax.all_to_all(copies, plane, 0, 0, axis_index_groups=groups)  17.1 us
    pallas_call x7, Pallas kernels, call(): pl.pallas_call(kernel, out_shape=outs, in_specs=[vmem] * len(args), out_s...  15.6 us
    ppermute x6, waiting for transfers between devices, send(): return lax.ppermute(values, ring, pairs)  15.3 us
    ppermute x4, starting transfers between devices, swap_cores(): return lax.ppermute(values, 'rep', [(0, 1), (1, 0), (2, 3), (3, 2)])  9.82 us
    all_to_all x1, starting transfers between devices, gather(): parts = lax.all_to_all(copies, plane, 0, 0, axis_index_groups=groups)  4.78 us
    ppermute x4, waiting for transfers between devices, swap_cores(): return lax.ppermute(values, 'rep', [(0, 1), (1, 0), (2, 3), (3, 2)])  3.22 us
  transfers between devices with their start and end apart: 12, of which 8 were waited for; matrix products, arithmetic and copies ran while one was open for 1% of the time, Pallas kernels for 14%

profile of v15, /device:TPU:2, one launch (start us, length us, event | category | flops | bytes accessed | tf_op | source)
XLA Modules:
  0.0 125.0 jit_solution(16584483016372033574)
XLA Ops:
  7.9 1.3 %fusion.7 = bf16[64,1536]{1,0:T(8,128)(2,1)S(1)} fusion(bf16[64,1536]{1,0:T(8,128)(2,1)} %param.8, bf16[64,1536]{1,0:T(8,128)(2,1)} %param.9), kind=kLoop, calls=%fused_computation.14 | loop fusion | flops 2064384 | bytes 589824 | tf_op jit(solution)/shard_map/convert_element_type | solution.py:244
  9.2 74.7 %conditional.1 = (bf16[2,2,64,768]{3,2,1,0:T(8,128)(2,1)}, f32[2,64,768]{2,1,0:T(8,128)}, f32[2,64,768]{2,1,0:T(8,128)}, bf16[16,64,1536]{2,1,0:T(8,128)(2,1)}) conditional(s32[]{:T(128)} %convert_element_type.12, () %tuple.18, (bf16[64,1536]{1,0:T(8,128)(2,1)S(1)}, bf16[384,1536]{1,0:T(8,128)(2,1)}) %tuple.19), branch_computations={%region_0.0_spmd, %region_1.0_spmd} | conditional | flops 7247757312 | bytes 41484580 | solution.py:175
  9.3 17.1 %all_to_all.8 = bf16[4,64,1536]{2,1,0:T(8,128)(2,1)} all-to-all(bf16[4,64,1536]{2,1,0:T(8,128)(2,1)S(1)} %broadcast_in_dim.0), channel_id=1, replica_groups={{0,128,256,384},{2,130,258,386},{64,192,320,448},{66,194,322,450},{1,3,..., dimensions={0} | all-to-all | bytes 1572864 | tf_op jit(solution)/shard_map/cond/branch_1_fun/all_to_all | solution.py:63
  26.3 2.9 %branch_1_fun.4 = bf16[4,256,1536]{2,1,0:T(8,128)(2,1)} custom-call(bf16[256,1536]{1,0:T(8,128)(2,1)} %bitcast.5), custom_call_target="tpu_custom_call" | custom-call | tf_op jit(solution)/shard_map/cond/branch_1_fun/pallas_call | solution.py:52
  29.2 4.8 %all-to-all-start.1 = ((bf16[4,256,1536]{2,1,0:T(8,128)(2,1)}), bf16[4,256,1536]{2,1,0:T(8,128)(2,1)}, u32[]{:S(2)}, u32[]{:S(2)}) async-start(bf16[4,256,1536]{2,1,0:T(8,128)(2,1)} %branch_1_fun.4), calls=%async_computation.1 | async-start | bytes 6291456 | tf_op jit(solution)/shard_map/cond/branch_1_fun/all_to_all | solution.py:63
  34.0 1.9 %collective-permute-start = (bf16[384,1536]{1,0:T(8,128)(2,1)S(1)}, bf16[384,1536]{1,0:T(8,128)(2,1)S(1)}, u32[]{:S(2)}, u32[]{:S(2)}) collective-permute-start(bf16[384,1536]{1,0:T(8,128)(2,1)S(1)} %copy-done.3), channel_id=1, source_target_pairs={{0,1},{1,0},{2,3},{3,2},{4,5},{5,4},{6,7},{7,6},{8,9},{9,8},{10,11... | collective-permute-start | bytes 3538952 | tf_op jit(solution)/shard_map/cond/branch_1_fun/ppermute | solution.py:68
  35.9 2.8 %collective-permute-done.other_ref = bf16[384,1536]{1,0:T(8,128)(2,1)S(1)} collective-permute-done((bf16[384,1536]{1,0:T(8,128)(2,1)S(1)}, bf16[384,1536]{1,0:T(8,128)(2,1)S(1)}, u32[]{:S(2)}, u32[]{:S(2)}) %collective-permute-start) | collective-permute-done | bytes 1179680 | tf_op jit(solution)/shard_map/cond/branch_1_fun/ppermute | solution.py:68
  38.7 17.1 %all-to-all-done.1 = bf16[4,256,1536]{2,1,0:T(8,128)(2,1)} async-done(((bf16[4,256,1536]{2,1,0:T(8,128)(2,1)}), bf16[4,256,1536]{2,1,0:T(8,128)(2,1)}, u32[]{:S(2)}, u32[]{:S(2)}) %all-to-all-start.1) | async-done | bytes 3145760 | tf_op jit(solution)/shard_map/cond/branch_1_fun/all_to_all | solution.py:63
  55.9 3.9 %branch_1_fun.5 = (bf16[1,64,768]{2,1,0:T(8,128)(2,1)S(1)}, bf16[4,64,768]{2,1,0:T(8,128)(2,1)S(1)}, bf16[4,64,768]{2,1,0:T(8,128)(2,1)S(1)}) custom-call(bf16[16,64,1536]{2,1,0:T(8,128)(2,1)} %bitcast.1.grad_ref, bf16[384,1536]{1,0:T(8,128)(2,1)S(1)} %copy-done.3, bf16[384,1536]{1,0:T(8,128)(2,1)S(1)} %collective-permute-done.other_ref), custom_call_target="tpu_custom_call" | custom-call | flops 4076863488 | bytes 6389760 | tf_op jit(solution)/shard_map/cond/branch_1_fun/pallas_call | solution.py:91
  59.8 1.9 %collective-permute-start.3 = (bf16[1,64,768]{2,1,0:T(8,128)(2,1)S(1)}, bf16[1,64,768]{2,1,0:T(8,128)(2,1)S(1)}, u32[]{:S(2)}, u32[]{:S(2)}) collective-permute-start(bf16[1,64,768]{2,1,0:T(8,128)(2,1)S(1)} %get-tuple-element.10), channel_id=1, source_target_pairs={{0,8},{1,57},{2,10},{3,59},{4,12},{5,61},{6,14},{7,63},{8,16},{9,1... | collective-permute-start | bytes 294920 | tf_op jit(solution)/shard_map/cond/branch_1_fun/ppermute | solution.py:77
  61.7 2.8 %collective-permute-start.1 = (bf16[4,64,768]{2,1,0:T(8,128)(2,1)S(1)}, bf16[4,64,768]{2,1,0:T(8,128)(2,1)S(1)}, u32[]{:S(2)}, u32[]{:S(2)}) collective-permute-start(bf16[4,64,768]{2,1,0:T(8,128)(2,1)S(1)} %get-tuple-element.6), channel_id=1, source_target_pairs={{0,4},{1,61},{2,6},{3,63},{4,8},{5,1},{6,10},{7,3},{8,12},{9,5},{1... | collective-permute-start | bytes 1179656 | tf_op jit(solution)/shard_map/cond/branch_1_fun/ppermute | solution.py:77
  64.5 5.7 %collective-permute-start.2 = (bf16[4,64,768]{2,1,0:T(8,128)(2,1)S(1)}, bf16[4,64,768]{2,1,0:T(8,128)(2,1)S(1)}, u32[]{:S(2)}, u32[]{:S(2)}) collective-permute-start(bf16[4,64,768]{2,1,0:T(8,128)(2,1)S(1)} %get-tuple-element.7), channel_id=1, source_target_pairs={{0,61},{1,4},{2,63},{3,6},{4,1},{5,8},{6,3},{7,10},{8,5},{9,12},{1... | collective-permute-start | bytes 1179656 | tf_op jit(solution)/shard_map/cond/branch_1_fun/ppermute | solution.py:77
  70.7 3.5 %branch_1_fun.6 = (bf16[4,64,768]{2,1,0:T(8,128)(2,1)S(1)}, bf16[3,64,768]{2,1,0:T(8,128)(2,1)S(1)}) custom-call(bf16[16,64,1536]{2,1,0:T(8,128)(2,1)} %bitcast.1.grad_ref, bf16[384,1536]{1,0:T(8,128)(2,1)S(1)} %copy-done.3, bf16[384,1536]{1,0:T(8,128)(2,1)S(1)} %collective-permute-done.other_ref, bf16[1,64,768]{2,1,0:T(8,128)(2,1)S(1)} %collective-permute-done.3.refs_0_), custom_call_target="tpu_custom_call" | custom-call | flops 3170893824 | bytes 6291456 | tf_op jit(solution)/shard_map/cond/branch_1_fun/pallas_call | solution.py:91
  74.2 1.9 %collective-permute-start.4 = (bf16[3,64,768]{2,1,0:T(8,128)(2,1)S(1)}, bf16[3,64,768]{2,1,0:T(8,128)(2,1)S(1)}, u32[]{:S(2)}, u32[]{:S(2)}) collective-permute-start(bf16[3,64,768]{2,1,0:T(8,128)(2,1)S(1)} %get-tuple-element.12), channel_id=1, source_target_pairs={{0,1},{1,0},{2,3},{3,2},{4,5},{5,4},{6,7},{7,6},{8,9},{9,8},{10,11... | collective-permute-start | bytes 884744 | tf_op jit(solution)/shard_map/cond/branch_1_fun/ppermute | solution.py:68
  76.1 6.7 %collective-permute-done.1.own_ref = bf16[4,64,768]{2,1,0:T(8,128)(2,1)S(1)} collective-permute-done((bf16[4,64,768]{2,1,0:T(8,128)(2,1)S(1)}, bf16[4,64,768]{2,1,0:T(8,128)(2,1)S(1)}, u32[]{:S(2)}, u32[]{:S(2)}) %collective-permute-start.1) | collective-permute-done | bytes 393248 | tf_op jit(solution)/shard_map/cond/branch_1_fun/ppermute | solution.py:77
  83.9 1.9 %collective-permute-start.5 = (bf16[2,2,64,768]{3,2,1,0:T(8,128)(2,1)}, bf16[2,2,64,768]{3,2,1,0:T(8,128)(2,1)S(1)}, u32[]{:S(2)}, u32[]{:S(2)}) collective-permute-start(bf16[2,2,64,768]{3,2,1,0:T(8,128)(2,1)} %get-tuple-element.28), channel_id=1, source_target_pairs={{0,8},{1,57},{2,10},{3,59},{4,12},{5,61},{6,14},{7,63},{8,16},{9,1... | collective-permute-start | bytes 1179656 | tf_op jit(solution)/shard_map/ppermute | solution.py:77
  85.8 2.6 %collective-permute-start.6 = (bf16[16,64,1536]{2,1,0:T(8,128)(2,1)}, bf16[16,64,1536]{2,1,0:T(8,128)(2,1)S(1)}, u32[]{:S(2)}, u32[]{:S(2)}) collective-permute-start(bf16[16,64,1536]{2,1,0:T(8,128)(2,1)} %get-tuple-element.29.grad_ref), channel_id=1, source_target_pairs={{0,1},{1,0},{2,3},{3,2},{4,5},{5,4},{6,7},{7,6},{8,9},{9,8},{10,11... | collective-permute-start | bytes 9437192 | tf_op jit(solution)/shard_map/ppermute | solution.py:68
  88.7 1.4 %copy-done = bf16[2048,384]{1,0:T(8,128)(2,1)S(1)} copy-done((bf16[2048,384]{1,0:T(8,128)(2,1)S(1)}, bf16[2048,384]{1,0:T(8,128)(2,1)}, u32[]{:S(2)}) %copy-start) | copy-done | bytes 1572888
  90.1 3.4 %shard_map.60.refs_0_ = f32[384,1536]{1,0:T(8,128)S(1)} custom-call(bf16[16,2,64,384]{3,2,1,0:T(8,128)(2,1)S(1)} %bitcast.3, bf16[16,64,1536]{2,1,0:T(8,128)(2,1)} %get-tuple-element.29.grad_ref), custom_call_target="tpu_custom_call" | custom-call | flops 48318382080 | bytes 7077888 | tf_op jit(solution)/shard_map/pallas_call | solution.py:91
  93.9 2.9 %shard_map.61 = f32[384,1536]{1,0:T(8,128)} custom-call(bf16[16,2,64,384]{3,2,1,0:T(8,128)(2,1)S(1)} %bitcast.4, bf16[16,64,1536]{2,1,0:T(8,128)(2,1)S(1)} %collective-permute-done.6.grad_ref, f32[384,1536]{1,0:T(8,128)S(1)} %shard_map.60.refs_0_), custom_call_target="tpu_custom_call" | custom-call | flops 1207959552 | bytes 9437184 | tf_op jit(solution)/shard_map/pallas_call | solution.py:91
  98.0 7.1 %collective-permute-start.7 = (bf16[2,64,384]{2,1,0:T(8,128)(2,1)S(1)}, bf16[2,64,384]{2,1,0:T(8,128)(2,1)S(1)}, u32[]{:S(2)}, u32[]{:S(2)}) collective-permute-start(bf16[2,64,384]{2,1,0:T(8,128)(2,1)S(1)} %get-tuple-element.33), channel_id=1, source_target_pairs={{0,16},{1,49},{2,18},{3,51},{4,20},{5,53},{6,22},{7,55},{8,24},{9,... | collective-permute-start | bytes 294920 | tf_op jit(solution)/shard_map/ppermute | solution.py:77
  105.0 1.9 %collective-permute-start.8 = (bf16[2,64,384]{2,1,0:T(8,128)(2,1)S(1)}, bf16[2,64,384]{2,1,0:T(8,128)(2,1)S(1)}, u32[]{:S(2)}, u32[]{:S(2)}) collective-permute-start(bf16[2,64,384]{2,1,0:T(8,128)(2,1)S(1)} %get-tuple-element.34), channel_id=1, source_target_pairs={{0,17},{1,48},{2,19},{3,50},{4,21},{5,52},{6,23},{7,54},{8,25},{9,... | collective-permute-start | bytes 294920 | tf_op jit(solution)/shard_map/ppermute | solution.py:77
  107.0 3.4 %collective-permute-start.9 = (bf16[2,64,384]{2,1,0:T(8,128)(2,1)S(1)}, bf16[2,64,384]{2,1,0:T(8,128)(2,1)S(1)}, u32[]{:S(2)}, u32[]{:S(2)}) collective-permute-start(bf16[2,64,384]{2,1,0:T(8,128)(2,1)S(1)} %get-tuple-element.36), channel_id=1, source_target_pairs={{0,1},{1,0},{2,3},{3,2},{4,5},{5,4},{6,7},{7,6},{8,9},{9,8},{10,11... | collective-permute-start | bytes 294920 | tf_op jit(solution)/shard_map/ppermute | solution.py:68
  110.4 7.1 %collective-permute-done.8.cross_ref = bf16[2,64,384]{2,1,0:T(8,128)(2,1)S(1)} collective-permute-done((bf16[2,64,384]{2,1,0:T(8,128)(2,1)S(1)}, bf16[2,64,384]{2,1,0:T(8,128)(2,1)S(1)}, u32[]{:S(2)}, u32[]{:S(2)}) %collective-permute-start.8) | collective-permute-done | bytes 98336 | tf_op jit(solution)/shard_map/ppermute | solution.py:77
  (21 shorter events, 4.8 us)
Async XLA Ops:
  7.2 81.5 %all-gather.2.cloned.1.call-start = ((), (), s32[]{:S(2)}) async-start(), calls=%async_computation.2 | async-start | bytes 1671168 | tf_op jit(solution)/shard_map/all_gather | solution.py:243
  29.2 4.8 %copy-start.3 = (bf16[384,1536]{1,0:T(8,128)(2,1)S(1)}, bf16[384,1536]{1,0:T(8,128)(2,1)}, u32[]{:S(2)}) copy-start(bf16[384,1536]{1,0:T(8,128)(2,1)} %get-tuple-element.39.own_ref) | copy-start | bytes 3538948 | tf_op jit(solution)/shard_map/cond
  29.2 26.7 %all-to-all-start.1 = ((bf16[4,256,1536]{2,1,0:T(8,128)(2,1)}), bf16[4,256,1536]{2,1,0:T(8,128)(2,1)}, u32[]{:S(2)}, u32[]{:S(2)}) async-start(bf16[4,256,1536]{2,1,0:T(8,128)(2,1)} %branch_1_fun.4), calls=%async_computation.1 | async-start | bytes 6291456 | tf_op jit(solution)/shard_map/cond/branch_1_fun/all_to_all | solution.py:63
  34.0 4.7 %collective-permute-start = (bf16[384,1536]{1,0:T(8,128)(2,1)S(1)}, bf16[384,1536]{1,0:T(8,128)(2,1)S(1)}, u32[]{:S(2)}, u32[]{:S(2)}) collective-permute-start(bf16[384,1536]{1,0:T(8,128)(2,1)S(1)} %copy-done.3), channel_id=1, source_target_pairs={{0,1},{1,0},{2,3},{3,2},{4,5},{5,4},{6,7},{7,6},{8,9},{9,8},{10,11... | collective-permute-start | bytes 3538952 | tf_op jit(solution)/shard_map/cond/branch_1_fun/ppermute | solution.py:68
  59.8 10.9 %collective-permute-start.3 = (bf16[1,64,768]{2,1,0:T(8,128)(2,1)S(1)}, bf16[1,64,768]{2,1,0:T(8,128)(2,1)S(1)}, u32[]{:S(2)}, u32[]{:S(2)}) collective-permute-start(bf16[1,64,768]{2,1,0:T(8,128)(2,1)S(1)} %get-tuple-element.10), channel_id=1, source_target_pairs={{0,8},{1,57},{2,10},{3,59},{4,12},{5,61},{6,14},{7,63},{8,16},{9,1... | collective-permute-start | bytes 294920 | tf_op jit(solution)/shard_map/cond/branch_1_fun/ppermute | solution.py:77
  61.7 21.1 %collective-permute-start.1 = (bf16[4,64,768]{2,1,0:T(8,128)(2,1)S(1)}, bf16[4,64,768]{2,1,0:T(8,128)(2,1)S(1)}, u32[]{:S(2)}, u32[]{:S(2)}) collective-permute-start(bf16[4,64,768]{2,1,0:T(8,128)(2,1)S(1)} %get-tuple-element.6), channel_id=1, source_target_pairs={{0,4},{1,61},{2,6},{3,63},{4,8},{5,1},{6,10},{7,3},{8,12},{9,5},{1... | collective-permute-start | bytes 1179656 | tf_op jit(solution)/shard_map/cond/branch_1_fun/ppermute | solution.py:77
  64.5 18.3 %collective-permute-start.2 = (bf16[4,64,768]{2,1,0:T(8,128)(2,1)S(1)}, bf16[4,64,768]{2,1,0:T(8,128)(2,1)S(1)}, u32[]{:S(2)}, u32[]{:S(2)}) collective-permute-start(bf16[4,64,768]{2,1,0:T(8,128)(2,1)S(1)} %get-tuple-element.7), channel_id=1, source_target_pairs={{0,61},{1,4},{2,63},{3,6},{4,1},{5,8},{6,3},{7,10},{8,5},{9,12},{1... | collective-permute-start | bytes 1179656 | tf_op jit(solution)/shard_map/cond/branch_1_fun/ppermute | solution.py:77
  74.2 8.6 %collective-permute-start.4 = (bf16[3,64,768]{2,1,0:T(8,128)(2,1)S(1)}, bf16[3,64,768]{2,1,0:T(8,128)(2,1)S(1)}, u32[]{:S(2)}, u32[]{:S(2)}) collective-permute-start(bf16[3,64,768]{2,1,0:T(8,128)(2,1)S(1)} %get-tuple-element.12), channel_id=1, source_target_pairs={{0,1},{1,0},{2,3},{3,2},{4,5},{5,4},{6,7},{7,6},{8,9},{9,8},{10,11... | collective-permute-start | bytes 884744 | tf_op jit(solution)/shard_map/cond/branch_1_fun/ppermute | solution.py:68
  83.9 14.0 %collective-permute-start.5 = (bf16[2,2,64,768]{3,2,1,0:T(8,128)(2,1)}, bf16[2,2,64,768]{3,2,1,0:T(8,128)(2,1)S(1)}, u32[]{:S(2)}, u32[]{:S(2)}) collective-permute-start(bf16[2,2,64,768]{3,2,1,0:T(8,128)(2,1)} %get-tuple-element.28), channel_id=1, source_target_pairs={{0,8},{1,57},{2,10},{3,59},{4,12},{5,61},{6,14},{7,63},{8,16},{9,1... | collective-permute-start | bytes 1179656 | tf_op jit(solution)/shard_map/ppermute | solution.py:77
  85.8 8.1 %collective-permute-start.6 = (bf16[16,64,1536]{2,1,0:T(8,128)(2,1)}, bf16[16,64,1536]{2,1,0:T(8,128)(2,1)S(1)}, u32[]{:S(2)}, u32[]{:S(2)}) collective-permute-start(bf16[16,64,1536]{2,1,0:T(8,128)(2,1)} %get-tuple-element.29.grad_ref), channel_id=1, source_target_pairs={{0,1},{1,0},{2,3},{3,2},{4,5},{5,4},{6,7},{7,6},{8,9},{9,8},{10,11... | collective-permute-start | bytes 9437192 | tf_op jit(solution)/shard_map/ppermute | solution.py:68
  88.7 1.4 %copy-start = (bf16[2048,384]{1,0:T(8,128)(2,1)S(1)}, bf16[2048,384]{1,0:T(8,128)(2,1)}, u32[]{:S(2)}) copy-start(bf16[2048,384]{1,0:T(8,128)(2,1)} %all-gather.2.cloned.1.call-done) | copy-start | bytes 4718596
  93.5 4.4 %copy-start.1 = (f32[2,64,768]{2,1,0:T(8,128)S(1)}, f32[2,64,768]{2,1,0:T(8,128)}, u32[]{:S(2)}) copy-start(f32[2,64,768]{2,1,0:T(8,128)} %get-tuple-element.31.middle_ref) | copy-start | bytes 1179652
  93.5 4.4 %copy-start.2 = (f32[2,64,768]{2,1,0:T(8,128)S(1)}, f32[2,64,768]{2,1,0:T(8,128)}, u32[]{:S(2)}) copy-start(f32[2,64,768]{2,1,0:T(8,128)} %get-tuple-element.32.here_ref) | copy-start | bytes 1179652
  98.0 12.4 %collective-permute-start.7 = (bf16[2,64,384]{2,1,0:T(8,128)(2,1)S(1)}, bf16[2,64,384]{2,1,0:T(8,128)(2,1)S(1)}, u32[]{:S(2)}, u32[]{:S(2)}) collective-permute-start(bf16[2,64,384]{2,1,0:T(8,128)(2,1)S(1)} %get-tuple-element.33), channel_id=1, source_target_pairs={{0,16},{1,49},{2,18},{3,51},{4,20},{5,53},{6,22},{7,55},{8,24},{9,... | collective-permute-start | bytes 294920 | tf_op jit(solution)/shard_map/ppermute | solution.py:77
  105.0 12.4 %collective-permute-start.8 = (bf16[2,64,384]{2,1,0:T(8,128)(2,1)S(1)}, bf16[2,64,384]{2,1,0:T(8,128)(2,1)S(1)}, u32[]{:S(2)}, u32[]{:S(2)}) collective-permute-start(bf16[2,64,384]{2,1,0:T(8,128)(2,1)S(1)} %get-tuple-element.34), channel_id=1, source_target_pairs={{0,17},{1,48},{2,19},{3,50},{4,21},{5,52},{6,23},{7,54},{8,25},{9,... | collective-permute-start | bytes 294920 | tf_op jit(solution)/shard_map/ppermute | solution.py:77
  107.0 10.5 %collective-permute-start.9 = (bf16[2,64,384]{2,1,0:T(8,128)(2,1)S(1)}, bf16[2,64,384]{2,1,0:T(8,128)(2,1)S(1)}, u32[]{:S(2)}, u32[]{:S(2)}) collective-permute-start(bf16[2,64,384]{2,1,0:T(8,128)(2,1)S(1)} %get-tuple-element.36), channel_id=1, source_target_pairs={{0,1},{1,0},{2,3},{3,2},{4,5},{5,4},{6,7},{7,6},{8,9},{9,8},{10,11... | collective-permute-start | bytes 294920 | tf_op jit(solution)/shard_map/ppermute | solution.py:68
Sparse Core Ops, SparseCore 0:
  10.1 78.5 all-gather.1
